TPU v7x, 256 devices: a whole 4x4x8 slice. The times are simulated.
256 devices in a mesh: mem: 8 (over x, core), state: 32 (over y, z).
Axes of the slice: x: 4, y: 4, z: 8, core: 2. Of those that a mesh axis runs over, the one named last changes fastest.
Arguments:
- ensemble: float32 [512, 1024, 256], P('mem', 'state'), may hold values from -12 to 12
- spreading_coefficient: float32 [1024, 256], P('state'), may hold values from 0.1 to 0.24
- obs_anom: bfloat16 [32, 128, 512], P('state'), may hold values from -6 to 6
- obs_weight: bfloat16 [32, 128, 512], P('state'), may hold values from -6 to 6
- taper_table: float32 [8, 128, 128], replicated, may hold values from 0.1 to 1
- obs_block: int32 [2048, 4], P('state'), may hold values from 0 to 31, as said below
- taper_id: int32 [2048, 4], P('state'), may hold values from 0 to 7
Outputs:
- forecast: float32 [512, 1024, 256], P('mem', 'state')
Inputs may be any that keep to these rules, and one draw needn't show every extreme that they name: `obs_block`: the 4 block numbers of one tile are distinct.
All inputs are finite; a program needn't handle non-finite values.
Results may differ from a plain program's by a relative error of at most 0.00105.
Values may be sent and summed in bfloat16 or wider, within the bound.
No kernel may reach another device: no remote copies, remote signals or barrier semaphores. Data moves between devices by JAX's collectives and lax.ppermute only.
A program may use at most 64 MiB of HBM per device.

v0:
```python
import jax
import jax.numpy as jnp
from jax import lax
from jax.sharding import PartitionSpec as P

TILE = 128
SLOTS = 4
FSTEPS = 4


def padded_2(shard, sides, width):
    for axis, dim in sides:
        size, length = (lax.axis_size(axis), shard.shape[dim])
        up = [(i, (i + 1) % size) for i in range(size - 1)]
        down = [(j, i) for i, j in up]
        last = lax.slice_in_dim(shard, length - width, length, axis=dim)
        first = lax.slice_in_dim(shard, 0, width, axis=dim)
        before = lax.ppermute(last, axis, up)
        after = lax.ppermute(first, axis, down)
        shard = jnp.concatenate([before, shard, after], axis=dim)
    return shard


def advance(model_variable, padded, smoothing_speed):
    beside_all = (
        padded[:, 2:]
        + padded[:, :-2]
        + jnp.roll(model_variable, 1, 2)
        + jnp.roll(model_variable, -1, 2)
    )
    return model_variable + smoothing_speed * (beside_all - 4.0 * model_variable)


def body(ensemble, spreading_coefficient, obs_anom, obs_weight, taper_table, obs_block, taper_id):
    rows = ensemble.shape[1]
    columns = ensemble.shape[2]
    every_anom, every_weight = (
        lax.all_gather(obs_anom, "state", axis=0, tiled=True),
        lax.all_gather(obs_weight, "state", axis=0, tiled=True),
    )
    model_variable = ensemble
    for number in range(FSTEPS):
        padded = padded_2(model_variable, (("state", 1),), 1)
        model_variable = advance(model_variable, padded, spreading_coefficient)
    members_here = model_variable.shape[0]
    tiles_slab = rows * columns // TILE
    blocks = model_variable.reshape(members_here, tiles_slab, TILE)
    gathered = lax.all_to_all(blocks, "mem", split_axis=1, concat_axis=0, tiled=True)
    centred = (gathered - jnp.mean(gathered, axis=0, keepdims=True)).astype(jnp.bfloat16)
    realizations = centred.shape[0]
    count = centred.shape[1]
    first_tile = lax.axis_index("mem") * count
    mine_block = lax.dynamic_slice_in_dim(obs_block, first_tile, count, 0)
    mine_taper = lax.dynamic_slice_in_dim(taper_id, first_tile, count, 0)
    denom = realizations - 1.0
    empty = jnp.zeros(centred.shape, jnp.float32)
    increment = empty
    for slot in range(SLOTS):
        chosen = mine_block[:, slot]
        anoms = every_anom[chosen]
        weights = every_weight[chosen]
        taper = taper_table[mine_taper[:, slot]]
        cov = jnp.einsum("mgc,gom->gco", centred, anoms, preferred_element_type=jnp.float32)
        tapered_update = (taper * (cov / denom)).astype(jnp.bfloat16)
        increment = increment + jnp.einsum(
            "gco,gom->mgc", tapered_update, weights, preferred_element_type=jnp.float32
        )
    updated = gathered + increment
    returned = lax.all_to_all(updated, "mem", split_axis=0, concat_axis=1, tiled=True)
    posterior_estimate = returned.reshape(members_here, rows, columns)
    padded = padded_2(posterior_estimate, (("state", 1),), 1)
    return advance(posterior_estimate, padded, spreading_coefficient)


def solution(mesh):
    placed = (
        P("mem", "state", None),
        P("state", None),
        P("state", None, None),
        P("state", None, None),
        P(),
        P("state", None),
        P("state", None),
    )
    return jax.shard_map(
        body, mesh=mesh, in_specs=placed, out_specs=P("mem", "state", None), check_vma=False
    )
```

profile of v0, /device:TPU:8, one launch (start us, length us, event | category | flops | bytes accessed | tf_op | source)
XLA Modules:
  0.0 281.3 jit_solution(15263932497082804095)
XLA Ops:
  9.3 7.7 %collective-permute-start = (f32[64,1,256]{2,1,0:T(1,128)S(1)}, f32[64,1,256]{2,1,0:T(1,128)S(1)}, u32[]{:S(2)}, u32[]{:S(2)}) collective-permute-start(f32[64,1,256]{2,1,0:T(1,128)S(1)} %get-tuple-element.33), channel_id=1, source_target_pairs={{1,0},{2,1},{3,2},{4,3},{5,4},{6,5},{7,6},{8,7},{9,8},{10,9},{11,1... | collective-permute-start | bytes 196616 | tf_op jit(solution)/shard_map/ppermute | solution.py:19
  27.3 3.4 %collective-permute-start.2 = (f32[64,1,256]{2,1,0:T(1,128)S(1)}, f32[64,1,256]{2,1,0:T(1,128)S(1)}, u32[]{:S(2)}, u32[]{:S(2)}) collective-permute-start(f32[64,1,256]{2,1,0:T(1,128)S(1)} %get-tuple-element.27), channel_id=1, source_target_pairs={{1,0},{2,1},{3,2},{4,3},{5,4},{6,5},{7,6},{8,7},{9,8},{10,9},{11,1... | collective-permute-start | bytes 196616 | tf_op jit(solution)/shard_map/ppermute | solution.py:19
  34.4 5.2 %collective-permute-done.3 = f32[64,1,256]{2,1,0:T(1,128)S(1)} collective-permute-done((f32[64,1,256]{2,1,0:T(1,128)S(1)}, f32[64,1,256]{2,1,0:T(1,128)S(1)}, u32[]{:S(2)}, u32[]{:S(2)}) %collective-permute-start.3) | collective-permute-done | bytes 65568 | tf_op jit(solution)/shard_map/ppermute | solution.py:18
  43.4 3.9 %collective-permute-start.5 = (f32[64,1,256]{2,1,0:T(1,128)S(1)}, f32[64,1,256]{2,1,0:T(1,128)S(1)}, u32[]{:S(2)}, u32[]{:S(2)}) collective-permute-start(f32[64,1,256]{2,1,0:T(1,128)S(1)} %get-tuple-element.22), channel_id=1, source_target_pairs={{0,1},{1,2},{2,3},{3,4},{4,5},{5,6},{6,7},{7,8},{8,9},{9,10},{10,1... | collective-permute-start | bytes 196616 | tf_op jit(solution)/shard_map/ppermute | solution.py:18
  55.5 3.9 %collective-permute-start.7 = (f32[64,1,256]{2,1,0:T(1,128)S(1)}, f32[64,1,256]{2,1,0:T(1,128)S(1)}, u32[]{:S(2)}, u32[]{:S(2)}) collective-permute-start(f32[64,1,256]{2,1,0:T(1,128)S(1)} %get-tuple-element.16), channel_id=1, source_target_pairs={{0,1},{1,2},{2,3},{3,4},{4,5},{5,6},{6,7},{7,8},{8,9},{9,10},{10,1... | collective-permute-start | bytes 196616 | tf_op jit(solution)/shard_map/ppermute | solution.py:18
  60.7 3.2 %collective-permute-done.7 = f32[64,1,256]{2,1,0:T(1,128)S(1)} collective-permute-done((f32[64,1,256]{2,1,0:T(1,128)S(1)}, f32[64,1,256]{2,1,0:T(1,128)S(1)}, u32[]{:S(2)}, u32[]{:S(2)}) %collective-permute-start.7) | collective-permute-done | bytes 65568 | tf_op jit(solution)/shard_map/ppermute | solution.py:18
  70.8 4.7 %all-to-all-start = ((f32[64,64,128]{2,0,1:T(8,128)}), f32[64,64,128]{2,0,1:T(8,128)}, u32[]{:S(2)}, u32[]{:S(2)}) async-start(f32[64,64,128]{2,0,1:T(8,128)} %copy.31), calls=%async_computation | async-start | bytes 4194304 | tf_op jit(solution)/shard_map/all_to_all | solution.py:48
  81.2 21.2 %all-to-all-done = f32[64,64,128]{2,0,1:T(8,128)} async-done(((f32[64,64,128]{2,0,1:T(8,128)}), f32[64,64,128]{2,0,1:T(8,128)}, u32[]{:S(2)}, u32[]{:S(2)}) %all-to-all-start) | async-done | bytes 2097184 | tf_op jit(solution)/shard_map/all_to_all | solution.py:48
  107.1 3.8 %gather_fusion = bf16[8,128,512]{2,1,0:T(8,128)(2,1)} fusion(bf16[32,128,512]{2,1,0:T(8,128)(2,1)} %all-gather.3.cloned.1.call-done, s32[1024]{0:T(1024)S(1)} %pad_clamp_fusion.7), kind=kCustom, calls=%fused_computation | custom fusion | bytes 2097184 | tf_op jit(solution)/shard_map/gather | solution.py:61
  110.9 64.1 %all-gather.5.cloned.1.call-done = bf16[32,128,512]{2,1,0:T(8,128)(2,1)} async-done(((bf16[1,128,512]{2,1,0:T(8,128)(2,1)}), bf16[32,128,512]{2,1,0:T(8,128)(2,1)}) %all-gather.5.cloned.1.call-update) | async-done | bytes 4194320 | tf_op jit(solution)/shard_map/all_gather | solution.py:38
  175.0 3.8 %gather_fusion.2 = bf16[8,128,512]{2,1,0:T(8,128)(2,1)} fusion(bf16[32,128,512]{2,1,0:T(8,128)(2,1)} %all-gather.5.cloned.1.call-done, s32[1024]{0:T(1024)S(1)} %pad_clamp_fusion.7), kind=kCustom, calls=%fused_computation.2 | custom fusion | bytes 2097184 | tf_op jit(solution)/shard_map/gather | solution.py:60
  178.8 3.8 %fusion.39 = f32[8,512,128]{2,1,0:T(8,128)} fusion(bf16[8,128,512]{2,1,0:T(8,128)(2,1)} %gather_fusion, f32[8,128,128]{2,1,0:T(8,128)} %gather_fusion.1, bf16[512,8,128]{2,0,1:T(8,128)(2,1)S(1)} %fusion.30, bf16[8,128,512]{2,1,0:T(8,128)(2,1)} %gather_fusion.2), kind=kOutput, calls=%fused_computation.68 | convolution fusion | flops 268828672 | bytes 5767168 | tf_op jit(solution)/shard_map/gco,gom->mgc/dot_general | solution.py:65
  182.6 3.8 %gather_fusion.3 = bf16[8,128,512]{2,1,0:T(8,128)(2,1)} fusion(bf16[32,128,512]{2,1,0:T(8,128)(2,1)} %all-gather.3.cloned.1.call-done, s32[1024]{0:T(1024)S(1)} %pad_clamp_fusion.5), kind=kCustom, calls=%fused_computation.3 | custom fusion | bytes 2097184 | tf_op jit(solution)/shard_map/gather | solution.py:61
  186.4 3.8 %gather_fusion.5 = bf16[8,128,512]{2,1,0:T(8,128)(2,1)} fusion(bf16[32,128,512]{2,1,0:T(8,128)(2,1)} %all-gather.5.cloned.1.call-done, s32[1024]{0:T(1024)S(1)} %pad_clamp_fusion.5), kind=kCustom, calls=%fused_computation.5 | custom fusion | bytes 2097184 | tf_op jit(solution)/shard_map/gather | solution.py:60
  190.2 3.8 %fusion.40 = f32[8,512,128]{2,1,0:T(8,128)} fusion(bf16[8,128,512]{2,1,0:T(8,128)(2,1)} %gather_fusion.3, f32[8,128,128]{2,1,0:T(8,128)} %gather_fusion.4, bf16[512,8,128]{2,0,1:T(8,128)(2,1)S(1)} %fusion.30, bf16[8,128,512]{2,1,0:T(8,128)(2,1)} %gather_fusion.5), kind=kOutput, calls=%fused_computation.69 | convolution fusion | flops 268828672 | bytes 5767168 | tf_op jit(solution)/shard_map/gco,gom->mgc/dot_general | solution.py:65
  194.0 3.8 %gather_fusion.6 = bf16[8,128,512]{2,1,0:T(8,128)(2,1)} fusion(bf16[32,128,512]{2,1,0:T(8,128)(2,1)} %all-gather.3.cloned.1.call-done, s32[1024]{0:T(1024)S(1)} %pad_clamp_fusion.3), kind=kCustom, calls=%fused_computation.6 | custom fusion | bytes 2097184 | tf_op jit(solution)/shard_map/gather | solution.py:61
  197.8 3.8 %gather_fusion.8 = bf16[8,128,512]{2,1,0:T(8,128)(2,1)} fusion(bf16[32,128,512]{2,1,0:T(8,128)(2,1)} %all-gather.5.cloned.1.call-done, s32[1024]{0:T(1024)S(1)} %pad_clamp_fusion.3), kind=kCustom, calls=%fused_computation.8 | custom fusion | bytes 2097184 | tf_op jit(solution)/shard_map/gather | solution.py:60
  201.6 3.8 %fusion.41 = f32[8,512,128]{2,1,0:T(8,128)} fusion(bf16[8,128,512]{2,1,0:T(8,128)(2,1)} %gather_fusion.6, f32[8,128,128]{2,1,0:T(8,128)} %gather_fusion.7, bf16[512,8,128]{2,0,1:T(8,128)(2,1)S(1)} %fusion.30, bf16[8,128,512]{2,1,0:T(8,128)(2,1)} %gather_fusion.8), kind=kOutput, calls=%fused_computation.70 | convolution fusion | flops 268828672 | bytes 5767168 | tf_op jit(solution)/shard_map/gco,gom->mgc/dot_general | solution.py:65
  205.4 3.8 %gather_fusion.11 = bf16[8,128,512]{2,1,0:T(8,128)(2,1)} fusion(bf16[32,128,512]{2,1,0:T(8,128)(2,1)} %all-gather.5.cloned.1.call-done, s32[1024]{0:T(1024)S(1)} %pad_clamp_fusion.1), kind=kCustom, calls=%fused_computation.11 | custom fusion | bytes 2097184 | tf_op jit(solution)/shard_map/gather | solution.py:60
  209.1 3.8 %gather_fusion.9 = bf16[8,128,512]{2,1,0:T(8,128)(2,1)} fusion(bf16[32,128,512]{2,1,0:T(8,128)(2,1)} %all-gather.3.cloned.1.call-done, s32[1024]{0:T(1024)S(1)} %pad_clamp_fusion.1), kind=kCustom, calls=%fused_computation.9 | custom fusion | bytes 2097184 | tf_op jit(solution)/shard_map/gather | solution.py:61
  213.0 5.9 %bitcast_add_fusion = f32[512,8,128]{2,0,1:T(8,128)} fusion(f32[8,64,8,128]{3,1,0,2:T(8,128)S(1)} %copy.33, f32[8,512,128]{2,1,0:T(8,128)} %fusion.41, f32[8,512,128]{2,1,0:T(8,128)} %fusion.39, f32[8,512,128]{2,1,0:T(8,128)} %fusion.40, bf16[8,128,512]{2,1,0:T(8,128)(2,1)} %gather_fusion.9, f32[8,128,128]{2,1,0:T(8,128)} %gather_fusion.10, ...), kind=kOutput, calls=%fused_computation.52 | convolution fusion | flops 270925824 | bytes 14155776 | tf_op jit(solution)/shard_map/gco,gom->mgc/dot_general | solution.py:65
  221.7 31.6 %all_to_all.33 = f32[512,8,128]{2,1,0:T(8,128)S(1)} all-to-all(f32[512,8,128]{2,1,0:T(8,128)S(1)} %copy.42), channel_id=1, replica_groups=mesh['mem'=8,'state'=32] {'mem'}, dimensions={0} | all-to-all | bytes 4194304 | tf_op jit(solution)/shard_map/all_to_all | solution.py:69
  257.7 5.7 %collective-permute-start.8 = (f32[64,1,256]{2,1,0:T(1,128)S(1)}, f32[64,1,256]{2,1,0:T(1,128)S(1)}, u32[]{:S(2)}, u32[]{:S(2)}) collective-permute-start(f32[64,1,256]{2,1,0:T(1,128)S(1)} %get-tuple-element.9), channel_id=1, source_target_pairs={{1,0},{2,1},{3,2},{4,3},{5,4},{6,5},{7,6},{8,7},{9,8},{10,9},{11,1... | collective-permute-start | bytes 196616 | tf_op jit(solution)/shard_map/ppermute | solution.py:19
  265.7 6.0 %collective-permute-done.9 = f32[64,1,256]{2,1,0:T(1,128)S(1)} collective-permute-done((f32[64,1,256]{2,1,0:T(1,128)S(1)}, f32[64,1,256]{2,1,0:T(1,128)S(1)}, u32[]{:S(2)}, u32[]{:S(2)}) %collective-permute-start.9) | collective-permute-done | bytes 65568 | tf_op jit(solution)/shard_map/ppermute | solution.py:18
  (73 shorter events, 59.2 us)
Async XLA Ops:
  6.5 69.1 %copy-start = (f32[8,128,128]{2,1,0:T(8,128)S(1)}, f32[8,128,128]{2,1,0:T(8,128)}, u32[]{:S(2)}) copy-start(f32[8,128,128]{2,1,0:T(8,128)} %param.11) | copy-start | bytes 1572868
  6.5 100.6 %all-gather.3.cloned.1.call-start = ((), (), s32[]{:S(2)}) async-start(), calls=%async_computation.2 | async-start | bytes 4325376 | tf_op jit(solution)/shard_map/all_gather | solution.py:39
  7.3 167.8 %all-gather.5.cloned.1.call-start = ((), (), s32[]{:S(2)}) async-start(), calls=%async_computation.3 | async-start | bytes 4325376 | tf_op jit(solution)/shard_map/all_gather | solution.py:38
  9.3 13.1 %collective-permute-start = (f32[64,1,256]{2,1,0:T(1,128)S(1)}, f32[64,1,256]{2,1,0:T(1,128)S(1)}, u32[]{:S(2)}, u32[]{:S(2)}) collective-permute-start(f32[64,1,256]{2,1,0:T(1,128)S(1)} %get-tuple-element.33), channel_id=1, source_target_pairs={{1,0},{2,1},{3,2},{4,3},{5,4},{6,5},{7,6},{8,7},{9,8},{10,9},{11,1... | collective-permute-start | bytes 196616 | tf_op jit(solution)/shard_map/ppermute | solution.py:19
  17.0 5.1 %copy-start.2 = (f32[64,32,256]{2,1,0:T(8,128)S(1)}, f32[64,32,256]{2,1,0:T(8,128)}, u32[]{:S(2)}) copy-start(f32[64,32,256]{2,1,0:T(8,128)} %param.7) | copy-start | bytes 6291460
  17.0 8.4 %collective-permute-start.1 = (f32[64,1,256]{2,1,0:T(1,128)S(1)}, f32[64,1,256]{2,1,0:T(1,128)S(1)}, u32[]{:S(2)}, u32[]{:S(2)}) collective-permute-start(f32[64,1,256]{2,1,0:T(1,128)S(1)} %get-tuple-element.34), channel_id=1, source_target_pairs={{0,1},{1,2},{2,3},{3,4},{4,5},{5,6},{6,7},{7,8},{8,9},{9,10},{10,1... | collective-permute-start | bytes 196616 | tf_op jit(solution)/shard_map/ppermute | solution.py:18
  22.0 3.4 %copy-start.3 = (f32[32,256]{1,0:T(8,128)S(1)}, f32[32,256]{1,0:T(8,128)}, u32[]{:S(2)}) copy-start(f32[32,256]{1,0:T(8,128)} %param.8) | copy-start | bytes 98308
  27.3 7.1 %collective-permute-start.2 = (f32[64,1,256]{2,1,0:T(1,128)S(1)}, f32[64,1,256]{2,1,0:T(1,128)S(1)}, u32[]{:S(2)}, u32[]{:S(2)}) collective-permute-start(f32[64,1,256]{2,1,0:T(1,128)S(1)} %get-tuple-element.27), channel_id=1, source_target_pairs={{1,0},{2,1},{3,2},{4,3},{5,4},{6,5},{7,6},{8,7},{9,8},{10,9},{11,1... | collective-permute-start | bytes 196616 | tf_op jit(solution)/shard_map/ppermute | solution.py:19
  30.7 8.9 %collective-permute-start.3 = (f32[64,1,256]{2,1,0:T(1,128)S(1)}, f32[64,1,256]{2,1,0:T(1,128)S(1)}, u32[]{:S(2)}, u32[]{:S(2)}) collective-permute-start(f32[64,1,256]{2,1,0:T(1,128)S(1)} %get-tuple-element.28), channel_id=1, source_target_pairs={{0,1},{1,2},{2,3},{3,4},{4,5},{5,6},{6,7},{7,8},{8,9},{9,10},{10,1... | collective-permute-start | bytes 196616 | tf_op jit(solution)/shard_map/ppermute | solution.py:18
  41.5 7.1 %collective-permute-start.4 = (f32[64,1,256]{2,1,0:T(1,128)S(1)}, f32[64,1,256]{2,1,0:T(1,128)S(1)}, u32[]{:S(2)}, u32[]{:S(2)}) collective-permute-start(f32[64,1,256]{2,1,0:T(1,128)S(1)} %get-tuple-element.21), channel_id=1, source_target_pairs={{1,0},{2,1},{3,2},{4,3},{5,4},{6,5},{7,6},{8,7},{9,8},{10,9},{11,1... | collective-permute-start | bytes 196616 | tf_op jit(solution)/shard_map/ppermute | solution.py:19
  43.4 8.3 %collective-permute-start.5 = (f32[64,1,256]{2,1,0:T(1,128)S(1)}, f32[64,1,256]{2,1,0:T(1,128)S(1)}, u32[]{:S(2)}, u32[]{:S(2)}) collective-permute-start(f32[64,1,256]{2,1,0:T(1,128)S(1)} %get-tuple-element.22), channel_id=1, source_target_pairs={{0,1},{1,2},{2,3},{3,4},{4,5},{5,6},{6,7},{7,8},{8,9},{9,10},{10,1... | collective-permute-start | bytes 196616 | tf_op jit(solution)/shard_map/ppermute | solution.py:18
  53.6 7.1 %collective-permute-start.6 = (f32[64,1,256]{2,1,0:T(1,128)S(1)}, f32[64,1,256]{2,1,0:T(1,128)S(1)}, u32[]{:S(2)}, u32[]{:S(2)}) collective-permute-start(f32[64,1,256]{2,1,0:T(1,128)S(1)} %get-tuple-element.15), channel_id=1, source_target_pairs={{1,0},{2,1},{3,2},{4,3},{5,4},{6,5},{7,6},{8,7},{9,8},{10,9},{11,1... | collective-permute-start | bytes 196616 | tf_op jit(solution)/shard_map/ppermute | solution.py:19
  55.5 8.3 %collective-permute-start.7 = (f32[64,1,256]{2,1,0:T(1,128)S(1)}, f32[64,1,256]{2,1,0:T(1,128)S(1)}, u32[]{:S(2)}, u32[]{:S(2)}) collective-permute-start(f32[64,1,256]{2,1,0:T(1,128)S(1)} %get-tuple-element.16), channel_id=1, source_target_pairs={{0,1},{1,2},{2,3},{3,4},{4,5},{5,6},{6,7},{7,8},{8,9},{9,10},{10,1... | collective-permute-start | bytes 196616 | tf_op jit(solution)/shard_map/ppermute | solution.py:18
  70.8 4.7 %copy-start.4 = (s32[64,4]{0,1:T(4,128)S(1)}, s32[64,4]{0,1:T(4,128)}, u32[]{:S(2)}) copy-start(s32[64,4]{0,1:T(4,128)} %param.13) | copy-start | bytes 3076
  70.8 4.8 %copy-start.5 = (s32[64,4]{0,1:T(4,128)S(1)}, s32[64,4]{0,1:T(4,128)}, u32[]{:S(2)}) copy-start(s32[64,4]{0,1:T(4,128)} %param.12) | copy-start | bytes 3076
  70.8 31.7 %all-to-all-start = ((f32[64,64,128]{2,0,1:T(8,128)}), f32[64,64,128]{2,0,1:T(8,128)}, u32[]{:S(2)}, u32[]{:S(2)}) async-start(f32[64,64,128]{2,0,1:T(8,128)} %copy.31), calls=%async_computation | async-start | bytes 4194304 | tf_op jit(solution)/shard_map/all_to_all | solution.py:48
  257.7 8.1 %collective-permute-start.8 = (f32[64,1,256]{2,1,0:T(1,128)S(1)}, f32[64,1,256]{2,1,0:T(1,128)S(1)}, u32[]{:S(2)}, u32[]{:S(2)}) collective-permute-start(f32[64,1,256]{2,1,0:T(1,128)S(1)} %get-tuple-element.9), channel_id=1, source_target_pairs={{1,0},{2,1},{3,2},{4,3},{5,4},{6,5},{7,6},{8,7},{9,8},{10,9},{11,1... | collective-permute-start | bytes 196616 | tf_op jit(solution)/shard_map/ppermute | solution.py:19
  263.4 8.3 %collective-permute-start.9 = (f32[64,1,256]{2,1,0:T(1,128)S(1)}, f32[64,1,256]{2,1,0:T(1,128)S(1)}, u32[]{:S(2)}, u32[]{:S(2)}) collective-permute-start(f32[64,1,256]{2,1,0:T(1,128)S(1)} %get-tuple-element.10), channel_id=1, source_target_pairs={{0,1},{1,2},{2,3},{3,4},{4,5},{5,6},{6,7},{7,8},{8,9},{9,10},{10,1... | collective-permute-start | bytes 196616 | tf_op jit(solution)/shard_map/ppermute | solution.py:18
  271.7 2.8 copy-start.1
Sparse Core Ops, SparseCore 0:
  10.0 83.4 all-gather.2
  96.0 78.9 all-gather.4
where the time goes:
time: 282 us; the launch traced here: 281 us
  waiting for transfers between devices  107 us (38%)
  local copies, waits for them, and re-layouts  58 us (21%)
  starting transfers between devices  39.6 us (14%)
  blocking collectives  31.6 us (11%)
  matrix products  17.3 us (6%)
  other arithmetic  13.8 us (5%)
  between operations  13.8 us (5%)
    all_gather x1, waiting for transfers between devices, body(): lax.all_gather(obs_anom, 'state', axis=0, tiled=True)  64.1 us
    all_to_all x1, blocking collectives, body(): lax.all_to_all(updated, 'mem', split_axis=0, concat_axis=1, tiled=True)  31.6 us
    all_to_all x1, waiting for transfers between devices, body(): lax.all_to_all(blocks, 'mem', split_axis=1, concat_axis=0, tiled=True)  21.2 us
    ppermute x5, starting transfers between devices, padded_2(): after = lax.ppermute(first, axis, down)  20.7 us
    ppermute x5, waiting for transfers between devices, padded_2(): before = lax.ppermute(last, axis, up)  20.4 us
    dot_general x4, matrix products, body(): jnp.einsum('gco,gom->mgc', tapered_update, weights, preferred_element_typ...  17.3 us
    gather x4, local copies, waits for them, and re-layouts, body(): weights = every_weight[chosen]  15.2 us
    gather x4, local copies, waits for them, and re-layouts, body(): anoms = every_anom[chosen]  15.1 us
  transfers between devices with their start and end apart: 13, of which 7 were waited for; matrix products, arithmetic and copies ran while one was open for 13% of the time, Pallas kernels for 0%

commit v1 on v0

v1 whole, which is shorter than its diff:
```python
import jax
import jax.numpy as jnp
from jax import lax
from jax.experimental import pallas as pl
from jax.experimental.pallas import tpu as pltpu
from jax.sharding import PartitionSpec as P

F32, BF16 = jnp.float32, jnp.bfloat16
TILE = 128
SLOTS = 4
FSTEPS = 4
HALO = FSTEPS + 1
VMEM = pl.BlockSpec(memory_space=pltpu.VMEM)
SMEM = pl.BlockSpec(memory_space=pltpu.SMEM)


def pack_obs_kernel(anom_ref, weight_ref, out_ref):
    obs, members = anom_ref.shape[1:]
    for q in range(members // TILE):
        cols = slice(q * TILE, (q + 1) * TILE)
        out_ref[0, q * TILE : (q + 1) * TILE, :] = anom_ref[0, :, cols]
        out_ref[0, members + q * TILE : members + (q + 1) * TILE, :] = weight_ref[0, :, cols].T


def pack_halo_kernel(first_ref, last_ref, coef_ref, block_ref, taper_ref, up_ref, down_ref):
    members, depth, columns = first_ref.shape
    rows = coef_ref.shape[0]
    tiles = block_ref.shape[1]
    lane = lax.broadcasted_iota(jnp.int32, (8, columns), 1)
    for out_ref, x_ref, start, row0, tile0, far in (
        (up_ref, first_ref, 0, 0, 0, HALO - 1),
        (down_ref, last_ref, depth - HALO, rows - HALO, tiles - 2, 0),
    ):
        for r in range(HALO):
            out_ref[r, 0:members, :] = x_ref[:, start + r, :]
            out_ref[r, members : members + 8, :] = jnp.broadcast_to(coef_ref[row0 + r : row0 + r + 1, :], (8, columns))
        ids = jnp.zeros((8, columns), jnp.int32)
        for t in range(2):
            for k in range(SLOTS):
                ids = jnp.where(lane == t * SLOTS + k, block_ref[k, tile0 + t], ids)
                ids = jnp.where(lane == 8 + t * SLOTS + k, taper_ref[k, tile0 + t], ids)
        out_ref[far, members : members + 8, :] = ids.astype(F32)


def forecast_kernel(x_ref, above_ref, below_ref, coef_ref, prior_ref, pay_ref, a_ref, b_ref, c_ref, m_ref):
    members, rows, columns = x_ref.shape
    total = rows + 2 * HALO
    group = pay_ref.shape[0]
    per = rows // group
    tiles = 2 * per + 1
    for r in range(HALO):
        a_ref[r] = above_ref[r, 0:members, :]
        a_ref[HALO + rows + r] = below_ref[r, 0:members, :]
        c_ref[r] = above_ref[r, members : members + 8, :]
        c_ref[HALO + rows + r] = below_ref[r, members : members + 8, :]
    for r in range(rows):
        a_ref[HALO + r] = x_ref[:, r, :]
        c_ref[HALO + r] = jnp.broadcast_to(coef_ref[r : r + 1, :], (8, columns))
    src, dst = a_ref, b_ref
    for step in range(1, FSTEPS + 1):

        def one(r, carry, src=src, dst=dst):
            up, mid = carry
            down = src[r + 1]
            beside = up + down + pltpu.roll(mid, 1, 1) + pltpu.roll(mid, columns - 1, 1)
            delta = (beside - 4.0 * mid).reshape(members // 8, 8, columns)
            dst[r] = mid + (c_ref[r][None] * delta).reshape(members, columns)
            return mid, down

        lax.fori_loop(step, total - step, one, (src[step - 1], src[step]))
        src, dst = dst, src

    m_ref[...] = jnp.zeros_like(m_ref)

    def tile(index, dest, slot, half, keep):
        value = src[index, :, half * TILE : (half + 1) * TILE]
        mean = jnp.sum(value, axis=0, keepdims=True) * (1.0 / members)
        pay_ref[dest, slot * members : (slot + 1) * members, :] = (value - mean).astype(BF16)
        high = mean.astype(BF16).astype(F32)
        middle = (mean - high).astype(BF16).astype(F32)
        m_ref[dest, 3 * slot : 3 * slot + 1, :] = high
        m_ref[dest, 3 * slot + 1 : 3 * slot + 2, :] = middle
        m_ref[dest, 3 * slot + 2 : 3 * slot + 3, :] = mean - high - middle

    for j in range(group):
        for i in range(per):
            for half in range(2):
                tile(HALO + j * per + i, j, 2 * i + half, half, True)
    for half in range(2):
        tile(HALO - 1, half, tiles - 1, half, True)
        tile(HALO + rows, 2 + half, tiles - 1, half, True)
    for j in range(4, group):
        pay_ref[j, (tiles - 1) * members : tiles * members, :] = jnp.zeros((members, TILE), BF16)
    for j in range(group):
        pay_ref[j, tiles * members :, :] = m_ref[j].astype(BF16)
    prior_ref[...] = src[HALO - 1 : HALO + rows + 1]


def analysis_kernel(blocks_ref, tapers_ref, recv_ref, taper_ref, *rest):
    obs_refs, (ret_ref, shift_ref) = rest[:SLOTS], rest[SLOTS:]
    group, size, _ = recv_ref.shape
    tiles = pl.num_programs(0)
    count = ret_ref.shape[1]
    t = pl.program_id(0)
    members = group * count

    @pl.when(t == 0)
    def _():
        parts = recv_ref[:, size - 32 :, :].astype(F32)
        for i in range((size - 32) // count):
            own = parts[:, 3 * i, :] + parts[:, 3 * i + 1, :] + parts[:, 3 * i + 2, :]
            shift_ref[i] = own - jnp.mean(own, axis=0, keepdims=True)

    here = pl.ds(pl.multiple_of(t * count, count), count)
    delta = shift_ref[t]
    centred = (recv_ref[:, here, :].astype(F32) + delta[:, None, :]).astype(BF16).reshape(members, TILE)
    total = jnp.zeros((members, TILE), F32)
    for pair in range(SLOTS // 2):
        lhs, rhs = [], []
        for k in (2 * pair, 2 * pair + 1):
            anom = jnp.concatenate([obs_refs[k][0, q * TILE : (q + 1) * TILE, :] for q in range(members // TILE)], axis=1)
            cov = jnp.dot(anom, centred, preferred_element_type=F32)
            taper = taper_ref[tapers_ref[t, k]]
            rhs.append((taper * (cov * (1.0 / (members - 1.0)))).astype(BF16))
            lhs.append(obs_refs[k][0, members:, :])
        total += jnp.dot(jnp.concatenate(lhs, axis=1), jnp.concatenate(rhs, axis=0), preferred_element_type=F32)
    ret_ref[:, :, :] = total.astype(BF16).reshape(group, count, TILE)


def final_kernel(prior_ref, inc_ref, coef_ref, out_ref, v_ref):
    members, rows, columns = out_ref.shape
    group, size, _ = inc_ref.shape
    per = rows // group
    last = size // members - 1

    def put(index, j, slot, half):
        lanes = slice(half * TILE, (half + 1) * TILE)
        inc = inc_ref[j, slot * members : (slot + 1) * members, :].astype(F32)
        v_ref[index, :, lanes] = prior_ref[index, :, lanes] + inc

    for half in range(2):
        put(0, half, last, half)
        put(rows + 1, 2 + half, last, half)
    for r in range(rows):
        for half in range(2):
            put(r + 1, r // per, 2 * (r % per) + half, half)
    for r in range(rows):
        mid = v_ref[r + 1]
        beside = v_ref[r] + v_ref[r + 2] + pltpu.roll(mid, 1, 1) + pltpu.roll(mid, columns - 1, 1)
        out_ref[:, r, :] = mid + coef_ref[r : r + 1, :] * (beside - 4.0 * mid)


def body(ensemble, spreading_coefficient, obs_anom, obs_weight, taper_table, obs_block, taper_id):
    members, rows, columns = ensemble.shape
    group = lax.axis_size("mem")
    states = lax.axis_size("state")
    per = rows // group
    tiles = 2 * per + 1
    size = tiles * members + 32
    limit = pltpu.CompilerParams(vmem_limit_bytes=48 << 20)

    packed = pl.pallas_call(
        pack_obs_kernel,
        out_shape=jax.ShapeDtypeStruct((1, 2 * obs_anom.shape[2], TILE), BF16),
        in_specs=[VMEM] * 2,
        out_specs=VMEM,
        name="pack_obs",
    )(obs_anom, obs_weight)
    every = lax.all_gather(packed, "state", axis=0, tiled=True)

    up, down = pl.pallas_call(
        pack_halo_kernel,
        grid=(1,),
        out_shape=[jax.ShapeDtypeStruct((HALO, members + 8, columns), F32)] * 2,
        in_specs=[
            pl.BlockSpec((members, 8, columns), lambda i: (0, 0, 0)),
            pl.BlockSpec((members, 8, columns), lambda i: (0, rows // 8 - 1, 0)),
            VMEM,
            SMEM,
            SMEM,
        ],
        out_specs=[VMEM] * 2,
        name="pack_halo",
    )(ensemble, ensemble, spreading_coefficient, obs_block.T, taper_id.T)
    below = lax.ppermute(up, "state", [(i + 1, i) for i in range(states - 1)])
    above = lax.ppermute(down, "state", [(i, i + 1) for i in range(states - 1)])

    prior, payload = pl.pallas_call(
        forecast_kernel,
        out_shape=[
            jax.ShapeDtypeStruct((rows + 2, members, columns), F32),
            jax.ShapeDtypeStruct((group, size, TILE), BF16),
        ],
        in_specs=[VMEM] * 4,
        out_specs=[VMEM] * 2,
        scratch_shapes=[
            pltpu.VMEM((rows + 2 * HALO, members, columns), F32),
            pltpu.VMEM((rows + 2 * HALO, members, columns), F32),
            pltpu.VMEM((rows + 2 * HALO, 8, columns), F32),
            pltpu.VMEM((group, 32, TILE), F32),
        ],
        compiler_params=limit,
        name="forecast4",
    )(ensemble, above, below, spreading_coefficient)
    gathered = lax.all_to_all(payload, "mem", split_axis=0, concat_axis=0, tiled=True)

    j = lax.axis_index("mem")
    edge = jnp.where(j < 2, above[0, members, :16], below[HALO - 1, members, :16])
    edge = jnp.where(j % 2 == 0, edge.reshape(-1, 4)[:3:2], edge.reshape(-1, 4)[1:4:2]).astype(jnp.int32)
    mine = 2 * per * j
    blocks = jnp.concatenate([lax.dynamic_slice_in_dim(obs_block, mine, 2 * per, 0), edge[0:1]], axis=0)
    tapers = jnp.concatenate([lax.dynamic_slice_in_dim(taper_id, mine, 2 * per, 0), edge[1:2]], axis=0)

    increments = pl.pallas_call(
        analysis_kernel,
        out_shape=jax.ShapeDtypeStruct((group, tiles * members, TILE), BF16),
        grid_spec=pltpu.PrefetchScalarGridSpec(
            num_scalar_prefetch=2,
            grid=(tiles,),
            in_specs=[
                VMEM,
                VMEM,
                *(
                    pl.BlockSpec((1, every.shape[1], TILE), lambda t, b, p, k=k: (b[t, k], 0, 0))
                    for k in range(SLOTS)
                ),
            ],
            out_specs=pl.BlockSpec((group, members, TILE), lambda t, b, p: (0, t, 0)),
            scratch_shapes=[pltpu.VMEM((tiles, group, TILE), F32)],
        ),
        compiler_params=limit,
        name="analysis",
    )(blocks, tapers, gathered, jnp.swapaxes(taper_table, 1, 2), *([every] * SLOTS))
    returned = lax.all_to_all(increments, "mem", split_axis=0, concat_axis=0, tiled=True)

    return pl.pallas_call(
        final_kernel,
        out_shape=jax.ShapeDtypeStruct((members, rows, columns), F32),
        in_specs=[VMEM] * 3,
        out_specs=VMEM,
        scratch_shapes=[pltpu.VMEM((rows + 2, members, columns), F32)],
        compiler_params=limit,
        name="final_step",
    )(prior, returned, spreading_coefficient)


def solution(mesh):
    placed = (
        P("mem", "state", None),
        P("state", None),
        P("state", None, None),
        P("state", None, None),
        P(),
        P("state", None),
        P("state", None),
    )
    return jax.shard_map(
        body, mesh=mesh, in_specs=placed, out_specs=P("mem", "state", None), check_vma=False
    )
```

time: 282 us -> 154 us (0.55)
  the two profiles are of different devices: /device:TPU:8 before, /device:TPU:1 now
where the time goes in v1:
time: 154 us
  waiting for transfers between devices  68.8 us (45%)
  Pallas kernels  36.8 us (24%)
  blocking collectives  22 us (14%)
  between operations  13.5 us (9%)
  starting transfers between devices  11.8 us (8%)
    all_gather x1, waiting for transfers between devices, body(): every = lax.all_gather(packed, 'state', axis=0, tiled=True)  42 us
    all_to_all x1, blocking collectives, body(): lax.all_to_all(increments, 'mem', split_axis=0, concat_axis=0, tiled=True)  22 us
    pallas_call x1, Pallas kernels, body(): pl.pallas_call(forecast_kernel, out_shape=[jax.ShapeDtypeStruct((rows + 2...  19.7 us
    all_to_all x1, waiting for transfers between devices, body(): lax.all_to_all(payload, 'mem', split_axis=0, concat_axis=0, tiled=True)  16.5 us
    pallas_call x1, Pallas kernels, body(): pl.pallas_call(analysis_kernel, out_shape=jax.ShapeDtypeStruct((group, ti...  9.81 us
    ppermute x1, waiting for transfers between devices, body(): above = lax.ppermute(down, 'state', [(i, i + 1) for i in range(states - 1)])  6.06 us
    all_to_all x1, starting transfers between devices, body(): lax.all_to_all(payload, 'mem', split_axis=0, concat_axis=0, tiled=True)  5.97 us
    ppermute x1, starting transfers between devices, body(): above = lax.ppermute(down, 'state', [(i, i + 1) for i in range(states - 1)])  4.38 us
  transfers between devices with their start and end apart: 4, of which 4 were waited for; matrix products, arithmetic and copies ran while one was open for 0% of the time, Pallas kernels for 14%

profile of v1, /device:TPU:1, one launch (start us, length us, event | category | flops | bytes accessed | tf_op | source)
XLA Modules:
  0.0 153.6 jit_solution(8357925459130606083)
XLA Ops:
  6.5 1.8 %pack_obs.1 = bf16[1,1024,128]{2,1,0:T(8,128)(2,1)} custom-call(bf16[1,128,512]{2,1,0:T(8,128)(2,1)} %anom_ref.1, bf16[1,128,512]{2,1,0:T(8,128)(2,1)} %weight_ref.1), custom_call_target="tpu_custom_call" | custom-call | tf_op jit(solution)/shard_map/pack_obs/pallas_call | solution.py:162
  8.3 0.0 all-gather.2.cloned.1.call-update
  8.3 0.0 copy-start
  8.3 0.0 copy-start.2
  8.4 2.4 %pack_halo.1 = (f32[5,72,256]{2,1,0:T(8,128)}, f32[5,72,256]{2,1,0:T(8,128)}) custom-call(f32[64,32,256]{2,1,0:T(8,128)} %x_ref.1, f32[64,32,256]{2,1,0:T(8,128)} %x_ref.1, f32[32,256]{1,0:T(8,128)} %coef_ref.5, s32[4,64]{1,0:T(4,128)} %bitcast.4, s32[4,64]{1,0:T(4,128)} %bitcast.5), custom_call_target="tpu_custom_call" | custom-call | tf_op jit(solution)/shard_map/pack_halo/pallas_call | solution.py:171
  10.7 4.4 %collective-permute-start = (f32[5,72,256]{2,1,0:T(8,128)}, f32[5,72,256]{2,1,0:T(8,128)S(1)}, u32[]{:S(2)}, u32[]{:S(2)}) collective-permute-start(f32[5,72,256]{2,1,0:T(8,128)} %get-tuple-element.9), channel_id=1, source_target_pairs={{0,1},{1,2},{2,3},{3,4},{4,5},{5,6},{6,7},{7,8},{8,9},{9,10},{10,1... | collective-permute-start | bytes 1105928 | tf_op jit(solution)/shard_map/ppermute | solution.py:186
  15.1 0.0 copy-start.4
  15.1 0.0 copy-start.5
  15.1 1.4 collective-permute-start.1
  16.6 6.1 %collective-permute-done.above_ref = f32[5,72,256]{2,1,0:T(8,128)S(1)} collective-permute-done((f32[5,72,256]{2,1,0:T(8,128)}, f32[5,72,256]{2,1,0:T(8,128)S(1)}, u32[]{:S(2)}, u32[]{:S(2)}) %collective-permute-start) | collective-permute-done | bytes 368672 | tf_op jit(solution)/shard_map/ppermute | solution.py:186
  22.6 4.2 %collective-permute-done.1.below_ref = f32[5,72,256]{2,1,0:T(8,128)S(1)} collective-permute-done((f32[5,72,256]{2,1,0:T(8,128)}, f32[5,72,256]{2,1,0:T(8,128)S(1)}, u32[]{:S(2)}, u32[]{:S(2)}) %collective-permute-start.1) | collective-permute-done | bytes 368672 | tf_op jit(solution)/shard_map/ppermute | solution.py:185
  26.9 19.7 %forecast4.1 = (f32[34,64,256]{2,1,0:T(8,128)}, bf16[8,608,128]{2,1,0:T(8,128)(2,1)}) custom-call(f32[64,32,256]{2,1,0:T(8,128)S(1)} %copy-done, f32[5,72,256]{2,1,0:T(8,128)S(1)} %collective-permute-done.above_ref, f32[5,72,256]{2,1,0:T(8,128)S(1)} %collective-permute-done.1.below_ref, f32[32,256]{1,0:T(8,128)S(1)} %copy-done.2), custom_call_target="tpu_custom_call" | custom-call | tf_op jit(solution)/shard_map/forecast4/pallas_call | solution.py:188
  46.6 6.0 %all-to-all-start = ((bf16[8,608,128]{2,1,0:T(8,128)(2,1)}), bf16[8,608,128]{2,1,0:T(8,128)(2,1)S(1)}, u32[]{:S(2)}, u32[]{:S(2)}) async-start(bf16[8,608,128]{2,1,0:T(8,128)(2,1)} %get-tuple-element.12), calls=%async_computation | async-start | bytes 2490368 | tf_op jit(solution)/shard_map/all_to_all | solution.py:205
  52.6 0.1 constant_dynamic-slice_fusion.1
  52.7 0.1 copy.19
  52.7 0.1 constant_dynamic-slice_fusion
  52.8 0.1 copy.20
  52.9 0.2 copy.18
  53.1 0.1 select_n.36
  53.3 16.5 %all-to-all-done.recv_ref = bf16[8,608,128]{2,1,0:T(8,128)(2,1)S(1)} async-done(((bf16[8,608,128]{2,1,0:T(8,128)(2,1)}), bf16[8,608,128]{2,1,0:T(8,128)(2,1)S(1)}, u32[]{:S(2)}, u32[]{:S(2)}) %all-to-all-start) | async-done | bytes 1245216 | tf_op jit(solution)/shard_map/all_to_all | solution.py:205
  69.8 42.0 %all-gather.2.cloned.1.call-done.rest_0_.rest_1_.rest_2_.rest_3_ = bf16[32,1024,128]{2,1,0:T(8,128)(2,1)} async-done(((bf16[1,1024,128]{2,1,0:T(8,128)(2,1)}), bf16[32,1024,128]{2,1,0:T(8,128)(2,1)}) %all-gather.2.cloned.1.call-update) | async-done | bytes 8388624 | tf_op jit(solution)/shard_map/all_gather | solution.py:169
  111.8 9.8 %analysis.1 = bf16[8,576,128]{2,1,0:T(8,128)(2,1)S(1)} custom-call(s32[9,4]{1,0:T(8,128)S(1)} %get-tuple-element.15.blocks_ref, s32[9,4]{1,0:T(8,128)S(1)} %get-tuple-element.16.tapers_ref, bf16[8,608,128]{2,1,0:T(8,128)(2,1)S(1)} %all-to-all-done.recv_ref, f32[8,128,128]{2,1,0:T(8,128)S(1)} %bitcast.3, ...), custom_call_target="tpu_custom_call" | custom-call | tf_op jit(solution)/shard_map/analysis/pallas_call | solution.py:214
  121.6 22.0 %all_to_all.10.inc_ref = bf16[8,576,128]{2,1,0:T(8,128)(2,1)S(1)} all-to-all(bf16[8,576,128]{2,1,0:T(8,128)(2,1)S(1)} %analysis.1), channel_id=1, replica_groups=mesh['mem'=8,'state'=32] {'mem'}, dimensions={0} | all-to-all | bytes 2359296 | tf_op jit(solution)/shard_map/all_to_all | solution.py:234
  143.5 3.2 %final_step.1 = f32[64,32,256]{2,1,0:T(8,128)} custom-call(f32[34,64,256]{2,1,0:T(8,128)S(1)} %copy-done.1, bf16[8,576,128]{2,1,0:T(8,128)(2,1)S(1)} %all_to_all.10.inc_ref, f32[32,256]{1,0:T(8,128)S(1)} %copy-done.2), custom_call_target="tpu_custom_call" | custom-call | tf_op jit(solution)/shard_map/final_step/pallas_call | solution.py:236
  (15 shorter events, 0.1 us)
Async XLA Ops:
  6.5 105.2 %all-gather.2.cloned.1.call-start = ((), (), s32[]{:S(2)}) async-start(), calls=%async_computation.2 | async-start | bytes 8650752 | tf_op jit(solution)/shard_map/all_gather | solution.py:169
  8.3 18.5 %copy-start = (f32[64,32,256]{2,1,0:T(8,128)S(1)}, f32[64,32,256]{2,1,0:T(8,128)}, u32[]{:S(2)}) copy-start(f32[64,32,256]{2,1,0:T(8,128)} %x_ref.1) | copy-start | bytes 6291460
  8.3 18.5 %copy-start.2 = (f32[32,256]{1,0:T(8,128)S(1)}, f32[32,256]{1,0:T(8,128)}, u32[]{:S(2)}) copy-start(f32[32,256]{1,0:T(8,128)} %coef_ref.5) | copy-start | bytes 98308
  10.7 11.9 %collective-permute-start = (f32[5,72,256]{2,1,0:T(8,128)}, f32[5,72,256]{2,1,0:T(8,128)S(1)}, u32[]{:S(2)}, u32[]{:S(2)}) collective-permute-start(f32[5,72,256]{2,1,0:T(8,128)} %get-tuple-element.9), channel_id=1, source_target_pairs={{0,1},{1,2},{2,3},{3,4},{4,5},{5,6},{6,7},{7,8},{8,9},{9,10},{10,1... | collective-permute-start | bytes 1105928 | tf_op jit(solution)/shard_map/ppermute | solution.py:186
  15.1 37.5 %copy-start.4 = (s32[64,4]{0,1:T(4,128)S(1)}, s32[64,4]{0,1:T(4,128)}, u32[]{:S(2)}) copy-start(s32[64,4]{0,1:T(4,128)} %param.12) | copy-start | bytes 3076
  15.1 37.6 %copy-start.5 = (s32[64,4]{0,1:T(4,128)S(1)}, s32[64,4]{0,1:T(4,128)}, u32[]{:S(2)}) copy-start(s32[64,4]{0,1:T(4,128)} %param.13) | copy-start | bytes 3076
  15.1 37.8 %copy-start.3 = (f32[8,128,128]{2,1,0:T(8,128)S(1)}, f32[8,128,128]{2,1,0:T(8,128)}, u32[]{:S(2)}) copy-start(f32[8,128,128]{2,1,0:T(8,128)} %param.11) | copy-start | bytes 1572868
  15.1 11.7 %collective-permute-start.1 = (f32[5,72,256]{2,1,0:T(8,128)}, f32[5,72,256]{2,1,0:T(8,128)S(1)}, u32[]{:S(2)}, u32[]{:S(2)}) collective-permute-start(f32[5,72,256]{2,1,0:T(8,128)} %get-tuple-element.10), channel_id=1, source_target_pairs={{1,0},{2,1},{3,2},{4,3},{5,4},{6,5},{7,6},{8,7},{9,8},{10,9},{11,1... | collective-permute-start | bytes 1105928 | tf_op jit(solution)/shard_map/ppermute | solution.py:185
  46.6 23.2 %all-to-all-start = ((bf16[8,608,128]{2,1,0:T(8,128)(2,1)}), bf16[8,608,128]{2,1,0:T(8,128)(2,1)S(1)}, u32[]{:S(2)}, u32[]{:S(2)}) async-start(bf16[8,608,128]{2,1,0:T(8,128)(2,1)} %get-tuple-element.12), calls=%async_computation | async-start | bytes 2490368 | tf_op jit(solution)/shard_map/all_to_all | solution.py:205
  121.6 22.0 %copy-start.1 = (f32[34,64,256]{2,1,0:T(8,128)S(1)}, f32[34,64,256]{2,1,0:T(8,128)}, u32[]{:S(2)}) copy-start(f32[34,64,256]{2,1,0:T(8,128)} %get-tuple-element.11.prior_ref) | copy-start | bytes 6684676
Sparse Core Ops, SparseCore 0:
  9.9 101.7 all-gather.1

commit v2 on v1

--- a/solution.py
+++ b/solution.py
@@ -15,11 +15,18 @@
 
 
 def pack_obs_kernel(anom_ref, weight_ref, out_ref):
-    obs, members = anom_ref.shape[1:]
-    for q in range(members // TILE):
-        cols = slice(q * TILE, (q + 1) * TILE)
-        out_ref[0, q * TILE : (q + 1) * TILE, :] = anom_ref[0, :, cols]
-        out_ref[0, members + q * TILE : members + (q + 1) * TILE, :] = weight_ref[0, :, cols].T
+    members = anom_ref.shape[2]
+    core = lax.rem(lax.axis_index("mem"), 2)
+
+    @pl.when(core == 0)
+    def _():
+        for q in range(members // TILE):
+            out_ref[0, q * TILE : (q + 1) * TILE, :] = anom_ref[0, :, q * TILE : (q + 1) * TILE]
+
+    @pl.when(core == 1)
+    def _():
+        for q in range(members // TILE):
+            out_ref[0, q * TILE : (q + 1) * TILE, :] = weight_ref[0, :, q * TILE : (q + 1) * TILE].T
 
 
 def pack_halo_kernel(first_ref, last_ref, coef_ref, block_ref, taper_ref, up_ref, down_ref):
@@ -49,27 +56,31 @@
     per = rows // group
     tiles = 2 * per + 1
     for r in range(HALO):
-        a_ref[r] = above_ref[r, 0:members, :]
-        a_ref[HALO + rows + r] = below_ref[r, 0:members, :]
         c_ref[r] = above_ref[r, members : members + 8, :]
         c_ref[HALO + rows + r] = below_ref[r, members : members + 8, :]
     for r in range(rows):
-        a_ref[HALO + r] = x_ref[:, r, :]
         c_ref[HALO + r] = jnp.broadcast_to(coef_ref[r : r + 1, :], (8, columns))
-    src, dst = a_ref, b_ref
-    for step in range(1, FSTEPS + 1):
-
-        def one(r, carry, src=src, dst=dst):
-            up, mid = carry
-            down = src[r + 1]
-            beside = up + down + pltpu.roll(mid, 1, 1) + pltpu.roll(mid, columns - 1, 1)
-            delta = (beside - 4.0 * mid).reshape(members // 8, 8, columns)
-            dst[r] = mid + (c_ref[r][None] * delta).reshape(members, columns)
-            return mid, down
-
-        lax.fori_loop(step, total - step, one, (src[step - 1], src[step]))
-        src, dst = dst, src
-
+    chunk = 16
+
+    def advance(number, carry):
+        here = pl.ds(pl.multiple_of(number * chunk, chunk), chunk)
+        for r in range(HALO):
+            a_ref[r, here, :] = above_ref[r, here, :]
+            a_ref[HALO + rows + r, here, :] = below_ref[r, here, :]
+        for r in range(rows):
+            a_ref[HALO + r, here, :] = x_ref[here, r, :]
+        src, dst = a_ref, b_ref
+        for step in range(1, FSTEPS + 1):
+            for r in range(step, total - step):
+                mid = src[r, here, :]
+                beside = src[r - 1, here, :] + src[r + 1, here, :] + pltpu.roll(mid, 1, 1) + pltpu.roll(mid, columns - 1, 1)
+                delta = (beside - 4.0 * mid).reshape(chunk // 8, 8, columns)
+                dst[r, here, :] = mid + (c_ref[r][None] * delta).reshape(chunk, columns)
+            src, dst = dst, src
+        return carry
+
+    lax.fori_loop(0, members // chunk, advance, 0)
+    src = a_ref if FSTEPS % 2 == 0 else b_ref
     m_ref[...] = jnp.zeros_like(m_ref)
 
     def tile(index, dest, slot, half, keep):
@@ -96,35 +107,50 @@
     prior_ref[...] = src[HALO - 1 : HALO + rows + 1]
 
 
-def analysis_kernel(blocks_ref, tapers_ref, recv_ref, taper_ref, *rest):
-    obs_refs, (ret_ref, shift_ref) = rest[:SLOTS], rest[SLOTS:]
+def analysis_kernel(anom_at_ref, weight_at_ref, tapers_ref, recv_ref, taper_ref, *rest):
+    pieces, (ret_ref, obs_ref, shift_ref, sems) = rest[:-4], rest[-4:]
     group, size, _ = recv_ref.shape
-    tiles = pl.num_programs(0)
-    count = ret_ref.shape[1]
-    t = pl.program_id(0)
+    count = ret_ref.shape[1] // anom_at_ref.shape[0]
+    tiles = anom_at_ref.shape[0]
     members = group * count
-
-    @pl.when(t == 0)
-    def _():
-        parts = recv_ref[:, size - 32 :, :].astype(F32)
-        for i in range((size - 32) // count):
-            own = parts[:, 3 * i, :] + parts[:, 3 * i + 1, :] + parts[:, 3 * i + 2, :]
-            shift_ref[i] = own - jnp.mean(own, axis=0, keepdims=True)
-
-    here = pl.ds(pl.multiple_of(t * count, count), count)
-    delta = shift_ref[t]
-    centred = (recv_ref[:, here, :].astype(F32) + delta[:, None, :]).astype(BF16).reshape(members, TILE)
-    total = jnp.zeros((members, TILE), F32)
-    for pair in range(SLOTS // 2):
-        lhs, rhs = [], []
-        for k in (2 * pair, 2 * pair + 1):
-            anom = jnp.concatenate([obs_refs[k][0, q * TILE : (q + 1) * TILE, :] for q in range(members // TILE)], axis=1)
-            cov = jnp.dot(anom, centred, preferred_element_type=F32)
-            taper = taper_ref[tapers_ref[t, k]]
-            rhs.append((taper * (cov * (1.0 / (members - 1.0)))).astype(BF16))
-            lhs.append(obs_refs[k][0, members:, :])
-        total += jnp.dot(jnp.concatenate(lhs, axis=1), jnp.concatenate(rhs, axis=0), preferred_element_type=F32)
-    ret_ref[:, :, :] = total.astype(BF16).reshape(group, count, TILE)
+    core = lax.rem(lax.axis_index("mem"), 2)
+    copies = []
+    for side in range(2):
+        start = 0
+        for piece in pieces[side * len(pieces) // 2 : (side + 1) * len(pieces) // 2]:
+            length = piece.shape[0]
+            to = obs_ref.at[core if side == 0 else 1 - core, pl.ds(start, length)]
+            copies.append(pltpu.make_async_copy(piece, to, sems.at[len(copies)]))
+            start += length
+    for copy in copies:
+        copy.start()
+
+    parts = recv_ref[:, size - 32 :, :].astype(F32)
+    for t in range(tiles):
+        own = parts[:, 3 * t, :] + parts[:, 3 * t + 1, :] + parts[:, 3 * t + 2, :]
+        shift_ref[t] = own - jnp.mean(own, axis=0, keepdims=True)
+    for copy in copies:
+        copy.wait()
+
+    def one(t, carry):
+        here = pl.ds(pl.multiple_of(t * count, count), count)
+        delta = shift_ref[t]
+        centred = (recv_ref[:, here, :].astype(F32) + delta[:, None, :]).astype(BF16).reshape(members, TILE)
+        total = jnp.zeros((members, TILE), F32)
+        for pair in range(SLOTS // 2):
+            lhs, rhs = [], []
+            for k in (2 * pair, 2 * pair + 1):
+                at = anom_at_ref[t, k]
+                anom = jnp.concatenate([obs_ref[0, at, q * TILE : (q + 1) * TILE, :] for q in range(members // TILE)], axis=1)
+                cov = jnp.dot(anom, centred, preferred_element_type=F32)
+                taper = taper_ref[tapers_ref[t, k]]
+                rhs.append((taper * (cov * (1.0 / (members - 1.0)))).astype(BF16))
+                lhs.append(obs_ref[1, weight_at_ref[t, k]])
+            total += jnp.dot(jnp.concatenate(lhs, axis=1), jnp.concatenate(rhs, axis=0), preferred_element_type=F32)
+        ret_ref[:, here, :] = total.astype(BF16).reshape(group, count, TILE)
+        return carry
+
+    lax.fori_loop(0, tiles, one, 0, unroll=3)
 
 
 def final_kernel(prior_ref, inc_ref, coef_ref, out_ref, v_ref):
@@ -150,6 +176,77 @@
         out_ref[:, r, :] = mid + coef_ref[r : r + 1, :] * (beside - 4.0 * mid)
 
 
+AXES = ("mem", "state")
+
+
+def fetch(value, mesh, source):
+    xs, ys, zs = mesh
+    pairs = []
+    for x in range(xs):
+        for c in range(2):
+            for y in range(ys):
+                for z in range(zs):
+                    a, b, d, e = source(x, c, y, z)
+                    pairs.append((((a * 2 + b) * ys + d % ys) * zs + e % zs, ((x * 2 + c) * ys + y) * zs + z))
+    return lax.ppermute(value, AXES, pairs)
+
+
+def ring(first, step):
+    return lambda x, c, y, z: (x, c, y + step, z) if (c == 0) == first else (x, c, y, z + step)
+
+
+def other_core(x, c, y, z):
+    return (x, 1 - c, y, z)
+
+
+def move(outs, plan, operands, name, after=()):
+    def kernel(*refs):
+        sources, targets, sems = refs[: len(operands)], refs[len(operands) + len(after) : -1], refs[-1]
+        core = lax.rem(lax.axis_index("mem"), 2)
+        copies = []
+        for i, (a, first, b, to, length) in enumerate(plan):
+            first = first(core) if callable(first) else first
+            copies.append(pltpu.make_async_copy(sources[a].at[pl.ds(first, length)], targets[b].at[pl.ds(to, length)], sems.at[i]))
+        for copy in copies:
+            copy.start()
+        for copy in copies:
+            copy.wait()
+
+    anywhere = pl.BlockSpec(memory_space=pl.ANY)
+    return pl.pallas_call(
+        kernel,
+        out_shape=[jax.ShapeDtypeStruct((n, *operands[0].shape[1:]), operands[0].dtype) for n in outs],
+        in_specs=[anywhere] * (len(operands) + len(after)),
+        out_specs=[anywhere] * len(outs),
+        scratch_shapes=[pltpu.SemaphoreType.DMA((len(plan),))],
+        name=name,
+    )(*operands, *after)
+
+
+def gather_obs(own, mesh, after_first, after_second, after_third):
+    far = fetch(own, mesh, lambda x, c, y, z: (x, c, y, z + 4))
+    (held,) = move([2], [(0, 0, 0, 0, 1), (1, 0, 0, 1, 1)], [own, far], "merge_two", after_first)
+    p, m, q = (fetch(held, mesh, ring(True, step)) for step in (1, -1, 2))
+    plan = [(a, i, 0, 4 * i + a, 1) for i in range(2) for a in range(4)]
+    (held,) = move([8], plan, [held, p, m, q], "merge_eight", after_second())
+    p, m = (fetch(held, mesh, ring(False, step)) for step in (1, -1))
+    swapped = [fetch(held, mesh, other_core)]
+    plan = [(0, 0, 0, 0, 4), (1, lambda core: 4 * core, 1, 0, 4)]
+    q, r = move([4, 4], plan, [p, m], "halves", after_third())
+    q = fetch(q, mesh, ring(False, 1))
+    r = fetch(r, mesh, ring(False, -1))
+    swapped += [fetch(v, mesh, other_core) for v in (p, m, q, r)]
+    return [held, p, m, q, r], swapped
+
+
+def places(block, y, z):
+    dy, dz = (block // 8 - y) % 4, (block % 8 - z) % 8
+    low = dz % 4
+    gray_y, gray_z = dy ^ (dy >> 1), low ^ (low >> 1)
+    high = 4 * ((dz // 4) ^ (low == 3).astype(jnp.int32))
+    return 8 * gray_z + high + gray_y, 8 * gray_y + high + gray_z
+
+
 def body(ensemble, spreading_coefficient, obs_anom, obs_weight, taper_table, obs_block, taper_id):
     members, rows, columns = ensemble.shape
     group = lax.axis_size("mem")
@@ -159,15 +256,14 @@
     size = tiles * members + 32
     limit = pltpu.CompilerParams(vmem_limit_bytes=48 << 20)
 
+    j, at = lax.axis_index("mem"), lax.axis_index("state")
     packed = pl.pallas_call(
         pack_obs_kernel,
-        out_shape=jax.ShapeDtypeStruct((1, 2 * obs_anom.shape[2], TILE), BF16),
+        out_shape=jax.ShapeDtypeStruct((1, obs_anom.shape[2], TILE), BF16),
         in_specs=[VMEM] * 2,
         out_specs=VMEM,
         name="pack_obs",
     )(obs_anom, obs_weight)
-    every = lax.all_gather(packed, "state", axis=0, tiled=True)
-
     up, down = pl.pallas_call(
         pack_halo_kernel,
         grid=(1,),
@@ -202,35 +298,31 @@
         compiler_params=limit,
         name="forecast4",
     )(ensemble, above, below, spreading_coefficient)
+    own, swapped = gather_obs(
+        packed, (group // 2, states // 8, 8), [up, down], lambda: [above, below], lambda: [payload]
+    )
     gathered = lax.all_to_all(payload, "mem", split_axis=0, concat_axis=0, tiled=True)
 
-    j = lax.axis_index("mem")
     edge = jnp.where(j < 2, above[0, members, :16], below[HALO - 1, members, :16])
     edge = jnp.where(j % 2 == 0, edge.reshape(-1, 4)[:3:2], edge.reshape(-1, 4)[1:4:2]).astype(jnp.int32)
     mine = 2 * per * j
     blocks = jnp.concatenate([lax.dynamic_slice_in_dim(obs_block, mine, 2 * per, 0), edge[0:1]], axis=0)
     tapers = jnp.concatenate([lax.dynamic_slice_in_dim(taper_id, mine, 2 * per, 0), edge[1:2]], axis=0)
 
+    anom_at, weight_at = places(blocks, at // 8, at % 8)
     increments = pl.pallas_call(
         analysis_kernel,
         out_shape=jax.ShapeDtypeStruct((group, tiles * members, TILE), BF16),
-        grid_spec=pltpu.PrefetchScalarGridSpec(
-            num_scalar_prefetch=2,
-            grid=(tiles,),
-            in_specs=[
-                VMEM,
-                VMEM,
-                *(
-                    pl.BlockSpec((1, every.shape[1], TILE), lambda t, b, p, k=k: (b[t, k], 0, 0))
-                    for k in range(SLOTS)
-                ),
-            ],
-            out_specs=pl.BlockSpec((group, members, TILE), lambda t, b, p: (0, t, 0)),
-            scratch_shapes=[pltpu.VMEM((tiles, group, TILE), F32)],
-        ),
+        in_specs=[SMEM] * 3 + [VMEM] * 2 + [pl.BlockSpec(memory_space=pl.ANY)] * (len(own) + len(swapped)),
+        out_specs=VMEM,
+        scratch_shapes=[
+            pltpu.VMEM((2, states, *packed.shape[1:]), BF16),
+            pltpu.VMEM((tiles, group, TILE), F32),
+            pltpu.SemaphoreType.DMA((len(own) + len(swapped),)),
+        ],
         compiler_params=limit,
         name="analysis",
-    )(blocks, tapers, gathered, jnp.swapaxes(taper_table, 1, 2), *([every] * SLOTS))
+    )(anom_at, weight_at, tapers, gathered, jnp.swapaxes(taper_table, 1, 2), *own, *swapped)
     returned = lax.all_to_all(increments, "mem", split_axis=0, concat_axis=0, tiled=True)
 
     return pl.pallas_call(

time: 154 us -> 175 us (1.14)
  Pallas kernels: 36.8 us -> 99.3 us
  waiting for transfers between devices: 68.8 us -> 14.6 us
  starting transfers between devices: 11.8 us -> 33.1 us
  between operations: 13.5 us -> 0.24 us
  local copies, waits for them, and re-layouts: 0.69 us -> 5.33 us
    pallas_call x1 -> x4, Pallas kernels: 1.77 us -> 76.6 us  [the longest x3 74.9 us: move(): pl.pallas_call(kernel, out_shape=[jax.ShapeDtypeStruct((n, *operands[0].s...]
    all_gather x1 -> x0, waiting for transfers between devices: 42 us -> none  [body(): every = lax.all_gather(packed, 'state', axis=0, tiled=True)]
    ppermute x0 -> x13, starting transfers between devices: none -> 22 us  [fetch(): return lax.ppermute(value, AXES, pairs)]
    all_to_all x1, waiting for transfers between devices: 16.5 us -> 0.01 us  [body(): lax.all_to_all(payload, 'mem', split_axis=0, concat_axis=0, tiled=True)]
    ppermute x0 -> x13, waiting for transfers between devices: none -> 14.6 us  [fetch(): return lax.ppermute(value, AXES, pairs)]
    pallas_call x1, Pallas kernels: 19.7 us -> 7.74 us  [body(): pl.pallas_call(forecast_kernel, out_shape=[jax.ShapeDtypeStruct((rows + 2...]
    ppermute x1, waiting for transfers between devices: 6.06 us -> 0.01 us  [body(): above = lax.ppermute(down, 'state', [(i, i + 1) for i in range(states - 1)])]
    unnamed x15 -> x33, local copies, waits for them, and re-layouts: 0.4 us -> 5.04 us
  transfers between devices with their start and end apart: 4 -> 16, of which waited for: 4 -> 6; matrix products, arithmetic and copies ran while one was open for 0% -> 1% of each run, Pallas kernels for 14% -> 30%
where the time goes in v2:
time: 175 us
  Pallas kernels  99.3 us (57%)
  starting transfers between devices  33.1 us (19%)
  blocking collectives  21.4 us (12%)
  waiting for transfers between devices  14.6 us (8%)
  local copies, waits for them, and re-layouts  5.33 us (3%)
    pallas_call x3, Pallas kernels, move(): pl.pallas_call(kernel, out_shape=[jax.ShapeDtypeStruct((n, *operands[0].s...  74.9 us
    ppermute x13, starting transfers between devices, fetch(): return lax.ppermute(value, AXES, pairs)  22 us
    all_to_all x1, blocking collectives, body(): lax.all_to_all(increments, 'mem', split_axis=0, concat_axis=0, tiled=True)  21.4 us
    ppermute x13, waiting for transfers between devices, fetch(): return lax.ppermute(value, AXES, pairs)  14.6 us
    pallas_call x1, Pallas kernels, body(): pl.pallas_call(analysis_kernel, out_shape=jax.ShapeDtypeStruct((group, ti...  9.62 us
    pallas_call x1, Pallas kernels, body(): pl.pallas_call(forecast_kernel, out_shape=[jax.ShapeDtypeStruct((rows + 2...  7.74 us
    all_to_all x1, starting transfers between devices, body(): lax.all_to_all(payload, 'mem', split_axis=0, concat_axis=0, tiled=True)  7.09 us
    unnamed x33, local copies, waits for them, and re-layouts  5.04 us
  transfers between devices with their start and end apart: 16, of which 6 were waited for; matrix products, arithmetic and copies ran while one was open for 1% of the time, Pallas kernels for 30%

profile of v2, /device:TPU:1, one launch (start us, length us, event | category | flops | bytes accessed | tf_op | source)
XLA Modules:
  0.0 174.7 jit_solution(11410248106423836917)
XLA Ops:
  0.0 1.7 pack_obs.1.refs_0_
  1.7 7.7 %collective-permute-start.2 = (bf16[1,512,128]{2,1,0:T(8,128)(2,1)}, bf16[1,512,128]{2,1,0:T(8,128)(2,1)S(1)}, u32[]{:S(2)}, u32[]{:S(2)}) collective-permute-start(bf16[1,512,128]{2,1,0:T(8,128)(2,1)} %pack_obs.1.refs_0_), channel_id=1, source_target_pairs={{4,0},{5,1},{6,2},{7,3},{0,4},{1,5},{2,6},{3,7},{12,8},{13,9},{14,... | collective-permute-start | bytes 393224 | tf_op jit(solution)/shard_map/ppermute | solution.py:191
  9.4 2.2 %pack_halo.1 = (f32[5,72,256]{2,1,0:T(8,128)}, f32[5,72,256]{2,1,0:T(8,128)}) custom-call(f32[64,32,256]{2,1,0:T(8,128)} %x_ref.1, f32[64,32,256]{2,1,0:T(8,128)} %x_ref.1, f32[32,256]{1,0:T(8,128)} %coef_ref.5, s32[4,64]{1,0:T(4,128)} %bitcast.5, s32[4,64]{1,0:T(4,128)} %bitcast.4), custom_call_target="tpu_custom_call" | custom-call | tf_op jit(solution)/shard_map/pack_halo/pallas_call | solution.py:267
  11.6 2.7 %collective-permute-start = (f32[5,72,256]{2,1,0:T(8,128)}, f32[5,72,256]{2,1,0:T(8,128)S(1)}, u32[]{:S(2)}, u32[]{:S(2)}) collective-permute-start(f32[5,72,256]{2,1,0:T(8,128)} %get-tuple-element.11.refs_3_), channel_id=1, source_target_pairs={{0,1},{1,2},{2,3},{3,4},{4,5},{5,6},{6,7},{7,8},{8,9},{9,10},{10,1... | collective-permute-start | bytes 1105928 | tf_op jit(solution)/shard_map/ppermute | solution.py:282
  14.3 1.3 collective-permute-start.1
  16.3 9.1 %merge_two.1.refs_0_ = bf16[2,512,128]{2,1,0:T(8,128)(2,1)} custom-call(bf16[1,512,128]{2,1,0:T(8,128)(2,1)} %pack_obs.1.refs_0_, bf16[1,512,128]{2,1,0:T(8,128)(2,1)} %copy-done.12, f32[5,72,256]{2,1,0:T(8,128)} %get-tuple-element.12.refs_2_, f32[5,72,256]{2,1,0:T(8,128)} %get-tuple-element.11.refs_3_), custom_call_target="tpu_custom_call" | custom-call | tf_op jit(solution)/shard_map/merge_two/pallas_call | solution.py:216
  25.4 4.4 %collective-permute-start.5 = (bf16[2,512,128]{2,1,0:T(8,128)(2,1)}, bf16[2,512,128]{2,1,0:T(8,128)(2,1)S(1)}, u32[]{:S(2)}, u32[]{:S(2)}) collective-permute-start(bf16[2,512,128]{2,1,0:T(8,128)(2,1)} %merge_two.1.refs_0_), channel_id=1, source_target_pairs={{16,0},{17,1},{18,2},{19,3},{20,4},{21,5},{22,6},{23,7},{24,8},{25... | collective-permute-start | bytes 786440 | tf_op jit(solution)/shard_map/ppermute | solution.py:191
  30.2 2.2 %collective-permute-start.3 = (bf16[2,512,128]{2,1,0:T(8,128)(2,1)}, bf16[2,512,128]{2,1,0:T(8,128)(2,1)}, u32[]{:S(2)}, u32[]{:S(2)}) collective-permute-start(bf16[2,512,128]{2,1,0:T(8,128)(2,1)} %merge_two.1.refs_0_), channel_id=1, source_target_pairs={{8,0},{9,1},{10,2},{11,3},{12,4},{13,5},{14,6},{15,7},{16,8},{17,9... | collective-permute-start | bytes 786440 | tf_op jit(solution)/shard_map/ppermute | solution.py:191
  32.4 3.7 %collective-permute-done.5.refs_3_ = bf16[2,512,128]{2,1,0:T(8,128)(2,1)S(1)} collective-permute-done((bf16[2,512,128]{2,1,0:T(8,128)(2,1)}, bf16[2,512,128]{2,1,0:T(8,128)(2,1)S(1)}, u32[]{:S(2)}, u32[]{:S(2)}) %collective-permute-start.5) | collective-permute-done | bytes 262176 | tf_op jit(solution)/shard_map/ppermute | solution.py:191
  36.7 2.3 %collective-permute-done.3.refs_1_ = bf16[2,512,128]{2,1,0:T(8,128)(2,1)} collective-permute-done((bf16[2,512,128]{2,1,0:T(8,128)(2,1)}, bf16[2,512,128]{2,1,0:T(8,128)(2,1)}, u32[]{:S(2)}, u32[]{:S(2)}) %collective-permute-start.3) | collective-permute-done | bytes 262176 | tf_op jit(solution)/shard_map/ppermute | solution.py:191
  39.0 32.9 %merge_eight.1.rest_0_ = bf16[8,512,128]{2,1,0:T(8,128)(2,1)} custom-call(bf16[2,512,128]{2,1,0:T(8,128)(2,1)} %merge_two.1.refs_0_, bf16[2,512,128]{2,1,0:T(8,128)(2,1)} %collective-permute-done.3.refs_1_, bf16[2,512,128]{2,1,0:T(8,128)(2,1)} %copy-done.11, bf16[2,512,128]{2,1,0:T(8,128)(2,1)} %copy-done.10, f32[5,72,256]{2,1,0:T(8,128)} %copy-done.5, ...), custom_call_target="tpu_custom_call" | custom-call | tf_op jit(solution)/shard_map/merge_eight/pallas_call | solution.py:216
  72.0 2.6 %collective-permute-start.7 = (bf16[8,512,128]{2,1,0:T(8,128)(2,1)}, bf16[8,512,128]{2,1,0:T(8,128)(2,1)S(1)}, u32[]{:S(2)}, u32[]{:S(2)}) collective-permute-start(bf16[8,512,128]{2,1,0:T(8,128)(2,1)} %merge_eight.1.rest_0_), channel_id=1, source_target_pairs={{7,0},{0,1},{1,2},{2,3},{3,4},{4,5},{5,6},{6,7},{15,8},{8,9},{9,10... | collective-permute-start | bytes 3145736 | tf_op jit(solution)/shard_map/ppermute | solution.py:191
  75.5 1.0 copy-done.6
  77.5 7.7 %forecast4.1 = (f32[34,64,256]{2,1,0:T(8,128)}, bf16[8,608,128]{2,1,0:T(8,128)(2,1)}) custom-call(f32[64,32,256]{2,1,0:T(8,128)S(1)} %copy-done, f32[5,72,256]{2,1,0:T(8,128)S(1)} %copy-done.6, f32[5,72,256]{2,1,0:T(8,128)S(1)} %copy-done.8, f32[32,256]{1,0:T(8,128)S(1)} %copy-done.9), custom_call_target="tpu_custom_call" | custom-call | tf_op jit(solution)/shard_map/forecast4/pallas_call | solution.py:284
  85.2 7.1 %all-to-all-start = ((bf16[8,608,128]{2,1,0:T(8,128)(2,1)}), bf16[8,608,128]{2,1,0:T(8,128)(2,1)}, u32[]{:S(2)}, u32[]{:S(2)}) async-start(bf16[8,608,128]{2,1,0:T(8,128)(2,1)} %get-tuple-element.14.refs_2_), calls=%async_computation | async-start | bytes 2490368 | tf_op jit(solution)/shard_map/all_to_all | solution.py:304
  93.3 32.9 %halves.1 = (bf16[4,512,128]{2,1,0:T(8,128)(2,1)}, bf16[4,512,128]{2,1,0:T(8,128)(2,1)}) custom-call(bf16[8,512,128]{2,1,0:T(8,128)(2,1)} %collective-permute-done.6.refs_0_.rest_1_, bf16[8,512,128]{2,1,0:T(8,128)(2,1)} %copy-done.1, bf16[8,608,128]{2,1,0:T(8,128)(2,1)} %get-tuple-element.14.refs_2_), custom_call_target="tpu_custom_call" | custom-call | tf_op jit(solution)/shard_map/halves/pallas_call | solution.py:216
  126.2 2.5 %collective-permute-start.8 = (bf16[4,512,128]{2,1,0:T(8,128)(2,1)}, bf16[4,512,128]{2,1,0:T(8,128)(2,1)S(1)}, u32[]{:S(2)}, u32[]{:S(2)}) collective-permute-start(bf16[4,512,128]{2,1,0:T(8,128)(2,1)} %get-tuple-element.15), channel_id=1, source_target_pairs={{1,0},{2,1},{3,2},{4,3},{5,4},{6,5},{7,6},{0,7},{9,8},{10,9},{11,1... | collective-permute-start | bytes 1572872 | tf_op jit(solution)/shard_map/ppermute | solution.py:191
  129.6 1.2 copy.21
  131.7 3.4 %collective-permute-done.8.rest_3_ = bf16[4,512,128]{2,1,0:T(8,128)(2,1)S(1)} collective-permute-done((bf16[4,512,128]{2,1,0:T(8,128)(2,1)}, bf16[4,512,128]{2,1,0:T(8,128)(2,1)S(1)}, u32[]{:S(2)}, u32[]{:S(2)}) %collective-permute-start.8) | collective-permute-done | bytes 524320 | tf_op jit(solution)/shard_map/ppermute | solution.py:191
  135.7 2.5 %collective-permute-done.9.rest_4_ = bf16[4,512,128]{2,1,0:T(8,128)(2,1)} collective-permute-done((bf16[4,512,128]{2,1,0:T(8,128)(2,1)}, bf16[4,512,128]{2,1,0:T(8,128)(2,1)}, u32[]{:S(2)}, u32[]{:S(2)}) %collective-permute-start.9) | collective-permute-done | bytes 524320 | tf_op jit(solution)/shard_map/ppermute | solution.py:191
  138.4 2.1 %collective-permute-done.14.rest_9_ = bf16[4,512,128]{2,1,0:T(8,128)(2,1)} collective-permute-done((bf16[4,512,128]{2,1,0:T(8,128)(2,1)}, bf16[4,512,128]{2,1,0:T(8,128)(2,1)}, u32[]{:S(2)}, u32[]{:S(2)}) %collective-permute-start.14) | collective-permute-done | bytes 524320 | tf_op jit(solution)/shard_map/ppermute | solution.py:191
  140.5 9.6 %analysis.1 = bf16[8,576,128]{2,1,0:T(8,128)(2,1)} custom-call(s32[9,4]{1,0:T(8,128)S(1)} %get-tuple-element.18.anom_at_ref, s32[9,4]{1,0:T(8,128)S(1)} %get-tuple-element.17.weight_at_ref, s32[9,4]{1,0:T(8,128)S(1)} %get-tuple-element.21.tapers_ref, bf16[8,608,128]{2,1,0:T(8,128)(2,1)} %all-to-all-done.recv_ref, f32[8,128,128]{2,1,0:T(8,128)S(1)} %bitcast.3, ...), custom_call_target="tpu_custom_call" | custom-call | tf_op jit(solution)/shard_map/analysis/pallas_call | solution.py:313
  150.1 21.4 %all_to_all.10.inc_ref = bf16[8,576,128]{2,1,0:T(8,128)(2,1)S(1)} all-to-all(bf16[8,576,128]{2,1,0:T(8,128)(2,1)} %analysis.1), channel_id=1, replica_groups=mesh['mem'=8,'state'=32] {'mem'}, dimensions={0} | all-to-all | bytes 2359296 | tf_op jit(solution)/shard_map/all_to_all | solution.py:326
  171.5 3.2 %final_step.1 = f32[64,32,256]{2,1,0:T(8,128)} custom-call(f32[34,64,256]{2,1,0:T(8,128)S(1)} %copy-done.4, bf16[8,576,128]{2,1,0:T(8,128)(2,1)S(1)} %all_to_all.10.inc_ref, f32[32,256]{1,0:T(8,128)S(1)} %copy-done.9), custom_call_target="tpu_custom_call" | custom-call | tf_op jit(solution)/shard_map/final_step/pallas_call | solution.py:328
  (59 shorter events, 7.0 us)
Async XLA Ops:
  1.7 13.9 %collective-permute-start.2 = (bf16[1,512,128]{2,1,0:T(8,128)(2,1)}, bf16[1,512,128]{2,1,0:T(8,128)(2,1)S(1)}, u32[]{:S(2)}, u32[]{:S(2)}) collective-permute-start(bf16[1,512,128]{2,1,0:T(8,128)(2,1)} %pack_obs.1.refs_0_), channel_id=1, source_target_pairs={{4,0},{5,1},{6,2},{7,3},{0,4},{1,5},{2,6},{3,7},{12,8},{13,9},{14,... | collective-permute-start | bytes 393224 | tf_op jit(solution)/shard_map/ppermute | solution.py:191
  11.6 20.8 %collective-permute-start = (f32[5,72,256]{2,1,0:T(8,128)}, f32[5,72,256]{2,1,0:T(8,128)S(1)}, u32[]{:S(2)}, u32[]{:S(2)}) collective-permute-start(f32[5,72,256]{2,1,0:T(8,128)} %get-tuple-element.11.refs_3_), channel_id=1, source_target_pairs={{0,1},{1,2},{2,3},{3,4},{4,5},{5,6},{6,7},{7,8},{8,9},{9,10},{10,1... | collective-permute-start | bytes 1105928 | tf_op jit(solution)/shard_map/ppermute | solution.py:282
  14.3 18.1 %collective-permute-start.1 = (f32[5,72,256]{2,1,0:T(8,128)}, f32[5,72,256]{2,1,0:T(8,128)S(1)}, u32[]{:S(2)}, u32[]{:S(2)}) collective-permute-start(f32[5,72,256]{2,1,0:T(8,128)} %get-tuple-element.12.refs_2_), channel_id=1, source_target_pairs={{1,0},{2,1},{3,2},{4,3},{5,4},{6,5},{7,6},{8,7},{9,8},{10,9},{11,1... | collective-permute-start | bytes 1105928 | tf_op jit(solution)/shard_map/ppermute | solution.py:281
  25.3 50.1 %copy-start = (f32[64,32,256]{2,1,0:T(8,128)S(1)}, f32[64,32,256]{2,1,0:T(8,128)}, u32[]{:S(2)}) copy-start(f32[64,32,256]{2,1,0:T(8,128)} %x_ref.1) | copy-start | bytes 6291460
  25.3 50.1 %copy-start.9 = (f32[32,256]{1,0:T(8,128)S(1)}, f32[32,256]{1,0:T(8,128)}, u32[]{:S(2)}) copy-start(f32[32,256]{1,0:T(8,128)} %coef_ref.5) | copy-start | bytes 98308
  25.4 10.8 %collective-permute-start.5 = (bf16[2,512,128]{2,1,0:T(8,128)(2,1)}, bf16[2,512,128]{2,1,0:T(8,128)(2,1)S(1)}, u32[]{:S(2)}, u32[]{:S(2)}) collective-permute-start(bf16[2,512,128]{2,1,0:T(8,128)(2,1)} %merge_two.1.refs_0_), channel_id=1, source_target_pairs={{16,0},{17,1},{18,2},{19,3},{20,4},{21,5},{22,6},{23,7},{24,8},{25... | collective-permute-start | bytes 786440 | tf_op jit(solution)/shard_map/ppermute | solution.py:191
  29.7 6.9 %collective-permute-start.4 = (bf16[2,512,128]{2,1,0:T(8,128)(2,1)}, bf16[2,512,128]{2,1,0:T(8,128)(2,1)S(1)}, u32[]{:S(2)}, u32[]{:S(2)}) collective-permute-start(bf16[2,512,128]{2,1,0:T(8,128)(2,1)} %merge_two.1.refs_0_), channel_id=1, source_target_pairs={{24,0},{25,1},{26,2},{27,3},{28,4},{29,5},{30,6},{31,7},{0,8},{1,9... | collective-permute-start | bytes 786440 | tf_op jit(solution)/shard_map/ppermute | solution.py:191
  30.2 8.8 %collective-permute-start.3 = (bf16[2,512,128]{2,1,0:T(8,128)(2,1)}, bf16[2,512,128]{2,1,0:T(8,128)(2,1)}, u32[]{:S(2)}, u32[]{:S(2)}) collective-permute-start(bf16[2,512,128]{2,1,0:T(8,128)(2,1)} %merge_two.1.refs_0_), channel_id=1, source_target_pairs={{8,0},{9,1},{10,2},{11,3},{12,4},{13,5},{14,6},{15,7},{16,8},{17,9... | collective-permute-start | bytes 786440 | tf_op jit(solution)/shard_map/ppermute | solution.py:191
  32.4 6.6 %copy-start.5 = (f32[5,72,256]{2,1,0:T(8,128)}, f32[5,72,256]{2,1,0:T(8,128)S(1)}, u32[]{:S(2)}) copy-start(f32[5,72,256]{2,1,0:T(8,128)S(1)} %collective-permute-done.above_ref.refs_4_) | copy-start | bytes 1105924
  72.0 20.3 %collective-permute-start.7 = (bf16[8,512,128]{2,1,0:T(8,128)(2,1)}, bf16[8,512,128]{2,1,0:T(8,128)(2,1)S(1)}, u32[]{:S(2)}, u32[]{:S(2)}) collective-permute-start(bf16[8,512,128]{2,1,0:T(8,128)(2,1)} %merge_eight.1.rest_0_), channel_id=1, source_target_pairs={{7,0},{0,1},{1,2},{2,3},{3,4},{4,5},{5,6},{6,7},{15,8},{8,9},{9,10... | collective-permute-start | bytes 3145736 | tf_op jit(solution)/shard_map/ppermute | solution.py:191
  74.5 17.8 %collective-permute-start.6 = (bf16[8,512,128]{2,1,0:T(8,128)(2,1)}, bf16[8,512,128]{2,1,0:T(8,128)(2,1)}, u32[]{:S(2)}, u32[]{:S(2)}) collective-permute-start(bf16[8,512,128]{2,1,0:T(8,128)(2,1)} %merge_eight.1.rest_0_), channel_id=1, source_target_pairs={{1,0},{2,1},{3,2},{4,3},{5,4},{6,5},{7,6},{0,7},{9,8},{10,9},{11,1... | collective-permute-start | bytes 3145736 | tf_op jit(solution)/shard_map/ppermute | solution.py:191
  85.2 53.1 %all-to-all-start = ((bf16[8,608,128]{2,1,0:T(8,128)(2,1)}), bf16[8,608,128]{2,1,0:T(8,128)(2,1)}, u32[]{:S(2)}, u32[]{:S(2)}) async-start(bf16[8,608,128]{2,1,0:T(8,128)(2,1)} %get-tuple-element.14.refs_2_), calls=%async_computation | async-start | bytes 2490368 | tf_op jit(solution)/shard_map/all_to_all | solution.py:304
  92.3 36.4 %copy-start.3 = (bf16[8,512,128]{2,1,0:T(8,128)(2,1)S(1)}, bf16[8,512,128]{2,1,0:T(8,128)(2,1)}, u32[]{:S(2)}) copy-start(bf16[8,512,128]{2,1,0:T(8,128)(2,1)} %merge_eight.1.rest_0_) | copy-start | bytes 3145732
  92.3 37.0 %copy-start.13 = (s32[64,4]{0,1:T(4,128)S(1)}, s32[64,4]{0,1:T(4,128)}, u32[]{:S(2)}) copy-start(s32[64,4]{0,1:T(4,128)} %param.13) | copy-start | bytes 3076
  92.3 37.1 %copy-start.14 = (s32[64,4]{0,1:T(4,128)S(1)}, s32[64,4]{0,1:T(4,128)}, u32[]{:S(2)}) copy-start(s32[64,4]{0,1:T(4,128)} %param.12) | copy-start | bytes 3076
  126.2 14.3 %copy-start.2 = (bf16[8,512,128]{2,1,0:T(8,128)(2,1)S(1)}, bf16[8,512,128]{2,1,0:T(8,128)(2,1)}, u32[]{:S(2)}) copy-start(bf16[8,512,128]{2,1,0:T(8,128)(2,1)} %copy-done.1) | copy-start | bytes 3145732
  126.2 8.9 %collective-permute-start.8 = (bf16[4,512,128]{2,1,0:T(8,128)(2,1)}, bf16[4,512,128]{2,1,0:T(8,128)(2,1)S(1)}, u32[]{:S(2)}, u32[]{:S(2)}) collective-permute-start(bf16[4,512,128]{2,1,0:T(8,128)(2,1)} %get-tuple-element.15), channel_id=1, source_target_pairs={{1,0},{2,1},{3,2},{4,3},{5,4},{6,5},{7,6},{0,7},{9,8},{10,9},{11,1... | collective-permute-start | bytes 1572872 | tf_op jit(solution)/shard_map/ppermute | solution.py:191
  128.7 9.6 %collective-permute-start.9 = (bf16[4,512,128]{2,1,0:T(8,128)(2,1)}, bf16[4,512,128]{2,1,0:T(8,128)(2,1)}, u32[]{:S(2)}, u32[]{:S(2)}) collective-permute-start(bf16[4,512,128]{2,1,0:T(8,128)(2,1)} %get-tuple-element.16), channel_id=1, source_target_pairs={{7,0},{0,1},{1,2},{2,3},{3,4},{4,5},{5,6},{6,7},{15,8},{8,9},{9,10... | collective-permute-start | bytes 1572872 | tf_op jit(solution)/shard_map/ppermute | solution.py:191
  128.7 9.7 %collective-permute-start.10 = (bf16[8,512,128]{2,1,0:T(8,128)(2,1)S(1)}, bf16[8,512,128]{2,1,0:T(8,128)(2,1)}, u32[]{:S(2)}, u32[]{:S(2)}) collective-permute-start(bf16[8,512,128]{2,1,0:T(8,128)(2,1)S(1)} %copy-done.3), channel_id=1, source_target_pairs={{32,0},{33,1},{34,2},{35,3},{36,4},{37,5},{38,6},{39,7},{40,8},{41... | collective-permute-start | bytes 3145736 | tf_op jit(solution)/shard_map/ppermute | solution.py:191
  128.7 9.7 %collective-permute-start.12 = (bf16[8,512,128]{2,1,0:T(8,128)(2,1)}, bf16[8,512,128]{2,1,0:T(8,128)(2,1)}, u32[]{:S(2)}, u32[]{:S(2)}) collective-permute-start(bf16[8,512,128]{2,1,0:T(8,128)(2,1)} %copy-done.1), channel_id=1, source_target_pairs={{32,0},{33,1},{34,2},{35,3},{36,4},{37,5},{38,6},{39,7},{40,8},{41... | collective-permute-start | bytes 3145736 | tf_op jit(solution)/shard_map/ppermute | solution.py:191
  129.2 9.2 %collective-permute-start.11 = (bf16[8,512,128]{2,1,0:T(8,128)(2,1)}, bf16[8,512,128]{2,1,0:T(8,128)(2,1)}, u32[]{:S(2)}, u32[]{:S(2)}) collective-permute-start(bf16[8,512,128]{2,1,0:T(8,128)(2,1)} %collective-permute-done.6.refs_0_.rest_1_), channel_id=1, source_target_pairs={{32,0},{33,1},{34,2},{35,3},{36,4},{37,5},{38,6},{39,7},{40,8},{41... | collective-permute-start | bytes 3145736 | tf_op jit(solution)/shard_map/ppermute | solution.py:191
  135.1 3.3 %collective-permute-start.13 = (bf16[4,512,128]{2,1,0:T(8,128)(2,1)S(1)}, bf16[4,512,128]{2,1,0:T(8,128)(2,1)}, u32[]{:S(2)}, u32[]{:S(2)}) collective-permute-start(bf16[4,512,128]{2,1,0:T(8,128)(2,1)S(1)} %collective-permute-done.8.rest_3_), channel_id=1, source_target_pairs={{32,0},{33,1},{34,2},{35,3},{36,4},{37,5},{38,6},{39,7},{40,8},{41... | collective-permute-start | bytes 1572872 | tf_op jit(solution)/shard_map/ppermute | solution.py:191
  138.2 2.3 %collective-permute-start.14 = (bf16[4,512,128]{2,1,0:T(8,128)(2,1)}, bf16[4,512,128]{2,1,0:T(8,128)(2,1)}, u32[]{:S(2)}, u32[]{:S(2)}) collective-permute-start(bf16[4,512,128]{2,1,0:T(8,128)(2,1)} %collective-permute-done.9.rest_4_), channel_id=1, source_target_pairs={{32,0},{33,1},{34,2},{35,3},{36,4},{37,5},{38,6},{39,7},{40,8},{41... | collective-permute-start | bytes 1572872 | tf_op jit(solution)/shard_map/ppermute | solution.py:191
  150.1 21.4 %copy-start.4 = (f32[34,64,256]{2,1,0:T(8,128)S(1)}, f32[34,64,256]{2,1,0:T(8,128)}, u32[]{:S(2)}) copy-start(f32[34,64,256]{2,1,0:T(8,128)} %get-tuple-element.13.prior_ref) | copy-start | bytes 6684676
  (7 other events, 15.3 us)

commit v3 on v2

--- a/solution.py
+++ b/solution.py
@@ -199,40 +199,60 @@
     return (x, 1 - c, y, z)
 
 
-def move(outs, plan, operands, name, after=()):
-    def kernel(*refs):
-        sources, targets, sems = refs[: len(operands)], refs[len(operands) + len(after) : -1], refs[-1]
-        core = lax.rem(lax.axis_index("mem"), 2)
-        copies = []
-        for i, (a, first, b, to, length) in enumerate(plan):
-            first = first(core) if callable(first) else first
-            copies.append(pltpu.make_async_copy(sources[a].at[pl.ds(first, length)], targets[b].at[pl.ds(to, length)], sems.at[i]))
-        for copy in copies:
-            copy.start()
-        for copy in copies:
-            copy.wait()
-
-    anywhere = pl.BlockSpec(memory_space=pl.ANY)
+def whole(value):
+    return pl.BlockSpec(value.shape, lambda i, c: (0,) * len(value.shape))
+
+
+def join(operands, core, name, after=()):
+    count, blocks = len(operands), operands[0].shape[0]
+
+    def kernel(core_ref, *refs):
+        out_ref = refs[-1]
+        for i in range(blocks):
+            for a in range(count):
+                out_ref[i * count + a] = refs[a][i]
+
     return pl.pallas_call(
         kernel,
-        out_shape=[jax.ShapeDtypeStruct((n, *operands[0].shape[1:]), operands[0].dtype) for n in outs],
-        in_specs=[anywhere] * (len(operands) + len(after)),
-        out_specs=[anywhere] * len(outs),
-        scratch_shapes=[pltpu.SemaphoreType.DMA((len(plan),))],
+        out_shape=jax.ShapeDtypeStruct((count * blocks, *operands[0].shape[1:]), BF16),
+        grid_spec=pltpu.PrefetchScalarGridSpec(
+            num_scalar_prefetch=1,
+            grid=(1,),
+            in_specs=[whole(v) for v in operands] + [pl.BlockSpec((1, 16, TILE), lambda i, c: (0, 0, 0))] * len(after),
+            out_specs=pl.BlockSpec((count * blocks, *operands[0].shape[1:]), lambda i, c: (0, 0, 0)),
+        ),
         name=name,
-    )(*operands, *after)
-
-
-def gather_obs(own, mesh, after_first, after_second, after_third):
+    )(core, *operands, *after)
+
+
+def halves(p, m, core, after):
+    def kernel(core_ref, p_ref, m_ref, after_ref, q_ref, r_ref):
+        q_ref[...] = p_ref[...]
+        r_ref[...] = m_ref[...]
+
+    shape = (p.shape[0] // 2, *p.shape[1:])
+    first = pl.BlockSpec(shape, lambda i, c: (0, 0, 0))
+    return pl.pallas_call(
+        kernel,
+        out_shape=[jax.ShapeDtypeStruct(shape, BF16)] * 2,
+        grid_spec=pltpu.PrefetchScalarGridSpec(
+            num_scalar_prefetch=1,
+            grid=(1,),
+            in_specs=[first, pl.BlockSpec(shape, lambda i, c: (c[0], 0, 0)), pl.BlockSpec((1, 16, TILE), lambda i, c: (0, 0, 0))],
+            out_specs=[first] * 2,
+        ),
+        name="halves",
+    )(core, p, m, after)
+
+
+def gather_obs(own, mesh, core, edges, arrived, payload):
     far = fetch(own, mesh, lambda x, c, y, z: (x, c, y, z + 4))
-    (held,) = move([2], [(0, 0, 0, 0, 1), (1, 0, 0, 1, 1)], [own, far], "merge_two", after_first)
+    held = join([own, far], core, "join_two", edges)
     p, m, q = (fetch(held, mesh, ring(True, step)) for step in (1, -1, 2))
-    plan = [(a, i, 0, 4 * i + a, 1) for i in range(2) for a in range(4)]
-    (held,) = move([8], plan, [held, p, m, q], "merge_eight", after_second())
+    held = join([held, p, m, q], core, "join_eight", arrived)
     p, m = (fetch(held, mesh, ring(False, step)) for step in (1, -1))
     swapped = [fetch(held, mesh, other_core)]
-    plan = [(0, 0, 0, 0, 4), (1, lambda core: 4 * core, 1, 0, 4)]
-    q, r = move([4, 4], plan, [p, m], "halves", after_third())
+    q, r = halves(p, m, core, payload)
     q = fetch(q, mesh, ring(False, 1))
     r = fetch(r, mesh, ring(False, -1))
     swapped += [fetch(v, mesh, other_core) for v in (p, m, q, r)]
@@ -298,9 +318,8 @@
         compiler_params=limit,
         name="forecast4",
     )(ensemble, above, below, spreading_coefficient)
-    own, swapped = gather_obs(
-        packed, (group // 2, states // 8, 8), [up, down], lambda: [above, below], lambda: [payload]
-    )
+    core = (j % 2).reshape(1)
+    own, swapped = gather_obs(packed, (group // 2, states // 8, 8), core, [up, down], [above, below], payload)
     gathered = lax.all_to_all(payload, "mem", split_axis=0, concat_axis=0, tiled=True)
 
     edge = jnp.where(j < 2, above[0, members, :16], below[HALO - 1, members, :16])

time: 175 us -> 110 us (0.63)
  Pallas kernels: 99.3 us -> 30.7 us
  starting transfers between devices: 33.1 us -> 35.3 us
    pallas_call x3, Pallas kernels: 74.9 us -> 6.21 us  [the longest x2 3.97 us: join(): pl.pallas_call(kernel, out_shape=jax.ShapeDtypeStruct((count * blocks, *o...]
    ppermute x13, starting transfers between devices: 22 us -> 26.9 us  [fetch(): return lax.ppermute(value, AXES, pairs)]
    all_to_all x1, starting transfers between devices: 7.09 us -> 4.41 us  [body(): lax.all_to_all(payload, 'mem', split_axis=0, concat_axis=0, tiled=True)]
  transfers between devices with their start and end apart: 16 -> 16, of which waited for: 6 -> 6; matrix products, arithmetic and copies ran while one was open for 1% -> 2% of each run, Pallas kernels for 30% -> 13%
where the time goes in v3:
time: 110 us; the launch traced here: 109 us
  starting transfers between devices  35.3 us (32%)
  Pallas kernels  30.7 us (28%)
  blocking collectives  21.9 us (20%)
  waiting for transfers between devices  15.2 us (14%)
  local copies, waits for them, and re-layouts  5.32 us (5%)
    ppermute x13, starting transfers between devices, fetch(): return lax.ppermute(value, AXES, pairs)  26.9 us
    all_to_all x1, blocking collectives, body(): lax.all_to_all(increments, 'mem', split_axis=0, concat_axis=0, tiled=True)  21.9 us
    ppermute x13, waiting for transfers between devices, fetch(): return lax.ppermute(value, AXES, pairs)  14.9 us
    pallas_call x1, Pallas kernels, body(): pl.pallas_call(analysis_kernel, out_shape=jax.ShapeDtypeStruct((group, ti...  9.62 us
    pallas_call x1, Pallas kernels, body(): pl.pallas_call(forecast_kernel, out_shape=[jax.ShapeDtypeStruct((rows + 2...  7.74 us
    unnamed x33, local copies, waits for them, and re-layouts  5.03 us
    all_to_all x1, starting transfers between devices, body(): lax.all_to_all(payload, 'mem', split_axis=0, concat_axis=0, tiled=True)  4.41 us
    pallas_call x2, Pallas kernels, join(): pl.pallas_call(kernel, out_shape=jax.ShapeDtypeStruct((count * blocks, *o...  3.97 us
  transfers between devices with their start and end apart: 16, of which 6 were waited for; matrix products, arithmetic and copies ran while one was open for 2% of the time, Pallas kernels for 13%

profile of v3, /device:TPU:1, one launch (start us, length us, event | category | flops | bytes accessed | tf_op | source)
XLA Modules:
  0.0 109.4 jit_solution(5819017657045814904)
XLA Ops:
  0.0 1.7 %pack_obs.1.refs_0_ = bf16[1,512,128]{2,1,0:T(8,128)(2,1)} custom-call(bf16[1,128,512]{2,1,0:T(8,128)(2,1)} %anom_ref.1, bf16[1,128,512]{2,1,0:T(8,128)(2,1)} %weight_ref.1), custom_call_target="tpu_custom_call" | custom-call | tf_op jit(solution)/shard_map/pack_obs/pallas_call | solution.py:280
  1.7 7.7 %collective-permute-start.2 = (bf16[1,512,128]{2,1,0:T(8,128)(2,1)}, bf16[1,512,128]{2,1,0:T(8,128)(2,1)S(1)}, u32[]{:S(2)}, u32[]{:S(2)}) collective-permute-start(bf16[1,512,128]{2,1,0:T(8,128)(2,1)} %pack_obs.1.refs_0_), channel_id=1, source_target_pairs={{4,0},{5,1},{6,2},{7,3},{0,4},{1,5},{2,6},{3,7},{12,8},{13,9},{14,... | collective-permute-start | bytes 393224 | tf_op jit(solution)/shard_map/ppermute | solution.py:191
  9.4 2.2 %pack_halo.1 = (f32[5,72,256]{2,1,0:T(8,128)}, f32[5,72,256]{2,1,0:T(8,128)}) custom-call(f32[64,32,256]{2,1,0:T(8,128)} %x_ref.1, f32[64,32,256]{2,1,0:T(8,128)} %x_ref.1, f32[32,256]{1,0:T(8,128)} %coef_ref.5, s32[4,64]{1,0:T(4,128)} %bitcast.6, s32[4,64]{1,0:T(4,128)} %bitcast.5), custom_call_target="tpu_custom_call" | custom-call | tf_op jit(solution)/shard_map/pack_halo/pallas_call | solution.py:287
  11.6 2.7 %collective-permute-start = (f32[5,72,256]{2,1,0:T(8,128)}, f32[5,72,256]{2,1,0:T(8,128)S(1)}, u32[]{:S(2)}, u32[]{:S(2)}) collective-permute-start(f32[5,72,256]{2,1,0:T(8,128)} %get-tuple-element.11.refs_3_), channel_id=1, source_target_pairs={{0,1},{1,2},{2,3},{3,4},{4,5},{5,6},{6,7},{7,8},{8,9},{9,10},{10,1... | collective-permute-start | bytes 1105928 | tf_op jit(solution)/shard_map/ppermute | solution.py:302
  16.3 1.7 %join_two.1.refs_0_ = bf16[2,512,128]{2,1,0:T(8,128)(2,1)} custom-call(s32[1]{0:T(128)} %bitcast.3.core_ref, bf16[1,512,128]{2,1,0:T(8,128)(2,1)} %pack_obs.1.refs_0_, bf16[1,512,128]{2,1,0:T(8,128)(2,1)} %copy-done.12, f32[5,72,256]{2,1,0:T(8,128)} %get-tuple-element.12.refs_2_, f32[5,72,256]{2,1,0:T(8,128)} %get-tuple-element.11.refs_3_), custom_call_target="tpu_custom_call" | custom-call | tf_op jit(solution)/shard_map/join_two/pallas_call | solution.py:215
  18.0 4.3 %collective-permute-start.5 = (bf16[2,512,128]{2,1,0:T(8,128)(2,1)}, bf16[2,512,128]{2,1,0:T(8,128)(2,1)S(1)}, u32[]{:S(2)}, u32[]{:S(2)}) collective-permute-start(bf16[2,512,128]{2,1,0:T(8,128)(2,1)} %join_two.1.refs_0_), channel_id=1, source_target_pairs={{16,0},{17,1},{18,2},{19,3},{20,4},{21,5},{22,6},{23,7},{24,8},{25... | collective-permute-start | bytes 786440 | tf_op jit(solution)/shard_map/ppermute | solution.py:191
  22.7 2.2 %collective-permute-start.3 = (bf16[2,512,128]{2,1,0:T(8,128)(2,1)}, bf16[2,512,128]{2,1,0:T(8,128)(2,1)}, u32[]{:S(2)}, u32[]{:S(2)}) collective-permute-start(bf16[2,512,128]{2,1,0:T(8,128)(2,1)} %join_two.1.refs_0_), channel_id=1, source_target_pairs={{8,0},{9,1},{10,2},{11,3},{12,4},{13,5},{14,6},{15,7},{16,8},{17,9... | collective-permute-start | bytes 786440 | tf_op jit(solution)/shard_map/ppermute | solution.py:191
  25.3 7.8 %collective-permute-done.5.refs_3_ = bf16[2,512,128]{2,1,0:T(8,128)(2,1)S(1)} collective-permute-done((bf16[2,512,128]{2,1,0:T(8,128)(2,1)}, bf16[2,512,128]{2,1,0:T(8,128)(2,1)S(1)}, u32[]{:S(2)}, u32[]{:S(2)}) %collective-permute-start.5) | collective-permute-done | bytes 262176 | tf_op jit(solution)/shard_map/ppermute | solution.py:191
  33.1 2.1 %collective-permute-done.3.refs_1_ = bf16[2,512,128]{2,1,0:T(8,128)(2,1)} collective-permute-done((bf16[2,512,128]{2,1,0:T(8,128)(2,1)}, bf16[2,512,128]{2,1,0:T(8,128)(2,1)}, u32[]{:S(2)}, u32[]{:S(2)}) %collective-permute-start.3) | collective-permute-done | bytes 262176 | tf_op jit(solution)/shard_map/ppermute | solution.py:191
  35.3 2.3 %join_eight.1.rest_0_ = bf16[8,512,128]{2,1,0:T(8,128)(2,1)} custom-call(s32[1]{0:T(128)} %bitcast.3.core_ref, bf16[2,512,128]{2,1,0:T(8,128)(2,1)} %join_two.1.refs_0_, bf16[2,512,128]{2,1,0:T(8,128)(2,1)} %collective-permute-done.3.refs_1_, bf16[2,512,128]{2,1,0:T(8,128)(2,1)} %copy-done.11, bf16[2,512,128]{2,1,0:T(8,128)(2,1)} %copy-done.10, ...), custom_call_target="tpu_custom_call" | custom-call | tf_op jit(solution)/shard_map/join_eight/pallas_call | solution.py:215
  37.5 2.2 %collective-permute-start.7 = (bf16[8,512,128]{2,1,0:T(8,128)(2,1)}, bf16[8,512,128]{2,1,0:T(8,128)(2,1)S(1)}, u32[]{:S(2)}, u32[]{:S(2)}) collective-permute-start(bf16[8,512,128]{2,1,0:T(8,128)(2,1)} %join_eight.1.rest_0_), channel_id=1, source_target_pairs={{7,0},{0,1},{1,2},{2,3},{3,4},{4,5},{5,6},{6,7},{15,8},{8,9},{9,10... | collective-permute-start | bytes 3145736 | tf_op jit(solution)/shard_map/ppermute | solution.py:191
  39.7 1.4 %collective-permute-start.6 = (bf16[8,512,128]{2,1,0:T(8,128)(2,1)}, bf16[8,512,128]{2,1,0:T(8,128)(2,1)}, u32[]{:S(2)}, u32[]{:S(2)}) collective-permute-start(bf16[8,512,128]{2,1,0:T(8,128)(2,1)} %join_eight.1.rest_0_), channel_id=1, source_target_pairs={{1,0},{2,1},{3,2},{4,3},{5,4},{6,5},{7,6},{0,7},{9,8},{10,9},{11,1... | collective-permute-start | bytes 3145736 | tf_op jit(solution)/shard_map/ppermute | solution.py:191
  43.2 7.7 %forecast4.1 = (f32[34,64,256]{2,1,0:T(8,128)}, bf16[8,608,128]{2,1,0:T(8,128)(2,1)}) custom-call(f32[64,32,256]{2,1,0:T(8,128)S(1)} %copy-done, f32[5,72,256]{2,1,0:T(8,128)S(1)} %copy-done.6, f32[5,72,256]{2,1,0:T(8,128)S(1)} %copy-done.8, f32[32,256]{1,0:T(8,128)S(1)} %copy-done.9), custom_call_target="tpu_custom_call" | custom-call | tf_op jit(solution)/shard_map/forecast4/pallas_call | solution.py:304
  50.9 4.4 %all-to-all-start = ((bf16[8,608,128]{2,1,0:T(8,128)(2,1)}), bf16[8,608,128]{2,1,0:T(8,128)(2,1)}, u32[]{:S(2)}, u32[]{:S(2)}) async-start(bf16[8,608,128]{2,1,0:T(8,128)(2,1)} %get-tuple-element.14.after_ref), calls=%async_computation | async-start | bytes 2490368 | tf_op jit(solution)/shard_map/all_to_all | solution.py:323
  56.3 2.2 %halves.1 = (bf16[4,512,128]{2,1,0:T(8,128)(2,1)}, bf16[4,512,128]{2,1,0:T(8,128)(2,1)}) custom-call(s32[1]{0:T(128)} %bitcast.3.core_ref, bf16[8,512,128]{2,1,0:T(8,128)(2,1)} %collective-permute-done.6.p_ref.rest_1_, bf16[8,512,128]{2,1,0:T(8,128)(2,1)} %copy-done.2, bf16[8,608,128]{2,1,0:T(8,128)(2,1)} %get-tuple-element.14.after_ref), custom_call_target="tpu_custom_call" | custom-call | tf_op jit(solution)/shard_map/halves/pallas_call | solution.py:235
  58.6 1.5 %collective-permute-start.8 = (bf16[4,512,128]{2,1,0:T(8,128)(2,1)}, bf16[4,512,128]{2,1,0:T(8,128)(2,1)S(1)}, u32[]{:S(2)}, u32[]{:S(2)}) collective-permute-start(bf16[4,512,128]{2,1,0:T(8,128)(2,1)} %get-tuple-element.15), channel_id=1, source_target_pairs={{1,0},{2,1},{3,2},{4,3},{5,4},{6,5},{7,6},{0,7},{9,8},{10,9},{11,1... | collective-permute-start | bytes 1572872 | tf_op jit(solution)/shard_map/ppermute | solution.py:191
  60.1 2.0 %collective-permute-start.10 = (bf16[8,512,128]{2,1,0:T(8,128)(2,1)S(1)}, bf16[8,512,128]{2,1,0:T(8,128)(2,1)}, u32[]{:S(2)}, u32[]{:S(2)}) collective-permute-start(bf16[8,512,128]{2,1,0:T(8,128)(2,1)S(1)} %copy-done.1), channel_id=1, source_target_pairs={{32,0},{33,1},{34,2},{35,3},{36,4},{37,5},{38,6},{39,7},{40,8},{41... | collective-permute-start | bytes 3145736 | tf_op jit(solution)/shard_map/ppermute | solution.py:191
  64.9 2.3 %collective-permute-done.8.rest_3_ = bf16[4,512,128]{2,1,0:T(8,128)(2,1)S(1)} collective-permute-done((bf16[4,512,128]{2,1,0:T(8,128)(2,1)}, bf16[4,512,128]{2,1,0:T(8,128)(2,1)S(1)}, u32[]{:S(2)}, u32[]{:S(2)}) %collective-permute-start.8) | collective-permute-done | bytes 524320 | tf_op jit(solution)/shard_map/ppermute | solution.py:191
  67.2 1.8 %collective-permute-start.13 = (bf16[4,512,128]{2,1,0:T(8,128)(2,1)S(1)}, bf16[4,512,128]{2,1,0:T(8,128)(2,1)}, u32[]{:S(2)}, u32[]{:S(2)}) collective-permute-start(bf16[4,512,128]{2,1,0:T(8,128)(2,1)S(1)} %collective-permute-done.8.rest_3_), channel_id=1, source_target_pairs={{32,0},{33,1},{34,2},{35,3},{36,4},{37,5},{38,6},{39,7},{40,8},{41... | collective-permute-start | bytes 1572872 | tf_op jit(solution)/shard_map/ppermute | solution.py:191
  69.9 2.8 %collective-permute-start.14 = (bf16[4,512,128]{2,1,0:T(8,128)(2,1)}, bf16[4,512,128]{2,1,0:T(8,128)(2,1)}, u32[]{:S(2)}, u32[]{:S(2)}) collective-permute-start(bf16[4,512,128]{2,1,0:T(8,128)(2,1)} %collective-permute-done.9.rest_4_), channel_id=1, source_target_pairs={{32,0},{33,1},{34,2},{35,3},{36,4},{37,5},{38,6},{39,7},{40,8},{41... | collective-permute-start | bytes 1572872 | tf_op jit(solution)/shard_map/ppermute | solution.py:191
  72.8 1.8 %collective-permute-done.14.rest_9_ = bf16[4,512,128]{2,1,0:T(8,128)(2,1)} collective-permute-done((bf16[4,512,128]{2,1,0:T(8,128)(2,1)}, bf16[4,512,128]{2,1,0:T(8,128)(2,1)}, u32[]{:S(2)}, u32[]{:S(2)}) %collective-permute-start.14) | collective-permute-done | bytes 524320 | tf_op jit(solution)/shard_map/ppermute | solution.py:191
  74.6 9.6 %analysis.1 = bf16[8,576,128]{2,1,0:T(8,128)(2,1)} custom-call(s32[9,4]{1,0:T(8,128)S(1)} %get-tuple-element.18.anom_at_ref, s32[9,4]{1,0:T(8,128)S(1)} %get-tuple-element.17.weight_at_ref, s32[9,4]{1,0:T(8,128)S(1)} %get-tuple-element.21.tapers_ref, bf16[8,608,128]{2,1,0:T(8,128)(2,1)} %all-to-all-done.recv_ref, f32[8,128,128]{2,1,0:T(8,128)S(1)} %bitcast.4, ...), custom_call_target="tpu_custom_call" | custom-call | tf_op jit(solution)/shard_map/analysis/pallas_call | solution.py:332
  84.2 21.9 %all_to_all.10.inc_ref = bf16[8,576,128]{2,1,0:T(8,128)(2,1)S(1)} all-to-all(bf16[8,576,128]{2,1,0:T(8,128)(2,1)} %analysis.1), channel_id=1, replica_groups=mesh['mem'=8,'state'=32] {'mem'}, dimensions={0} | all-to-all | bytes 2359296 | tf_op jit(solution)/shard_map/all_to_all | solution.py:345
  106.2 3.2 %final_step.1 = f32[64,32,256]{2,1,0:T(8,128)} custom-call(f32[34,64,256]{2,1,0:T(8,128)S(1)} %copy-done.4, bf16[8,576,128]{2,1,0:T(8,128)(2,1)S(1)} %all_to_all.10.inc_ref, f32[32,256]{1,0:T(8,128)S(1)} %copy-done.9), custom_call_target="tpu_custom_call" | custom-call | tf_op jit(solution)/shard_map/final_step/pallas_call | solution.py:347
  (59 shorter events, 9.6 us)
Async XLA Ops:
  1.7 13.9 %collective-permute-start.2 = (bf16[1,512,128]{2,1,0:T(8,128)(2,1)}, bf16[1,512,128]{2,1,0:T(8,128)(2,1)S(1)}, u32[]{:S(2)}, u32[]{:S(2)}) collective-permute-start(bf16[1,512,128]{2,1,0:T(8,128)(2,1)} %pack_obs.1.refs_0_), channel_id=1, source_target_pairs={{4,0},{5,1},{6,2},{7,3},{0,4},{1,5},{2,6},{3,7},{12,8},{13,9},{14,... | collective-permute-start | bytes 393224 | tf_op jit(solution)/shard_map/ppermute | solution.py:191
  11.6 13.3 %collective-permute-start = (f32[5,72,256]{2,1,0:T(8,128)}, f32[5,72,256]{2,1,0:T(8,128)S(1)}, u32[]{:S(2)}, u32[]{:S(2)}) collective-permute-start(f32[5,72,256]{2,1,0:T(8,128)} %get-tuple-element.11.refs_3_), channel_id=1, source_target_pairs={{0,1},{1,2},{2,3},{3,4},{4,5},{5,6},{6,7},{7,8},{8,9},{9,10},{10,1... | collective-permute-start | bytes 1105928 | tf_op jit(solution)/shard_map/ppermute | solution.py:302
  14.3 11.0 %collective-permute-start.1 = (f32[5,72,256]{2,1,0:T(8,128)}, f32[5,72,256]{2,1,0:T(8,128)S(1)}, u32[]{:S(2)}, u32[]{:S(2)}) collective-permute-start(f32[5,72,256]{2,1,0:T(8,128)} %get-tuple-element.12.refs_2_), channel_id=1, source_target_pairs={{1,0},{2,1},{3,2},{4,3},{5,4},{6,5},{7,6},{8,7},{9,8},{10,9},{11,1... | collective-permute-start | bytes 1105928 | tf_op jit(solution)/shard_map/ppermute | solution.py:301
  18.0 23.2 %copy-start = (f32[64,32,256]{2,1,0:T(8,128)S(1)}, f32[64,32,256]{2,1,0:T(8,128)}, u32[]{:S(2)}) copy-start(f32[64,32,256]{2,1,0:T(8,128)} %x_ref.1) | copy-start | bytes 6291460
  18.0 23.2 %copy-start.9 = (f32[32,256]{1,0:T(8,128)S(1)}, f32[32,256]{1,0:T(8,128)}, u32[]{:S(2)}) copy-start(f32[32,256]{1,0:T(8,128)} %coef_ref.5) | copy-start | bytes 98308
  18.0 15.1 %collective-permute-start.5 = (bf16[2,512,128]{2,1,0:T(8,128)(2,1)}, bf16[2,512,128]{2,1,0:T(8,128)(2,1)S(1)}, u32[]{:S(2)}, u32[]{:S(2)}) collective-permute-start(bf16[2,512,128]{2,1,0:T(8,128)(2,1)} %join_two.1.refs_0_), channel_id=1, source_target_pairs={{16,0},{17,1},{18,2},{19,3},{20,4},{21,5},{22,6},{23,7},{24,8},{25... | collective-permute-start | bytes 786440 | tf_op jit(solution)/shard_map/ppermute | solution.py:191
  22.3 10.8 %collective-permute-start.4 = (bf16[2,512,128]{2,1,0:T(8,128)(2,1)}, bf16[2,512,128]{2,1,0:T(8,128)(2,1)S(1)}, u32[]{:S(2)}, u32[]{:S(2)}) collective-permute-start(bf16[2,512,128]{2,1,0:T(8,128)(2,1)} %join_two.1.refs_0_), channel_id=1, source_target_pairs={{24,0},{25,1},{26,2},{27,3},{28,4},{29,5},{30,6},{31,7},{0,8},{1,9... | collective-permute-start | bytes 786440 | tf_op jit(solution)/shard_map/ppermute | solution.py:191
  22.7 12.5 %collective-permute-start.3 = (bf16[2,512,128]{2,1,0:T(8,128)(2,1)}, bf16[2,512,128]{2,1,0:T(8,128)(2,1)}, u32[]{:S(2)}, u32[]{:S(2)}) collective-permute-start(bf16[2,512,128]{2,1,0:T(8,128)(2,1)} %join_two.1.refs_0_), channel_id=1, source_target_pairs={{8,0},{9,1},{10,2},{11,3},{12,4},{13,5},{14,6},{15,7},{16,8},{17,9... | collective-permute-start | bytes 786440 | tf_op jit(solution)/shard_map/ppermute | solution.py:191
  25.0 10.3 %copy-start.5 = (f32[5,72,256]{2,1,0:T(8,128)}, f32[5,72,256]{2,1,0:T(8,128)S(1)}, u32[]{:S(2)}) copy-start(f32[5,72,256]{2,1,0:T(8,128)S(1)} %collective-permute-done.above_ref.refs_4_) | copy-start | bytes 1105924
  25.3 9.9 %copy-start.7 = (f32[5,72,256]{2,1,0:T(8,128)}, f32[5,72,256]{2,1,0:T(8,128)S(1)}, u32[]{:S(2)}) copy-start(f32[5,72,256]{2,1,0:T(8,128)S(1)} %collective-permute-done.1.below_ref.refs_5_) | copy-start | bytes 1105924
  37.5 17.8 %collective-permute-start.7 = (bf16[8,512,128]{2,1,0:T(8,128)(2,1)}, bf16[8,512,128]{2,1,0:T(8,128)(2,1)S(1)}, u32[]{:S(2)}, u32[]{:S(2)}) collective-permute-start(bf16[8,512,128]{2,1,0:T(8,128)(2,1)} %join_eight.1.rest_0_), channel_id=1, source_target_pairs={{7,0},{0,1},{1,2},{2,3},{3,4},{4,5},{5,6},{6,7},{15,8},{8,9},{9,10... | collective-permute-start | bytes 3145736 | tf_op jit(solution)/shard_map/ppermute | solution.py:191
  39.7 15.6 %collective-permute-start.6 = (bf16[8,512,128]{2,1,0:T(8,128)(2,1)}, bf16[8,512,128]{2,1,0:T(8,128)(2,1)}, u32[]{:S(2)}, u32[]{:S(2)}) collective-permute-start(bf16[8,512,128]{2,1,0:T(8,128)(2,1)} %join_eight.1.rest_0_), channel_id=1, source_target_pairs={{1,0},{2,1},{3,2},{4,3},{5,4},{6,5},{7,6},{0,7},{9,8},{10,9},{11,1... | collective-permute-start | bytes 3145736 | tf_op jit(solution)/shard_map/ppermute | solution.py:191
  50.9 21.9 %all-to-all-start = ((bf16[8,608,128]{2,1,0:T(8,128)(2,1)}), bf16[8,608,128]{2,1,0:T(8,128)(2,1)}, u32[]{:S(2)}, u32[]{:S(2)}) async-start(bf16[8,608,128]{2,1,0:T(8,128)(2,1)} %get-tuple-element.14.after_ref), calls=%async_computation | async-start | bytes 2490368 | tf_op jit(solution)/shard_map/all_to_all | solution.py:323
  55.3 7.2 %copy-start.13 = (s32[64,4]{0,1:T(4,128)S(1)}, s32[64,4]{0,1:T(4,128)}, u32[]{:S(2)}) copy-start(s32[64,4]{0,1:T(4,128)} %param.13) | copy-start | bytes 3076
  55.3 7.4 %copy-start.14 = (s32[64,4]{0,1:T(4,128)S(1)}, s32[64,4]{0,1:T(4,128)}, u32[]{:S(2)}) copy-start(s32[64,4]{0,1:T(4,128)} %param.12) | copy-start | bytes 3076
  58.6 16.0 %copy-start.3 = (bf16[8,512,128]{2,1,0:T(8,128)(2,1)S(1)}, bf16[8,512,128]{2,1,0:T(8,128)(2,1)}, u32[]{:S(2)}) copy-start(bf16[8,512,128]{2,1,0:T(8,128)(2,1)} %copy-done.2) | copy-start | bytes 3145732
  58.6 8.6 %collective-permute-start.8 = (bf16[4,512,128]{2,1,0:T(8,128)(2,1)}, bf16[4,512,128]{2,1,0:T(8,128)(2,1)S(1)}, u32[]{:S(2)}, u32[]{:S(2)}) collective-permute-start(bf16[4,512,128]{2,1,0:T(8,128)(2,1)} %get-tuple-element.15), channel_id=1, source_target_pairs={{1,0},{2,1},{3,2},{4,3},{5,4},{6,5},{7,6},{0,7},{9,8},{10,9},{11,1... | collective-permute-start | bytes 1572872 | tf_op jit(solution)/shard_map/ppermute | solution.py:191
  60.0 9.9 %collective-permute-start.9 = (bf16[4,512,128]{2,1,0:T(8,128)(2,1)}, bf16[4,512,128]{2,1,0:T(8,128)(2,1)}, u32[]{:S(2)}, u32[]{:S(2)}) collective-permute-start(bf16[4,512,128]{2,1,0:T(8,128)(2,1)} %get-tuple-element.16), channel_id=1, source_target_pairs={{7,0},{0,1},{1,2},{2,3},{3,4},{4,5},{5,6},{6,7},{15,8},{8,9},{9,10... | collective-permute-start | bytes 1572872 | tf_op jit(solution)/shard_map/ppermute | solution.py:191
  60.1 12.7 %collective-permute-start.10 = (bf16[8,512,128]{2,1,0:T(8,128)(2,1)S(1)}, bf16[8,512,128]{2,1,0:T(8,128)(2,1)}, u32[]{:S(2)}, u32[]{:S(2)}) collective-permute-start(bf16[8,512,128]{2,1,0:T(8,128)(2,1)S(1)} %copy-done.1), channel_id=1, source_target_pairs={{32,0},{33,1},{34,2},{35,3},{36,4},{37,5},{38,6},{39,7},{40,8},{41... | collective-permute-start | bytes 3145736 | tf_op jit(solution)/shard_map/ppermute | solution.py:191
  62.0 10.8 %collective-permute-start.12 = (bf16[8,512,128]{2,1,0:T(8,128)(2,1)}, bf16[8,512,128]{2,1,0:T(8,128)(2,1)}, u32[]{:S(2)}, u32[]{:S(2)}) collective-permute-start(bf16[8,512,128]{2,1,0:T(8,128)(2,1)} %copy-done.2), channel_id=1, source_target_pairs={{32,0},{33,1},{34,2},{35,3},{36,4},{37,5},{38,6},{39,7},{40,8},{41... | collective-permute-start | bytes 3145736 | tf_op jit(solution)/shard_map/ppermute | solution.py:191
  62.1 10.7 %collective-permute-start.11 = (bf16[8,512,128]{2,1,0:T(8,128)(2,1)}, bf16[8,512,128]{2,1,0:T(8,128)(2,1)}, u32[]{:S(2)}, u32[]{:S(2)}) collective-permute-start(bf16[8,512,128]{2,1,0:T(8,128)(2,1)} %collective-permute-done.6.p_ref.rest_1_), channel_id=1, source_target_pairs={{32,0},{33,1},{34,2},{35,3},{36,4},{37,5},{38,6},{39,7},{40,8},{41... | collective-permute-start | bytes 3145736 | tf_op jit(solution)/shard_map/ppermute | solution.py:191
  67.2 5.6 %collective-permute-start.13 = (bf16[4,512,128]{2,1,0:T(8,128)(2,1)S(1)}, bf16[4,512,128]{2,1,0:T(8,128)(2,1)}, u32[]{:S(2)}, u32[]{:S(2)}) collective-permute-start(bf16[4,512,128]{2,1,0:T(8,128)(2,1)S(1)} %collective-permute-done.8.rest_3_), channel_id=1, source_target_pairs={{32,0},{33,1},{34,2},{35,3},{36,4},{37,5},{38,6},{39,7},{40,8},{41... | collective-permute-start | bytes 1572872 | tf_op jit(solution)/shard_map/ppermute | solution.py:191
  69.9 4.7 %collective-permute-start.14 = (bf16[4,512,128]{2,1,0:T(8,128)(2,1)}, bf16[4,512,128]{2,1,0:T(8,128)(2,1)}, u32[]{:S(2)}, u32[]{:S(2)}) collective-permute-start(bf16[4,512,128]{2,1,0:T(8,128)(2,1)} %collective-permute-done.9.rest_4_), channel_id=1, source_target_pairs={{32,0},{33,1},{34,2},{35,3},{36,4},{37,5},{38,6},{39,7},{40,8},{41... | collective-permute-start | bytes 1572872 | tf_op jit(solution)/shard_map/ppermute | solution.py:191
  84.2 22.0 %copy-start.4 = (f32[34,64,256]{2,1,0:T(8,128)S(1)}, f32[34,64,256]{2,1,0:T(8,128)}, u32[]{:S(2)}) copy-start(f32[34,64,256]{2,1,0:T(8,128)} %get-tuple-element.13.prior_ref) | copy-start | bytes 6684676
  (7 other events, 12.6 us)

commit v4 on v3

--- a/solution.py
+++ b/solution.py
@@ -108,7 +108,7 @@
 
 
 def analysis_kernel(anom_at_ref, weight_at_ref, tapers_ref, recv_ref, taper_ref, *rest):
-    pieces, (ret_ref, obs_ref, shift_ref, sems) = rest[:-4], rest[-4:]
+    pieces, (ret_ref, obs_ref, centred_ref, sems) = rest[:-4], rest[-4:]
     group, size, _ = recv_ref.shape
     count = ret_ref.shape[1] // anom_at_ref.shape[0]
     tiles = anom_at_ref.shape[0]
@@ -128,25 +128,24 @@
     parts = recv_ref[:, size - 32 :, :].astype(F32)
     for t in range(tiles):
         own = parts[:, 3 * t, :] + parts[:, 3 * t + 1, :] + parts[:, 3 * t + 2, :]
-        shift_ref[t] = own - jnp.mean(own, axis=0, keepdims=True)
+        delta = own - jnp.mean(own, axis=0, keepdims=True)
+        local = recv_ref[:, t * count : (t + 1) * count, :].astype(F32)
+        centred_ref[t] = (local + delta[:, None, :]).astype(BF16).reshape(members, TILE)
     for copy in copies:
         copy.wait()
 
     def one(t, carry):
+        anoms, weights = [], []
+        for k in range(SLOTS):
+            at = anom_at_ref[t, k]
+            anoms.append(jnp.concatenate([obs_ref[0, at, q * TILE : (q + 1) * TILE, :] for q in range(members // TILE)], axis=1))
+            weights.append(obs_ref[1, weight_at_ref[t, k]])
+        cov = jnp.dot(jnp.concatenate(anoms, axis=0), centred_ref[t], preferred_element_type=F32) * (1.0 / (members - 1.0))
+        tapered = [
+            (taper_ref[tapers_ref[t, k]] * cov[k * TILE : (k + 1) * TILE]).astype(BF16) for k in range(SLOTS)
+        ]
+        total = jnp.dot(jnp.concatenate(weights, axis=1), jnp.concatenate(tapered, axis=0), preferred_element_type=F32)
         here = pl.ds(pl.multiple_of(t * count, count), count)
-        delta = shift_ref[t]
-        centred = (recv_ref[:, here, :].astype(F32) + delta[:, None, :]).astype(BF16).reshape(members, TILE)
-        total = jnp.zeros((members, TILE), F32)
-        for pair in range(SLOTS // 2):
-            lhs, rhs = [], []
-            for k in (2 * pair, 2 * pair + 1):
-                at = anom_at_ref[t, k]
-                anom = jnp.concatenate([obs_ref[0, at, q * TILE : (q + 1) * TILE, :] for q in range(members // TILE)], axis=1)
-                cov = jnp.dot(anom, centred, preferred_element_type=F32)
-                taper = taper_ref[tapers_ref[t, k]]
-                rhs.append((taper * (cov * (1.0 / (members - 1.0)))).astype(BF16))
-                lhs.append(obs_ref[1, weight_at_ref[t, k]])
-            total += jnp.dot(jnp.concatenate(lhs, axis=1), jnp.concatenate(rhs, axis=0), preferred_element_type=F32)
         ret_ref[:, here, :] = total.astype(BF16).reshape(group, count, TILE)
         return carry
 
@@ -154,26 +153,30 @@
 
 
 def final_kernel(prior_ref, inc_ref, coef_ref, out_ref, v_ref):
-    members, rows, columns = out_ref.shape
+    members, depth, columns = out_ref.shape
     group, size, _ = inc_ref.shape
+    rows = prior_ref.shape[0] - 2
     per = rows // group
-    last = size // members - 1
+    extra = size // members - 1
+    i, steps = pl.program_id(0), pl.num_programs(0)
 
     def put(index, j, slot, half):
         lanes = slice(half * TILE, (half + 1) * TILE)
-        inc = inc_ref[j, slot * members : (slot + 1) * members, :].astype(F32)
-        v_ref[index, :, lanes] = prior_ref[index, :, lanes] + inc
-
+        here = pl.ds(pl.multiple_of(slot * members, members), members)
+        v_ref[index, :, lanes] = prior_ref[i * depth + index, :, lanes] + inc_ref[j, here, :].astype(F32)
+
+    first = i * (depth // per)
     for half in range(2):
-        put(0, half, last, half)
-        put(rows + 1, 2 + half, last, half)
-    for r in range(rows):
-        for half in range(2):
-            put(r + 1, r // per, 2 * (r % per) + half, half)
-    for r in range(rows):
+        top, bottom = i == 0, i == steps - 1
+        put(0, jnp.where(top, half, first - 1), jnp.where(top, extra, 2 * (per - 1) + half), half)
+        put(depth + 1, jnp.where(bottom, 2 + half, first + depth // per), jnp.where(bottom, extra, half), half)
+        for r in range(depth):
+            put(r + 1, first + r // per, 2 * (r % per) + half, half)
+    coef = coef_ref[...]
+    for r in range(depth):
         mid = v_ref[r + 1]
         beside = v_ref[r] + v_ref[r + 2] + pltpu.roll(mid, 1, 1) + pltpu.roll(mid, columns - 1, 1)
-        out_ref[:, r, :] = mid + coef_ref[r : r + 1, :] * (beside - 4.0 * mid)
+        out_ref[:, r, :] = mid + coef[r : r + 1, :] * (beside - 4.0 * mid)
 
 
 AXES = ("mem", "state")
@@ -203,60 +206,43 @@
     return pl.BlockSpec(value.shape, lambda i, c: (0,) * len(value.shape))
 
 
-def join(operands, core, name, after=()):
+def join(operands, core, name, after=(), split=False):
     count, blocks = len(operands), operands[0].shape[0]
 
     def kernel(core_ref, *refs):
-        out_ref = refs[-1]
+        outs = refs[count + len(after) :]
         for i in range(blocks):
             for a in range(count):
-                out_ref[i * count + a] = refs[a][i]
-
+                outs[0][i * count + a] = refs[a][i]
+        if split:
+            for a in range(count):
+                outs[1][a] = refs[a][0]
+                outs[2][a] = refs[a][core_ref[0]]
+
+    shapes = [(count * blocks, *operands[0].shape[1:])] + [(count, *operands[0].shape[1:])] * (2 * split)
     return pl.pallas_call(
         kernel,
-        out_shape=jax.ShapeDtypeStruct((count * blocks, *operands[0].shape[1:]), BF16),
+        out_shape=[jax.ShapeDtypeStruct(shape, BF16) for shape in shapes],
         grid_spec=pltpu.PrefetchScalarGridSpec(
             num_scalar_prefetch=1,
             grid=(1,),
             in_specs=[whole(v) for v in operands] + [pl.BlockSpec((1, 16, TILE), lambda i, c: (0, 0, 0))] * len(after),
-            out_specs=pl.BlockSpec((count * blocks, *operands[0].shape[1:]), lambda i, c: (0, 0, 0)),
+            out_specs=[pl.BlockSpec(shape, lambda i, c: (0, 0, 0)) for shape in shapes],
         ),
         name=name,
     )(core, *operands, *after)
 
 
-def halves(p, m, core, after):
-    def kernel(core_ref, p_ref, m_ref, after_ref, q_ref, r_ref):
-        q_ref[...] = p_ref[...]
-        r_ref[...] = m_ref[...]
-
-    shape = (p.shape[0] // 2, *p.shape[1:])
-    first = pl.BlockSpec(shape, lambda i, c: (0, 0, 0))
-    return pl.pallas_call(
-        kernel,
-        out_shape=[jax.ShapeDtypeStruct(shape, BF16)] * 2,
-        grid_spec=pltpu.PrefetchScalarGridSpec(
-            num_scalar_prefetch=1,
-            grid=(1,),
-            in_specs=[first, pl.BlockSpec(shape, lambda i, c: (c[0], 0, 0)), pl.BlockSpec((1, 16, TILE), lambda i, c: (0, 0, 0))],
-            out_specs=[first] * 2,
-        ),
-        name="halves",
-    )(core, p, m, after)
-
-
-def gather_obs(own, mesh, core, edges, arrived, payload):
+def gather_obs(own, mesh, core, edges, payload):
     far = fetch(own, mesh, lambda x, c, y, z: (x, c, y, z + 4))
-    held = join([own, far], core, "join_two", edges)
+    (held,) = join([own, far], core, "join_two", edges)
     p, m, q = (fetch(held, mesh, ring(True, step)) for step in (1, -1, 2))
-    held = join([held, p, m, q], core, "join_eight", arrived)
+    held, first, second = join([held, p, m, q], core, "join_eight", [payload], split=True)
     p, m = (fetch(held, mesh, ring(False, step)) for step in (1, -1))
-    swapped = [fetch(held, mesh, other_core)]
-    q, r = halves(p, m, core, payload)
-    q = fetch(q, mesh, ring(False, 1))
-    r = fetch(r, mesh, ring(False, -1))
-    swapped += [fetch(v, mesh, other_core) for v in (p, m, q, r)]
-    return [held, p, m, q, r], swapped
+    q = fetch(first, mesh, ring(False, 2))
+    r = fetch(second, mesh, ring(False, -2))
+    own = [held, p, m, q, r]
+    return own, [fetch(v, mesh, other_core) for v in own]
 
 
 def places(block, y, z):
@@ -319,7 +305,7 @@
         name="forecast4",
     )(ensemble, above, below, spreading_coefficient)
     core = (j % 2).reshape(1)
-    own, swapped = gather_obs(packed, (group // 2, states // 8, 8), core, [up, down], [above, below], payload)
+    own, swapped = gather_obs(packed, (group // 2, states // 8, 8), core, [up, down], payload)
     gathered = lax.all_to_all(payload, "mem", split_axis=0, concat_axis=0, tiled=True)
 
     edge = jnp.where(j < 2, above[0, members, :16], below[HALO - 1, members, :16])
@@ -336,7 +322,7 @@
         out_specs=VMEM,
         scratch_shapes=[
             pltpu.VMEM((2, states, *packed.shape[1:]), BF16),
-            pltpu.VMEM((tiles, group, TILE), F32),
+            pltpu.VMEM((tiles, group * members, TILE), BF16),
             pltpu.SemaphoreType.DMA((len(own) + len(swapped),)),
         ],
         compiler_params=limit,
@@ -346,10 +332,11 @@
 
     return pl.pallas_call(
         final_kernel,
+        grid=(rows // 8,),
         out_shape=jax.ShapeDtypeStruct((members, rows, columns), F32),
-        in_specs=[VMEM] * 3,
-        out_specs=VMEM,
-        scratch_shapes=[pltpu.VMEM((rows + 2, members, columns), F32)],
+        in_specs=[VMEM] * 2 + [pl.BlockSpec((8, columns), lambda i: (i, 0))],
+        out_specs=pl.BlockSpec((members, 8, columns), lambda i: (0, i, 0)),
+        scratch_shapes=[pltpu.VMEM((10, members, columns), F32)],
         compiler_params=limit,
         name="final_step",
     )(prior, returned, spreading_coefficient)

time: 110 us -> 113 us (1.027)
  starting transfers between devices: 35.3 us -> 47.7 us
  waiting for transfers between devices: 15.2 us -> 7.22 us
  Pallas kernels: 30.7 us -> 27.8 us
  local copies, waits for them, and re-layouts: 5.32 us -> 6.72 us
    ppermute x13, waiting for transfers between devices: 14.9 us -> 6.58 us  [fetch(): return lax.ppermute(value, AXES, pairs)]
    all_to_all x1, starting transfers between devices: 4.41 us -> 11.1 us  [body(): lax.all_to_all(payload, 'mem', split_axis=0, concat_axis=0, tiled=True)]
    ppermute x13, starting transfers between devices: 26.9 us -> 32.5 us  [fetch(): return lax.ppermute(value, AXES, pairs)]
    pallas_call x4 -> x3, Pallas kernels: 9.39 us -> 7.33 us  [the longest x2 4.38 us: join(): pl.pallas_call(kernel, out_shape=[jax.ShapeDtypeStruct(shape, BF16) for s...]
    unnamed x33 -> x31, local copies, waits for them, and re-layouts: 5.03 us -> 5.84 us
  transfers between devices with their start and end apart: 16 -> 16, of which waited for: 6 -> 5; matrix products, arithmetic and copies ran while one was open for 2% -> 3% of each run, Pallas kernels for 13% -> 10%
where the time goes in v4:
time: 113 us; the launch traced here: 112 us
  starting transfers between devices  47.7 us (42%)
  Pallas kernels  27.8 us (25%)
  blocking collectives  21.5 us (19%)
  waiting for transfers between devices  7.22 us (6%)
  local copies, waits for them, and re-layouts  6.72 us (6%)
  other arithmetic  1.32 us (1%)
    ppermute x13, starting transfers between devices, fetch(): return lax.ppermute(value, AXES, pairs)  32.5 us
    all_to_all x1, blocking collectives, body(): lax.all_to_all(increments, 'mem', split_axis=0, concat_axis=0, tiled=True)  21.5 us
    all_to_all x1, starting transfers between devices, body(): lax.all_to_all(payload, 'mem', split_axis=0, concat_axis=0, tiled=True)  11.1 us
    pallas_call x1, Pallas kernels, body(): pl.pallas_call(analysis_kernel, out_shape=jax.ShapeDtypeStruct((group, ti...  8.71 us
    pallas_call x1, Pallas kernels, body(): pl.pallas_call(forecast_kernel, out_shape=[jax.ShapeDtypeStruct((rows + 2...  7.73 us
    ppermute x13, waiting for transfers between devices, fetch(): return lax.ppermute(value, AXES, pairs)  6.58 us
    unnamed x31, local copies, waits for them, and re-layouts  5.84 us
    pallas_call x2, Pallas kernels, join(): pl.pallas_call(kernel, out_shape=[jax.ShapeDtypeStruct(shape, BF16) for s...  4.38 us
  transfers between devices with their start and end apart: 16, of which 5 were waited for; matrix products, arithmetic and copies ran while one was open for 3% of the time, Pallas kernels for 10%

profile of v4, /device:TPU:1, one launch (start us, length us, event | category | flops | bytes accessed | tf_op | source)
XLA Modules:
  0.0 112.4 jit_solution(8921537908345884860)
XLA Ops:
  0.0 1.7 %pack_obs.1.refs_0_ = bf16[1,512,128]{2,1,0:T(8,128)(2,1)} custom-call(bf16[1,128,512]{2,1,0:T(8,128)(2,1)} %anom_ref.1, bf16[1,128,512]{2,1,0:T(8,128)(2,1)} %weight_ref.1), custom_call_target="tpu_custom_call" | custom-call | tf_op jit(solution)/shard_map/pack_obs/pallas_call | solution.py:266
  1.7 7.7 %collective-permute-start.2 = (bf16[1,512,128]{2,1,0:T(8,128)(2,1)}, bf16[1,512,128]{2,1,0:T(8,128)(2,1)S(1)}, u32[]{:S(2)}, u32[]{:S(2)}) collective-permute-start(bf16[1,512,128]{2,1,0:T(8,128)(2,1)} %pack_obs.1.refs_0_), channel_id=1, source_target_pairs={{4,0},{5,1},{6,2},{7,3},{0,4},{1,5},{2,6},{3,7},{12,8},{13,9},{14,... | collective-permute-start | bytes 393224 | tf_op jit(solution)/shard_map/ppermute | solution.py:194
  9.4 2.3 %pack_halo.1 = (f32[5,72,256]{2,1,0:T(8,128)}, f32[5,72,256]{2,1,0:T(8,128)}) custom-call(f32[64,32,256]{2,1,0:T(8,128)} %x_ref.1, f32[64,32,256]{2,1,0:T(8,128)} %x_ref.1, f32[32,256]{1,0:T(8,128)} %coef_ref.5, s32[4,64]{1,0:T(4,128)} %bitcast.5, s32[4,64]{1,0:T(4,128)} %bitcast.6), custom_call_target="tpu_custom_call" | custom-call | tf_op jit(solution)/shard_map/pack_halo/pallas_call | solution.py:273
  11.8 2.8 %collective-permute-start = (f32[5,72,256]{2,1,0:T(8,128)}, f32[5,72,256]{2,1,0:T(8,128)S(1)}, u32[]{:S(2)}, u32[]{:S(2)}) collective-permute-start(f32[5,72,256]{2,1,0:T(8,128)} %get-tuple-element.12.refs_3_), channel_id=1, source_target_pairs={{0,1},{1,2},{2,3},{3,4},{4,5},{5,6},{6,7},{7,8},{8,9},{9,10},{10,1... | collective-permute-start | bytes 1105928 | tf_op jit(solution)/shard_map/ppermute | solution.py:288
  14.6 1.3 %collective-permute-start.1 = (f32[5,72,256]{2,1,0:T(8,128)}, f32[5,72,256]{2,1,0:T(8,128)S(1)}, u32[]{:S(2)}, u32[]{:S(2)}) collective-permute-start(f32[5,72,256]{2,1,0:T(8,128)} %get-tuple-element.13.refs_2_), channel_id=1, source_target_pairs={{1,0},{2,1},{3,2},{4,3},{5,4},{6,5},{7,6},{8,7},{9,8},{10,9},{11,1... | collective-permute-start | bytes 1105928 | tf_op jit(solution)/shard_map/ppermute | solution.py:287
  16.6 1.7 %join_two.1.refs_0_ = bf16[2,512,128]{2,1,0:T(8,128)(2,1)} custom-call(s32[1]{0:T(128)} %bitcast.3.core_ref, bf16[1,512,128]{2,1,0:T(8,128)(2,1)} %pack_obs.1.refs_0_, bf16[1,512,128]{2,1,0:T(8,128)(2,1)} %copy-done.11, f32[5,72,256]{2,1,0:T(8,128)} %get-tuple-element.13.refs_2_, f32[5,72,256]{2,1,0:T(8,128)} %get-tuple-element.12.refs_3_), custom_call_target="tpu_custom_call" | custom-call | tf_op jit(solution)/shard_map/join_two/pallas_call | solution.py:223
  18.3 4.0 %collective-permute-start.5 = (bf16[2,512,128]{2,1,0:T(8,128)(2,1)}, bf16[2,512,128]{2,1,0:T(8,128)(2,1)S(1)}, u32[]{:S(2)}, u32[]{:S(2)}) collective-permute-start(bf16[2,512,128]{2,1,0:T(8,128)(2,1)} %join_two.1.refs_0_), channel_id=1, source_target_pairs={{16,0},{17,1},{18,2},{19,3},{20,4},{21,5},{22,6},{23,7},{24,8},{25... | collective-permute-start | bytes 786440 | tf_op jit(solution)/shard_map/ppermute | solution.py:194
  23.0 2.0 %collective-permute-start.3 = (bf16[2,512,128]{2,1,0:T(8,128)(2,1)}, bf16[2,512,128]{2,1,0:T(8,128)(2,1)}, u32[]{:S(2)}, u32[]{:S(2)}) collective-permute-start(bf16[2,512,128]{2,1,0:T(8,128)(2,1)} %join_two.1.refs_0_), channel_id=1, source_target_pairs={{8,0},{9,1},{10,2},{11,3},{12,4},{13,5},{14,6},{15,7},{16,8},{17,9... | collective-permute-start | bytes 786440 | tf_op jit(solution)/shard_map/ppermute | solution.py:194
  25.6 7.7 %forecast4.1 = (f32[34,64,256]{2,1,0:T(8,128)}, bf16[8,608,128]{2,1,0:T(8,128)(2,1)}) custom-call(f32[64,32,256]{2,1,0:T(8,128)S(1)} %copy-done, f32[5,72,256]{2,1,0:T(8,128)S(1)} %collective-permute-done.above_ref, f32[5,72,256]{2,1,0:T(8,128)S(1)} %collective-permute-done.1.below_ref, f32[32,256]{1,0:T(8,128)S(1)} %copy-done.8), custom_call_target="tpu_custom_call" | custom-call | tf_op jit(solution)/shard_map/forecast4/pallas_call | solution.py:290
  33.4 2.1 %collective-permute-done.3.refs_1_ = bf16[2,512,128]{2,1,0:T(8,128)(2,1)} collective-permute-done((bf16[2,512,128]{2,1,0:T(8,128)(2,1)}, bf16[2,512,128]{2,1,0:T(8,128)(2,1)}, u32[]{:S(2)}, u32[]{:S(2)}) %collective-permute-start.3) | collective-permute-done | bytes 262176 | tf_op jit(solution)/shard_map/ppermute | solution.py:194
  35.5 2.7 %join_eight.1 = (bf16[8,512,128]{2,1,0:T(8,128)(2,1)}, bf16[4,512,128]{2,1,0:T(8,128)(2,1)}, bf16[4,512,128]{2,1,0:T(8,128)(2,1)}) custom-call(s32[1]{0:T(128)} %bitcast.3.core_ref, bf16[2,512,128]{2,1,0:T(8,128)(2,1)} %join_two.1.refs_0_, bf16[2,512,128]{2,1,0:T(8,128)(2,1)} %collective-permute-done.3.refs_1_, bf16[2,512,128]{2,1,0:T(8,128)(2,1)} %copy-done.10, ...), custom_call_target="tpu_custom_call" | custom-call | tf_op jit(solution)/shard_map/join_eight/pallas_call | solution.py:223
  38.2 2.2 %collective-permute-start.7 = (bf16[8,512,128]{2,1,0:T(8,128)(2,1)}, bf16[8,512,128]{2,1,0:T(8,128)(2,1)S(1)}, u32[]{:S(2)}, u32[]{:S(2)}) collective-permute-start(bf16[8,512,128]{2,1,0:T(8,128)(2,1)} %get-tuple-element.16.rest_0_), channel_id=1, source_target_pairs={{7,0},{0,1},{1,2},{2,3},{3,4},{4,5},{5,6},{6,7},{15,8},{8,9},{9,10... | collective-permute-start | bytes 3145736 | tf_op jit(solution)/shard_map/ppermute | solution.py:194
  40.4 1.5 %collective-permute-start.6 = (bf16[8,512,128]{2,1,0:T(8,128)(2,1)}, bf16[8,512,128]{2,1,0:T(8,128)(2,1)}, u32[]{:S(2)}, u32[]{:S(2)}) collective-permute-start(bf16[8,512,128]{2,1,0:T(8,128)(2,1)} %get-tuple-element.16.rest_0_), channel_id=1, source_target_pairs={{1,0},{2,1},{3,2},{4,3},{5,4},{6,5},{7,6},{0,7},{9,8},{10,9},{11,1... | collective-permute-start | bytes 3145736 | tf_op jit(solution)/shard_map/ppermute | solution.py:194
  41.9 1.6 %collective-permute-start.8 = (bf16[4,512,128]{2,1,0:T(8,128)(2,1)}, bf16[4,512,128]{2,1,0:T(8,128)(2,1)S(1)}, u32[]{:S(2)}, u32[]{:S(2)}) collective-permute-start(bf16[4,512,128]{2,1,0:T(8,128)(2,1)} %get-tuple-element.17), channel_id=1, source_target_pairs={{2,0},{3,1},{4,2},{5,3},{6,4},{7,5},{0,6},{1,7},{10,8},{11,9},{12,... | collective-permute-start | bytes 1572872 | tf_op jit(solution)/shard_map/ppermute | solution.py:194
  43.5 1.4 %collective-permute-start.9 = (bf16[4,512,128]{2,1,0:T(8,128)(2,1)}, bf16[4,512,128]{2,1,0:T(8,128)(2,1)}, u32[]{:S(2)}, u32[]{:S(2)}) collective-permute-start(bf16[4,512,128]{2,1,0:T(8,128)(2,1)} %get-tuple-element.18), channel_id=1, source_target_pairs={{6,0},{7,1},{0,2},{1,3},{2,4},{3,5},{4,6},{5,7},{14,8},{15,9},{8,1... | collective-permute-start | bytes 1572872 | tf_op jit(solution)/shard_map/ppermute | solution.py:194
  44.9 11.1 %all-to-all-start = ((bf16[8,608,128]{2,1,0:T(8,128)(2,1)}), bf16[8,608,128]{2,1,0:T(8,128)(2,1)}, u32[]{:S(2)}, u32[]{:S(2)}) async-start(bf16[8,608,128]{2,1,0:T(8,128)(2,1)} %get-tuple-element.15.refs_4_), calls=%async_computation | async-start | bytes 2490368 | tf_op jit(solution)/shard_map/all_to_all | solution.py:309
  56.1 5.6 %collective-permute-start.12 = (bf16[8,512,128]{2,1,0:T(8,128)(2,1)S(1)}, bf16[8,512,128]{2,1,0:T(8,128)(2,1)}, u32[]{:S(2)}, u32[]{:S(2)}) collective-permute-start(bf16[8,512,128]{2,1,0:T(8,128)(2,1)S(1)} %collective-permute-done.7.rest_2_), channel_id=1, source_target_pairs={{32,0},{33,1},{34,2},{35,3},{36,4},{37,5},{38,6},{39,7},{40,8},{41... | collective-permute-start | bytes 3145736 | tf_op jit(solution)/shard_map/ppermute | solution.py:194
  61.7 3.5 %collective-permute-done.6.rest_1_ = bf16[8,512,128]{2,1,0:T(8,128)(2,1)} collective-permute-done((bf16[8,512,128]{2,1,0:T(8,128)(2,1)}, bf16[8,512,128]{2,1,0:T(8,128)(2,1)}, u32[]{:S(2)}, u32[]{:S(2)}) %collective-permute-start.6) | collective-permute-done | bytes 1048608 | tf_op jit(solution)/shard_map/ppermute | solution.py:194
  67.1 1.3 %fusion.13 = f32[16]{0:T(128)} fusion(pred[]{:T(512)S(6)} %lt.39, f32[5,72,256]{2,1,0:T(8,128)} %copy-done.7, f32[5,72,256]{2,1,0:T(8,128)S(1)} %collective-permute-done.above_ref), kind=kLoop, calls=%fused_computation.38 | loop fusion | flops 16 | bytes 193 | tf_op jit(solution)/shard_map/jit(_where)/select_n | solution.py:311
  69.2 3.5 %collective-permute-start.13 = (bf16[4,512,128]{2,1,0:T(8,128)(2,1)S(1)}, bf16[4,512,128]{2,1,0:T(8,128)(2,1)S(1)}, u32[]{:S(2)}, u32[]{:S(2)}) collective-permute-start(bf16[4,512,128]{2,1,0:T(8,128)(2,1)S(1)} %collective-permute-done.8.rest_3_), channel_id=1, source_target_pairs={{32,0},{33,1},{34,2},{35,3},{36,4},{37,5},{38,6},{39,7},{40,8},{41... | collective-permute-start | bytes 1572872 | tf_op jit(solution)/shard_map/ppermute | solution.py:194
  72.7 1.8 %collective-permute-start.14 = (bf16[4,512,128]{2,1,0:T(8,128)(2,1)}, bf16[4,512,128]{2,1,0:T(8,128)(2,1)S(1)}, u32[]{:S(2)}, u32[]{:S(2)}) collective-permute-start(bf16[4,512,128]{2,1,0:T(8,128)(2,1)} %collective-permute-done.9.rest_4_), channel_id=1, source_target_pairs={{32,0},{33,1},{34,2},{35,3},{36,4},{37,5},{38,6},{39,7},{40,8},{41... | collective-permute-start | bytes 1572872 | tf_op jit(solution)/shard_map/ppermute | solution.py:194
  79.2 8.7 %analysis.1 = bf16[8,576,128]{2,1,0:T(8,128)(2,1)} custom-call(s32[9,4]{1,0:T(8,128)S(1)} %get-tuple-element.20.anom_at_ref, s32[9,4]{1,0:T(8,128)S(1)} %get-tuple-element.19.weight_at_ref, s32[9,4]{1,0:T(8,128)S(1)} %pad_add_fusion.1.tapers_ref, bf16[8,608,128]{2,1,0:T(8,128)(2,1)} %all-to-all-done.recv_ref, f32[8,128,128]{2,1,0:T(8,128)S(1)} %bitcast.4, ...), custom_call_target="tpu_custom_call" | custom-call | tf_op jit(solution)/shard_map/analysis/pallas_call | solution.py:318
  87.9 21.5 %all_to_all.10.inc_ref = bf16[8,576,128]{2,1,0:T(8,128)(2,1)S(1)} all-to-all(bf16[8,576,128]{2,1,0:T(8,128)(2,1)} %analysis.1), channel_id=1, replica_groups=mesh['mem'=8,'state'=32] {'mem'}, dimensions={0} | all-to-all | bytes 2359296 | tf_op jit(solution)/shard_map/all_to_all | solution.py:331
  109.4 2.9 %final_step.1 = f32[64,32,256]{2,1,0:T(8,128)} custom-call(f32[34,64,256]{2,1,0:T(8,128)S(1)} %copy-done.1, bf16[8,576,128]{2,1,0:T(8,128)(2,1)S(1)} %all_to_all.10.inc_ref, f32[32,256]{1,0:T(8,128)S(1)} %copy-done.8), custom_call_target="tpu_custom_call" | custom-call | tf_op jit(solution)/shard_map/final_step/pallas_call | solution.py:333
  (56 shorter events, 9.5 us)
Async XLA Ops:
  1.7 14.2 %collective-permute-start.2 = (bf16[1,512,128]{2,1,0:T(8,128)(2,1)}, bf16[1,512,128]{2,1,0:T(8,128)(2,1)S(1)}, u32[]{:S(2)}, u32[]{:S(2)}) collective-permute-start(bf16[1,512,128]{2,1,0:T(8,128)(2,1)} %pack_obs.1.refs_0_), channel_id=1, source_target_pairs={{4,0},{5,1},{6,2},{7,3},{0,4},{1,5},{2,6},{3,7},{12,8},{13,9},{14,... | collective-permute-start | bytes 393224 | tf_op jit(solution)/shard_map/ppermute | solution.py:194
  9.4 16.2 %copy-start = (f32[64,32,256]{2,1,0:T(8,128)S(1)}, f32[64,32,256]{2,1,0:T(8,128)}, u32[]{:S(2)}) copy-start(f32[64,32,256]{2,1,0:T(8,128)} %x_ref.1) | copy-start | bytes 6291460
  11.8 13.8 %copy-start.8 = (f32[32,256]{1,0:T(8,128)S(1)}, f32[32,256]{1,0:T(8,128)}, u32[]{:S(2)}) copy-start(f32[32,256]{1,0:T(8,128)} %coef_ref.5) | copy-start | bytes 98308
  11.8 13.2 %collective-permute-start = (f32[5,72,256]{2,1,0:T(8,128)}, f32[5,72,256]{2,1,0:T(8,128)S(1)}, u32[]{:S(2)}, u32[]{:S(2)}) collective-permute-start(f32[5,72,256]{2,1,0:T(8,128)} %get-tuple-element.12.refs_3_), channel_id=1, source_target_pairs={{0,1},{1,2},{2,3},{3,4},{4,5},{5,6},{6,7},{7,8},{8,9},{9,10},{10,1... | collective-permute-start | bytes 1105928 | tf_op jit(solution)/shard_map/ppermute | solution.py:288
  14.6 11.0 %collective-permute-start.1 = (f32[5,72,256]{2,1,0:T(8,128)}, f32[5,72,256]{2,1,0:T(8,128)S(1)}, u32[]{:S(2)}, u32[]{:S(2)}) collective-permute-start(f32[5,72,256]{2,1,0:T(8,128)} %get-tuple-element.13.refs_2_), channel_id=1, source_target_pairs={{1,0},{2,1},{3,2},{4,3},{5,4},{6,5},{7,6},{8,7},{9,8},{10,9},{11,1... | collective-permute-start | bytes 1105928 | tf_op jit(solution)/shard_map/ppermute | solution.py:287
  18.3 15.1 %collective-permute-start.5 = (bf16[2,512,128]{2,1,0:T(8,128)(2,1)}, bf16[2,512,128]{2,1,0:T(8,128)(2,1)S(1)}, u32[]{:S(2)}, u32[]{:S(2)}) collective-permute-start(bf16[2,512,128]{2,1,0:T(8,128)(2,1)} %join_two.1.refs_0_), channel_id=1, source_target_pairs={{16,0},{17,1},{18,2},{19,3},{20,4},{21,5},{22,6},{23,7},{24,8},{25... | collective-permute-start | bytes 786440 | tf_op jit(solution)/shard_map/ppermute | solution.py:194
  22.3 11.1 %collective-permute-start.4 = (bf16[2,512,128]{2,1,0:T(8,128)(2,1)}, bf16[2,512,128]{2,1,0:T(8,128)(2,1)S(1)}, u32[]{:S(2)}, u32[]{:S(2)}) collective-permute-start(bf16[2,512,128]{2,1,0:T(8,128)(2,1)} %join_two.1.refs_0_), channel_id=1, source_target_pairs={{24,0},{25,1},{26,2},{27,3},{28,4},{29,5},{30,6},{31,7},{0,8},{1,9... | collective-permute-start | bytes 786440 | tf_op jit(solution)/shard_map/ppermute | solution.py:194
  23.0 12.5 %collective-permute-start.3 = (bf16[2,512,128]{2,1,0:T(8,128)(2,1)}, bf16[2,512,128]{2,1,0:T(8,128)(2,1)}, u32[]{:S(2)}, u32[]{:S(2)}) collective-permute-start(bf16[2,512,128]{2,1,0:T(8,128)(2,1)} %join_two.1.refs_0_), channel_id=1, source_target_pairs={{8,0},{9,1},{10,2},{11,3},{12,4},{13,5},{14,6},{15,7},{16,8},{17,9... | collective-permute-start | bytes 786440 | tf_op jit(solution)/shard_map/ppermute | solution.py:194
  25.6 12.6 %copy-start.7 = (f32[5,72,256]{2,1,0:T(8,128)}, f32[5,72,256]{2,1,0:T(8,128)S(1)}, u32[]{:S(2)}) copy-start(f32[5,72,256]{2,1,0:T(8,128)S(1)} %collective-permute-done.1.below_ref) | copy-start | bytes 1105924
  33.4 2.1 %copy-start.9 = (bf16[2,512,128]{2,1,0:T(8,128)(2,1)}, bf16[2,512,128]{2,1,0:T(8,128)(2,1)S(1)}, u32[]{:S(2)}) copy-start(bf16[2,512,128]{2,1,0:T(8,128)(2,1)S(1)} %collective-permute-done.5.refs_3_) | copy-start | bytes 786436
  38.2 17.9 %collective-permute-start.7 = (bf16[8,512,128]{2,1,0:T(8,128)(2,1)}, bf16[8,512,128]{2,1,0:T(8,128)(2,1)S(1)}, u32[]{:S(2)}, u32[]{:S(2)}) collective-permute-start(bf16[8,512,128]{2,1,0:T(8,128)(2,1)} %get-tuple-element.16.rest_0_), channel_id=1, source_target_pairs={{7,0},{0,1},{1,2},{2,3},{3,4},{4,5},{5,6},{6,7},{15,8},{8,9},{9,10... | collective-permute-start | bytes 3145736 | tf_op jit(solution)/shard_map/ppermute | solution.py:194
  40.4 24.8 %collective-permute-start.6 = (bf16[8,512,128]{2,1,0:T(8,128)(2,1)}, bf16[8,512,128]{2,1,0:T(8,128)(2,1)}, u32[]{:S(2)}, u32[]{:S(2)}) collective-permute-start(bf16[8,512,128]{2,1,0:T(8,128)(2,1)} %get-tuple-element.16.rest_0_), channel_id=1, source_target_pairs={{1,0},{2,1},{3,2},{4,3},{5,4},{6,5},{7,6},{0,7},{9,8},{10,9},{11,1... | collective-permute-start | bytes 3145736 | tf_op jit(solution)/shard_map/ppermute | solution.py:194
  41.9 27.3 %collective-permute-start.8 = (bf16[4,512,128]{2,1,0:T(8,128)(2,1)}, bf16[4,512,128]{2,1,0:T(8,128)(2,1)S(1)}, u32[]{:S(2)}, u32[]{:S(2)}) collective-permute-start(bf16[4,512,128]{2,1,0:T(8,128)(2,1)} %get-tuple-element.17), channel_id=1, source_target_pairs={{2,0},{3,1},{4,2},{5,3},{6,4},{7,5},{0,6},{1,7},{10,8},{11,9},{12,... | collective-permute-start | bytes 1572872 | tf_op jit(solution)/shard_map/ppermute | solution.py:194
  43.5 12.5 %copy-start.2 = (bf16[8,512,128]{2,1,0:T(8,128)(2,1)S(1)}, bf16[8,512,128]{2,1,0:T(8,128)(2,1)}, u32[]{:S(2)}) copy-start(bf16[8,512,128]{2,1,0:T(8,128)(2,1)} %get-tuple-element.16.rest_0_) | copy-start | bytes 3145732
  43.5 22.1 %copy-start.12 = (s32[64,4]{0,1:T(4,128)S(1)}, s32[64,4]{0,1:T(4,128)}, u32[]{:S(2)}) copy-start(s32[64,4]{0,1:T(4,128)} %param.12) | copy-start | bytes 3076
  43.5 22.1 %copy-start.13 = (s32[64,4]{0,1:T(4,128)S(1)}, s32[64,4]{0,1:T(4,128)}, u32[]{:S(2)}) copy-start(s32[64,4]{0,1:T(4,128)} %param.13) | copy-start | bytes 3076
  43.5 29.2 %collective-permute-start.9 = (bf16[4,512,128]{2,1,0:T(8,128)(2,1)}, bf16[4,512,128]{2,1,0:T(8,128)(2,1)}, u32[]{:S(2)}, u32[]{:S(2)}) collective-permute-start(bf16[4,512,128]{2,1,0:T(8,128)(2,1)} %get-tuple-element.18), channel_id=1, source_target_pairs={{6,0},{7,1},{0,2},{1,3},{2,4},{3,5},{4,6},{5,7},{14,8},{15,9},{8,1... | collective-permute-start | bytes 1572872 | tf_op jit(solution)/shard_map/ppermute | solution.py:194
  44.9 32.2 %all-to-all-start = ((bf16[8,608,128]{2,1,0:T(8,128)(2,1)}), bf16[8,608,128]{2,1,0:T(8,128)(2,1)}, u32[]{:S(2)}, u32[]{:S(2)}) async-start(bf16[8,608,128]{2,1,0:T(8,128)(2,1)} %get-tuple-element.15.refs_4_), calls=%async_computation | async-start | bytes 2490368 | tf_op jit(solution)/shard_map/all_to_all | solution.py:309
  56.0 18.6 %collective-permute-start.10 = (bf16[8,512,128]{2,1,0:T(8,128)(2,1)S(1)}, bf16[8,512,128]{2,1,0:T(8,128)(2,1)}, u32[]{:S(2)}, u32[]{:S(2)}) collective-permute-start(bf16[8,512,128]{2,1,0:T(8,128)(2,1)S(1)} %copy-done.2), channel_id=1, source_target_pairs={{32,0},{33,1},{34,2},{35,3},{36,4},{37,5},{38,6},{39,7},{40,8},{41... | collective-permute-start | bytes 3145736 | tf_op jit(solution)/shard_map/ppermute | solution.py:194
  56.1 21.0 %collective-permute-start.12 = (bf16[8,512,128]{2,1,0:T(8,128)(2,1)S(1)}, bf16[8,512,128]{2,1,0:T(8,128)(2,1)}, u32[]{:S(2)}, u32[]{:S(2)}) collective-permute-start(bf16[8,512,128]{2,1,0:T(8,128)(2,1)S(1)} %collective-permute-done.7.rest_2_), channel_id=1, source_target_pairs={{32,0},{33,1},{34,2},{35,3},{36,4},{37,5},{38,6},{39,7},{40,8},{41... | collective-permute-start | bytes 3145736 | tf_op jit(solution)/shard_map/ppermute | solution.py:194
  65.3 11.9 %collective-permute-start.11 = (bf16[8,512,128]{2,1,0:T(8,128)(2,1)}, bf16[8,512,128]{2,1,0:T(8,128)(2,1)}, u32[]{:S(2)}, u32[]{:S(2)}) collective-permute-start(bf16[8,512,128]{2,1,0:T(8,128)(2,1)} %collective-permute-done.6.rest_1_), channel_id=1, source_target_pairs={{32,0},{33,1},{34,2},{35,3},{36,4},{37,5},{38,6},{39,7},{40,8},{41... | collective-permute-start | bytes 3145736 | tf_op jit(solution)/shard_map/ppermute | solution.py:194
  69.2 5.4 %collective-permute-start.13 = (bf16[4,512,128]{2,1,0:T(8,128)(2,1)S(1)}, bf16[4,512,128]{2,1,0:T(8,128)(2,1)S(1)}, u32[]{:S(2)}, u32[]{:S(2)}) collective-permute-start(bf16[4,512,128]{2,1,0:T(8,128)(2,1)S(1)} %collective-permute-done.8.rest_3_), channel_id=1, source_target_pairs={{32,0},{33,1},{34,2},{35,3},{36,4},{37,5},{38,6},{39,7},{40,8},{41... | collective-permute-start | bytes 1572872 | tf_op jit(solution)/shard_map/ppermute | solution.py:194
  72.7 3.6 %collective-permute-start.14 = (bf16[4,512,128]{2,1,0:T(8,128)(2,1)}, bf16[4,512,128]{2,1,0:T(8,128)(2,1)S(1)}, u32[]{:S(2)}, u32[]{:S(2)}) collective-permute-start(bf16[4,512,128]{2,1,0:T(8,128)(2,1)} %collective-permute-done.9.rest_4_), channel_id=1, source_target_pairs={{32,0},{33,1},{34,2},{35,3},{36,4},{37,5},{38,6},{39,7},{40,8},{41... | collective-permute-start | bytes 1572872 | tf_op jit(solution)/shard_map/ppermute | solution.py:194
  87.9 21.5 %copy-start.1 = (f32[34,64,256]{2,1,0:T(8,128)S(1)}, f32[34,64,256]{2,1,0:T(8,128)}, u32[]{:S(2)}) copy-start(f32[34,64,256]{2,1,0:T(8,128)} %get-tuple-element.14.prior_ref) | copy-start | bytes 6684676
  (6 other events, 6.6 us)

commit v5 on v4

--- a/solution.py
+++ b/solution.py
@@ -29,7 +29,7 @@
             out_ref[0, q * TILE : (q + 1) * TILE, :] = weight_ref[0, :, q * TILE : (q + 1) * TILE].T
 
 
-def pack_halo_kernel(first_ref, last_ref, coef_ref, block_ref, taper_ref, up_ref, down_ref):
+def pack_halo_kernel(first_ref, last_ref, coef_ref, block_ref, taper_ref, up_ref, down_ref, token_ref):
     members, depth, columns = first_ref.shape
     rows = coef_ref.shape[0]
     tiles = block_ref.shape[1]
@@ -47,9 +47,10 @@
                 ids = jnp.where(lane == t * SLOTS + k, block_ref[k, tile0 + t], ids)
                 ids = jnp.where(lane == 8 + t * SLOTS + k, taper_ref[k, tile0 + t], ids)
         out_ref[far, members : members + 8, :] = ids.astype(F32)
-
-
-def forecast_kernel(x_ref, above_ref, below_ref, coef_ref, prior_ref, pay_ref, a_ref, b_ref, c_ref, m_ref):
+    token_ref[...] = jnp.zeros(TOKEN.shape, F32)
+
+
+def forecast_kernel(x_ref, above_ref, below_ref, coef_ref, token_ref, prior_ref, pay_ref, a_ref, b_ref, c_ref, m_ref):
     members, rows, columns = x_ref.shape
     total = rows + 2 * HALO
     group = pay_ref.shape[0]
@@ -108,22 +109,23 @@
 
 
 def analysis_kernel(anom_at_ref, weight_at_ref, tapers_ref, recv_ref, taper_ref, *rest):
-    pieces, (ret_ref, obs_ref, centred_ref, sems) = rest[:-4], rest[-4:]
+    pieces, (ret_ref, obs_ref, centred_ref) = rest[:-3], rest[-3:]
     group, size, _ = recv_ref.shape
     count = ret_ref.shape[1] // anom_at_ref.shape[0]
     tiles = anom_at_ref.shape[0]
     members = group * count
     core = lax.rem(lax.axis_index("mem"), 2)
-    copies = []
     for side in range(2):
         start = 0
+        kind = core if side == 0 else 1 - core
         for piece in pieces[side * len(pieces) // 2 : (side + 1) * len(pieces) // 2]:
-            length = piece.shape[0]
-            to = obs_ref.at[core if side == 0 else 1 - core, pl.ds(start, length)]
-            copies.append(pltpu.make_async_copy(piece, to, sems.at[len(copies)]))
-            start += length
-    for copy in copies:
-        copy.start()
+
+            def keep(i, carry, piece=piece, start=start, kind=kind):
+                obs_ref[kind, start + i] = piece[i]
+                return carry
+
+            lax.fori_loop(0, piece.shape[0], keep, 0)
+            start += piece.shape[0]
 
     parts = recv_ref[:, size - 32 :, :].astype(F32)
     for t in range(tiles):
@@ -131,9 +133,6 @@
         delta = own - jnp.mean(own, axis=0, keepdims=True)
         local = recv_ref[:, t * count : (t + 1) * count, :].astype(F32)
         centred_ref[t] = (local + delta[:, None, :]).astype(BF16).reshape(members, TILE)
-    for copy in copies:
-        copy.wait()
-
     def one(t, carry):
         anoms, weights = [], []
         for k in range(SLOTS):
@@ -202,42 +201,43 @@
     return (x, 1 - c, y, z)
 
 
-def whole(value):
-    return pl.BlockSpec(value.shape, lambda i, c: (0,) * len(value.shape))
-
-
-def join(operands, core, name, after=(), split=False):
+TOKEN = jax.ShapeDtypeStruct((8, TILE), F32)
+
+
+def join(operands, name, after=(), split=False):
     count, blocks = len(operands), operands[0].shape[0]
 
-    def kernel(core_ref, *refs):
+    def kernel(*refs):
         outs = refs[count + len(after) :]
+        core = lax.rem(lax.axis_index("mem"), 2)
         for i in range(blocks):
             for a in range(count):
                 outs[0][i * count + a] = refs[a][i]
         if split:
             for a in range(count):
                 outs[1][a] = refs[a][0]
-                outs[2][a] = refs[a][core_ref[0]]
+                outs[2][a] = refs[a][core]
+        outs[-1][...] = jnp.zeros(TOKEN.shape, F32)
 
     shapes = [(count * blocks, *operands[0].shape[1:])] + [(count, *operands[0].shape[1:])] * (2 * split)
     return pl.pallas_call(
         kernel,
-        out_shape=[jax.ShapeDtypeStruct(shape, BF16) for shape in shapes],
-        grid_spec=pltpu.PrefetchScalarGridSpec(
-            num_scalar_prefetch=1,
-            grid=(1,),
-            in_specs=[whole(v) for v in operands] + [pl.BlockSpec((1, 16, TILE), lambda i, c: (0, 0, 0))] * len(after),
-            out_specs=[pl.BlockSpec(shape, lambda i, c: (0, 0, 0)) for shape in shapes],
-        ),
+        out_shape=[jax.ShapeDtypeStruct(shape, BF16) for shape in shapes] + [TOKEN],
+        in_specs=[VMEM] * (count + len(after)),
+        out_specs=[VMEM] * (len(shapes) + 1),
+        compiler_params=pltpu.CompilerParams(vmem_limit_bytes=6 << 20),
         name=name,
-    )(core, *operands, *after)
-
-
-def gather_obs(own, mesh, core, edges, payload):
+    )(*operands, *after)
+
+
+def gather_start(own, mesh, packed_halo, arrived):
     far = fetch(own, mesh, lambda x, c, y, z: (x, c, y, z + 4))
-    (held,) = join([own, far], core, "join_two", edges)
+    held, _ = join([own, far], "join_two", [packed_halo])
     p, m, q = (fetch(held, mesh, ring(True, step)) for step in (1, -1, 2))
-    held, first, second = join([held, p, m, q], core, "join_eight", [payload], split=True)
+    return join([held, p, m, q], "join_eight", arrived, split=True)
+
+
+def gather_rest(held, first, second, mesh):
     p, m = (fetch(held, mesh, ring(False, step)) for step in (1, -1))
     q = fetch(first, mesh, ring(False, 2))
     r = fetch(second, mesh, ring(False, -2))
@@ -260,7 +260,6 @@
     per = rows // group
     tiles = 2 * per + 1
     size = tiles * members + 32
-    limit = pltpu.CompilerParams(vmem_limit_bytes=48 << 20)
 
     j, at = lax.axis_index("mem"), lax.axis_index("state")
     packed = pl.pallas_call(
@@ -270,10 +269,10 @@
         out_specs=VMEM,
         name="pack_obs",
     )(obs_anom, obs_weight)
-    up, down = pl.pallas_call(
+    up, down, packed_halo = pl.pallas_call(
         pack_halo_kernel,
         grid=(1,),
-        out_shape=[jax.ShapeDtypeStruct((HALO, members + 8, columns), F32)] * 2,
+        out_shape=[jax.ShapeDtypeStruct((HALO, members + 8, columns), F32)] * 2 + [TOKEN],
         in_specs=[
             pl.BlockSpec((members, 8, columns), lambda i: (0, 0, 0)),
             pl.BlockSpec((members, 8, columns), lambda i: (0, rows // 8 - 1, 0)),
@@ -281,19 +280,22 @@
             SMEM,
             SMEM,
         ],
-        out_specs=[VMEM] * 2,
+        out_specs=[VMEM] * 3,
         name="pack_halo",
     )(ensemble, ensemble, spreading_coefficient, obs_block.T, taper_id.T)
     below = lax.ppermute(up, "state", [(i + 1, i) for i in range(states - 1)])
     above = lax.ppermute(down, "state", [(i, i + 1) for i in range(states - 1)])
 
+    chips = (group // 2, states // 8, 8)
+    held, first, second, joined = gather_start(packed, chips, packed_halo, [above, below])
+    own, swapped = gather_rest(held, first, second, chips)
     prior, payload = pl.pallas_call(
         forecast_kernel,
         out_shape=[
             jax.ShapeDtypeStruct((rows + 2, members, columns), F32),
             jax.ShapeDtypeStruct((group, size, TILE), BF16),
         ],
-        in_specs=[VMEM] * 4,
+        in_specs=[VMEM] * 5,
         out_specs=[VMEM] * 2,
         scratch_shapes=[
             pltpu.VMEM((rows + 2 * HALO, members, columns), F32),
@@ -301,11 +303,9 @@
             pltpu.VMEM((rows + 2 * HALO, 8, columns), F32),
             pltpu.VMEM((group, 32, TILE), F32),
         ],
-        compiler_params=limit,
+        compiler_params=pltpu.CompilerParams(vmem_limit_bytes=14 << 20),
         name="forecast4",
-    )(ensemble, above, below, spreading_coefficient)
-    core = (j % 2).reshape(1)
-    own, swapped = gather_obs(packed, (group // 2, states // 8, 8), core, [up, down], payload)
+    )(ensemble, above, below, spreading_coefficient, joined)
     gathered = lax.all_to_all(payload, "mem", split_axis=0, concat_axis=0, tiled=True)
 
     edge = jnp.where(j < 2, above[0, members, :16], below[HALO - 1, members, :16])
@@ -318,14 +318,13 @@
     increments = pl.pallas_call(
         analysis_kernel,
         out_shape=jax.ShapeDtypeStruct((group, tiles * members, TILE), BF16),
-        in_specs=[SMEM] * 3 + [VMEM] * 2 + [pl.BlockSpec(memory_space=pl.ANY)] * (len(own) + len(swapped)),
+        in_specs=[SMEM] * 3 + [VMEM] * (2 + len(own) + len(swapped)),
         out_specs=VMEM,
         scratch_shapes=[
             pltpu.VMEM((2, states, *packed.shape[1:]), BF16),
             pltpu.VMEM((tiles, group * members, TILE), BF16),
-            pltpu.SemaphoreType.DMA((len(own) + len(swapped),)),
         ],
-        compiler_params=limit,
+        compiler_params=pltpu.CompilerParams(vmem_limit_bytes=22 << 20),
         name="analysis",
     )(anom_at, weight_at, tapers, gathered, jnp.swapaxes(taper_table, 1, 2), *own, *swapped)
     returned = lax.all_to_all(increments, "mem", split_axis=0, concat_axis=0, tiled=True)
@@ -337,7 +336,7 @@
         in_specs=[VMEM] * 2 + [pl.BlockSpec((8, columns), lambda i: (i, 0))],
         out_specs=pl.BlockSpec((members, 8, columns), lambda i: (0, i, 0)),
         scratch_shapes=[pltpu.VMEM((10, members, columns), F32)],
-        compiler_params=limit,
+        compiler_params=pltpu.CompilerParams(vmem_limit_bytes=10 << 20),
         name="final_step",
     )(prior, returned, spreading_coefficient)
 

time: 113 us -> 108 us (0.956); the launches traced: 112 us -> 106 us
  waiting for transfers between devices: 7.22 us -> 20.5 us
  starting transfers between devices: 47.7 us -> 35.5 us
  Pallas kernels: 27.8 us -> 23 us
  local copies, waits for them, and re-layouts: 6.72 us -> 4.8 us
  other arithmetic: 1.32 us -> 0.07 us
    ppermute x13, waiting for transfers between devices: 6.58 us -> 17.5 us  [fetch(): return lax.ppermute(value, AXES, pairs)]
    all_to_all x1, starting transfers between devices: 11.1 us -> 4.54 us  [body(): lax.all_to_all(payload, 'mem', split_axis=0, concat_axis=0, tiled=True)]
    ppermute x13, starting transfers between devices: 32.5 us -> 26.9 us  [fetch(): return lax.ppermute(value, AXES, pairs)]
    ppermute x1, waiting for transfers between devices: 0.63 us -> 2.91 us  [body(): below = lax.ppermute(up, 'state', [(i + 1, i) for i in range(states - 1)])]
    pallas_call x2, Pallas kernels: 4.38 us -> 2.14 us  [join(): pl.pallas_call(kernel, out_shape=[jax.ShapeDtypeStruct(shape, BF16) for s...]
    pallas_call x1, Pallas kernels: 7.73 us -> 5.97 us  [body(): pl.pallas_call(forecast_kernel, out_shape=[jax.ShapeDtypeStruct((rows + 2...]
    unnamed x31 -> x21, local copies, waits for them, and re-layouts: 5.84 us -> 4.51 us
    select_n x1, other arithmetic: 1.27 us -> 0.02 us  [body(): jnp.where(j < 2, above[0, members, :16], below[HALO - 1, members, :16])]
  transfers between devices with their start and end apart: 16 -> 16, of which waited for: 5 -> 6; matrix products, arithmetic and copies ran while one was open for 3% -> 2% of each run, Pallas kernels for 10% -> 8%
where the time goes in v5:
time: 108 us; the launch traced here: 106 us
  starting transfers between devices  35.5 us (33%)
  Pallas kernels  23 us (21%)
  blocking collectives  21.7 us (20%)
  waiting for transfers between devices  20.5 us (19%)
  local copies, waits for them, and re-layouts  4.8 us (4%)
    ppermute x13, starting transfers between devices, fetch(): return lax.ppermute(value, AXES, pairs)  26.9 us
    all_to_all x1, blocking collectives, body(): lax.all_to_all(increments, 'mem', split_axis=0, concat_axis=0, tiled=True)  21.7 us
    ppermute x13, waiting for transfers between devices, fetch(): return lax.ppermute(value, AXES, pairs)  17.5 us
    pallas_call x1, Pallas kernels, body(): pl.pallas_call(analysis_kernel, out_shape=jax.ShapeDtypeStruct((group, ti...  7.89 us
    pallas_call x1, Pallas kernels, body(): pl.pallas_call(forecast_kernel, out_shape=[jax.ShapeDtypeStruct((rows + 2...  5.97 us
    all_to_all x1, starting transfers between devices, body(): lax.all_to_all(payload, 'mem', split_axis=0, concat_axis=0, tiled=True)  4.54 us
    unnamed x21, local copies, waits for them, and re-layouts  4.51 us
    pallas_call x1, Pallas kernels, body(): pl.pallas_call(final_kernel, grid=(rows // 8,), out_shape=jax.ShapeDtypeS...  2.95 us
  transfers between devices with their start and end apart: 16, of which 6 were waited for; matrix products, arithmetic and copies ran while one was open for 2% of the time, Pallas kernels for 8%

profile of v5, /device:TPU:1, one launch (start us, length us, event | category | flops | bytes accessed | tf_op | source)
XLA Modules:
  0.0 105.7 jit_solution(4756292149637386127)
XLA Ops:
  0.0 1.7 %pack_obs.1.refs_0_ = bf16[1,512,128]{2,1,0:T(8,128)(2,1)} custom-call(bf16[1,128,512]{2,1,0:T(8,128)(2,1)} %anom_ref.1, bf16[1,128,512]{2,1,0:T(8,128)(2,1)} %weight_ref.1), custom_call_target="tpu_custom_call" | custom-call | tf_op jit(solution)/shard_map/pack_obs/pallas_call | solution.py:265
  1.7 7.7 %collective-permute-start.2 = (bf16[1,512,128]{2,1,0:T(8,128)(2,1)}, bf16[1,512,128]{2,1,0:T(8,128)(2,1)S(1)}, u32[]{:S(2)}, u32[]{:S(2)}) collective-permute-start(bf16[1,512,128]{2,1,0:T(8,128)(2,1)} %pack_obs.1.refs_0_), channel_id=1, source_target_pairs={{4,0},{5,1},{6,2},{7,3},{0,4},{1,5},{2,6},{3,7},{12,8},{13,9},{14,... | collective-permute-start | bytes 393224 | tf_op jit(solution)/shard_map/ppermute | solution.py:193
  9.4 2.3 %pack_halo.1 = (f32[5,72,256]{2,1,0:T(8,128)}, f32[5,72,256]{2,1,0:T(8,128)}, f32[8,128]{1,0:T(8,128)}) custom-call(f32[64,32,256]{2,1,0:T(8,128)} %x_ref.1, f32[64,32,256]{2,1,0:T(8,128)} %x_ref.1, f32[32,256]{1,0:T(8,128)} %coef_ref.5, s32[4,64]{1,0:T(4,128)} %bitcast.4, s32[4,64]{1,0:T(4,128)} %bitcast.5), custom_call_target="tpu_custom_call" | custom-call | tf_op jit(solution)/shard_map/pack_halo/pallas_call | solution.py:272
  11.8 2.8 %collective-permute-start = (f32[5,72,256]{2,1,0:T(8,128)}, f32[5,72,256]{2,1,0:T(8,128)S(1)}, u32[]{:S(2)}, u32[]{:S(2)}) collective-permute-start(f32[5,72,256]{2,1,0:T(8,128)} %get-tuple-element.15), channel_id=1, source_target_pairs={{0,1},{1,2},{2,3},{3,4},{4,5},{5,6},{6,7},{7,8},{8,9},{9,10},{10,1... | collective-permute-start | bytes 1105928 | tf_op jit(solution)/shard_map/ppermute | solution.py:287
  17.2 3.6 %collective-permute-start.3 = (bf16[2,512,128]{2,1,0:T(8,128)(2,1)S(1)}, bf16[2,512,128]{2,1,0:T(8,128)(2,1)S(1)}, u32[]{:S(2)}, u32[]{:S(2)}) collective-permute-start(bf16[2,512,128]{2,1,0:T(8,128)(2,1)S(1)} %get-tuple-element.18.refs_0_), channel_id=1, source_target_pairs={{8,0},{9,1},{10,2},{11,3},{12,4},{13,5},{14,6},{15,7},{16,8},{17,9... | collective-permute-start | bytes 786440 | tf_op jit(solution)/shard_map/ppermute | solution.py:193
  20.8 1.9 %collective-permute-start.5 = (bf16[2,512,128]{2,1,0:T(8,128)(2,1)S(1)}, bf16[2,512,128]{2,1,0:T(8,128)(2,1)S(1)}, u32[]{:S(2)}, u32[]{:S(2)}) collective-permute-start(bf16[2,512,128]{2,1,0:T(8,128)(2,1)S(1)} %get-tuple-element.18.refs_0_), channel_id=1, source_target_pairs={{16,0},{17,1},{18,2},{19,3},{20,4},{21,5},{22,6},{23,7},{24,8},{25... | collective-permute-start | bytes 786440 | tf_op jit(solution)/shard_map/ppermute | solution.py:193
  22.7 2.9 %collective-permute-done.1.refs_5_.below_ref = f32[5,72,256]{2,1,0:T(8,128)S(1)} collective-permute-done((f32[5,72,256]{2,1,0:T(8,128)}, f32[5,72,256]{2,1,0:T(8,128)S(1)}, u32[]{:S(2)}, u32[]{:S(2)}) %collective-permute-start.1) | collective-permute-done | bytes 368672 | tf_op jit(solution)/shard_map/ppermute | solution.py:286
  25.6 4.5 %collective-permute-done.3.refs_1_ = bf16[2,512,128]{2,1,0:T(8,128)(2,1)S(1)} collective-permute-done((bf16[2,512,128]{2,1,0:T(8,128)(2,1)S(1)}, bf16[2,512,128]{2,1,0:T(8,128)(2,1)S(1)}, u32[]{:S(2)}, u32[]{:S(2)}) %collective-permute-start.3) | collective-permute-done | bytes 262176 | tf_op jit(solution)/shard_map/ppermute | solution.py:193
  30.1 5.8 %collective-permute-done.5.refs_3_ = bf16[2,512,128]{2,1,0:T(8,128)(2,1)S(1)} collective-permute-done((bf16[2,512,128]{2,1,0:T(8,128)(2,1)S(1)}, bf16[2,512,128]{2,1,0:T(8,128)(2,1)S(1)}, u32[]{:S(2)}, u32[]{:S(2)}) %collective-permute-start.5) | collective-permute-done | bytes 262176 | tf_op jit(solution)/shard_map/ppermute | solution.py:193
  35.9 1.5 %join_eight.1 = (bf16[8,512,128]{2,1,0:T(8,128)(2,1)}, bf16[4,512,128]{2,1,0:T(8,128)(2,1)}, bf16[4,512,128]{2,1,0:T(8,128)(2,1)}, f32[8,128]{1,0:T(8,128)S(1)}) custom-call(bf16[2,512,128]{2,1,0:T(8,128)(2,1)S(1)} %get-tuple-element.18.refs_0_, bf16[2,512,128]{2,1,0:T(8,128)(2,1)S(1)} %collective-permute-done.3.refs_1_, ...), custom_call_target="tpu_custom_call" | custom-call | tf_op jit(solution)/shard_map/join_eight/pallas_call | solution.py:223
  37.4 3.3 %collective-permute-start.6 = (bf16[8,512,128]{2,1,0:T(8,128)(2,1)}, bf16[8,512,128]{2,1,0:T(8,128)(2,1)}, u32[]{:S(2)}, u32[]{:S(2)}) collective-permute-start(bf16[8,512,128]{2,1,0:T(8,128)(2,1)} %get-tuple-element.22.rest_0_), channel_id=1, source_target_pairs={{1,0},{2,1},{3,2},{4,3},{5,4},{6,5},{7,6},{0,7},{9,8},{10,9},{11,1... | collective-permute-start | bytes 3145736 | tf_op jit(solution)/shard_map/ppermute | solution.py:193
  40.7 6.0 %forecast4.1 = (f32[34,64,256]{2,1,0:T(8,128)S(1)}, bf16[8,608,128]{2,1,0:T(8,128)(2,1)S(1)}) custom-call(f32[64,32,256]{2,1,0:T(8,128)S(1)} %copy-done, f32[5,72,256]{2,1,0:T(8,128)S(1)} %collective-permute-done.refs_4_.above_ref, f32[5,72,256]{2,1,0:T(8,128)S(1)} %collective-permute-done.1.refs_5_.below_ref, f32[32,256]{1,0:T(8,128)S(1)} %copy-done.5, ...), custom_call_target="tpu_custom_call" | custom-call | tf_op jit(solution)/shard_map/forecast4/pallas_call | solution.py:292
  46.6 1.4 %copy-done.1 = f32[34,64,256]{2,1,0:T(8,128)} copy-done((f32[34,64,256]{2,1,0:T(8,128)}, f32[34,64,256]{2,1,0:T(8,128)S(1)}, u32[]{:S(2)}) %copy-start.1) | copy-done | bytes 2228248
  49.1 4.5 %all-to-all-start = ((bf16[8,608,128]{2,1,0:T(8,128)(2,1)}), bf16[8,608,128]{2,1,0:T(8,128)(2,1)S(1)}, u32[]{:S(2)}, u32[]{:S(2)}) async-start(bf16[8,608,128]{2,1,0:T(8,128)(2,1)} %copy-done.3), calls=%async_computation | async-start | bytes 2490368 | tf_op jit(solution)/shard_map/all_to_all | solution.py:309
  53.6 1.6 %collective-permute-start.8 = (bf16[4,512,128]{2,1,0:T(8,128)(2,1)}, bf16[4,512,128]{2,1,0:T(8,128)(2,1)S(1)}, u32[]{:S(2)}, u32[]{:S(2)}) collective-permute-start(bf16[4,512,128]{2,1,0:T(8,128)(2,1)} %get-tuple-element.23), channel_id=1, source_target_pairs={{2,0},{3,1},{4,2},{5,3},{6,4},{7,5},{0,6},{1,7},{10,8},{11,9},{12,... | collective-permute-start | bytes 1572872 | tf_op jit(solution)/shard_map/ppermute | solution.py:193
  56.6 1.3 %collective-permute-start.10 = (bf16[8,512,128]{2,1,0:T(8,128)(2,1)}, bf16[8,512,128]{2,1,0:T(8,128)(2,1)}, u32[]{:S(2)}, u32[]{:S(2)}) collective-permute-start(bf16[8,512,128]{2,1,0:T(8,128)(2,1)} %get-tuple-element.22.rest_0_), channel_id=1, source_target_pairs={{32,0},{33,1},{34,2},{35,3},{36,4},{37,5},{38,6},{39,7},{40,8},{41... | collective-permute-start | bytes 3145736 | tf_op jit(solution)/shard_map/ppermute | solution.py:193
  60.2 3.6 %collective-permute-done.8.rest_3_ = bf16[4,512,128]{2,1,0:T(8,128)(2,1)S(1)} collective-permute-done((bf16[4,512,128]{2,1,0:T(8,128)(2,1)}, bf16[4,512,128]{2,1,0:T(8,128)(2,1)S(1)}, u32[]{:S(2)}, u32[]{:S(2)}) %collective-permute-start.8) | collective-permute-done | bytes 524320 | tf_op jit(solution)/shard_map/ppermute | solution.py:193
  63.8 3.6 %collective-permute-start.13 = (bf16[4,512,128]{2,1,0:T(8,128)(2,1)S(1)}, bf16[4,512,128]{2,1,0:T(8,128)(2,1)S(1)}, u32[]{:S(2)}, u32[]{:S(2)}) collective-permute-start(bf16[4,512,128]{2,1,0:T(8,128)(2,1)S(1)} %collective-permute-done.8.rest_3_), channel_id=1, source_target_pairs={{32,0},{33,1},{34,2},{35,3},{36,4},{37,5},{38,6},{39,7},{40,8},{41... | collective-permute-start | bytes 1572872 | tf_op jit(solution)/shard_map/ppermute | solution.py:193
  67.4 2.0 %collective-permute-done.9.rest_4_ = bf16[4,512,128]{2,1,0:T(8,128)(2,1)} collective-permute-done((bf16[4,512,128]{2,1,0:T(8,128)(2,1)}, bf16[4,512,128]{2,1,0:T(8,128)(2,1)}, u32[]{:S(2)}, u32[]{:S(2)}) %collective-permute-start.9) | collective-permute-done | bytes 524320 | tf_op jit(solution)/shard_map/ppermute | solution.py:193
  69.4 2.0 %collective-permute-start.14 = (bf16[4,512,128]{2,1,0:T(8,128)(2,1)}, bf16[4,512,128]{2,1,0:T(8,128)(2,1)S(1)}, u32[]{:S(2)}, u32[]{:S(2)}) collective-permute-start(bf16[4,512,128]{2,1,0:T(8,128)(2,1)} %collective-permute-done.9.rest_4_), channel_id=1, source_target_pairs={{32,0},{33,1},{34,2},{35,3},{36,4},{37,5},{38,6},{39,7},{40,8},{41... | collective-permute-start | bytes 1572872 | tf_op jit(solution)/shard_map/ppermute | solution.py:193
  71.4 1.7 %collective-permute-done.14.rest_9_ = bf16[4,512,128]{2,1,0:T(8,128)(2,1)S(1)} collective-permute-done((bf16[4,512,128]{2,1,0:T(8,128)(2,1)}, bf16[4,512,128]{2,1,0:T(8,128)(2,1)S(1)}, u32[]{:S(2)}, u32[]{:S(2)}) %collective-permute-start.14) | collective-permute-done | bytes 524320 | tf_op jit(solution)/shard_map/ppermute | solution.py:193
  73.1 7.9 %analysis.1 = bf16[8,576,128]{2,1,0:T(8,128)(2,1)S(1)} custom-call(s32[9,4]{1,0:T(8,128)S(1)} %get-tuple-element.26.anom_at_ref, s32[9,4]{1,0:T(8,128)S(1)} %get-tuple-element.25.weight_at_ref, s32[9,4]{1,0:T(8,128)S(1)} %get-tuple-element.29.tapers_ref, bf16[8,608,128]{2,1,0:T(8,128)(2,1)S(1)} %all-to-all-done.recv_ref, f32[8,128,128]{2,1,0:T(8,128)S(1)} %bitcast.3, ...), custom_call_target="tpu_custom_call" | custom-call | tf_op jit(solution)/shard_map/analysis/pallas_call | solution.py:318
  81.0 21.7 %all_to_all.10.inc_ref = bf16[8,576,128]{2,1,0:T(8,128)(2,1)S(1)} all-to-all(bf16[8,576,128]{2,1,0:T(8,128)(2,1)S(1)} %analysis.1), channel_id=1, replica_groups=mesh['mem'=8,'state'=32] {'mem'}, dimensions={0} | all-to-all | bytes 2359296 | tf_op jit(solution)/shard_map/all_to_all | solution.py:330
  102.8 2.9 %final_step.1 = f32[64,32,256]{2,1,0:T(8,128)} custom-call(f32[34,64,256]{2,1,0:T(8,128)S(1)} %copy-done.2, bf16[8,576,128]{2,1,0:T(8,128)(2,1)S(1)} %all_to_all.10.inc_ref, f32[32,256]{1,0:T(8,128)S(1)} %copy-done.5), custom_call_target="tpu_custom_call" | custom-call | tf_op jit(solution)/shard_map/final_step/pallas_call | solution.py:332
  (46 shorter events, 7.3 us)
Async XLA Ops:
  1.7 14.2 %collective-permute-start.2 = (bf16[1,512,128]{2,1,0:T(8,128)(2,1)}, bf16[1,512,128]{2,1,0:T(8,128)(2,1)S(1)}, u32[]{:S(2)}, u32[]{:S(2)}) collective-permute-start(bf16[1,512,128]{2,1,0:T(8,128)(2,1)} %pack_obs.1.refs_0_), channel_id=1, source_target_pairs={{4,0},{5,1},{6,2},{7,3},{0,4},{1,5},{2,6},{3,7},{12,8},{13,9},{14,... | collective-permute-start | bytes 393224 | tf_op jit(solution)/shard_map/ppermute | solution.py:193
  9.4 6.5 %copy-start.4 = (bf16[1,512,128]{2,1,0:T(8,128)(2,1)S(1)}, bf16[1,512,128]{2,1,0:T(8,128)(2,1)}, u32[]{:S(2)}) copy-start(bf16[1,512,128]{2,1,0:T(8,128)(2,1)} %pack_obs.1.refs_0_) | copy-start | bytes 393220
  9.4 31.2 %copy-start = (f32[64,32,256]{2,1,0:T(8,128)S(1)}, f32[64,32,256]{2,1,0:T(8,128)}, u32[]{:S(2)}) copy-start(f32[64,32,256]{2,1,0:T(8,128)} %x_ref.1) | copy-start | bytes 6291460
  11.8 28.9 %copy-start.5 = (f32[32,256]{1,0:T(8,128)S(1)}, f32[32,256]{1,0:T(8,128)}, u32[]{:S(2)}) copy-start(f32[32,256]{1,0:T(8,128)} %coef_ref.5) | copy-start | bytes 98308
  11.8 10.9 %collective-permute-start = (f32[5,72,256]{2,1,0:T(8,128)}, f32[5,72,256]{2,1,0:T(8,128)S(1)}, u32[]{:S(2)}, u32[]{:S(2)}) collective-permute-start(f32[5,72,256]{2,1,0:T(8,128)} %get-tuple-element.15), channel_id=1, source_target_pairs={{0,1},{1,2},{2,3},{3,4},{4,5},{5,6},{6,7},{7,8},{8,9},{9,10},{10,1... | collective-permute-start | bytes 1105928 | tf_op jit(solution)/shard_map/ppermute | solution.py:287
  14.6 11.0 %collective-permute-start.1 = (f32[5,72,256]{2,1,0:T(8,128)}, f32[5,72,256]{2,1,0:T(8,128)S(1)}, u32[]{:S(2)}, u32[]{:S(2)}) collective-permute-start(f32[5,72,256]{2,1,0:T(8,128)} %get-tuple-element.16), channel_id=1, source_target_pairs={{1,0},{2,1},{3,2},{4,3},{5,4},{6,5},{7,6},{8,7},{9,8},{10,9},{11,1... | collective-permute-start | bytes 1105928 | tf_op jit(solution)/shard_map/ppermute | solution.py:286
  17.2 12.9 %collective-permute-start.3 = (bf16[2,512,128]{2,1,0:T(8,128)(2,1)S(1)}, bf16[2,512,128]{2,1,0:T(8,128)(2,1)S(1)}, u32[]{:S(2)}, u32[]{:S(2)}) collective-permute-start(bf16[2,512,128]{2,1,0:T(8,128)(2,1)S(1)} %get-tuple-element.18.refs_0_), channel_id=1, source_target_pairs={{8,0},{9,1},{10,2},{11,3},{12,4},{13,5},{14,6},{15,7},{16,8},{17,9... | collective-permute-start | bytes 786440 | tf_op jit(solution)/shard_map/ppermute | solution.py:193
  20.8 9.4 %collective-permute-start.4 = (bf16[2,512,128]{2,1,0:T(8,128)(2,1)S(1)}, bf16[2,512,128]{2,1,0:T(8,128)(2,1)S(1)}, u32[]{:S(2)}, u32[]{:S(2)}) collective-permute-start(bf16[2,512,128]{2,1,0:T(8,128)(2,1)S(1)} %get-tuple-element.18.refs_0_), channel_id=1, source_target_pairs={{24,0},{25,1},{26,2},{27,3},{28,4},{29,5},{30,6},{31,7},{0,8},{1,9... | collective-permute-start | bytes 786440 | tf_op jit(solution)/shard_map/ppermute | solution.py:193
  20.8 15.1 %collective-permute-start.5 = (bf16[2,512,128]{2,1,0:T(8,128)(2,1)S(1)}, bf16[2,512,128]{2,1,0:T(8,128)(2,1)S(1)}, u32[]{:S(2)}, u32[]{:S(2)}) collective-permute-start(bf16[2,512,128]{2,1,0:T(8,128)(2,1)S(1)} %get-tuple-element.18.refs_0_), channel_id=1, source_target_pairs={{16,0},{17,1},{18,2},{19,3},{20,4},{21,5},{22,6},{23,7},{24,8},{25... | collective-permute-start | bytes 786440 | tf_op jit(solution)/shard_map/ppermute | solution.py:193
  37.4 20.5 %collective-permute-start.6 = (bf16[8,512,128]{2,1,0:T(8,128)(2,1)}, bf16[8,512,128]{2,1,0:T(8,128)(2,1)}, u32[]{:S(2)}, u32[]{:S(2)}) collective-permute-start(bf16[8,512,128]{2,1,0:T(8,128)(2,1)} %get-tuple-element.22.rest_0_), channel_id=1, source_target_pairs={{1,0},{2,1},{3,2},{4,3},{5,4},{6,5},{7,6},{0,7},{9,8},{10,9},{11,1... | collective-permute-start | bytes 3145736 | tf_op jit(solution)/shard_map/ppermute | solution.py:193
  40.7 17.4 %collective-permute-start.7 = (bf16[8,512,128]{2,1,0:T(8,128)(2,1)}, bf16[8,512,128]{2,1,0:T(8,128)(2,1)}, u32[]{:S(2)}, u32[]{:S(2)}) collective-permute-start(bf16[8,512,128]{2,1,0:T(8,128)(2,1)} %get-tuple-element.22.rest_0_), channel_id=1, source_target_pairs={{7,0},{0,1},{1,2},{2,3},{3,4},{4,5},{5,6},{6,7},{15,8},{8,9},{9,10... | collective-permute-start | bytes 3145736 | tf_op jit(solution)/shard_map/ppermute | solution.py:193
  46.6 1.4 %copy-start.1 = (f32[34,64,256]{2,1,0:T(8,128)}, f32[34,64,256]{2,1,0:T(8,128)S(1)}, u32[]{:S(2)}) copy-start(f32[34,64,256]{2,1,0:T(8,128)S(1)} %get-tuple-element.20.prior_ref) | copy-start | bytes 6684676
  48.0 1.0 copy-start.3
  49.1 9.4 %copy-start.7 = (s32[64,4]{0,1:T(4,128)S(1)}, s32[64,4]{0,1:T(4,128)}, u32[]{:S(2)}) copy-start(s32[64,4]{0,1:T(4,128)} %param.12) | copy-start | bytes 3076
  49.1 9.5 %copy-start.8 = (s32[64,4]{0,1:T(4,128)S(1)}, s32[64,4]{0,1:T(4,128)}, u32[]{:S(2)}) copy-start(s32[64,4]{0,1:T(4,128)} %param.13) | copy-start | bytes 3076
  49.1 24.0 %all-to-all-start = ((bf16[8,608,128]{2,1,0:T(8,128)(2,1)}), bf16[8,608,128]{2,1,0:T(8,128)(2,1)S(1)}, u32[]{:S(2)}, u32[]{:S(2)}) async-start(bf16[8,608,128]{2,1,0:T(8,128)(2,1)} %copy-done.3), calls=%async_computation | async-start | bytes 2490368 | tf_op jit(solution)/shard_map/all_to_all | solution.py:309
  53.6 10.1 %collective-permute-start.8 = (bf16[4,512,128]{2,1,0:T(8,128)(2,1)}, bf16[4,512,128]{2,1,0:T(8,128)(2,1)S(1)}, u32[]{:S(2)}, u32[]{:S(2)}) collective-permute-start(bf16[4,512,128]{2,1,0:T(8,128)(2,1)} %get-tuple-element.23), channel_id=1, source_target_pairs={{2,0},{3,1},{4,2},{5,3},{6,4},{7,5},{0,6},{1,7},{10,8},{11,9},{12,... | collective-permute-start | bytes 1572872 | tf_op jit(solution)/shard_map/ppermute | solution.py:193
  55.3 14.1 %collective-permute-start.9 = (bf16[4,512,128]{2,1,0:T(8,128)(2,1)}, bf16[4,512,128]{2,1,0:T(8,128)(2,1)}, u32[]{:S(2)}, u32[]{:S(2)}) collective-permute-start(bf16[4,512,128]{2,1,0:T(8,128)(2,1)} %get-tuple-element.24), channel_id=1, source_target_pairs={{6,0},{7,1},{0,2},{1,3},{2,4},{3,5},{4,6},{5,7},{14,8},{15,9},{8,1... | collective-permute-start | bytes 1572872 | tf_op jit(solution)/shard_map/ppermute | solution.py:193
  56.6 14.8 %collective-permute-start.10 = (bf16[8,512,128]{2,1,0:T(8,128)(2,1)}, bf16[8,512,128]{2,1,0:T(8,128)(2,1)}, u32[]{:S(2)}, u32[]{:S(2)}) collective-permute-start(bf16[8,512,128]{2,1,0:T(8,128)(2,1)} %get-tuple-element.22.rest_0_), channel_id=1, source_target_pairs={{32,0},{33,1},{34,2},{35,3},{36,4},{37,5},{38,6},{39,7},{40,8},{41... | collective-permute-start | bytes 3145736 | tf_op jit(solution)/shard_map/ppermute | solution.py:193
  57.9 15.2 %collective-permute-start.11 = (bf16[8,512,128]{2,1,0:T(8,128)(2,1)}, bf16[8,512,128]{2,1,0:T(8,128)(2,1)}, u32[]{:S(2)}, u32[]{:S(2)}) collective-permute-start(bf16[8,512,128]{2,1,0:T(8,128)(2,1)} %collective-permute-done.6.rest_1_), channel_id=1, source_target_pairs={{32,0},{33,1},{34,2},{35,3},{36,4},{37,5},{38,6},{39,7},{40,8},{41... | collective-permute-start | bytes 3145736 | tf_op jit(solution)/shard_map/ppermute | solution.py:193
  58.0 15.1 %collective-permute-start.12 = (bf16[8,512,128]{2,1,0:T(8,128)(2,1)}, bf16[8,512,128]{2,1,0:T(8,128)(2,1)}, u32[]{:S(2)}, u32[]{:S(2)}) collective-permute-start(bf16[8,512,128]{2,1,0:T(8,128)(2,1)} %collective-permute-done.7.rest_2_), channel_id=1, source_target_pairs={{32,0},{33,1},{34,2},{35,3},{36,4},{37,5},{38,6},{39,7},{40,8},{41... | collective-permute-start | bytes 3145736 | tf_op jit(solution)/shard_map/ppermute | solution.py:193
  63.8 7.7 %collective-permute-start.13 = (bf16[4,512,128]{2,1,0:T(8,128)(2,1)S(1)}, bf16[4,512,128]{2,1,0:T(8,128)(2,1)S(1)}, u32[]{:S(2)}, u32[]{:S(2)}) collective-permute-start(bf16[4,512,128]{2,1,0:T(8,128)(2,1)S(1)} %collective-permute-done.8.rest_3_), channel_id=1, source_target_pairs={{32,0},{33,1},{34,2},{35,3},{36,4},{37,5},{38,6},{39,7},{40,8},{41... | collective-permute-start | bytes 1572872 | tf_op jit(solution)/shard_map/ppermute | solution.py:193
  69.4 3.7 %collective-permute-start.14 = (bf16[4,512,128]{2,1,0:T(8,128)(2,1)}, bf16[4,512,128]{2,1,0:T(8,128)(2,1)S(1)}, u32[]{:S(2)}, u32[]{:S(2)}) collective-permute-start(bf16[4,512,128]{2,1,0:T(8,128)(2,1)} %collective-permute-done.9.rest_4_), channel_id=1, source_target_pairs={{32,0},{33,1},{34,2},{35,3},{36,4},{37,5},{38,6},{39,7},{40,8},{41... | collective-permute-start | bytes 1572872 | tf_op jit(solution)/shard_map/ppermute | solution.py:193
  81.0 21.8 %copy-start.2 = (f32[34,64,256]{2,1,0:T(8,128)S(1)}, f32[34,64,256]{2,1,0:T(8,128)}, u32[]{:S(2)}) copy-start(f32[34,64,256]{2,1,0:T(8,128)} %copy-done.1) | copy-start | bytes 6684676
  (1 other events, 0.7 us)

commit v6 on v5

--- a/solution.py
+++ b/solution.py
@@ -12,9 +12,10 @@
 HALO = FSTEPS + 1
 VMEM = pl.BlockSpec(memory_space=pltpu.VMEM)
 SMEM = pl.BlockSpec(memory_space=pltpu.SMEM)
-
-
-def pack_obs_kernel(anom_ref, weight_ref, out_ref):
+HBM = pl.BlockSpec(memory_space=pltpu.HBM)
+
+
+def pack_obs(anom_ref, weight_ref, out_ref):
     members = anom_ref.shape[2]
     core = lax.rem(lax.axis_index("mem"), 2)
 
@@ -29,7 +30,8 @@
             out_ref[0, q * TILE : (q + 1) * TILE, :] = weight_ref[0, :, q * TILE : (q + 1) * TILE].T
 
 
-def pack_halo_kernel(first_ref, last_ref, coef_ref, block_ref, taper_ref, up_ref, down_ref, token_ref):
+def pack_kernel(first_ref, last_ref, coef_ref, block_ref, taper_ref, anom_ref, weight_ref, up_ref, down_ref, own_ref):
+    pack_obs(anom_ref, weight_ref, own_ref)
     members, depth, columns = first_ref.shape
     rows = coef_ref.shape[0]
     tiles = block_ref.shape[1]
@@ -47,10 +49,9 @@
                 ids = jnp.where(lane == t * SLOTS + k, block_ref[k, tile0 + t], ids)
                 ids = jnp.where(lane == 8 + t * SLOTS + k, taper_ref[k, tile0 + t], ids)
         out_ref[far, members : members + 8, :] = ids.astype(F32)
-    token_ref[...] = jnp.zeros(TOKEN.shape, F32)
-
-
-def forecast_kernel(x_ref, above_ref, below_ref, coef_ref, token_ref, prior_ref, pay_ref, a_ref, b_ref, c_ref, m_ref):
+
+
+def forecast_kernel(x_ref, above_ref, below_ref, coef_ref, prior_ref, out_ref, token_ref, a_ref, b_ref, c_ref, m_ref, pay_ref, sems):
     members, rows, columns = x_ref.shape
     total = rows + 2 * HALO
     group = pay_ref.shape[0]
@@ -82,9 +83,11 @@
 
     lax.fori_loop(0, members // chunk, advance, 0)
     src = a_ref if FSTEPS % 2 == 0 else b_ref
+    copies = [pltpu.make_async_copy(src.at[pl.ds(HALO - 1, rows + 2)], prior_ref, sems.at[group])]
+    copies[0].start()
     m_ref[...] = jnp.zeros_like(m_ref)
 
-    def tile(index, dest, slot, half, keep):
+    def tile(index, dest, slot, half):
         value = src[index, :, half * TILE : (half + 1) * TILE]
         mean = jnp.sum(value, axis=0, keepdims=True) * (1.0 / members)
         pay_ref[dest, slot * members : (slot + 1) * members, :] = (value - mean).astype(BF16)
@@ -97,23 +100,21 @@
     for j in range(group):
         for i in range(per):
             for half in range(2):
-                tile(HALO + j * per + i, j, 2 * i + half, half, True)
-    for half in range(2):
-        tile(HALO - 1, half, tiles - 1, half, True)
-        tile(HALO + rows, 2 + half, tiles - 1, half, True)
-    for j in range(4, group):
-        pay_ref[j, (tiles - 1) * members : tiles * members, :] = jnp.zeros((members, TILE), BF16)
-    for j in range(group):
+                tile(HALO + j * per + i, j, 2 * i + half, half)
+        if j < 2:
+            tile(HALO - 1, j, tiles - 1, j)
+        elif j < 4:
+            tile(HALO + rows, j, tiles - 1, j - 2)
+        else:
+            pay_ref[j, (tiles - 1) * members : tiles * members, :] = jnp.zeros((members, TILE), BF16)
         pay_ref[j, tiles * members :, :] = m_ref[j].astype(BF16)
-    prior_ref[...] = src[HALO - 1 : HALO + rows + 1]
-
-
-def analysis_kernel(anom_at_ref, weight_at_ref, tapers_ref, recv_ref, taper_ref, *rest):
-    pieces, (ret_ref, obs_ref, centred_ref) = rest[:-3], rest[-3:]
-    group, size, _ = recv_ref.shape
-    count = ret_ref.shape[1] // anom_at_ref.shape[0]
-    tiles = anom_at_ref.shape[0]
-    members = group * count
+        copies.append(pltpu.make_async_copy(pay_ref.at[j], out_ref.at[j], sems.at[j]))
+        copies[-1].start()
+    for copy in copies:
+        copy.wait()
+
+
+def fill(pieces, obs_ref):
     core = lax.rem(lax.axis_index("mem"), 2)
     for side in range(2):
         start = 0
@@ -127,18 +128,40 @@
             lax.fori_loop(0, piece.shape[0], keep, 0)
             start += piece.shape[0]
 
+
+def collect_kernel(recv_ref, *rest):
+    pieces, (obs_ref, centred_ref) = rest[:-2], rest[-2:]
+    group, size, _ = recv_ref.shape
+    tiles, members, _ = centred_ref.shape
+    count = members // group
+    fill(pieces, obs_ref)
     parts = recv_ref[:, size - 32 :, :].astype(F32)
     for t in range(tiles):
         own = parts[:, 3 * t, :] + parts[:, 3 * t + 1, :] + parts[:, 3 * t + 2, :]
         delta = own - jnp.mean(own, axis=0, keepdims=True)
         local = recv_ref[:, t * count : (t + 1) * count, :].astype(F32)
         centred_ref[t] = (local + delta[:, None, :]).astype(BF16).reshape(members, TILE)
+
+
+def analysis_kernel(anom_at_ref, weight_at_ref, tapers_ref, taper_ref, centred_ref, early_ref, *rest):
+    pieces, (ret_ref, late_ref) = rest[:-2], rest[-2:]
+    tiles, members, _ = centred_ref.shape
+    group = ret_ref.shape[0]
+    count = members // group
+    early = early_ref.shape[1]
+    fill(pieces, late_ref)
+
+    def block(kind, at):
+        near = early_ref[kind, jnp.minimum(at, early - 1)]
+        far = late_ref[kind, jnp.maximum(at - early, 0)]
+        return jnp.where(at < early, near, far)
+
     def one(t, carry):
         anoms, weights = [], []
         for k in range(SLOTS):
-            at = anom_at_ref[t, k]
-            anoms.append(jnp.concatenate([obs_ref[0, at, q * TILE : (q + 1) * TILE, :] for q in range(members // TILE)], axis=1))
-            weights.append(obs_ref[1, weight_at_ref[t, k]])
+            anom = block(0, anom_at_ref[t, k])
+            anoms.append(jnp.concatenate([anom[q * TILE : (q + 1) * TILE] for q in range(members // TILE)], axis=1))
+            weights.append(block(1, weight_at_ref[t, k]))
         cov = jnp.dot(jnp.concatenate(anoms, axis=0), centred_ref[t], preferred_element_type=F32) * (1.0 / (members - 1.0))
         tapered = [
             (taper_ref[tapers_ref[t, k]] * cov[k * TILE : (k + 1) * TILE]).astype(BF16) for k in range(SLOTS)
@@ -217,24 +240,23 @@
             for a in range(count):
                 outs[1][a] = refs[a][0]
                 outs[2][a] = refs[a][core]
-        outs[-1][...] = jnp.zeros(TOKEN.shape, F32)
 
     shapes = [(count * blocks, *operands[0].shape[1:])] + [(count, *operands[0].shape[1:])] * (2 * split)
     return pl.pallas_call(
         kernel,
-        out_shape=[jax.ShapeDtypeStruct(shape, BF16) for shape in shapes] + [TOKEN],
-        in_specs=[VMEM] * (count + len(after)),
-        out_specs=[VMEM] * (len(shapes) + 1),
+        out_shape=[jax.ShapeDtypeStruct(shape, BF16) for shape in shapes],
+        in_specs=[VMEM] * count + [HBM] * len(after),
+        out_specs=[VMEM] * len(shapes),
         compiler_params=pltpu.CompilerParams(vmem_limit_bytes=6 << 20),
         name=name,
     )(*operands, *after)
 
 
-def gather_start(own, mesh, packed_halo, arrived):
+def gather_start(own, mesh, after):
     far = fetch(own, mesh, lambda x, c, y, z: (x, c, y, z + 4))
-    held, _ = join([own, far], "join_two", [packed_halo])
+    (held,) = join([own, far], "join_two")
     p, m, q = (fetch(held, mesh, ring(True, step)) for step in (1, -1, 2))
-    return join([held, p, m, q], "join_eight", arrived, split=True)
+    return join([held, p, m, q], "join_eight", after, split=True)
 
 
 def gather_rest(held, first, second, mesh):
@@ -262,50 +284,49 @@
     size = tiles * members + 32
 
     j, at = lax.axis_index("mem"), lax.axis_index("state")
-    packed = pl.pallas_call(
-        pack_obs_kernel,
-        out_shape=jax.ShapeDtypeStruct((1, obs_anom.shape[2], TILE), BF16),
-        in_specs=[VMEM] * 2,
-        out_specs=VMEM,
-        name="pack_obs",
-    )(obs_anom, obs_weight)
-    up, down, packed_halo = pl.pallas_call(
-        pack_halo_kernel,
+    up, down, packed = pl.pallas_call(
+        pack_kernel,
         grid=(1,),
-        out_shape=[jax.ShapeDtypeStruct((HALO, members + 8, columns), F32)] * 2 + [TOKEN],
+        out_shape=[jax.ShapeDtypeStruct((HALO, members + 8, columns), F32)] * 2
+        + [jax.ShapeDtypeStruct((1, obs_anom.shape[2], TILE), BF16)],
         in_specs=[
             pl.BlockSpec((members, 8, columns), lambda i: (0, 0, 0)),
             pl.BlockSpec((members, 8, columns), lambda i: (0, rows // 8 - 1, 0)),
             VMEM,
             SMEM,
             SMEM,
+            VMEM,
+            VMEM,
         ],
         out_specs=[VMEM] * 3,
-        name="pack_halo",
-    )(ensemble, ensemble, spreading_coefficient, obs_block.T, taper_id.T)
+        name="pack",
+    )(ensemble, ensemble, spreading_coefficient, obs_block.T, taper_id.T, obs_anom, obs_weight)
     below = lax.ppermute(up, "state", [(i + 1, i) for i in range(states - 1)])
     above = lax.ppermute(down, "state", [(i, i + 1) for i in range(states - 1)])
 
     chips = (group // 2, states // 8, 8)
-    held, first, second, joined = gather_start(packed, chips, packed_halo, [above, below])
-    own, swapped = gather_rest(held, first, second, chips)
-    prior, payload = pl.pallas_call(
+    prior, payload, forecast_done = pl.pallas_call(
         forecast_kernel,
         out_shape=[
             jax.ShapeDtypeStruct((rows + 2, members, columns), F32),
             jax.ShapeDtypeStruct((group, size, TILE), BF16),
+            TOKEN,
         ],
-        in_specs=[VMEM] * 5,
-        out_specs=[VMEM] * 2,
+        in_specs=[VMEM] * 4,
+        out_specs=[HBM] * 3,
         scratch_shapes=[
             pltpu.VMEM((rows + 2 * HALO, members, columns), F32),
             pltpu.VMEM((rows + 2 * HALO, members, columns), F32),
             pltpu.VMEM((rows + 2 * HALO, 8, columns), F32),
             pltpu.VMEM((group, 32, TILE), F32),
+            pltpu.VMEM((group, size, TILE), BF16),
+            pltpu.SemaphoreType.DMA((group + 1,)),
         ],
         compiler_params=pltpu.CompilerParams(vmem_limit_bytes=14 << 20),
         name="forecast4",
-    )(ensemble, above, below, spreading_coefficient, joined)
+    )(ensemble, above, below, spreading_coefficient)
+    held, first, second = gather_start(packed, chips, [forecast_done])
+    own, swapped = gather_rest(held, first, second, chips)
     gathered = lax.all_to_all(payload, "mem", split_axis=0, concat_axis=0, tiled=True)
 
     edge = jnp.where(j < 2, above[0, members, :16], below[HALO - 1, members, :16])
@@ -315,18 +336,28 @@
     tapers = jnp.concatenate([lax.dynamic_slice_in_dim(taper_id, mine, 2 * per, 0), edge[1:2]], axis=0)
 
     anom_at, weight_at = places(blocks, at // 8, at % 8)
+    late = 2
+    early = own[:-late] + swapped[:-late]
+    held_early, centred = pl.pallas_call(
+        collect_kernel,
+        out_shape=[
+            jax.ShapeDtypeStruct((2, sum(v.shape[0] for v in own[:-late]), *packed.shape[1:]), BF16),
+            jax.ShapeDtypeStruct((tiles, group * members, TILE), BF16),
+        ],
+        in_specs=[VMEM] * (1 + len(early)),
+        out_specs=[VMEM] * 2,
+        compiler_params=pltpu.CompilerParams(vmem_limit_bytes=18 << 20),
+        name="collect",
+    )(gathered, *early)
     increments = pl.pallas_call(
         analysis_kernel,
         out_shape=jax.ShapeDtypeStruct((group, tiles * members, TILE), BF16),
-        in_specs=[SMEM] * 3 + [VMEM] * (2 + len(own) + len(swapped)),
+        in_specs=[SMEM] * 3 + [VMEM] * (3 + 2 * late),
         out_specs=VMEM,
-        scratch_shapes=[
-            pltpu.VMEM((2, states, *packed.shape[1:]), BF16),
-            pltpu.VMEM((tiles, group * members, TILE), BF16),
-        ],
-        compiler_params=pltpu.CompilerParams(vmem_limit_bytes=22 << 20),
+        scratch_shapes=[pltpu.VMEM((2, sum(v.shape[0] for v in own[-late:]), *packed.shape[1:]), BF16)],
+        compiler_params=pltpu.CompilerParams(vmem_limit_bytes=18 << 20),
         name="analysis",
-    )(anom_at, weight_at, tapers, gathered, jnp.swapaxes(taper_table, 1, 2), *own, *swapped)
+    )(anom_at, weight_at, tapers, jnp.swapaxes(taper_table, 1, 2), centred, held_early, *own[-late:], *swapped[-late:])
     returned = lax.all_to_all(increments, "mem", split_axis=0, concat_axis=0, tiled=True)
 
     return pl.pallas_call(

time: 108 us -> 103 us (0.954); the launches traced: 106 us -> 102 us
  waiting for transfers between devices: 20.5 us -> 17.4 us
    all_to_all x1, starting transfers between devices: 4.54 us -> 8.69 us  [body(): lax.all_to_all(payload, 'mem', split_axis=0, concat_axis=0, tiled=True)]
    ppermute x13, starting transfers between devices: 26.9 us -> 23.7 us  [fetch(): return lax.ppermute(value, AXES, pairs)]
    pallas_call x1, Pallas kernels: 7.89 us -> 5.42 us  [body(): pl.pallas_call(analysis_kernel, out_shape=jax.ShapeDtypeStruct((group, ti...]
    ppermute x1, waiting for transfers between devices: 2.91 us -> 0.8 us  [body(): below = lax.ppermute(up, 'state', [(i + 1, i) for i in range(states - 1)])]
    pallas_call x2, Pallas kernels: 4.05 us -> 5.92 us  [the longest x1 3.36 us: body(): pl.pallas_call(collect_kernel, out_shape=[jax.ShapeDtypeStruct((2, sum((v...]
    ppermute x13, waiting for transfers between devices: 17.5 us -> 16 us  [fetch(): return lax.ppermute(value, AXES, pairs)]
  transfers between devices with their start and end apart: 16 -> 16, of which waited for: 6 -> 5; matrix products, arithmetic and copies ran while one was open for 2% -> 2% of each run, Pallas kernels for 8% -> 10%
where the time goes in v6:
time: 103 us; the launch traced here: 102 us
  starting transfers between devices  36.3 us (35%)
  Pallas kernels  22.5 us (22%)
  blocking collectives  21 us (20%)
  waiting for transfers between devices  17.4 us (17%)
  local copies, waits for them, and re-layouts  3.95 us (4%)
    ppermute x13, starting transfers between devices, fetch(): return lax.ppermute(value, AXES, pairs)  23.7 us
    all_to_all x1, blocking collectives, body(): lax.all_to_all(increments, 'mem', split_axis=0, concat_axis=0, tiled=True)  21 us
    ppermute x13, waiting for transfers between devices, fetch(): return lax.ppermute(value, AXES, pairs)  16 us
    all_to_all x1, starting transfers between devices, body(): lax.all_to_all(payload, 'mem', split_axis=0, concat_axis=0, tiled=True)  8.69 us
    pallas_call x1, Pallas kernels, body(): pl.pallas_call(forecast_kernel, out_shape=[jax.ShapeDtypeStruct((rows + 2...  7.01 us
    pallas_call x1, Pallas kernels, body(): pl.pallas_call(analysis_kernel, out_shape=jax.ShapeDtypeStruct((group, ti...  5.42 us
    unnamed x21, local copies, waits for them, and re-layouts  3.73 us
    pallas_call x1, Pallas kernels, body(): pl.pallas_call(collect_kernel, out_shape=[jax.ShapeDtypeStruct((2, sum((v...  3.36 us
  transfers between devices with their start and end apart: 16, of which 5 were waited for; matrix products, arithmetic and copies ran while one was open for 2% of the time, Pallas kernels for 10%

profile of v6, /device:TPU:1, one launch (start us, length us, event | category | flops | bytes accessed | tf_op | source)
XLA Modules:
  0.0 102.1 jit_solution(7116063141872527062)
XLA Ops:
  0.0 2.6 %pack.1 = (f32[5,72,256]{2,1,0:T(8,128)}, f32[5,72,256]{2,1,0:T(8,128)}, bf16[1,512,128]{2,1,0:T(8,128)(2,1)}) custom-call(f32[64,32,256]{2,1,0:T(8,128)} %x_ref.1, f32[64,32,256]{2,1,0:T(8,128)} %x_ref.1, f32[32,256]{1,0:T(8,128)} %coef_ref.5, s32[4,64]{1,0:T(4,128)} %bitcast.4, s32[4,64]{1,0:T(4,128)} %bitcast.5, bf16[1,128,512]{2,1,0:T(8,128)(2,1)} %anom_ref.1, ...), custom_call_target="tpu_custom_call" | custom-call | tf_op jit(solution)/shard_map/pack/pallas_call | solution.py:287
  2.6 7.7 %collective-permute-start.2 = (bf16[1,512,128]{2,1,0:T(8,128)(2,1)}, bf16[1,512,128]{2,1,0:T(8,128)(2,1)S(1)}, u32[]{:S(2)}, u32[]{:S(2)}) collective-permute-start(bf16[1,512,128]{2,1,0:T(8,128)(2,1)} %get-tuple-element.20.refs_0_), channel_id=1, source_target_pairs={{4,0},{5,1},{6,2},{7,3},{0,4},{1,5},{2,6},{3,7},{12,8},{13,9},{14,... | collective-permute-start | bytes 393224 | tf_op jit(solution)/shard_map/ppermute | solution.py:216
  10.3 2.7 %collective-permute-start = (f32[5,72,256]{2,1,0:T(8,128)}, f32[5,72,256]{2,1,0:T(8,128)S(1)}, u32[]{:S(2)}, u32[]{:S(2)}) collective-permute-start(f32[5,72,256]{2,1,0:T(8,128)} %get-tuple-element.16), channel_id=1, source_target_pairs={{0,1},{1,2},{2,3},{3,4},{4,5},{5,6},{6,7},{7,8},{8,9},{9,10},{10,1... | collective-permute-start | bytes 1105928 | tf_op jit(solution)/shard_map/ppermute | solution.py:305
  13.0 1.3 %collective-permute-start.1 = (f32[5,72,256]{2,1,0:T(8,128)}, f32[5,72,256]{2,1,0:T(8,128)S(1)}, u32[]{:S(2)}, u32[]{:S(2)}) collective-permute-start(f32[5,72,256]{2,1,0:T(8,128)} %get-tuple-element.17), channel_id=1, source_target_pairs={{1,0},{2,1},{3,2},{4,3},{5,4},{6,5},{7,6},{8,7},{9,8},{10,9},{11,1... | collective-permute-start | bytes 1105928 | tf_op jit(solution)/shard_map/ppermute | solution.py:304
  14.3 0.9 copy-done.6
  15.2 5.3 %collective-permute-start.3 = (bf16[2,512,128]{2,1,0:T(8,128)(2,1)S(1)}, bf16[2,512,128]{2,1,0:T(8,128)(2,1)S(1)}, u32[]{:S(2)}, u32[]{:S(2)}) collective-permute-start(bf16[2,512,128]{2,1,0:T(8,128)(2,1)S(1)} %join_two.1.refs_0_), channel_id=1, source_target_pairs={{8,0},{9,1},{10,2},{11,3},{12,4},{13,5},{14,6},{15,7},{16,8},{17,9... | collective-permute-start | bytes 786440 | tf_op jit(solution)/shard_map/ppermute | solution.py:216
  20.5 2.8 %collective-permute-start.5 = (bf16[2,512,128]{2,1,0:T(8,128)(2,1)S(1)}, bf16[2,512,128]{2,1,0:T(8,128)(2,1)S(1)}, u32[]{:S(2)}, u32[]{:S(2)}) collective-permute-start(bf16[2,512,128]{2,1,0:T(8,128)(2,1)S(1)} %join_two.1.refs_0_), channel_id=1, source_target_pairs={{16,0},{17,1},{18,2},{19,3},{20,4},{21,5},{22,6},{23,7},{24,8},{25... | collective-permute-start | bytes 786440 | tf_op jit(solution)/shard_map/ppermute | solution.py:216
  23.8 0.8 collective-permute-done.1.below_ref
  24.6 7.0 %forecast4.1 = (f32[34,64,256]{2,1,0:T(8,128)S(1)}, bf16[8,608,128]{2,1,0:T(8,128)(2,1)}, f32[8,128]{1,0:T(8,128)S(1)}) custom-call(f32[64,32,256]{2,1,0:T(8,128)S(1)} %copy-done, f32[5,72,256]{2,1,0:T(8,128)S(1)} %collective-permute-done.above_ref, f32[5,72,256]{2,1,0:T(8,128)S(1)} %collective-permute-done.1.below_ref, f32[32,256]{1,0:T(8,128)S(1)} %copy-done.5), custom_call_target="tpu_custom_call" | custom-call | tf_op jit(solution)/shard_map/forecast4/pallas_call | solution.py:308
  31.7 1.4 %copy-done.1 = f32[34,64,256]{2,1,0:T(8,128)} copy-done((f32[34,64,256]{2,1,0:T(8,128)}, f32[34,64,256]{2,1,0:T(8,128)S(1)}, u32[]{:S(2)}) %copy-start.1) | copy-done | bytes 2228248
  33.1 1.2 %collective-permute-done.5.refs_3_ = bf16[2,512,128]{2,1,0:T(8,128)(2,1)S(1)} collective-permute-done((bf16[2,512,128]{2,1,0:T(8,128)(2,1)S(1)}, bf16[2,512,128]{2,1,0:T(8,128)(2,1)S(1)}, u32[]{:S(2)}, u32[]{:S(2)}) %collective-permute-start.5) | collective-permute-done | bytes 262176 | tf_op jit(solution)/shard_map/ppermute | solution.py:216
  34.3 1.2 %join_eight.1 = (bf16[8,512,128]{2,1,0:T(8,128)(2,1)S(1)}, bf16[4,512,128]{2,1,0:T(8,128)(2,1)}, bf16[4,512,128]{2,1,0:T(8,128)(2,1)}) custom-call(bf16[2,512,128]{2,1,0:T(8,128)(2,1)S(1)} %join_two.1.refs_0_, bf16[2,512,128]{2,1,0:T(8,128)(2,1)S(1)} %collective-permute-done.3.refs_1_, bf16[2,512,128]{2,1,0:T(8,128)(2,1)S(1)} %collective-permute-done.4.refs_2_, ...), custom_call_target="tpu_custom_call" | custom-call | tf_op jit(solution)/shard_map/join_eight/pallas_call | solution.py:245
  35.4 3.3 %collective-permute-start.6 = (bf16[8,512,128]{2,1,0:T(8,128)(2,1)S(1)}, bf16[8,512,128]{2,1,0:T(8,128)(2,1)}, u32[]{:S(2)}, u32[]{:S(2)}) collective-permute-start(bf16[8,512,128]{2,1,0:T(8,128)(2,1)S(1)} %get-tuple-element.22.rest_0_), channel_id=1, source_target_pairs={{1,0},{2,1},{3,2},{4,3},{5,4},{6,5},{7,6},{0,7},{9,8},{10,9},{11,1... | collective-permute-start | bytes 3145736 | tf_op jit(solution)/shard_map/ppermute | solution.py:216
  38.7 1.6 %collective-permute-start.11 = (bf16[4,512,128]{2,1,0:T(8,128)(2,1)}, bf16[4,512,128]{2,1,0:T(8,128)(2,1)S(1)}, u32[]{:S(2)}, u32[]{:S(2)}) collective-permute-start(bf16[4,512,128]{2,1,0:T(8,128)(2,1)} %get-tuple-element.25), channel_id=1, source_target_pairs={{2,0},{3,1},{4,2},{5,3},{6,4},{7,5},{0,6},{1,7},{10,8},{11,9},{12,... | collective-permute-start | bytes 1572872 | tf_op jit(solution)/shard_map/ppermute | solution.py:216
  40.3 1.3 %collective-permute-start.12 = (bf16[4,512,128]{2,1,0:T(8,128)(2,1)}, bf16[4,512,128]{2,1,0:T(8,128)(2,1)}, u32[]{:S(2)}, u32[]{:S(2)}) collective-permute-start(bf16[4,512,128]{2,1,0:T(8,128)(2,1)} %get-tuple-element.26), channel_id=1, source_target_pairs={{6,0},{7,1},{0,2},{1,3},{2,4},{3,5},{4,6},{5,7},{14,8},{15,9},{8,1... | collective-permute-start | bytes 1572872 | tf_op jit(solution)/shard_map/ppermute | solution.py:216
  41.7 8.7 %all-to-all-start = ((bf16[8,608,128]{2,1,0:T(8,128)(2,1)}), bf16[8,608,128]{2,1,0:T(8,128)(2,1)S(1)}, u32[]{:S(2)}, u32[]{:S(2)}) async-start(bf16[8,608,128]{2,1,0:T(8,128)(2,1)} %get-tuple-element.19), calls=%async_computation | async-start | bytes 2490368 | tf_op jit(solution)/shard_map/all_to_all | solution.py:330
  50.4 11.3 %collective-permute-done.6.rest_1_ = bf16[8,512,128]{2,1,0:T(8,128)(2,1)} collective-permute-done((bf16[8,512,128]{2,1,0:T(8,128)(2,1)S(1)}, bf16[8,512,128]{2,1,0:T(8,128)(2,1)}, u32[]{:S(2)}, u32[]{:S(2)}) %collective-permute-start.6) | collective-permute-done | bytes 1048608 | tf_op jit(solution)/shard_map/ppermute | solution.py:216
  61.7 3.5 %collective-permute-done.7.rest_2_ = bf16[8,512,128]{2,1,0:T(8,128)(2,1)} collective-permute-done((bf16[8,512,128]{2,1,0:T(8,128)(2,1)S(1)}, bf16[8,512,128]{2,1,0:T(8,128)(2,1)}, u32[]{:S(2)}, u32[]{:S(2)}) %collective-permute-start.7) | collective-permute-done | bytes 1048608 | tf_op jit(solution)/shard_map/ppermute | solution.py:216
  65.4 1.2 %copy.21 = f32[8,128,128]{1,2,0:T(8,128)S(1)} copy(f32[8,128,128]{2,1,0:T(8,128)} %param.11) | data formatting | bytes 1048576 | tf_op args[4]
  68.1 1.1 %collective-permute-start.14 = (bf16[4,512,128]{2,1,0:T(8,128)(2,1)}, bf16[4,512,128]{2,1,0:T(8,128)(2,1)}, u32[]{:S(2)}, u32[]{:S(2)}) collective-permute-start(bf16[4,512,128]{2,1,0:T(8,128)(2,1)} %collective-permute-done.12.rest_1_), channel_id=1, source_target_pairs={{32,0},{33,1},{34,2},{35,3},{36,4},{37,5},{38,6},{39,7},{40,8},{41... | collective-permute-start | bytes 1572872 | tf_op jit(solution)/shard_map/ppermute | solution.py:216
  69.3 3.4 %collect.1 = (bf16[2,24,512,128]{3,2,1,0:T(8,128)(2,1)S(1)}, bf16[9,512,128]{2,1,0:T(8,128)(2,1)S(1)}) custom-call(bf16[8,608,128]{2,1,0:T(8,128)(2,1)S(1)} %all-to-all-done.recv_ref, bf16[8,512,128]{2,1,0:T(8,128)(2,1)S(1)} %get-tuple-element.22.rest_0_, bf16[8,512,128]{2,1,0:T(8,128)(2,1)} %collective-permute-done.6.rest_1_, ...), custom_call_target="tpu_custom_call" | custom-call | tf_op jit(solution)/shard_map/collect/pallas_call | solution.py:341
  72.7 5.4 %analysis.1 = bf16[8,576,128]{2,1,0:T(8,128)(2,1)S(1)} custom-call(s32[9,4]{1,0:T(8,128)S(1)} %get-tuple-element.28.anom_at_ref, s32[9,4]{1,0:T(8,128)S(1)} %get-tuple-element.27.weight_at_ref, s32[9,4]{1,0:T(8,128)S(1)} %pad_add_fusion.1.tapers_ref, f32[8,128,128]{2,1,0:T(8,128)S(1)} %bitcast.3, bf16[9,512,128]{2,1,0:T(8,128)(2,1)S(1)} %get-tuple-element.23.centred_ref, ...), custom_call_target="tpu_custom_call" | custom-call | tf_op jit(solution)/shard_map/analysis/pallas_call | solution.py:352
  78.1 21.0 %all_to_all.10.inc_ref = bf16[8,576,128]{2,1,0:T(8,128)(2,1)S(1)} all-to-all(bf16[8,576,128]{2,1,0:T(8,128)(2,1)S(1)} %analysis.1), channel_id=1, replica_groups=mesh['mem'=8,'state'=32] {'mem'}, dimensions={0} | all-to-all | bytes 2359296 | tf_op jit(solution)/shard_map/all_to_all | solution.py:361
  99.1 2.9 %final_step.1 = f32[64,32,256]{2,1,0:T(8,128)} custom-call(f32[34,64,256]{2,1,0:T(8,128)S(1)} %copy-done.2, bf16[8,576,128]{2,1,0:T(8,128)(2,1)S(1)} %all_to_all.10.inc_ref, f32[32,256]{1,0:T(8,128)S(1)} %copy-done.5), custom_call_target="tpu_custom_call" | custom-call | tf_op jit(solution)/shard_map/final_step/pallas_call | solution.py:363
  (46 shorter events, 2.4 us)
Async XLA Ops:
  0.0 24.6 %copy-start = (f32[64,32,256]{2,1,0:T(8,128)S(1)}, f32[64,32,256]{2,1,0:T(8,128)}, u32[]{:S(2)}) copy-start(f32[64,32,256]{2,1,0:T(8,128)} %x_ref.1) | copy-start | bytes 6291460
  0.0 24.6 %copy-start.5 = (f32[32,256]{1,0:T(8,128)S(1)}, f32[32,256]{1,0:T(8,128)}, u32[]{:S(2)}) copy-start(f32[32,256]{1,0:T(8,128)} %coef_ref.5) | copy-start | bytes 98308
  2.6 11.7 %collective-permute-start.2 = (bf16[1,512,128]{2,1,0:T(8,128)(2,1)}, bf16[1,512,128]{2,1,0:T(8,128)(2,1)S(1)}, u32[]{:S(2)}, u32[]{:S(2)}) collective-permute-start(bf16[1,512,128]{2,1,0:T(8,128)(2,1)} %get-tuple-element.20.refs_0_), channel_id=1, source_target_pairs={{4,0},{5,1},{6,2},{7,3},{0,4},{1,5},{2,6},{3,7},{12,8},{13,9},{14,... | collective-permute-start | bytes 393224 | tf_op jit(solution)/shard_map/ppermute | solution.py:216
  10.3 13.5 %collective-permute-start = (f32[5,72,256]{2,1,0:T(8,128)}, f32[5,72,256]{2,1,0:T(8,128)S(1)}, u32[]{:S(2)}, u32[]{:S(2)}) collective-permute-start(f32[5,72,256]{2,1,0:T(8,128)} %get-tuple-element.16), channel_id=1, source_target_pairs={{0,1},{1,2},{2,3},{3,4},{4,5},{5,6},{6,7},{7,8},{8,9},{9,10},{10,1... | collective-permute-start | bytes 1105928 | tf_op jit(solution)/shard_map/ppermute | solution.py:305
  13.0 11.7 %collective-permute-start.1 = (f32[5,72,256]{2,1,0:T(8,128)}, f32[5,72,256]{2,1,0:T(8,128)S(1)}, u32[]{:S(2)}, u32[]{:S(2)}) collective-permute-start(f32[5,72,256]{2,1,0:T(8,128)} %get-tuple-element.17), channel_id=1, source_target_pairs={{1,0},{2,1},{3,2},{4,3},{5,4},{6,5},{7,6},{8,7},{9,8},{10,9},{11,1... | collective-permute-start | bytes 1105928 | tf_op jit(solution)/shard_map/ppermute | solution.py:304
  15.2 17.9 %collective-permute-start.3 = (bf16[2,512,128]{2,1,0:T(8,128)(2,1)S(1)}, bf16[2,512,128]{2,1,0:T(8,128)(2,1)S(1)}, u32[]{:S(2)}, u32[]{:S(2)}) collective-permute-start(bf16[2,512,128]{2,1,0:T(8,128)(2,1)S(1)} %join_two.1.refs_0_), channel_id=1, source_target_pairs={{8,0},{9,1},{10,2},{11,3},{12,4},{13,5},{14,6},{15,7},{16,8},{17,9... | collective-permute-start | bytes 786440 | tf_op jit(solution)/shard_map/ppermute | solution.py:216
  20.5 12.6 %collective-permute-start.4 = (bf16[2,512,128]{2,1,0:T(8,128)(2,1)S(1)}, bf16[2,512,128]{2,1,0:T(8,128)(2,1)S(1)}, u32[]{:S(2)}, u32[]{:S(2)}) collective-permute-start(bf16[2,512,128]{2,1,0:T(8,128)(2,1)S(1)} %join_two.1.refs_0_), channel_id=1, source_target_pairs={{24,0},{25,1},{26,2},{27,3},{28,4},{29,5},{30,6},{31,7},{0,8},{1,9... | collective-permute-start | bytes 786440 | tf_op jit(solution)/shard_map/ppermute | solution.py:216
  20.5 13.8 %collective-permute-start.5 = (bf16[2,512,128]{2,1,0:T(8,128)(2,1)S(1)}, bf16[2,512,128]{2,1,0:T(8,128)(2,1)S(1)}, u32[]{:S(2)}, u32[]{:S(2)}) collective-permute-start(bf16[2,512,128]{2,1,0:T(8,128)(2,1)S(1)} %join_two.1.refs_0_), channel_id=1, source_target_pairs={{16,0},{17,1},{18,2},{19,3},{20,4},{21,5},{22,6},{23,7},{24,8},{25... | collective-permute-start | bytes 786440 | tf_op jit(solution)/shard_map/ppermute | solution.py:216
  23.8 7.8 %copy-start.3 = (f32[5,72,256]{2,1,0:T(8,128)}, f32[5,72,256]{2,1,0:T(8,128)S(1)}, u32[]{:S(2)}) copy-start(f32[5,72,256]{2,1,0:T(8,128)S(1)} %collective-permute-done.above_ref) | copy-start | bytes 1105924
  24.6 7.0 %copy-start.4 = (f32[5,72,256]{2,1,0:T(8,128)}, f32[5,72,256]{2,1,0:T(8,128)S(1)}, u32[]{:S(2)}) copy-start(f32[5,72,256]{2,1,0:T(8,128)S(1)} %collective-permute-done.1.below_ref) | copy-start | bytes 1105924
  31.7 1.4 %copy-start.1 = (f32[34,64,256]{2,1,0:T(8,128)}, f32[34,64,256]{2,1,0:T(8,128)S(1)}, u32[]{:S(2)}) copy-start(f32[34,64,256]{2,1,0:T(8,128)S(1)} %get-tuple-element.18.prior_ref) | copy-start | bytes 6684676
  35.4 26.2 %collective-permute-start.6 = (bf16[8,512,128]{2,1,0:T(8,128)(2,1)S(1)}, bf16[8,512,128]{2,1,0:T(8,128)(2,1)}, u32[]{:S(2)}, u32[]{:S(2)}) collective-permute-start(bf16[8,512,128]{2,1,0:T(8,128)(2,1)S(1)} %get-tuple-element.22.rest_0_), channel_id=1, source_target_pairs={{1,0},{2,1},{3,2},{4,3},{5,4},{6,5},{7,6},{0,7},{9,8},{10,9},{11,1... | collective-permute-start | bytes 3145736 | tf_op jit(solution)/shard_map/ppermute | solution.py:216
  38.7 26.5 %collective-permute-start.7 = (bf16[8,512,128]{2,1,0:T(8,128)(2,1)S(1)}, bf16[8,512,128]{2,1,0:T(8,128)(2,1)}, u32[]{:S(2)}, u32[]{:S(2)}) collective-permute-start(bf16[8,512,128]{2,1,0:T(8,128)(2,1)S(1)} %get-tuple-element.22.rest_0_), channel_id=1, source_target_pairs={{7,0},{0,1},{1,2},{2,3},{3,4},{4,5},{5,6},{6,7},{15,8},{8,9},{9,10... | collective-permute-start | bytes 3145736 | tf_op jit(solution)/shard_map/ppermute | solution.py:216
  38.7 28.9 %collective-permute-start.11 = (bf16[4,512,128]{2,1,0:T(8,128)(2,1)}, bf16[4,512,128]{2,1,0:T(8,128)(2,1)S(1)}, u32[]{:S(2)}, u32[]{:S(2)}) collective-permute-start(bf16[4,512,128]{2,1,0:T(8,128)(2,1)} %get-tuple-element.25), channel_id=1, source_target_pairs={{2,0},{3,1},{4,2},{5,3},{6,4},{7,5},{0,6},{1,7},{10,8},{11,9},{12,... | collective-permute-start | bytes 1572872 | tf_op jit(solution)/shard_map/ppermute | solution.py:216
  40.3 27.8 %collective-permute-start.12 = (bf16[4,512,128]{2,1,0:T(8,128)(2,1)}, bf16[4,512,128]{2,1,0:T(8,128)(2,1)}, u32[]{:S(2)}, u32[]{:S(2)}) collective-permute-start(bf16[4,512,128]{2,1,0:T(8,128)(2,1)} %get-tuple-element.26), channel_id=1, source_target_pairs={{6,0},{7,1},{0,2},{1,3},{2,4},{3,5},{4,6},{5,7},{14,8},{15,9},{8,1... | collective-permute-start | bytes 1572872 | tf_op jit(solution)/shard_map/ppermute | solution.py:216
  41.7 23.5 %copy-start.7 = (s32[64,4]{0,1:T(4,128)S(1)}, s32[64,4]{0,1:T(4,128)}, u32[]{:S(2)}) copy-start(s32[64,4]{0,1:T(4,128)} %param.12) | copy-start | bytes 3076
  41.7 23.5 %copy-start.8 = (s32[64,4]{0,1:T(4,128)S(1)}, s32[64,4]{0,1:T(4,128)}, u32[]{:S(2)}) copy-start(s32[64,4]{0,1:T(4,128)} %param.13) | copy-start | bytes 3076
  41.7 27.6 %all-to-all-start = ((bf16[8,608,128]{2,1,0:T(8,128)(2,1)}), bf16[8,608,128]{2,1,0:T(8,128)(2,1)S(1)}, u32[]{:S(2)}, u32[]{:S(2)}) async-start(bf16[8,608,128]{2,1,0:T(8,128)(2,1)} %get-tuple-element.19), calls=%async_computation | async-start | bytes 2490368 | tf_op jit(solution)/shard_map/all_to_all | solution.py:330
  50.4 18.9 %collective-permute-start.8 = (bf16[8,512,128]{2,1,0:T(8,128)(2,1)S(1)}, bf16[8,512,128]{2,1,0:T(8,128)(2,1)}, u32[]{:S(2)}, u32[]{:S(2)}) collective-permute-start(bf16[8,512,128]{2,1,0:T(8,128)(2,1)S(1)} %get-tuple-element.22.rest_0_), channel_id=1, source_target_pairs={{32,0},{33,1},{34,2},{35,3},{36,4},{37,5},{38,6},{39,7},{40,8},{41... | collective-permute-start | bytes 3145736 | tf_op jit(solution)/shard_map/ppermute | solution.py:216
  61.7 7.6 %collective-permute-start.9 = (bf16[8,512,128]{2,1,0:T(8,128)(2,1)}, bf16[8,512,128]{2,1,0:T(8,128)(2,1)}, u32[]{:S(2)}, u32[]{:S(2)}) collective-permute-start(bf16[8,512,128]{2,1,0:T(8,128)(2,1)} %collective-permute-done.6.rest_1_), channel_id=1, source_target_pairs={{32,0},{33,1},{34,2},{35,3},{36,4},{37,5},{38,6},{39,7},{40,8},{41... | collective-permute-start | bytes 3145736 | tf_op jit(solution)/shard_map/ppermute | solution.py:216
  65.2 4.1 %collective-permute-start.10 = (bf16[8,512,128]{2,1,0:T(8,128)(2,1)}, bf16[8,512,128]{2,1,0:T(8,128)(2,1)}, u32[]{:S(2)}, u32[]{:S(2)}) collective-permute-start(bf16[8,512,128]{2,1,0:T(8,128)(2,1)} %collective-permute-done.7.rest_2_), channel_id=1, source_target_pairs={{32,0},{33,1},{34,2},{35,3},{36,4},{37,5},{38,6},{39,7},{40,8},{41... | collective-permute-start | bytes 3145736 | tf_op jit(solution)/shard_map/ppermute | solution.py:216
  67.6 5.1 %collective-permute-start.13 = (bf16[4,512,128]{2,1,0:T(8,128)(2,1)S(1)}, bf16[4,512,128]{2,1,0:T(8,128)(2,1)}, u32[]{:S(2)}, u32[]{:S(2)}) collective-permute-start(bf16[4,512,128]{2,1,0:T(8,128)(2,1)S(1)} %collective-permute-done.11.rest_0_), channel_id=1, source_target_pairs={{32,0},{33,1},{34,2},{35,3},{36,4},{37,5},{38,6},{39,7},{40,8},{41... | collective-permute-start | bytes 1572872 | tf_op jit(solution)/shard_map/ppermute | solution.py:216
  68.1 4.6 %collective-permute-start.14 = (bf16[4,512,128]{2,1,0:T(8,128)(2,1)}, bf16[4,512,128]{2,1,0:T(8,128)(2,1)}, u32[]{:S(2)}, u32[]{:S(2)}) collective-permute-start(bf16[4,512,128]{2,1,0:T(8,128)(2,1)} %collective-permute-done.12.rest_1_), channel_id=1, source_target_pairs={{32,0},{33,1},{34,2},{35,3},{36,4},{37,5},{38,6},{39,7},{40,8},{41... | collective-permute-start | bytes 1572872 | tf_op jit(solution)/shard_map/ppermute | solution.py:216
  78.1 21.0 %copy-start.2 = (f32[34,64,256]{2,1,0:T(8,128)S(1)}, f32[34,64,256]{2,1,0:T(8,128)}, u32[]{:S(2)}) copy-start(f32[34,64,256]{2,1,0:T(8,128)} %copy-done.1) | copy-start | bytes 6684676
  (1 other events, 0.9 us)

commit v7 on v6

--- a/solution.py
+++ b/solution.py
@@ -36,79 +36,142 @@
     rows = coef_ref.shape[0]
     tiles = block_ref.shape[1]
     lane = lax.broadcasted_iota(jnp.int32, (8, columns), 1)
-    for out_ref, x_ref, start, row0, tile0, far in (
-        (up_ref, first_ref, 0, 0, 0, HALO - 1),
-        (down_ref, last_ref, depth - HALO, rows - HALO, tiles - 2, 0),
+    for out_ref, x_ref, start, row0, tile0 in (
+        (up_ref, first_ref, 0, 0, 0),
+        (down_ref, last_ref, depth - HALO, rows - HALO, tiles - 2),
     ):
         for r in range(HALO):
-            out_ref[r, 0:members, :] = x_ref[:, start + r, :]
-            out_ref[r, members : members + 8, :] = jnp.broadcast_to(coef_ref[row0 + r : row0 + r + 1, :], (8, columns))
+            out_ref[r * members : (r + 1) * members, :] = x_ref[:, start + r, :]
         ids = jnp.zeros((8, columns), jnp.int32)
         for t in range(2):
             for k in range(SLOTS):
                 ids = jnp.where(lane == t * SLOTS + k, block_ref[k, tile0 + t], ids)
                 ids = jnp.where(lane == 8 + t * SLOTS + k, taper_ref[k, tile0 + t], ids)
-        out_ref[far, members : members + 8, :] = ids.astype(F32)
-
-
-def forecast_kernel(x_ref, above_ref, below_ref, coef_ref, prior_ref, out_ref, token_ref, a_ref, b_ref, c_ref, m_ref, pay_ref, sems):
+        out_ref[HALO * members :, :] = ids.astype(F32)
+        out_ref[HALO * members : HALO * members + HALO, :] = coef_ref[row0 : row0 + HALO, :]
+
+
+def stepped(mid, one_side, other_side, coef):
+    chunk, columns = mid.shape
+    beside = one_side + other_side + pltpu.roll(mid, 1, 1) + pltpu.roll(mid, columns - 1, 1)
+    delta = (beside - 4.0 * mid).reshape(chunk // 8, 8, columns)
+    return mid + (coef[None] * delta).reshape(chunk, columns)
+
+
+def split_tile(value, slot, members, pay_ref, mean_ref):
+    mean = jnp.sum(value, axis=0, keepdims=True) * (1.0 / members)
+    pay_ref[slot * members : (slot + 1) * members, :] = (value - mean).astype(BF16)
+    high = mean.astype(BF16).astype(F32)
+    middle = (mean - high).astype(BF16).astype(F32)
+    mean_ref[3 * slot : 3 * slot + 1, :] = high
+    mean_ref[3 * slot + 1 : 3 * slot + 2, :] = middle
+    mean_ref[3 * slot + 2 : 3 * slot + 3, :] = mean - high - middle
+
+
+def interior_kernel(x_ref, coef_ref, taper_ref, token_ref, prior_ref, out_ref, edge_ref, mean_ref, turned_ref, a_ref, b_ref, c_ref, pay_ref, sems):
     members, rows, columns = x_ref.shape
-    total = rows + 2 * HALO
-    group = pay_ref.shape[0]
+    group = out_ref.shape[0]
+    per = rows // group
+    for r in range(rows):
+        c_ref[r] = jnp.broadcast_to(coef_ref[r : r + 1, :], (8, columns))
+    chunk = 16
+
+    def advance(number, carry):
+        here = pl.ds(pl.multiple_of(number * chunk, chunk), chunk)
+        for r in range(rows):
+            a_ref[r, here, :] = x_ref[here, r, :]
+        src, dst = a_ref, b_ref
+        for step in range(1, FSTEPS + 1):
+            done = step - 1
+            for i, r in enumerate((done, done + 1, rows - 1 - done, rows - 2 - done)):
+                edge_ref[4 * done + i, here, :] = src[r, here, :]
+            for r in range(step, rows - step):
+                dst[r, here, :] = stepped(src[r, here, :], src[r - 1, here, :], src[r + 1, here, :], c_ref[r])
+            src, dst = dst, src
+        return carry
+
+    lax.fori_loop(0, members // chunk, advance, 0)
+    src = a_ref if FSTEPS % 2 == 0 else b_ref
+    inner = rows - 2 * FSTEPS
+    copies = [pltpu.make_async_copy(src.at[pl.ds(FSTEPS, inner)], prior_ref.at[pl.ds(FSTEPS + 1, inner)], sems.at[0])]
+    copies[0].start()
+    mean_ref[...] = jnp.zeros_like(mean_ref)
+    for j in range(1, group - 1):
+        for i in range(per):
+            for half in range(2):
+                value = src[j * per + i, :, half * TILE : (half + 1) * TILE]
+                split_tile(value, 2 * i + half, members, pay_ref.at[j], mean_ref.at[j])
+        copies.append(pltpu.make_async_copy(pay_ref.at[j], out_ref.at[j, pl.ds(0, 2 * per * members)], sems.at[j]))
+        copies[-1].start()
+    for i in range(taper_ref.shape[0]):
+        turned_ref[i] = taper_ref[i].T
+    for copy in copies:
+        copy.wait()
+
+
+def edge_kernel(above_ref, below_ref, coef_ref, edge_ref, mean_ref, prior_in, pay_in, prior_ref, out_ref, token_ref, a_ref, b_ref, c_ref, pay_ref, m_ref, last_ref, sems):
+    rows, columns = coef_ref.shape
+    members = last_ref.shape[2]
+    group, size, _ = out_ref.shape
     per = rows // group
     tiles = 2 * per + 1
-    for r in range(HALO):
-        c_ref[r] = above_ref[r, members : members + 8, :]
-        c_ref[HALO + rows + r] = below_ref[r, members : members + 8, :]
-    for r in range(rows):
-        c_ref[HALO + r] = jnp.broadcast_to(coef_ref[r : r + 1, :], (8, columns))
+    halos = (above_ref, below_ref)
+    for side in range(2):
+        for t in range(HALO + FSTEPS):
+            if t < HALO:
+                r = HALO * members + (t if side == 0 else HALO - 1 - t)
+                row = halos[side][r : r + 1, :]
+            else:
+                r = t - HALO if side == 0 else rows - 1 - (t - HALO)
+                row = coef_ref[r : r + 1, :]
+            c_ref[side, t] = jnp.broadcast_to(row, (8, columns))
     chunk = 16
 
     def advance(number, carry):
         here = pl.ds(pl.multiple_of(number * chunk, chunk), chunk)
-        for r in range(HALO):
-            a_ref[r, here, :] = above_ref[r, here, :]
-            a_ref[HALO + rows + r, here, :] = below_ref[r, here, :]
-        for r in range(rows):
-            a_ref[HALO + r, here, :] = x_ref[here, r, :]
-        src, dst = a_ref, b_ref
-        for step in range(1, FSTEPS + 1):
-            for r in range(step, total - step):
-                mid = src[r, here, :]
-                beside = src[r - 1, here, :] + src[r + 1, here, :] + pltpu.roll(mid, 1, 1) + pltpu.roll(mid, columns - 1, 1)
-                delta = (beside - 4.0 * mid).reshape(chunk // 8, 8, columns)
-                dst[r, here, :] = mid + (c_ref[r][None] * delta).reshape(chunk, columns)
-            src, dst = dst, src
+        for side in range(2):
+
+            def value(step, t, side=side):
+                if t > step + HALO - 1:
+                    return edge_ref[4 * step + 2 * side + t - step - HALO, here, :]
+                if step == 0:
+                    r = t if side == 0 else HALO - 1 - t
+                    return halos[side][pl.ds(pl.multiple_of(r * members + number * chunk, chunk), chunk), :]
+                return (a_ref, b_ref)[step % 2][side, t, here, :]
+
+            for step in range(1, FSTEPS + 1):
+                for t in range(step, step + HALO):
+                    new = stepped(value(step - 1, t), value(step - 1, t - 1), value(step - 1, t + 1), c_ref[side, t])
+                    if step < FSTEPS:
+                        (a_ref, b_ref)[step % 2][side, t, here, :] = new
+                    else:
+                        last_ref[side, t - FSTEPS if side == 0 else 2 * FSTEPS - t, here, :] = new
         return carry
 
     lax.fori_loop(0, members // chunk, advance, 0)
-    src = a_ref if FSTEPS % 2 == 0 else b_ref
-    copies = [pltpu.make_async_copy(src.at[pl.ds(HALO - 1, rows + 2)], prior_ref, sems.at[group])]
-    copies[0].start()
-    m_ref[...] = jnp.zeros_like(m_ref)
-
-    def tile(index, dest, slot, half):
-        value = src[index, :, half * TILE : (half + 1) * TILE]
-        mean = jnp.sum(value, axis=0, keepdims=True) * (1.0 / members)
-        pay_ref[dest, slot * members : (slot + 1) * members, :] = (value - mean).astype(BF16)
-        high = mean.astype(BF16).astype(F32)
-        middle = (mean - high).astype(BF16).astype(F32)
-        m_ref[dest, 3 * slot : 3 * slot + 1, :] = high
-        m_ref[dest, 3 * slot + 1 : 3 * slot + 2, :] = middle
-        m_ref[dest, 3 * slot + 2 : 3 * slot + 3, :] = mean - high - middle
-
+    copies = [
+        pltpu.make_async_copy(last_ref.at[0], prior_ref.at[pl.ds(0, HALO)], sems.at[0]),
+        pltpu.make_async_copy(last_ref.at[1], prior_ref.at[pl.ds(rows + 2 - HALO, HALO)], sems.at[1]),
+    ]
+    for copy in copies:
+        copy.start()
+    m_ref[...] = mean_ref[...]
+    extra = tiles - 1
     for j in range(group):
-        for i in range(per):
-            for half in range(2):
-                tile(HALO + j * per + i, j, 2 * i + half, half)
-        if j < 2:
-            tile(HALO - 1, j, tiles - 1, j)
-        elif j < 4:
-            tile(HALO + rows, j, tiles - 1, j - 2)
+        if j in (0, group - 1):
+            for i in range(per):
+                for half in range(2):
+                    row = last_ref[0, i + 1] if j == 0 else last_ref[1, i]
+                    split_tile(row[:, half * TILE : (half + 1) * TILE], 2 * i + half, members, pay_ref.at[j], m_ref.at[j])
+        if j < 4:
+            row = last_ref[0, 0] if j < 2 else last_ref[1, HALO - 1]
+            split_tile(row[:, (j % 2) * TILE : (j % 2 + 1) * TILE], extra, members, pay_ref.at[j], m_ref.at[j])
         else:
-            pay_ref[j, (tiles - 1) * members : tiles * members, :] = jnp.zeros((members, TILE), BF16)
+            pay_ref[j, extra * members : tiles * members, :] = jnp.zeros((members, TILE), BF16)
         pay_ref[j, tiles * members :, :] = m_ref[j].astype(BF16)
-        copies.append(pltpu.make_async_copy(pay_ref.at[j], out_ref.at[j], sems.at[j]))
+        first = 0 if j in (0, group - 1) else extra * members
+        part = pl.ds(first, size - first)
+        copies.append(pltpu.make_async_copy(pay_ref.at[j, part], out_ref.at[j, part], sems.at[2 + j]))
         copies[-1].start()
     for copy in copies:
         copy.wait()
@@ -227,36 +290,72 @@
 TOKEN = jax.ShapeDtypeStruct((8, TILE), F32)
 
 
-def join(operands, name, after=(), split=False):
-    count, blocks = len(operands), operands[0].shape[0]
+def join(operands, name, after):
+    count = len(operands)
+    flat = [v for pair in operands for v in (pair if isinstance(pair, tuple) else (pair,))]
 
     def kernel(*refs):
-        outs = refs[count + len(after) :]
+        outs = refs[len(flat) + len(after) :]
         core = lax.rem(lax.axis_index("mem"), 2)
-        for i in range(blocks):
-            for a in range(count):
-                outs[0][i * count + a] = refs[a][i]
-        if split:
-            for a in range(count):
-                outs[1][a] = refs[a][0]
-                outs[2][a] = refs[a][core]
-
-    shapes = [(count * blocks, *operands[0].shape[1:])] + [(count, *operands[0].shape[1:])] * (2 * split)
+        halves = [[], []]
+        at = 0
+        for pair in operands:
+            for i in range(2):
+                halves[i].append((refs[at + i], 0) if isinstance(pair, tuple) else (refs[at], i))
+            at += 2 if isinstance(pair, tuple) else 1
+        for i in range(2):
+            for a, (ref, block) in enumerate(halves[i]):
+                outs[0][i * count + a] = ref[block]
+                if i == 0:
+                    outs[1][a] = ref[block]
+
+            @pl.when(core == i)
+            def _(i=i):
+                for a, (ref, block) in enumerate(halves[i]):
+                    outs[2][a] = ref[block]
+
+    shapes = [(n, *flat[0].shape[1:]) for n in (2 * count, count, count)]
     return pl.pallas_call(
         kernel,
         out_shape=[jax.ShapeDtypeStruct(shape, BF16) for shape in shapes],
-        in_specs=[VMEM] * count + [HBM] * len(after),
+        in_specs=[VMEM] * len(flat) + [HBM] * len(after),
         out_specs=[VMEM] * len(shapes),
         compiler_params=pltpu.CompilerParams(vmem_limit_bytes=6 << 20),
         name=name,
-    )(*operands, *after)
-
-
-def gather_start(own, mesh, after):
+    )(*flat, *after)
+
+
+def join_two_kernel(own_ref, far_ref, held_ref, other_ref, token_ref):
+    core = lax.rem(lax.axis_index("mem"), 2)
+    held_ref[0] = own_ref[0]
+    held_ref[1] = far_ref[0]
+
+    @pl.when(core == 0)
+    def _():
+        other_ref[0] = far_ref[0]
+
+    @pl.when(core == 1)
+    def _():
+        other_ref[0] = own_ref[0]
+
+
+def gather_first(own, mesh):
     far = fetch(own, mesh, lambda x, c, y, z: (x, c, y, z + 4))
-    (held,) = join([own, far], "join_two")
-    p, m, q = (fetch(held, mesh, ring(True, step)) for step in (1, -1, 2))
-    return join([held, p, m, q], "join_eight", after, split=True)
+    return pl.pallas_call(
+        join_two_kernel,
+        out_shape=[jax.ShapeDtypeStruct((n, *own.shape[1:]), BF16) for n in (2, 1)] + [TOKEN],
+        in_specs=[VMEM] * 2,
+        out_specs=[VMEM] * 2 + [HBM],
+        compiler_params=pltpu.CompilerParams(vmem_limit_bytes=6 << 20),
+        name="join_two",
+    )(own, far)
+
+
+def gather_second(own, held, alternate, mesh, after):
+    p, m = (fetch(held, mesh, ring(True, step)) for step in (1, -1))
+    near = fetch(own, mesh, ring(True, 2))
+    far = fetch(alternate, mesh, ring(True, -2))
+    return join([held, p, m, (near, far)], "join_eight", after)
 
 
 def gather_rest(held, first, second, mesh):
@@ -284,10 +383,11 @@
     size = tiles * members + 32
 
     j, at = lax.axis_index("mem"), lax.axis_index("state")
+    chips = (group // 2, states // 8, 8)
     up, down, packed = pl.pallas_call(
         pack_kernel,
         grid=(1,),
-        out_shape=[jax.ShapeDtypeStruct((HALO, members + 8, columns), F32)] * 2
+        out_shape=[jax.ShapeDtypeStruct((HALO * members + 8, columns), F32)] * 2
         + [jax.ShapeDtypeStruct((1, obs_anom.shape[2], TILE), BF16)],
         in_specs=[
             pl.BlockSpec((members, 8, columns), lambda i: (0, 0, 0)),
@@ -304,32 +404,52 @@
     below = lax.ppermute(up, "state", [(i + 1, i) for i in range(states - 1)])
     above = lax.ppermute(down, "state", [(i, i + 1) for i in range(states - 1)])
 
-    chips = (group // 2, states // 8, 8)
-    prior, payload, forecast_done = pl.pallas_call(
-        forecast_kernel,
+    held, alternate, started = gather_first(packed, chips)
+    row = (members, columns)
+    prior, payload, edges, means, turned = pl.pallas_call(
+        interior_kernel,
         out_shape=[
-            jax.ShapeDtypeStruct((rows + 2, members, columns), F32),
+            jax.ShapeDtypeStruct((rows + 2, *row), F32),
             jax.ShapeDtypeStruct((group, size, TILE), BF16),
-            TOKEN,
+            jax.ShapeDtypeStruct((4 * FSTEPS, *row), F32),
+            jax.ShapeDtypeStruct((group, 32, TILE), F32),
+            jax.ShapeDtypeStruct(taper_table.shape, F32),
         ],
-        in_specs=[VMEM] * 4,
-        out_specs=[HBM] * 3,
+        in_specs=[VMEM] * 3 + [HBM],
+        out_specs=[HBM] * 2 + [VMEM] * 3,
         scratch_shapes=[
-            pltpu.VMEM((rows + 2 * HALO, members, columns), F32),
-            pltpu.VMEM((rows + 2 * HALO, members, columns), F32),
-            pltpu.VMEM((rows + 2 * HALO, 8, columns), F32),
-            pltpu.VMEM((group, 32, TILE), F32),
-            pltpu.VMEM((group, size, TILE), BF16),
-            pltpu.SemaphoreType.DMA((group + 1,)),
+            pltpu.VMEM((rows, *row), F32),
+            pltpu.VMEM((rows, *row), F32),
+            pltpu.VMEM((rows, 8, columns), F32),
+            pltpu.VMEM((group, 2 * per * members, TILE), BF16),
+            pltpu.SemaphoreType.DMA((group,)),
         ],
         compiler_params=pltpu.CompilerParams(vmem_limit_bytes=14 << 20),
-        name="forecast4",
-    )(ensemble, above, below, spreading_coefficient)
-    held, first, second = gather_start(packed, chips, [forecast_done])
+        name="forecast_interior",
+    )(ensemble, spreading_coefficient, taper_table, started)
+    prior, payload, forecast_done = pl.pallas_call(
+        edge_kernel,
+        out_shape=[prior, payload, TOKEN],
+        in_specs=[VMEM] * 5 + [HBM] * 2,
+        out_specs=[HBM] * 3,
+        input_output_aliases={5: 0, 6: 1},
+        scratch_shapes=[
+            pltpu.VMEM((2, HALO + FSTEPS, *row), F32),
+            pltpu.VMEM((2, HALO + FSTEPS, *row), F32),
+            pltpu.VMEM((2, HALO + FSTEPS, 8, columns), F32),
+            pltpu.VMEM((group, size, TILE), BF16),
+            pltpu.VMEM((group, 32, TILE), F32),
+            pltpu.VMEM((2, HALO, *row), F32),
+            pltpu.SemaphoreType.DMA((group + 2,)),
+        ],
+        compiler_params=pltpu.CompilerParams(vmem_limit_bytes=14 << 20),
+        name="forecast_edges",
+    )(above, below, spreading_coefficient, edges, means, prior, payload)
+    held, first, second = gather_second(packed, held, alternate, chips, [forecast_done])
     own, swapped = gather_rest(held, first, second, chips)
     gathered = lax.all_to_all(payload, "mem", split_axis=0, concat_axis=0, tiled=True)
 
-    edge = jnp.where(j < 2, above[0, members, :16], below[HALO - 1, members, :16])
+    edge = jnp.where(j < 2, above[-1, :16], below[-1, :16])
     edge = jnp.where(j % 2 == 0, edge.reshape(-1, 4)[:3:2], edge.reshape(-1, 4)[1:4:2]).astype(jnp.int32)
     mine = 2 * per * j
     blocks = jnp.concatenate([lax.dynamic_slice_in_dim(obs_block, mine, 2 * per, 0), edge[0:1]], axis=0)
@@ -357,7 +477,7 @@
         scratch_shapes=[pltpu.VMEM((2, sum(v.shape[0] for v in own[-late:]), *packed.shape[1:]), BF16)],
         compiler_params=pltpu.CompilerParams(vmem_limit_bytes=18 << 20),
         name="analysis",
-    )(anom_at, weight_at, tapers, jnp.swapaxes(taper_table, 1, 2), centred, held_early, *own[-late:], *swapped[-late:])
+    )(anom_at, weight_at, tapers, turned, centred, held_early, *own[-late:], *swapped[-late:])
     returned = lax.all_to_all(increments, "mem", split_axis=0, concat_axis=0, tiled=True)
 
     return pl.pallas_call(

time: 103 us -> 107 us (1.039)
  waiting for transfers between devices: 17.4 us -> 24.9 us
  starting transfers between devices: 36.3 us -> 32.4 us
  Pallas kernels: 22.5 us -> 25.8 us
  local copies, waits for them, and re-layouts: 3.95 us -> 1.82 us
    ppermute x13 -> x14, waiting for transfers between devices: 16 us -> 24.9 us  [fetch(): return lax.ppermute(value, AXES, pairs)]
    ppermute x13 -> x14, starting transfers between devices: 23.7 us -> 19 us  [fetch(): return lax.ppermute(value, AXES, pairs)]
    pallas_call x1 -> x3, Pallas kernels: 7.01 us -> 10.4 us  [the longest x1 5.32 us: body(): pl.pallas_call(interior_kernel, out_shape=[jax.ShapeDtypeStruct((rows + 2...]
    unnamed x21 -> x24, local copies, waits for them, and re-layouts: 3.73 us -> 1.6 us
    ppermute x1, starting transfers between devices: 2.65 us -> 4.38 us  [body(): above = lax.ppermute(down, 'state', [(i, i + 1) for i in range(states - 1)])]
  transfers between devices with their start and end apart: 16 -> 17, of which waited for: 5 -> 3; matrix products, arithmetic and copies ran while one was open for 2% -> 1% of each run, Pallas kernels for 10% -> 13%
where the time goes in v7:
time: 107 us
  starting transfers between devices  32.4 us (30%)
  Pallas kernels  25.8 us (24%)
  waiting for transfers between devices  24.9 us (23%)
  blocking collectives  21 us (20%)
  local copies, waits for them, and re-layouts  1.82 us (2%)
    ppermute x14, waiting for transfers between devices, fetch(): return lax.ppermute(value, AXES, pairs)  24.9 us
    all_to_all x1, blocking collectives, body(): lax.all_to_all(increments, 'mem', split_axis=0, concat_axis=0, tiled=True)  21 us
    ppermute x14, starting transfers between devices, fetch(): return lax.ppermute(value, AXES, pairs)  19 us
    all_to_all x1, starting transfers between devices, body(): lax.all_to_all(payload, 'mem', split_axis=0, concat_axis=0, tiled=True)  7.75 us
    pallas_call x1, Pallas kernels, body(): pl.pallas_call(analysis_kernel, out_shape=jax.ShapeDtypeStruct((group, ti...  5.58 us
    pallas_call x1, Pallas kernels, body(): pl.pallas_call(interior_kernel, out_shape=[jax.ShapeDtypeStruct((rows + 2...  5.32 us
    ppermute x1, starting transfers between devices, body(): above = lax.ppermute(down, 'state', [(i, i + 1) for i in range(states - 1)])  4.38 us
    pallas_call x1, Pallas kernels, body(): pl.pallas_call(edge_kernel, out_shape=[prior, payload, TOKEN], in_specs=[...  4.1 us
  transfers between devices with their start and end apart: 17, of which 3 were waited for; matrix products, arithmetic and copies ran while one was open for 1% of the time, Pallas kernels for 13%

profile of v7, /device:TPU:1, one launch (start us, length us, event | category | flops | bytes accessed | tf_op | source)
XLA Modules:
  0.0 106.9 jit_solution(15785339961599163219)
XLA Ops:
  0.0 2.5 %pack.1 = (f32[328,256]{1,0:T(8,128)}, f32[328,256]{1,0:T(8,128)}, bf16[1,512,128]{2,1,0:T(8,128)(2,1)}) custom-call(f32[64,32,256]{2,1,0:T(8,128)} %x_ref.1, f32[64,32,256]{2,1,0:T(8,128)} %x_ref.1, f32[32,256]{1,0:T(8,128)} %coef_ref.7, s32[4,64]{1,0:T(4,128)} %bitcast.2, s32[4,64]{1,0:T(4,128)} %bitcast.3, bf16[1,128,512]{2,1,0:T(8,128)(2,1)} %anom_ref.1, ...), custom_call_target="tpu_custom_call" | custom-call | tf_op jit(solution)/shard_map/pack/pallas_call | solution.py:387
  2.6 4.4 %collective-permute-start = (f32[328,256]{1,0:T(8,128)}, f32[328,256]{1,0:T(8,128)S(1)}, u32[]{:S(2)}, u32[]{:S(2)}) collective-permute-start(f32[328,256]{1,0:T(8,128)} %get-tuple-element.24), channel_id=1, source_target_pairs={{0,1},{1,2},{2,3},{3,4},{4,5},{5,6},{6,7},{7,8},{8,9},{9,10},{10,1... | collective-permute-start | bytes 1007624 | tf_op jit(solution)/shard_map/ppermute | solution.py:405
  6.9 6.1 %collective-permute-start.2 = (bf16[1,512,128]{2,1,0:T(8,128)(2,1)}, bf16[1,512,128]{2,1,0:T(8,128)(2,1)S(1)}, u32[]{:S(2)}, u32[]{:S(2)}) collective-permute-start(bf16[1,512,128]{2,1,0:T(8,128)(2,1)} %get-tuple-element.26.own_ref), channel_id=1, source_target_pairs={{4,0},{5,1},{6,2},{7,3},{0,4},{1,5},{2,6},{3,7},{12,8},{13,9},{14,... | collective-permute-start | bytes 393224 | tf_op jit(solution)/shard_map/ppermute | solution.py:279
  13.0 1.3 %collective-permute-start.1 = (f32[328,256]{1,0:T(8,128)}, f32[328,256]{1,0:T(8,128)S(1)}, u32[]{:S(2)}, u32[]{:S(2)}) collective-permute-start(f32[328,256]{1,0:T(8,128)} %get-tuple-element.25), channel_id=1, source_target_pairs={{1,0},{2,1},{3,2},{4,3},{5,4},{6,5},{7,6},{8,7},{9,8},{10,9},{11,1... | collective-permute-start | bytes 1007624 | tf_op jit(solution)/shard_map/ppermute | solution.py:404
  14.3 9.1 %collective-permute-done.2.far_ref = bf16[1,512,128]{2,1,0:T(8,128)(2,1)S(1)} collective-permute-done((bf16[1,512,128]{2,1,0:T(8,128)(2,1)}, bf16[1,512,128]{2,1,0:T(8,128)(2,1)S(1)}, u32[]{:S(2)}, u32[]{:S(2)}) %collective-permute-start.2) | collective-permute-done | bytes 131104 | tf_op jit(solution)/shard_map/ppermute | solution.py:279
  23.4 0.9 join_two.1
  24.5 1.5 %collective-permute-start.4 = (bf16[2,512,128]{2,1,0:T(8,128)(2,1)S(1)}, bf16[2,512,128]{2,1,0:T(8,128)(2,1)S(1)}, u32[]{:S(2)}, u32[]{:S(2)}) collective-permute-start(bf16[2,512,128]{2,1,0:T(8,128)(2,1)S(1)} %get-tuple-element.35.refs_0_), channel_id=1, source_target_pairs={{24,0},{25,1},{26,2},{27,3},{28,4},{29,5},{30,6},{31,7},{0,8},{1,9... | collective-permute-start | bytes 786440 | tf_op jit(solution)/shard_map/ppermute | solution.py:279
  25.9 2.9 %collective-permute-start.5 = (bf16[1,512,128]{2,1,0:T(8,128)(2,1)}, bf16[1,512,128]{2,1,0:T(8,128)(2,1)S(1)}, u32[]{:S(2)}, u32[]{:S(2)}) collective-permute-start(bf16[1,512,128]{2,1,0:T(8,128)(2,1)} %get-tuple-element.26.own_ref), channel_id=1, source_target_pairs={{16,0},{17,1},{18,2},{19,3},{20,4},{21,5},{22,6},{23,7},{24,8},{25... | collective-permute-start | bytes 393224 | tf_op jit(solution)/shard_map/ppermute | solution.py:279
  28.9 0.8 collective-permute-start.6
  29.6 5.3 %forecast_interior.1 = (f32[34,64,256]{2,1,0:T(8,128)S(1)}, bf16[8,608,128]{2,1,0:T(8,128)(2,1)}, f32[16,64,256]{2,1,0:T(8,128)S(1)}, f32[8,32,128]{2,1,0:T(8,128)S(1)}, f32[8,128,128]{2,1,0:T(8,128)S(1)}) custom-call(f32[64,32,256]{2,1,0:T(8,128)S(1)} %copy-done, f32[32,256]{1,0:T(8,128)S(1)} %copy-done.3, f32[8,128,128]{2,1,0:T(8,128)S(1)} %copy-done.6, ...), custom_call_target="tpu_custom_call" | custom-call | tf_op jit(solution)/shard_map/forecast_interior/pallas_call | solution.py:409
  35.0 4.1 %forecast_edges.1 = (f32[34,64,256]{2,1,0:T(8,128)S(1)}, bf16[8,608,128]{2,1,0:T(8,128)(2,1)}, f32[8,128]{1,0:T(8,128)S(1)}) custom-call(f32[328,256]{1,0:T(8,128)S(1)} %collective-permute-done.above_ref, f32[328,256]{1,0:T(8,128)S(1)} %collective-permute-done.1.below_ref, f32[32,256]{1,0:T(8,128)S(1)} %copy-done.3, ...), custom_call_target="tpu_custom_call", output_to_operand_aliasing={{0}: (5, {}), {1}: (6, {})} | custom-call | tf_op jit(solution)/shard_map/forecast_edges/pallas_call | solution.py:430
  39.1 1.4 %copy-done.1 = f32[34,64,256]{2,1,0:T(8,128)} copy-done((f32[34,64,256]{2,1,0:T(8,128)}, f32[34,64,256]{2,1,0:T(8,128)S(1)}, u32[]{:S(2)}) %copy-start.1) | copy-done | bytes 2228248
  40.5 1.2 %join_eight.1 = (bf16[8,512,128]{2,1,0:T(8,128)(2,1)S(1)}, bf16[4,512,128]{2,1,0:T(8,128)(2,1)}, bf16[4,512,128]{2,1,0:T(8,128)(2,1)}) custom-call(bf16[2,512,128]{2,1,0:T(8,128)(2,1)S(1)} %get-tuple-element.35.refs_0_, bf16[2,512,128]{2,1,0:T(8,128)(2,1)S(1)} %collective-permute-done.3.refs_1_, bf16[2,512,128]{2,1,0:T(8,128)(2,1)S(1)} %collective-permute-done.4.refs_2_, ...), custom_call_target="tpu_custom_call" | custom-call | tf_op jit(solution)/shard_map/join_eight/pallas_call | solution.py:318
  41.8 2.7 %collective-permute-start.7 = (bf16[8,512,128]{2,1,0:T(8,128)(2,1)S(1)}, bf16[8,512,128]{2,1,0:T(8,128)(2,1)S(1)}, u32[]{:S(2)}, u32[]{:S(2)}) collective-permute-start(bf16[8,512,128]{2,1,0:T(8,128)(2,1)S(1)} %get-tuple-element.38.rest_0_), channel_id=1, source_target_pairs={{1,0},{2,1},{3,2},{4,3},{5,4},{6,5},{7,6},{0,7},{9,8},{10,9},{11,1... | collective-permute-start | bytes 3145736 | tf_op jit(solution)/shard_map/ppermute | solution.py:279
  44.5 1.6 %collective-permute-start.12 = (bf16[4,512,128]{2,1,0:T(8,128)(2,1)}, bf16[4,512,128]{2,1,0:T(8,128)(2,1)}, u32[]{:S(2)}, u32[]{:S(2)}) collective-permute-start(bf16[4,512,128]{2,1,0:T(8,128)(2,1)} %get-tuple-element.41), channel_id=1, source_target_pairs={{2,0},{3,1},{4,2},{5,3},{6,4},{7,5},{0,6},{1,7},{10,8},{11,9},{12,... | collective-permute-start | bytes 1572872 | tf_op jit(solution)/shard_map/ppermute | solution.py:279
  46.2 1.3 %collective-permute-start.13 = (bf16[4,512,128]{2,1,0:T(8,128)(2,1)}, bf16[4,512,128]{2,1,0:T(8,128)(2,1)}, u32[]{:S(2)}, u32[]{:S(2)}) collective-permute-start(bf16[4,512,128]{2,1,0:T(8,128)(2,1)} %get-tuple-element.42), channel_id=1, source_target_pairs={{6,0},{7,1},{0,2},{1,3},{2,4},{3,5},{4,6},{5,7},{14,8},{15,9},{8,1... | collective-permute-start | bytes 1572872 | tf_op jit(solution)/shard_map/ppermute | solution.py:279
  47.5 7.8 %all-to-all-start = ((bf16[8,608,128]{2,1,0:T(8,128)(2,1)}), bf16[8,608,128]{2,1,0:T(8,128)(2,1)S(1)}, u32[]{:S(2)}, u32[]{:S(2)}) async-start(bf16[8,608,128]{2,1,0:T(8,128)(2,1)} %get-tuple-element.34), calls=%async_computation | async-start | bytes 2490368 | tf_op jit(solution)/shard_map/all_to_all | solution.py:450
  55.3 12.2 %collective-permute-done.7.rest_1_ = bf16[8,512,128]{2,1,0:T(8,128)(2,1)S(1)} collective-permute-done((bf16[8,512,128]{2,1,0:T(8,128)(2,1)S(1)}, bf16[8,512,128]{2,1,0:T(8,128)(2,1)S(1)}, u32[]{:S(2)}, u32[]{:S(2)}) %collective-permute-start.7) | collective-permute-done | bytes 1048608 | tf_op jit(solution)/shard_map/ppermute | solution.py:279
  67.5 3.5 %collective-permute-done.8.rest_2_ = bf16[8,512,128]{2,1,0:T(8,128)(2,1)} collective-permute-done((bf16[8,512,128]{2,1,0:T(8,128)(2,1)S(1)}, bf16[8,512,128]{2,1,0:T(8,128)(2,1)}, u32[]{:S(2)}, u32[]{:S(2)}) %collective-permute-start.8) | collective-permute-done | bytes 1048608 | tf_op jit(solution)/shard_map/ppermute | solution.py:279
  72.7 1.4 %collective-permute-start.15 = (bf16[4,512,128]{2,1,0:T(8,128)(2,1)}, bf16[4,512,128]{2,1,0:T(8,128)(2,1)}, u32[]{:S(2)}, u32[]{:S(2)}) collective-permute-start(bf16[4,512,128]{2,1,0:T(8,128)(2,1)} %collective-permute-done.13.rest_1_), channel_id=1, source_target_pairs={{32,0},{33,1},{34,2},{35,3},{36,4},{37,5},{38,6},{39,7},{40,8},{41... | collective-permute-start | bytes 1572872 | tf_op jit(solution)/shard_map/ppermute | solution.py:279
  74.2 3.1 %collect.1 = (bf16[2,24,512,128]{3,2,1,0:T(8,128)(2,1)S(1)}, bf16[9,512,128]{2,1,0:T(8,128)(2,1)S(1)}) custom-call(bf16[8,608,128]{2,1,0:T(8,128)(2,1)S(1)} %all-to-all-done.recv_ref, bf16[8,512,128]{2,1,0:T(8,128)(2,1)S(1)} %get-tuple-element.38.rest_0_, bf16[8,512,128]{2,1,0:T(8,128)(2,1)S(1)} %collective-permute-done.7.rest_1_, ...), custom_call_target="tpu_custom_call" | custom-call | tf_op jit(solution)/shard_map/collect/pallas_call | solution.py:461
  77.4 5.6 %analysis.1 = bf16[8,576,128]{2,1,0:T(8,128)(2,1)S(1)} custom-call(s32[9,4]{1,0:T(8,128)S(1)} %get-tuple-element.44.anom_at_ref, s32[9,4]{1,0:T(8,128)S(1)} %get-tuple-element.43.weight_at_ref, s32[9,4]{1,0:T(8,128)S(1)} %pad_add_fusion.1.tapers_ref, f32[8,128,128]{2,1,0:T(8,128)S(1)} %copy-done.5, bf16[9,512,128]{2,1,0:T(8,128)(2,1)S(1)} %get-tuple-element.39.centred_ref, ...), custom_call_target="tpu_custom_call" | custom-call | tf_op jit(solution)/shard_map/analysis/pallas_call | solution.py:472
  83.0 21.0 %all_to_all.10.inc_ref = bf16[8,576,128]{2,1,0:T(8,128)(2,1)S(1)} all-to-all(bf16[8,576,128]{2,1,0:T(8,128)(2,1)S(1)} %analysis.1), channel_id=1, replica_groups=mesh['mem'=8,'state'=32] {'mem'}, dimensions={0} | all-to-all | bytes 2359296 | tf_op jit(solution)/shard_map/all_to_all | solution.py:481
  103.9 2.9 %final_step.1 = f32[64,32,256]{2,1,0:T(8,128)} custom-call(f32[34,64,256]{2,1,0:T(8,128)S(1)} %copy-done.2, bf16[8,576,128]{2,1,0:T(8,128)(2,1)S(1)} %all_to_all.10.inc_ref, f32[32,256]{1,0:T(8,128)S(1)} %copy-done.3), custom_call_target="tpu_custom_call" | custom-call | tf_op jit(solution)/shard_map/final_step/pallas_call | solution.py:483
  (52 shorter events, 1.9 us)
Async XLA Ops:
  0.0 29.6 %copy-start = (f32[64,32,256]{2,1,0:T(8,128)S(1)}, f32[64,32,256]{2,1,0:T(8,128)}, u32[]{:S(2)}) copy-start(f32[64,32,256]{2,1,0:T(8,128)} %x_ref.1) | copy-start | bytes 6291460
  0.0 29.6 %copy-start.3 = (f32[32,256]{1,0:T(8,128)S(1)}, f32[32,256]{1,0:T(8,128)}, u32[]{:S(2)}) copy-start(f32[32,256]{1,0:T(8,128)} %coef_ref.7) | copy-start | bytes 98308
  0.0 29.6 %copy-start.6 = (f32[8,128,128]{2,1,0:T(8,128)S(1)}, f32[8,128,128]{2,1,0:T(8,128)}, u32[]{:S(2)}) copy-start(f32[8,128,128]{2,1,0:T(8,128)} %taper_ref.1) | copy-start | bytes 1572868
  2.6 26.3 %collective-permute-start = (f32[328,256]{1,0:T(8,128)}, f32[328,256]{1,0:T(8,128)S(1)}, u32[]{:S(2)}, u32[]{:S(2)}) collective-permute-start(f32[328,256]{1,0:T(8,128)} %get-tuple-element.24), channel_id=1, source_target_pairs={{0,1},{1,2},{2,3},{3,4},{4,5},{5,6},{6,7},{7,8},{8,9},{9,10},{10,1... | collective-permute-start | bytes 1007624 | tf_op jit(solution)/shard_map/ppermute | solution.py:405
  6.9 16.5 %collective-permute-start.2 = (bf16[1,512,128]{2,1,0:T(8,128)(2,1)}, bf16[1,512,128]{2,1,0:T(8,128)(2,1)S(1)}, u32[]{:S(2)}, u32[]{:S(2)}) collective-permute-start(bf16[1,512,128]{2,1,0:T(8,128)(2,1)} %get-tuple-element.26.own_ref), channel_id=1, source_target_pairs={{4,0},{5,1},{6,2},{7,3},{0,4},{1,5},{2,6},{3,7},{12,8},{13,9},{14,... | collective-permute-start | bytes 393224 | tf_op jit(solution)/shard_map/ppermute | solution.py:279
  13.0 21.9 %collective-permute-start.1 = (f32[328,256]{1,0:T(8,128)}, f32[328,256]{1,0:T(8,128)S(1)}, u32[]{:S(2)}, u32[]{:S(2)}) collective-permute-start(f32[328,256]{1,0:T(8,128)} %get-tuple-element.25), channel_id=1, source_target_pairs={{1,0},{2,1},{3,2},{4,3},{5,4},{6,5},{7,6},{8,7},{9,8},{10,9},{11,1... | collective-permute-start | bytes 1007624 | tf_op jit(solution)/shard_map/ppermute | solution.py:404
  24.4 16.2 %collective-permute-start.3 = (bf16[2,512,128]{2,1,0:T(8,128)(2,1)S(1)}, bf16[2,512,128]{2,1,0:T(8,128)(2,1)S(1)}, u32[]{:S(2)}, u32[]{:S(2)}) collective-permute-start(bf16[2,512,128]{2,1,0:T(8,128)(2,1)S(1)} %get-tuple-element.35.refs_0_), channel_id=1, source_target_pairs={{8,0},{9,1},{10,2},{11,3},{12,4},{13,5},{14,6},{15,7},{16,8},{17,9... | collective-permute-start | bytes 786440 | tf_op jit(solution)/shard_map/ppermute | solution.py:279
  24.5 16.1 %collective-permute-start.4 = (bf16[2,512,128]{2,1,0:T(8,128)(2,1)S(1)}, bf16[2,512,128]{2,1,0:T(8,128)(2,1)S(1)}, u32[]{:S(2)}, u32[]{:S(2)}) collective-permute-start(bf16[2,512,128]{2,1,0:T(8,128)(2,1)S(1)} %get-tuple-element.35.refs_0_), channel_id=1, source_target_pairs={{24,0},{25,1},{26,2},{27,3},{28,4},{29,5},{30,6},{31,7},{0,8},{1,9... | collective-permute-start | bytes 786440 | tf_op jit(solution)/shard_map/ppermute | solution.py:279
  25.9 14.6 %collective-permute-start.5 = (bf16[1,512,128]{2,1,0:T(8,128)(2,1)}, bf16[1,512,128]{2,1,0:T(8,128)(2,1)S(1)}, u32[]{:S(2)}, u32[]{:S(2)}) collective-permute-start(bf16[1,512,128]{2,1,0:T(8,128)(2,1)} %get-tuple-element.26.own_ref), channel_id=1, source_target_pairs={{16,0},{17,1},{18,2},{19,3},{20,4},{21,5},{22,6},{23,7},{24,8},{25... | collective-permute-start | bytes 393224 | tf_op jit(solution)/shard_map/ppermute | solution.py:279
  28.9 11.7 %collective-permute-start.6 = (bf16[1,512,128]{2,1,0:T(8,128)(2,1)S(1)}, bf16[1,512,128]{2,1,0:T(8,128)(2,1)S(1)}, u32[]{:S(2)}, u32[]{:S(2)}) collective-permute-start(bf16[1,512,128]{2,1,0:T(8,128)(2,1)S(1)} %get-tuple-element.36), channel_id=1, source_target_pairs={{16,0},{17,1},{18,2},{19,3},{20,4},{21,5},{22,6},{23,7},{24,8},{25... | collective-permute-start | bytes 393224 | tf_op jit(solution)/shard_map/ppermute | solution.py:279
  35.0 6.8 %copy-start.8 = (f32[328,256]{1,0:T(8,128)}, f32[328,256]{1,0:T(8,128)S(1)}, u32[]{:S(2)}) copy-start(f32[328,256]{1,0:T(8,128)S(1)} %collective-permute-done.1.below_ref) | copy-start | bytes 1007620
  41.8 25.7 %collective-permute-start.7 = (bf16[8,512,128]{2,1,0:T(8,128)(2,1)S(1)}, bf16[8,512,128]{2,1,0:T(8,128)(2,1)S(1)}, u32[]{:S(2)}, u32[]{:S(2)}) collective-permute-start(bf16[8,512,128]{2,1,0:T(8,128)(2,1)S(1)} %get-tuple-element.38.rest_0_), channel_id=1, source_target_pairs={{1,0},{2,1},{3,2},{4,3},{5,4},{6,5},{7,6},{0,7},{9,8},{10,9},{11,1... | collective-permute-start | bytes 3145736 | tf_op jit(solution)/shard_map/ppermute | solution.py:279
  44.5 26.5 %collective-permute-start.8 = (bf16[8,512,128]{2,1,0:T(8,128)(2,1)S(1)}, bf16[8,512,128]{2,1,0:T(8,128)(2,1)}, u32[]{:S(2)}, u32[]{:S(2)}) collective-permute-start(bf16[8,512,128]{2,1,0:T(8,128)(2,1)S(1)} %get-tuple-element.38.rest_0_), channel_id=1, source_target_pairs={{7,0},{0,1},{1,2},{2,3},{3,4},{4,5},{5,6},{6,7},{15,8},{8,9},{9,10... | collective-permute-start | bytes 3145736 | tf_op jit(solution)/shard_map/ppermute | solution.py:279
  44.5 27.6 %collective-permute-start.12 = (bf16[4,512,128]{2,1,0:T(8,128)(2,1)}, bf16[4,512,128]{2,1,0:T(8,128)(2,1)}, u32[]{:S(2)}, u32[]{:S(2)}) collective-permute-start(bf16[4,512,128]{2,1,0:T(8,128)(2,1)} %get-tuple-element.41), channel_id=1, source_target_pairs={{2,0},{3,1},{4,2},{5,3},{6,4},{7,5},{0,6},{1,7},{10,8},{11,9},{12,... | collective-permute-start | bytes 1572872 | tf_op jit(solution)/shard_map/ppermute | solution.py:279
  46.2 26.5 %collective-permute-start.13 = (bf16[4,512,128]{2,1,0:T(8,128)(2,1)}, bf16[4,512,128]{2,1,0:T(8,128)(2,1)}, u32[]{:S(2)}, u32[]{:S(2)}) collective-permute-start(bf16[4,512,128]{2,1,0:T(8,128)(2,1)} %get-tuple-element.42), channel_id=1, source_target_pairs={{6,0},{7,1},{0,2},{1,3},{2,4},{3,5},{4,6},{5,7},{14,8},{15,9},{8,1... | collective-permute-start | bytes 1572872 | tf_op jit(solution)/shard_map/ppermute | solution.py:279
  47.5 23.5 %copy-start.9 = (s32[64,4]{0,1:T(4,128)S(1)}, s32[64,4]{0,1:T(4,128)}, u32[]{:S(2)}) copy-start(s32[64,4]{0,1:T(4,128)} %param.12) | copy-start | bytes 3076
  47.5 23.5 %copy-start.10 = (s32[64,4]{0,1:T(4,128)S(1)}, s32[64,4]{0,1:T(4,128)}, u32[]{:S(2)}) copy-start(s32[64,4]{0,1:T(4,128)} %param.13) | copy-start | bytes 3076
  47.5 26.7 %all-to-all-start = ((bf16[8,608,128]{2,1,0:T(8,128)(2,1)}), bf16[8,608,128]{2,1,0:T(8,128)(2,1)S(1)}, u32[]{:S(2)}, u32[]{:S(2)}) async-start(bf16[8,608,128]{2,1,0:T(8,128)(2,1)} %get-tuple-element.34), calls=%async_computation | async-start | bytes 2490368 | tf_op jit(solution)/shard_map/all_to_all | solution.py:450
  55.3 19.0 %collective-permute-start.9 = (bf16[8,512,128]{2,1,0:T(8,128)(2,1)S(1)}, bf16[8,512,128]{2,1,0:T(8,128)(2,1)}, u32[]{:S(2)}, u32[]{:S(2)}) collective-permute-start(bf16[8,512,128]{2,1,0:T(8,128)(2,1)S(1)} %get-tuple-element.38.rest_0_), channel_id=1, source_target_pairs={{32,0},{33,1},{34,2},{35,3},{36,4},{37,5},{38,6},{39,7},{40,8},{41... | collective-permute-start | bytes 3145736 | tf_op jit(solution)/shard_map/ppermute | solution.py:279
  67.5 6.7 %collective-permute-start.10 = (bf16[8,512,128]{2,1,0:T(8,128)(2,1)S(1)}, bf16[8,512,128]{2,1,0:T(8,128)(2,1)}, u32[]{:S(2)}, u32[]{:S(2)}) collective-permute-start(bf16[8,512,128]{2,1,0:T(8,128)(2,1)S(1)} %collective-permute-done.7.rest_1_), channel_id=1, source_target_pairs={{32,0},{33,1},{34,2},{35,3},{36,4},{37,5},{38,6},{39,7},{40,8},{41... | collective-permute-start | bytes 3145736 | tf_op jit(solution)/shard_map/ppermute | solution.py:279
  71.0 3.2 %collective-permute-start.11 = (bf16[8,512,128]{2,1,0:T(8,128)(2,1)}, bf16[8,512,128]{2,1,0:T(8,128)(2,1)}, u32[]{:S(2)}, u32[]{:S(2)}) collective-permute-start(bf16[8,512,128]{2,1,0:T(8,128)(2,1)} %collective-permute-done.8.rest_2_), channel_id=1, source_target_pairs={{32,0},{33,1},{34,2},{35,3},{36,4},{37,5},{38,6},{39,7},{40,8},{41... | collective-permute-start | bytes 3145736 | tf_op jit(solution)/shard_map/ppermute | solution.py:279
  72.1 5.2 %collective-permute-start.14 = (bf16[4,512,128]{2,1,0:T(8,128)(2,1)}, bf16[4,512,128]{2,1,0:T(8,128)(2,1)}, u32[]{:S(2)}, u32[]{:S(2)}) collective-permute-start(bf16[4,512,128]{2,1,0:T(8,128)(2,1)} %collective-permute-done.12.rest_0_), channel_id=1, source_target_pairs={{32,0},{33,1},{34,2},{35,3},{36,4},{37,5},{38,6},{39,7},{40,8},{41... | collective-permute-start | bytes 1572872 | tf_op jit(solution)/shard_map/ppermute | solution.py:279
  72.7 4.7 %collective-permute-start.15 = (bf16[4,512,128]{2,1,0:T(8,128)(2,1)}, bf16[4,512,128]{2,1,0:T(8,128)(2,1)}, u32[]{:S(2)}, u32[]{:S(2)}) collective-permute-start(bf16[4,512,128]{2,1,0:T(8,128)(2,1)} %collective-permute-done.13.rest_1_), channel_id=1, source_target_pairs={{32,0},{33,1},{34,2},{35,3},{36,4},{37,5},{38,6},{39,7},{40,8},{41... | collective-permute-start | bytes 1572872 | tf_op jit(solution)/shard_map/ppermute | solution.py:279
  82.9 21.0 %copy-start.2 = (f32[34,64,256]{2,1,0:T(8,128)S(1)}, f32[34,64,256]{2,1,0:T(8,128)}, u32[]{:S(2)}) copy-start(f32[34,64,256]{2,1,0:T(8,128)} %copy-done.1) | copy-start | bytes 6684676
  (4 other events, 14.8 us)

commit v8 on v7

--- a/solution.py
+++ b/solution.py
@@ -15,7 +15,7 @@
 HBM = pl.BlockSpec(memory_space=pltpu.HBM)
 
 
-def pack_obs(anom_ref, weight_ref, out_ref):
+def pack_obs_kernel(anom_ref, weight_ref, out_ref, token_ref):
     members = anom_ref.shape[2]
     core = lax.rem(lax.axis_index("mem"), 2)
 
@@ -30,8 +30,7 @@
             out_ref[0, q * TILE : (q + 1) * TILE, :] = weight_ref[0, :, q * TILE : (q + 1) * TILE].T
 
 
-def pack_kernel(first_ref, last_ref, coef_ref, block_ref, taper_ref, anom_ref, weight_ref, up_ref, down_ref, own_ref):
-    pack_obs(anom_ref, weight_ref, own_ref)
+def pack_halo_kernel(first_ref, last_ref, coef_ref, block_ref, taper_ref, after_ref, up_ref, down_ref, token_ref):
     members, depth, columns = first_ref.shape
     rows = coef_ref.shape[0]
     tiles = block_ref.shape[1]
@@ -292,70 +291,47 @@
 
 def join(operands, name, after):
     count = len(operands)
-    flat = [v for pair in operands for v in (pair if isinstance(pair, tuple) else (pair,))]
 
     def kernel(*refs):
-        outs = refs[len(flat) + len(after) :]
+        outs = refs[count + len(after) :]
         core = lax.rem(lax.axis_index("mem"), 2)
-        halves = [[], []]
-        at = 0
-        for pair in operands:
+        for a in range(count):
             for i in range(2):
-                halves[i].append((refs[at + i], 0) if isinstance(pair, tuple) else (refs[at], i))
-            at += 2 if isinstance(pair, tuple) else 1
-        for i in range(2):
-            for a, (ref, block) in enumerate(halves[i]):
-                outs[0][i * count + a] = ref[block]
-                if i == 0:
-                    outs[1][a] = ref[block]
-
-            @pl.when(core == i)
-            def _(i=i):
-                for a, (ref, block) in enumerate(halves[i]):
-                    outs[2][a] = ref[block]
-
-    shapes = [(n, *flat[0].shape[1:]) for n in (2 * count, count, count)]
+                outs[0][i * count + a] = refs[a][i]
+            outs[1][a] = refs[a][0]
+            outs[2][a] = refs[a][core]
+
+    shapes = [(n, *operands[0].shape[1:]) for n in (2 * count, count, count)]
     return pl.pallas_call(
         kernel,
         out_shape=[jax.ShapeDtypeStruct(shape, BF16) for shape in shapes],
-        in_specs=[VMEM] * len(flat) + [HBM] * len(after),
+        in_specs=[VMEM] * count + [HBM] * len(after),
         out_specs=[VMEM] * len(shapes),
         compiler_params=pltpu.CompilerParams(vmem_limit_bytes=6 << 20),
         name=name,
-    )(*flat, *after)
-
-
-def join_two_kernel(own_ref, far_ref, held_ref, other_ref, token_ref):
-    core = lax.rem(lax.axis_index("mem"), 2)
+    )(*operands, *after)
+
+
+def join_two_kernel(own_ref, far_ref, after_ref, held_ref, token_ref):
     held_ref[0] = own_ref[0]
     held_ref[1] = far_ref[0]
 
-    @pl.when(core == 0)
-    def _():
-        other_ref[0] = far_ref[0]
-
-    @pl.when(core == 1)
-    def _():
-        other_ref[0] = own_ref[0]
-
-
-def gather_first(own, mesh):
+
+def gather_first(own, mesh, after):
     far = fetch(own, mesh, lambda x, c, y, z: (x, c, y, z + 4))
     return pl.pallas_call(
         join_two_kernel,
-        out_shape=[jax.ShapeDtypeStruct((n, *own.shape[1:]), BF16) for n in (2, 1)] + [TOKEN],
-        in_specs=[VMEM] * 2,
-        out_specs=[VMEM] * 2 + [HBM],
+        out_shape=[jax.ShapeDtypeStruct((2, *own.shape[1:]), BF16), TOKEN],
+        in_specs=[VMEM] * 2 + [HBM],
+        out_specs=[VMEM, HBM],
         compiler_params=pltpu.CompilerParams(vmem_limit_bytes=6 << 20),
         name="join_two",
-    )(own, far)
-
-
-def gather_second(own, held, alternate, mesh, after):
-    p, m = (fetch(held, mesh, ring(True, step)) for step in (1, -1))
-    near = fetch(own, mesh, ring(True, 2))
-    far = fetch(alternate, mesh, ring(True, -2))
-    return join([held, p, m, (near, far)], "join_eight", after)
+    )(own, far, after)
+
+
+def gather_second(held, mesh, after):
+    p, m, q = (fetch(held, mesh, ring(True, step)) for step in (1, -1, 2))
+    return join([held, p, m, q], "join_eight", after)
 
 
 def gather_rest(held, first, second, mesh):
@@ -384,33 +360,39 @@
 
     j, at = lax.axis_index("mem"), lax.axis_index("state")
     chips = (group // 2, states // 8, 8)
-    up, down, packed = pl.pallas_call(
-        pack_kernel,
+    packed, obs_packed = pl.pallas_call(
+        pack_obs_kernel,
+        out_shape=[jax.ShapeDtypeStruct((1, obs_anom.shape[2], TILE), BF16), TOKEN],
+        in_specs=[VMEM] * 2,
+        out_specs=[VMEM, HBM],
+        compiler_params=pltpu.CompilerParams(vmem_limit_bytes=6 << 20),
+        name="pack_obs",
+    )(obs_anom, obs_weight)
+    up, down, halo_packed = pl.pallas_call(
+        pack_halo_kernel,
         grid=(1,),
-        out_shape=[jax.ShapeDtypeStruct((HALO * members + 8, columns), F32)] * 2
-        + [jax.ShapeDtypeStruct((1, obs_anom.shape[2], TILE), BF16)],
+        out_shape=[jax.ShapeDtypeStruct((HALO * members + 8, columns), F32)] * 2 + [TOKEN],
         in_specs=[
             pl.BlockSpec((members, 8, columns), lambda i: (0, 0, 0)),
             pl.BlockSpec((members, 8, columns), lambda i: (0, rows // 8 - 1, 0)),
             VMEM,
             SMEM,
             SMEM,
-            VMEM,
-            VMEM,
+            HBM,
         ],
-        out_specs=[VMEM] * 3,
-        name="pack",
-    )(ensemble, ensemble, spreading_coefficient, obs_block.T, taper_id.T, obs_anom, obs_weight)
+        out_specs=[VMEM] * 2 + [HBM],
+        name="pack_halo",
+    )(ensemble, ensemble, spreading_coefficient, obs_block.T, taper_id.T, obs_packed)
     below = lax.ppermute(up, "state", [(i + 1, i) for i in range(states - 1)])
     above = lax.ppermute(down, "state", [(i, i + 1) for i in range(states - 1)])
 
-    held, alternate, started = gather_first(packed, chips)
+    held, started = gather_first(packed, chips, halo_packed)
     row = (members, columns)
     prior, payload, edges, means, turned = pl.pallas_call(
         interior_kernel,
         out_shape=[
-            jax.ShapeDtypeStruct((rows + 2, *row), F32),
-            jax.ShapeDtypeStruct((group, size, TILE), BF16),
+            pltpu.HBM((rows + 2, *row), F32),
+            pltpu.HBM((group, size, TILE), BF16),
             jax.ShapeDtypeStruct((4 * FSTEPS, *row), F32),
             jax.ShapeDtypeStruct((group, 32, TILE), F32),
             jax.ShapeDtypeStruct(taper_table.shape, F32),
@@ -429,7 +411,7 @@
     )(ensemble, spreading_coefficient, taper_table, started)
     prior, payload, forecast_done = pl.pallas_call(
         edge_kernel,
-        out_shape=[prior, payload, TOKEN],
+        out_shape=[pltpu.HBM(prior.shape, F32), pltpu.HBM(payload.shape, BF16), TOKEN],
         in_specs=[VMEM] * 5 + [HBM] * 2,
         out_specs=[HBM] * 3,
         input_output_aliases={5: 0, 6: 1},
@@ -445,7 +427,7 @@
         compiler_params=pltpu.CompilerParams(vmem_limit_bytes=14 << 20),
         name="forecast_edges",
     )(above, below, spreading_coefficient, edges, means, prior, payload)
-    held, first, second = gather_second(packed, held, alternate, chips, [forecast_done])
+    held, first, second = gather_second(held, chips, [forecast_done])
     own, swapped = gather_rest(held, first, second, chips)
     gathered = lax.all_to_all(payload, "mem", split_axis=0, concat_axis=0, tiled=True)
 

time: 107 us -> 102 us (0.953)
  waiting for transfers between devices: 24.9 us -> 20.3 us
  local copies, waits for them, and re-layouts: 1.82 us -> 3.69 us
  starting transfers between devices: 32.4 us -> 31.1 us
    ppermute x14 -> x13, waiting for transfers between devices: 24.9 us -> 20.3 us  [fetch(): return lax.ppermute(value, AXES, pairs)]
    unnamed x24 -> x30, local copies, waits for them, and re-layouts: 1.6 us -> 3.47 us
    ppermute x1, starting transfers between devices: 4.38 us -> 2.65 us  [body(): above = lax.ppermute(down, 'state', [(i, i + 1) for i in range(states - 1)])]
    ppermute x14 -> x13, starting transfers between devices: 19 us -> 20.3 us  [fetch(): return lax.ppermute(value, AXES, pairs)]
    pallas_call x4 -> x5, Pallas kernels: 12.9 us -> 12 us  [the longest x1 5.56 us: body(): pl.pallas_call(interior_kernel, out_shape=[pltpu.HBM((rows + 2, *row), F3...]
  transfers between devices with their start and end apart: 17 -> 16, of which waited for: 3 -> 4; matrix products, arithmetic and copies ran while one was open for 1% -> 1% of each run, Pallas kernels for 13% -> 15%
where the time goes in v8:
time: 102 us
  starting transfers between devices  31.1 us (30%)
  Pallas kernels  24.8 us (24%)
  blocking collectives  21 us (21%)
  waiting for transfers between devices  20.3 us (20%)
  local copies, waits for them, and re-layouts  3.69 us (4%)
    all_to_all x1, blocking collectives, body(): lax.all_to_all(increments, 'mem', split_axis=0, concat_axis=0, tiled=True)  21 us
    ppermute x13, waiting for transfers between devices, fetch(): return lax.ppermute(value, AXES, pairs)  20.3 us
    ppermute x13, starting transfers between devices, fetch(): return lax.ppermute(value, AXES, pairs)  20.3 us
    all_to_all x1, starting transfers between devices, body(): lax.all_to_all(payload, 'mem', split_axis=0, concat_axis=0, tiled=True)  6.92 us
    pallas_call x1, Pallas kernels, body(): pl.pallas_call(analysis_kernel, out_shape=jax.ShapeDtypeStruct((group, ti...  5.58 us
    pallas_call x1, Pallas kernels, body(): pl.pallas_call(interior_kernel, out_shape=[pltpu.HBM((rows + 2, *row), F3...  5.56 us
    pallas_call x1, Pallas kernels, body(): pl.pallas_call(edge_kernel, out_shape=[pltpu.HBM(prior.shape, F32), pltpu...  4.04 us
    unnamed x30, local copies, waits for them, and re-layouts  3.47 us
  transfers between devices with their start and end apart: 16, of which 4 were waited for; matrix products, arithmetic and copies ran while one was open for 1% of the time, Pallas kernels for 15%

profile of v8, /device:TPU:1, one launch (start us, length us, event | category | flops | bytes accessed | tf_op | source)
XLA Modules:
  0.0 101.9 jit_solution(6372258535738863689)
XLA Ops:
  0.0 0.9 copy-done.8
  0.9 0.9 copy-done.9
  1.9 7.8 %collective-permute-start.2 = (bf16[1,512,128]{2,1,0:T(8,128)(2,1)S(1)}, bf16[1,512,128]{2,1,0:T(8,128)(2,1)S(1)}, u32[]{:S(2)}, u32[]{:S(2)}) collective-permute-start(bf16[1,512,128]{2,1,0:T(8,128)(2,1)S(1)} %get-tuple-element.28.own_ref), channel_id=1, source_target_pairs={{4,0},{5,1},{6,2},{7,3},{0,4},{1,5},{2,6},{3,7},{12,8},{13,9},{14,... | collective-permute-start | bytes 393224 | tf_op jit(solution)/shard_map/ppermute | solution.py:278
  9.7 2.3 %pack_halo.1 = (f32[328,256]{1,0:T(8,128)}, f32[328,256]{1,0:T(8,128)}, f32[8,128]{1,0:T(8,128)}) custom-call(f32[64,32,256]{2,1,0:T(8,128)} %x_ref.1, f32[64,32,256]{2,1,0:T(8,128)} %x_ref.1, f32[32,256]{1,0:T(8,128)} %coef_ref.7, s32[4,64]{1,0:T(4,128)} %bitcast.2, s32[4,64]{1,0:T(4,128)} %bitcast.3, f32[8,128]{1,0:T(8,128)} %copy-done.11), custom_call_target="tpu_custom_call" | custom-call | tf_op jit(solution)/shard_map/pack_halo/pallas_call | solution.py:371
  12.1 2.7 %collective-permute-start = (f32[328,256]{1,0:T(8,128)}, f32[328,256]{1,0:T(8,128)S(1)}, u32[]{:S(2)}, u32[]{:S(2)}) collective-permute-start(f32[328,256]{1,0:T(8,128)} %get-tuple-element.26), channel_id=1, source_target_pairs={{0,1},{1,2},{2,3},{3,4},{4,5},{5,6},{6,7},{7,8},{8,9},{9,10},{10,1... | collective-permute-start | bytes 1007624 | tf_op jit(solution)/shard_map/ppermute | solution.py:387
  14.7 1.3 %collective-permute-start.1 = (f32[328,256]{1,0:T(8,128)}, f32[328,256]{1,0:T(8,128)S(1)}, u32[]{:S(2)}, u32[]{:S(2)}) collective-permute-start(f32[328,256]{1,0:T(8,128)} %get-tuple-element.27), channel_id=1, source_target_pairs={{1,0},{2,1},{3,2},{4,3},{5,4},{6,5},{7,6},{8,7},{9,8},{10,9},{11,1... | collective-permute-start | bytes 1007624 | tf_op jit(solution)/shard_map/ppermute | solution.py:386
  16.8 3.6 %collective-permute-start.3 = (bf16[2,512,128]{2,1,0:T(8,128)(2,1)S(1)}, bf16[2,512,128]{2,1,0:T(8,128)(2,1)S(1)}, u32[]{:S(2)}, u32[]{:S(2)}) collective-permute-start(bf16[2,512,128]{2,1,0:T(8,128)(2,1)S(1)} %get-tuple-element.38.refs_0_), channel_id=1, source_target_pairs={{8,0},{9,1},{10,2},{11,3},{12,4},{13,5},{14,6},{15,7},{16,8},{17,9... | collective-permute-start | bytes 786440 | tf_op jit(solution)/shard_map/ppermute | solution.py:278
  20.4 1.9 %collective-permute-start.5 = (bf16[2,512,128]{2,1,0:T(8,128)(2,1)S(1)}, bf16[2,512,128]{2,1,0:T(8,128)(2,1)S(1)}, u32[]{:S(2)}, u32[]{:S(2)}) collective-permute-start(bf16[2,512,128]{2,1,0:T(8,128)(2,1)S(1)} %get-tuple-element.38.refs_0_), channel_id=1, source_target_pairs={{16,0},{17,1},{18,2},{19,3},{20,4},{21,5},{22,6},{23,7},{24,8},{25... | collective-permute-start | bytes 786440 | tf_op jit(solution)/shard_map/ppermute | solution.py:278
  22.3 5.6 %forecast_interior.1 = (f32[34,64,256]{2,1,0:T(8,128)}, bf16[8,608,128]{2,1,0:T(8,128)(2,1)}, f32[16,64,256]{2,1,0:T(8,128)S(1)}, f32[8,32,128]{2,1,0:T(8,128)S(1)}, f32[8,128,128]{2,1,0:T(8,128)S(1)}) custom-call(f32[64,32,256]{2,1,0:T(8,128)S(1)} %copy-done, f32[32,256]{1,0:T(8,128)S(1)} %copy-done.2, f32[8,128,128]{2,1,0:T(8,128)S(1)} %copy-done.5, ...), custom_call_target="tpu_custom_call" | custom-call | tf_op jit(solution)/shard_map/forecast_interior/pallas_call | solution.py:391
  27.8 0.8 copy-done.3
  28.6 4.0 %forecast_edges.1 = (f32[34,64,256]{2,1,0:T(8,128)}, bf16[8,608,128]{2,1,0:T(8,128)(2,1)}, f32[8,128]{1,0:T(8,128)S(1)}) custom-call(f32[328,256]{1,0:T(8,128)S(1)} %collective-permute-done.above_ref, f32[328,256]{1,0:T(8,128)S(1)} %collective-permute-done.1.below_ref, f32[32,256]{1,0:T(8,128)S(1)} %copy-done.2, ...), custom_call_target="tpu_custom_call", output_to_operand_aliasing={{0}: (5, {}), {1}: (6, {})} | custom-call | tf_op jit(solution)/shard_map/forecast_edges/pallas_call | solution.py:412
  32.7 2.6 %collective-permute-done.5.refs_3_ = bf16[2,512,128]{2,1,0:T(8,128)(2,1)S(1)} collective-permute-done((bf16[2,512,128]{2,1,0:T(8,128)(2,1)S(1)}, bf16[2,512,128]{2,1,0:T(8,128)(2,1)S(1)}, u32[]{:S(2)}, u32[]{:S(2)}) %collective-permute-start.5) | collective-permute-done | bytes 262176 | tf_op jit(solution)/shard_map/ppermute | solution.py:278
  35.3 1.2 %join_eight.1 = (bf16[8,512,128]{2,1,0:T(8,128)(2,1)S(1)}, bf16[4,512,128]{2,1,0:T(8,128)(2,1)}, bf16[4,512,128]{2,1,0:T(8,128)(2,1)}) custom-call(bf16[2,512,128]{2,1,0:T(8,128)(2,1)S(1)} %get-tuple-element.38.refs_0_, bf16[2,512,128]{2,1,0:T(8,128)(2,1)S(1)} %collective-permute-done.3.refs_1_, bf16[2,512,128]{2,1,0:T(8,128)(2,1)S(1)} %collective-permute-done.4.refs_2_, ...), custom_call_target="tpu_custom_call" | custom-call | tf_op jit(solution)/shard_map/join_eight/pallas_call | solution.py:305
  36.5 3.3 %collective-permute-start.6 = (bf16[8,512,128]{2,1,0:T(8,128)(2,1)S(1)}, bf16[8,512,128]{2,1,0:T(8,128)(2,1)S(1)}, u32[]{:S(2)}, u32[]{:S(2)}) collective-permute-start(bf16[8,512,128]{2,1,0:T(8,128)(2,1)S(1)} %get-tuple-element.40.rest_0_), channel_id=1, source_target_pairs={{1,0},{2,1},{3,2},{4,3},{5,4},{6,5},{7,6},{0,7},{9,8},{10,9},{11,1... | collective-permute-start | bytes 3145736 | tf_op jit(solution)/shard_map/ppermute | solution.py:278
  39.8 1.6 %collective-permute-start.11 = (bf16[4,512,128]{2,1,0:T(8,128)(2,1)}, bf16[4,512,128]{2,1,0:T(8,128)(2,1)}, u32[]{:S(2)}, u32[]{:S(2)}) collective-permute-start(bf16[4,512,128]{2,1,0:T(8,128)(2,1)} %get-tuple-element.43), channel_id=1, source_target_pairs={{2,0},{3,1},{4,2},{5,3},{6,4},{7,5},{0,6},{1,7},{10,8},{11,9},{12,... | collective-permute-start | bytes 1572872 | tf_op jit(solution)/shard_map/ppermute | solution.py:278
  41.4 1.3 %collective-permute-start.12 = (bf16[4,512,128]{2,1,0:T(8,128)(2,1)}, bf16[4,512,128]{2,1,0:T(8,128)(2,1)}, u32[]{:S(2)}, u32[]{:S(2)}) collective-permute-start(bf16[4,512,128]{2,1,0:T(8,128)(2,1)} %get-tuple-element.44), channel_id=1, source_target_pairs={{6,0},{7,1},{0,2},{1,3},{2,4},{3,5},{4,6},{5,7},{14,8},{15,9},{8,1... | collective-permute-start | bytes 1572872 | tf_op jit(solution)/shard_map/ppermute | solution.py:278
  42.7 6.9 %all-to-all-start = ((bf16[8,608,128]{2,1,0:T(8,128)(2,1)}), bf16[8,608,128]{2,1,0:T(8,128)(2,1)S(1)}, u32[]{:S(2)}, u32[]{:S(2)}) async-start(bf16[8,608,128]{2,1,0:T(8,128)(2,1)} %get-tuple-element.37), calls=%async_computation | async-start | bytes 2490368 | tf_op jit(solution)/shard_map/all_to_all | solution.py:432
  49.7 13.1 %collective-permute-done.6.rest_1_ = bf16[8,512,128]{2,1,0:T(8,128)(2,1)S(1)} collective-permute-done((bf16[8,512,128]{2,1,0:T(8,128)(2,1)S(1)}, bf16[8,512,128]{2,1,0:T(8,128)(2,1)S(1)}, u32[]{:S(2)}, u32[]{:S(2)}) %collective-permute-start.6) | collective-permute-done | bytes 1048608 | tf_op jit(solution)/shard_map/ppermute | solution.py:278
  62.7 3.5 %collective-permute-done.7.rest_2_ = bf16[8,512,128]{2,1,0:T(8,128)(2,1)} collective-permute-done((bf16[8,512,128]{2,1,0:T(8,128)(2,1)S(1)}, bf16[8,512,128]{2,1,0:T(8,128)(2,1)}, u32[]{:S(2)}, u32[]{:S(2)}) %collective-permute-start.7) | collective-permute-done | bytes 1048608 | tf_op jit(solution)/shard_map/ppermute | solution.py:278
  68.2 1.1 %collective-permute-done.10.rest_5_ = bf16[8,512,128]{2,1,0:T(8,128)(2,1)} collective-permute-done((bf16[8,512,128]{2,1,0:T(8,128)(2,1)}, bf16[8,512,128]{2,1,0:T(8,128)(2,1)}, u32[]{:S(2)}, u32[]{:S(2)}) %collective-permute-start.10) | collective-permute-done | bytes 1048608 | tf_op jit(solution)/shard_map/ppermute | solution.py:278
  69.3 3.0 %collect.1 = (bf16[2,24,512,128]{3,2,1,0:T(8,128)(2,1)S(1)}, bf16[9,512,128]{2,1,0:T(8,128)(2,1)S(1)}) custom-call(bf16[8,608,128]{2,1,0:T(8,128)(2,1)S(1)} %all-to-all-done.recv_ref, bf16[8,512,128]{2,1,0:T(8,128)(2,1)S(1)} %get-tuple-element.40.rest_0_, bf16[8,512,128]{2,1,0:T(8,128)(2,1)S(1)} %collective-permute-done.6.rest_1_, ...), custom_call_target="tpu_custom_call" | custom-call | tf_op jit(solution)/shard_map/collect/pallas_call | solution.py:443
  72.3 5.6 %analysis.1 = bf16[8,576,128]{2,1,0:T(8,128)(2,1)S(1)} custom-call(s32[9,4]{1,0:T(8,128)S(1)} %get-tuple-element.46.anom_at_ref, s32[9,4]{1,0:T(8,128)S(1)} %get-tuple-element.45.weight_at_ref, s32[9,4]{1,0:T(8,128)S(1)} %pad_add_fusion.1.tapers_ref, f32[8,128,128]{2,1,0:T(8,128)S(1)} %copy-done.4, bf16[9,512,128]{2,1,0:T(8,128)(2,1)S(1)} %get-tuple-element.41.centred_ref, ...), custom_call_target="tpu_custom_call" | custom-call | tf_op jit(solution)/shard_map/analysis/pallas_call | solution.py:454
  77.9 21.0 %all_to_all.10.inc_ref = bf16[8,576,128]{2,1,0:T(8,128)(2,1)S(1)} all-to-all(bf16[8,576,128]{2,1,0:T(8,128)(2,1)S(1)} %analysis.1), channel_id=1, replica_groups=mesh['mem'=8,'state'=32] {'mem'}, dimensions={0} | all-to-all | bytes 2359296 | tf_op jit(solution)/shard_map/all_to_all | solution.py:463
  99.0 2.9 %final_step.1 = f32[64,32,256]{2,1,0:T(8,128)} custom-call(f32[34,64,256]{2,1,0:T(8,128)S(1)} %copy-done.1, bf16[8,576,128]{2,1,0:T(8,128)(2,1)S(1)} %all_to_all.10.inc_ref, f32[32,256]{1,0:T(8,128)S(1)} %copy-done.2), custom_call_target="tpu_custom_call" | custom-call | tf_op jit(solution)/shard_map/final_step/pallas_call | solution.py:465
  (57 shorter events, 2.7 us)
Async XLA Ops:
  1.9 7.8 %copy-start.11 = (f32[8,128]{1,0:T(8,128)}, f32[8,128]{1,0:T(8,128)S(1)}, u32[]{:S(2)}) copy-start(f32[8,128]{1,0:T(8,128)S(1)} %get-tuple-element.25.after_ref) | copy-start | bytes 12292
  1.9 14.1 %collective-permute-start.2 = (bf16[1,512,128]{2,1,0:T(8,128)(2,1)S(1)}, bf16[1,512,128]{2,1,0:T(8,128)(2,1)S(1)}, u32[]{:S(2)}, u32[]{:S(2)}) collective-permute-start(bf16[1,512,128]{2,1,0:T(8,128)(2,1)S(1)} %get-tuple-element.28.own_ref), channel_id=1, source_target_pairs={{4,0},{5,1},{6,2},{7,3},{0,4},{1,5},{2,6},{3,7},{12,8},{13,9},{14,... | collective-permute-start | bytes 393224 | tf_op jit(solution)/shard_map/ppermute | solution.py:278
  9.7 12.5 %copy-start = (f32[64,32,256]{2,1,0:T(8,128)S(1)}, f32[64,32,256]{2,1,0:T(8,128)}, u32[]{:S(2)}) copy-start(f32[64,32,256]{2,1,0:T(8,128)} %x_ref.1) | copy-start | bytes 6291460
  9.7 12.5 %copy-start.2 = (f32[32,256]{1,0:T(8,128)S(1)}, f32[32,256]{1,0:T(8,128)}, u32[]{:S(2)}) copy-start(f32[32,256]{1,0:T(8,128)} %coef_ref.7) | copy-start | bytes 98308
  9.7 12.5 %copy-start.5 = (f32[8,128,128]{2,1,0:T(8,128)S(1)}, f32[8,128,128]{2,1,0:T(8,128)}, u32[]{:S(2)}) copy-start(f32[8,128,128]{2,1,0:T(8,128)} %taper_ref.1) | copy-start | bytes 1572868
  12.1 16.5 %collective-permute-start = (f32[328,256]{1,0:T(8,128)}, f32[328,256]{1,0:T(8,128)S(1)}, u32[]{:S(2)}, u32[]{:S(2)}) collective-permute-start(f32[328,256]{1,0:T(8,128)} %get-tuple-element.26), channel_id=1, source_target_pairs={{0,1},{1,2},{2,3},{3,4},{4,5},{5,6},{6,7},{7,8},{8,9},{9,10},{10,1... | collective-permute-start | bytes 1007624 | tf_op jit(solution)/shard_map/ppermute | solution.py:387
  14.7 13.9 %collective-permute-start.1 = (f32[328,256]{1,0:T(8,128)}, f32[328,256]{1,0:T(8,128)S(1)}, u32[]{:S(2)}, u32[]{:S(2)}) collective-permute-start(f32[328,256]{1,0:T(8,128)} %get-tuple-element.27), channel_id=1, source_target_pairs={{1,0},{2,1},{3,2},{4,3},{5,4},{6,5},{7,6},{8,7},{9,8},{10,9},{11,1... | collective-permute-start | bytes 1007624 | tf_op jit(solution)/shard_map/ppermute | solution.py:386
  16.8 16.0 %collective-permute-start.3 = (bf16[2,512,128]{2,1,0:T(8,128)(2,1)S(1)}, bf16[2,512,128]{2,1,0:T(8,128)(2,1)S(1)}, u32[]{:S(2)}, u32[]{:S(2)}) collective-permute-start(bf16[2,512,128]{2,1,0:T(8,128)(2,1)S(1)} %get-tuple-element.38.refs_0_), channel_id=1, source_target_pairs={{8,0},{9,1},{10,2},{11,3},{12,4},{13,5},{14,6},{15,7},{16,8},{17,9... | collective-permute-start | bytes 786440 | tf_op jit(solution)/shard_map/ppermute | solution.py:278
  20.4 12.3 %collective-permute-start.4 = (bf16[2,512,128]{2,1,0:T(8,128)(2,1)S(1)}, bf16[2,512,128]{2,1,0:T(8,128)(2,1)S(1)}, u32[]{:S(2)}, u32[]{:S(2)}) collective-permute-start(bf16[2,512,128]{2,1,0:T(8,128)(2,1)S(1)} %get-tuple-element.38.refs_0_), channel_id=1, source_target_pairs={{24,0},{25,1},{26,2},{27,3},{28,4},{29,5},{30,6},{31,7},{0,8},{1,9... | collective-permute-start | bytes 786440 | tf_op jit(solution)/shard_map/ppermute | solution.py:278
  20.4 14.9 %collective-permute-start.5 = (bf16[2,512,128]{2,1,0:T(8,128)(2,1)S(1)}, bf16[2,512,128]{2,1,0:T(8,128)(2,1)S(1)}, u32[]{:S(2)}, u32[]{:S(2)}) collective-permute-start(bf16[2,512,128]{2,1,0:T(8,128)(2,1)S(1)} %get-tuple-element.38.refs_0_), channel_id=1, source_target_pairs={{16,0},{17,1},{18,2},{19,3},{20,4},{21,5},{22,6},{23,7},{24,8},{25... | collective-permute-start | bytes 786440 | tf_op jit(solution)/shard_map/ppermute | solution.py:278
  28.6 7.9 %copy-start.7 = (f32[328,256]{1,0:T(8,128)}, f32[328,256]{1,0:T(8,128)S(1)}, u32[]{:S(2)}) copy-start(f32[328,256]{1,0:T(8,128)S(1)} %collective-permute-done.1.below_ref) | copy-start | bytes 1007620
  36.5 26.2 %collective-permute-start.6 = (bf16[8,512,128]{2,1,0:T(8,128)(2,1)S(1)}, bf16[8,512,128]{2,1,0:T(8,128)(2,1)S(1)}, u32[]{:S(2)}, u32[]{:S(2)}) collective-permute-start(bf16[8,512,128]{2,1,0:T(8,128)(2,1)S(1)} %get-tuple-element.40.rest_0_), channel_id=1, source_target_pairs={{1,0},{2,1},{3,2},{4,3},{5,4},{6,5},{7,6},{0,7},{9,8},{10,9},{11,1... | collective-permute-start | bytes 3145736 | tf_op jit(solution)/shard_map/ppermute | solution.py:278
  39.8 26.5 %collective-permute-start.7 = (bf16[8,512,128]{2,1,0:T(8,128)(2,1)S(1)}, bf16[8,512,128]{2,1,0:T(8,128)(2,1)}, u32[]{:S(2)}, u32[]{:S(2)}) collective-permute-start(bf16[8,512,128]{2,1,0:T(8,128)(2,1)S(1)} %get-tuple-element.40.rest_0_), channel_id=1, source_target_pairs={{7,0},{0,1},{1,2},{2,3},{3,4},{4,5},{5,6},{6,7},{15,8},{8,9},{9,10... | collective-permute-start | bytes 3145736 | tf_op jit(solution)/shard_map/ppermute | solution.py:278
  39.8 27.6 %collective-permute-start.11 = (bf16[4,512,128]{2,1,0:T(8,128)(2,1)}, bf16[4,512,128]{2,1,0:T(8,128)(2,1)}, u32[]{:S(2)}, u32[]{:S(2)}) collective-permute-start(bf16[4,512,128]{2,1,0:T(8,128)(2,1)} %get-tuple-element.43), channel_id=1, source_target_pairs={{2,0},{3,1},{4,2},{5,3},{6,4},{7,5},{0,6},{1,7},{10,8},{11,9},{12,... | collective-permute-start | bytes 1572872 | tf_op jit(solution)/shard_map/ppermute | solution.py:278
  41.4 26.5 %collective-permute-start.12 = (bf16[4,512,128]{2,1,0:T(8,128)(2,1)}, bf16[4,512,128]{2,1,0:T(8,128)(2,1)}, u32[]{:S(2)}, u32[]{:S(2)}) collective-permute-start(bf16[4,512,128]{2,1,0:T(8,128)(2,1)} %get-tuple-element.44), channel_id=1, source_target_pairs={{6,0},{7,1},{0,2},{1,3},{2,4},{3,5},{4,6},{5,7},{14,8},{15,9},{8,1... | collective-permute-start | bytes 1572872 | tf_op jit(solution)/shard_map/ppermute | solution.py:278
  42.7 23.5 %copy-start.12 = (s32[64,4]{0,1:T(4,128)S(1)}, s32[64,4]{0,1:T(4,128)}, u32[]{:S(2)}) copy-start(s32[64,4]{0,1:T(4,128)} %param.12) | copy-start | bytes 3076
  42.7 23.5 %copy-start.13 = (s32[64,4]{0,1:T(4,128)S(1)}, s32[64,4]{0,1:T(4,128)}, u32[]{:S(2)}) copy-start(s32[64,4]{0,1:T(4,128)} %param.13) | copy-start | bytes 3076
  42.7 25.4 %all-to-all-start = ((bf16[8,608,128]{2,1,0:T(8,128)(2,1)}), bf16[8,608,128]{2,1,0:T(8,128)(2,1)S(1)}, u32[]{:S(2)}, u32[]{:S(2)}) async-start(bf16[8,608,128]{2,1,0:T(8,128)(2,1)} %get-tuple-element.37), calls=%async_computation | async-start | bytes 2490368 | tf_op jit(solution)/shard_map/all_to_all | solution.py:432
  49.7 18.5 %collective-permute-start.8 = (bf16[8,512,128]{2,1,0:T(8,128)(2,1)S(1)}, bf16[8,512,128]{2,1,0:T(8,128)(2,1)}, u32[]{:S(2)}, u32[]{:S(2)}) collective-permute-start(bf16[8,512,128]{2,1,0:T(8,128)(2,1)S(1)} %get-tuple-element.40.rest_0_), channel_id=1, source_target_pairs={{32,0},{33,1},{34,2},{35,3},{36,4},{37,5},{38,6},{39,7},{40,8},{41... | collective-permute-start | bytes 3145736 | tf_op jit(solution)/shard_map/ppermute | solution.py:278
  62.7 5.4 %collective-permute-start.9 = (bf16[8,512,128]{2,1,0:T(8,128)(2,1)S(1)}, bf16[8,512,128]{2,1,0:T(8,128)(2,1)}, u32[]{:S(2)}, u32[]{:S(2)}) collective-permute-start(bf16[8,512,128]{2,1,0:T(8,128)(2,1)S(1)} %collective-permute-done.6.rest_1_), channel_id=1, source_target_pairs={{32,0},{33,1},{34,2},{35,3},{36,4},{37,5},{38,6},{39,7},{40,8},{41... | collective-permute-start | bytes 3145736 | tf_op jit(solution)/shard_map/ppermute | solution.py:278
  66.3 3.0 %collective-permute-start.10 = (bf16[8,512,128]{2,1,0:T(8,128)(2,1)}, bf16[8,512,128]{2,1,0:T(8,128)(2,1)}, u32[]{:S(2)}, u32[]{:S(2)}) collective-permute-start(bf16[8,512,128]{2,1,0:T(8,128)(2,1)} %collective-permute-done.7.rest_2_), channel_id=1, source_target_pairs={{32,0},{33,1},{34,2},{35,3},{36,4},{37,5},{38,6},{39,7},{40,8},{41... | collective-permute-start | bytes 3145736 | tf_op jit(solution)/shard_map/ppermute | solution.py:278
  67.4 4.9 %collective-permute-start.13 = (bf16[4,512,128]{2,1,0:T(8,128)(2,1)}, bf16[4,512,128]{2,1,0:T(8,128)(2,1)}, u32[]{:S(2)}, u32[]{:S(2)}) collective-permute-start(bf16[4,512,128]{2,1,0:T(8,128)(2,1)} %collective-permute-done.11.rest_0_), channel_id=1, source_target_pairs={{32,0},{33,1},{34,2},{35,3},{36,4},{37,5},{38,6},{39,7},{40,8},{41... | collective-permute-start | bytes 1572872 | tf_op jit(solution)/shard_map/ppermute | solution.py:278
  67.9 4.4 %collective-permute-start.14 = (bf16[4,512,128]{2,1,0:T(8,128)(2,1)}, bf16[4,512,128]{2,1,0:T(8,128)(2,1)}, u32[]{:S(2)}, u32[]{:S(2)}) collective-permute-start(bf16[4,512,128]{2,1,0:T(8,128)(2,1)} %collective-permute-done.12.rest_1_), channel_id=1, source_target_pairs={{32,0},{33,1},{34,2},{35,3},{36,4},{37,5},{38,6},{39,7},{40,8},{41... | collective-permute-start | bytes 1572872 | tf_op jit(solution)/shard_map/ppermute | solution.py:278
  77.9 21.0 %copy-start.1 = (f32[34,64,256]{2,1,0:T(8,128)S(1)}, f32[34,64,256]{2,1,0:T(8,128)}, u32[]{:S(2)}) copy-start(f32[34,64,256]{2,1,0:T(8,128)} %get-tuple-element.35.prior_ref) | copy-start | bytes 6684676
  (6 other events, 11.5 us)

commit v9 on v8

--- a/solution.py
+++ b/solution.py
@@ -15,22 +15,22 @@
 HBM = pl.BlockSpec(memory_space=pltpu.HBM)
 
 
-def pack_obs_kernel(anom_ref, weight_ref, out_ref, token_ref):
+def pack_obs_kernel(anom_ref, weight_ref, out_ref, token_ref, held_ref, sem):
     members = anom_ref.shape[2]
     core = lax.rem(lax.axis_index("mem"), 2)
-
-    @pl.when(core == 0)
-    def _():
-        for q in range(members // TILE):
-            out_ref[0, q * TILE : (q + 1) * TILE, :] = anom_ref[0, :, q * TILE : (q + 1) * TILE]
-
-    @pl.when(core == 1)
-    def _():
-        for q in range(members // TILE):
-            out_ref[0, q * TILE : (q + 1) * TILE, :] = weight_ref[0, :, q * TILE : (q + 1) * TILE].T
-
-
-def pack_halo_kernel(first_ref, last_ref, coef_ref, block_ref, taper_ref, after_ref, up_ref, down_ref, token_ref):
+    for kind, ref in enumerate((anom_ref, weight_ref)):
+
+        @pl.when(core == kind)
+        def _(kind=kind, ref=ref):
+            copy = pltpu.make_async_copy(ref.at[0], held_ref, sem.at[kind])
+            copy.start()
+            copy.wait()
+            for q in range(members // TILE):
+                part = held_ref[:, q * TILE : (q + 1) * TILE]
+                out_ref[0, q * TILE : (q + 1) * TILE, :] = part if kind == 0 else part.T
+
+
+def pack_halo_kernel(first_ref, last_ref, coef_ref, block_ref, taper_ref, after_ref, up_ref, down_ref):
     members, depth, columns = first_ref.shape
     rows = coef_ref.shape[0]
     tiles = block_ref.shape[1]
@@ -67,7 +67,7 @@
     mean_ref[3 * slot + 2 : 3 * slot + 3, :] = mean - high - middle
 
 
-def interior_kernel(x_ref, coef_ref, taper_ref, token_ref, prior_ref, out_ref, edge_ref, mean_ref, turned_ref, a_ref, b_ref, c_ref, pay_ref, sems):
+def interior_kernel(x_ref, coef_ref, taper_ref, token_ref, prior_ref, out_ref, edge_ref, mean_ref, turned_out, a_ref, b_ref, c_ref, pay_ref, turned_ref, sems):
     members, rows, columns = x_ref.shape
     group = out_ref.shape[0]
     per = rows // group
@@ -104,6 +104,8 @@
         copies[-1].start()
     for i in range(taper_ref.shape[0]):
         turned_ref[i] = taper_ref[i].T
+    copies.append(pltpu.make_async_copy(turned_ref, turned_out, sems.at[group]))
+    copies[-1].start()
     for copy in copies:
         copy.wait()
 
@@ -286,7 +288,7 @@
     return (x, 1 - c, y, z)
 
 
-TOKEN = jax.ShapeDtypeStruct((8, TILE), F32)
+TOKEN = pltpu.HBM((8, TILE), F32)
 
 
 def join(operands, name, after):
@@ -312,21 +314,21 @@
     )(*operands, *after)
 
 
-def join_two_kernel(own_ref, far_ref, after_ref, held_ref, token_ref):
+def join_two_kernel(own_ref, far_ref, held_ref, token_ref):
     held_ref[0] = own_ref[0]
     held_ref[1] = far_ref[0]
 
 
-def gather_first(own, mesh, after):
+def gather_first(own, mesh):
     far = fetch(own, mesh, lambda x, c, y, z: (x, c, y, z + 4))
     return pl.pallas_call(
         join_two_kernel,
         out_shape=[jax.ShapeDtypeStruct((2, *own.shape[1:]), BF16), TOKEN],
-        in_specs=[VMEM] * 2 + [HBM],
+        in_specs=[VMEM] * 2,
         out_specs=[VMEM, HBM],
         compiler_params=pltpu.CompilerParams(vmem_limit_bytes=6 << 20),
         name="join_two",
-    )(own, far, after)
+    )(own, far)
 
 
 def gather_second(held, mesh, after):
@@ -363,15 +365,15 @@
     packed, obs_packed = pl.pallas_call(
         pack_obs_kernel,
         out_shape=[jax.ShapeDtypeStruct((1, obs_anom.shape[2], TILE), BF16), TOKEN],
-        in_specs=[VMEM] * 2,
+        in_specs=[HBM] * 2,
         out_specs=[VMEM, HBM],
-        compiler_params=pltpu.CompilerParams(vmem_limit_bytes=6 << 20),
+        scratch_shapes=[pltpu.VMEM(obs_anom.shape[1:], BF16), pltpu.SemaphoreType.DMA((2,))],
         name="pack_obs",
     )(obs_anom, obs_weight)
-    up, down, halo_packed = pl.pallas_call(
+    up, down = pl.pallas_call(
         pack_halo_kernel,
         grid=(1,),
-        out_shape=[jax.ShapeDtypeStruct((HALO * members + 8, columns), F32)] * 2 + [TOKEN],
+        out_shape=[jax.ShapeDtypeStruct((HALO * members + 8, columns), F32)] * 2,
         in_specs=[
             pl.BlockSpec((members, 8, columns), lambda i: (0, 0, 0)),
             pl.BlockSpec((members, 8, columns), lambda i: (0, rows // 8 - 1, 0)),
@@ -380,13 +382,13 @@
             SMEM,
             HBM,
         ],
-        out_specs=[VMEM] * 2 + [HBM],
+        out_specs=[VMEM] * 2,
         name="pack_halo",
     )(ensemble, ensemble, spreading_coefficient, obs_block.T, taper_id.T, obs_packed)
     below = lax.ppermute(up, "state", [(i + 1, i) for i in range(states - 1)])
     above = lax.ppermute(down, "state", [(i, i + 1) for i in range(states - 1)])
 
-    held, started = gather_first(packed, chips, halo_packed)
+    held, started = gather_first(packed, chips)
     row = (members, columns)
     prior, payload, edges, means, turned = pl.pallas_call(
         interior_kernel,
@@ -395,16 +397,17 @@
             pltpu.HBM((group, size, TILE), BF16),
             jax.ShapeDtypeStruct((4 * FSTEPS, *row), F32),
             jax.ShapeDtypeStruct((group, 32, TILE), F32),
-            jax.ShapeDtypeStruct(taper_table.shape, F32),
+            pltpu.HBM(taper_table.shape, F32),
         ],
         in_specs=[VMEM] * 3 + [HBM],
-        out_specs=[HBM] * 2 + [VMEM] * 3,
+        out_specs=[HBM] * 2 + [VMEM] * 2 + [HBM],
         scratch_shapes=[
             pltpu.VMEM((rows, *row), F32),
             pltpu.VMEM((rows, *row), F32),
             pltpu.VMEM((rows, 8, columns), F32),
             pltpu.VMEM((group, 2 * per * members, TILE), BF16),
-            pltpu.SemaphoreType.DMA((group,)),
+            pltpu.VMEM(taper_table.shape, F32),
+            pltpu.SemaphoreType.DMA((group + 1,)),
         ],
         compiler_params=pltpu.CompilerParams(vmem_limit_bytes=14 << 20),
         name="forecast_interior",

time: 102 us -> 103 us (level)
  Pallas kernels: 24.8 us -> 26.8 us
  local copies, waits for them, and re-layouts: 3.69 us -> 1.78 us
    unnamed x30 -> x26, local copies, waits for them, and re-layouts: 3.47 us -> 1.56 us
    pallas_call x1, Pallas kernels: 0.08 us -> 1.66 us  [body(): pl.pallas_call(pack_obs_kernel, out_shape=[jax.ShapeDtypeStruct((1, obs_a...]
where the time goes in v9:
time: 103 us; the launch traced here: 102 us
  starting transfers between devices  31.3 us (30%)
  Pallas kernels  26.8 us (26%)
  blocking collectives  21 us (20%)
  waiting for transfers between devices  20.4 us (20%)
  local copies, waits for them, and re-layouts  1.78 us (2%)
    all_to_all x1, blocking collectives, body(): lax.all_to_all(increments, 'mem', split_axis=0, concat_axis=0, tiled=True)  21 us
    ppermute x13, starting transfers between devices, fetch(): return lax.ppermute(value, AXES, pairs)  20.5 us
    ppermute x13, waiting for transfers between devices, fetch(): return lax.ppermute(value, AXES, pairs)  20.4 us
    all_to_all x1, starting transfers between devices, body(): lax.all_to_all(payload, 'mem', split_axis=0, concat_axis=0, tiled=True)  6.92 us
    pallas_call x1, Pallas kernels, body(): pl.pallas_call(interior_kernel, out_shape=[pltpu.HBM((rows + 2, *row), F3...  5.95 us
    pallas_call x1, Pallas kernels, body(): pl.pallas_call(analysis_kernel, out_shape=jax.ShapeDtypeStruct((group, ti...  5.58 us
    pallas_call x1, Pallas kernels, body(): pl.pallas_call(edge_kernel, out_shape=[pltpu.HBM(prior.shape, F32), pltpu...  4.04 us
    pallas_call x1, Pallas kernels, body(): pl.pallas_call(collect_kernel, out_shape=[jax.ShapeDtypeStruct((2, sum((v...  3.04 us
  transfers between devices with their start and end apart: 16, of which 4 were waited for; matrix products, arithmetic and copies ran while one was open for 1% of the time, Pallas kernels for 15%

profile of v9, /device:TPU:1, one launch (start us, length us, event | category | flops | bytes accessed | tf_op | source)
XLA Modules:
  0.0 102.3 jit_solution(18029666553927346083)
XLA Ops:
  0.0 1.7 %pack_obs.1 = (bf16[1,512,128]{2,1,0:T(8,128)(2,1)}, f32[8,128]{1,0:T(8,128)}) custom-call(bf16[1,128,512]{2,1,0:T(8,128)(2,1)} %anom_ref.1, bf16[1,128,512]{2,1,0:T(8,128)(2,1)} %weight_ref.1), custom_call_target="tpu_custom_call" | custom-call | tf_op jit(solution)/shard_map/pack_obs/pallas_call | solution.py:365
  1.7 7.8 %collective-permute-start.2 = (bf16[1,512,128]{2,1,0:T(8,128)(2,1)}, bf16[1,512,128]{2,1,0:T(8,128)(2,1)S(1)}, u32[]{:S(2)}, u32[]{:S(2)}) collective-permute-start(bf16[1,512,128]{2,1,0:T(8,128)(2,1)} %get-tuple-element.27.own_ref), channel_id=1, source_target_pairs={{4,0},{5,1},{6,2},{7,3},{0,4},{1,5},{2,6},{3,7},{12,8},{13,9},{14,... | collective-permute-start | bytes 393224 | tf_op jit(solution)/shard_map/ppermute | solution.py:280
  9.5 2.3 %pack_halo.1 = (f32[328,256]{1,0:T(8,128)}, f32[328,256]{1,0:T(8,128)}) custom-call(f32[64,32,256]{2,1,0:T(8,128)} %x_ref.1, f32[64,32,256]{2,1,0:T(8,128)} %x_ref.1, f32[32,256]{1,0:T(8,128)} %coef_ref.7, s32[4,64]{1,0:T(4,128)} %bitcast.2, s32[4,64]{1,0:T(4,128)} %bitcast.3, f32[8,128]{1,0:T(8,128)} %get-tuple-element.24.after_ref), custom_call_target="tpu_custom_call" | custom-call | tf_op jit(solution)/shard_map/pack_halo/pallas_call | solution.py:373
  11.9 2.7 %collective-permute-start = (f32[328,256]{1,0:T(8,128)}, f32[328,256]{1,0:T(8,128)S(1)}, u32[]{:S(2)}, u32[]{:S(2)}) collective-permute-start(f32[328,256]{1,0:T(8,128)} %get-tuple-element.25), channel_id=1, source_target_pairs={{0,1},{1,2},{2,3},{3,4},{4,5},{5,6},{6,7},{7,8},{8,9},{9,10},{10,1... | collective-permute-start | bytes 1007624 | tf_op jit(solution)/shard_map/ppermute | solution.py:389
  14.5 1.3 %collective-permute-start.1 = (f32[328,256]{1,0:T(8,128)}, f32[328,256]{1,0:T(8,128)S(1)}, u32[]{:S(2)}, u32[]{:S(2)}) collective-permute-start(f32[328,256]{1,0:T(8,128)} %get-tuple-element.26), channel_id=1, source_target_pairs={{1,0},{2,1},{3,2},{4,3},{5,4},{6,5},{7,6},{8,7},{9,8},{10,9},{11,1... | collective-permute-start | bytes 1007624 | tf_op jit(solution)/shard_map/ppermute | solution.py:388
  15.9 3.6 %collective-permute-start.3 = (bf16[2,512,128]{2,1,0:T(8,128)(2,1)S(1)}, bf16[2,512,128]{2,1,0:T(8,128)(2,1)S(1)}, u32[]{:S(2)}, u32[]{:S(2)}) collective-permute-start(bf16[2,512,128]{2,1,0:T(8,128)(2,1)S(1)} %get-tuple-element.36.refs_0_), channel_id=1, source_target_pairs={{8,0},{9,1},{10,2},{11,3},{12,4},{13,5},{14,6},{15,7},{16,8},{17,9... | collective-permute-start | bytes 786440 | tf_op jit(solution)/shard_map/ppermute | solution.py:280
  19.5 2.1 %collective-permute-start.5 = (bf16[2,512,128]{2,1,0:T(8,128)(2,1)S(1)}, bf16[2,512,128]{2,1,0:T(8,128)(2,1)S(1)}, u32[]{:S(2)}, u32[]{:S(2)}) collective-permute-start(bf16[2,512,128]{2,1,0:T(8,128)(2,1)S(1)} %get-tuple-element.36.refs_0_), channel_id=1, source_target_pairs={{16,0},{17,1},{18,2},{19,3},{20,4},{21,5},{22,6},{23,7},{24,8},{25... | collective-permute-start | bytes 786440 | tf_op jit(solution)/shard_map/ppermute | solution.py:280
  21.6 0.7 copy-done.9
  22.3 6.0 %forecast_interior.1 = (f32[34,64,256]{2,1,0:T(8,128)}, bf16[8,608,128]{2,1,0:T(8,128)(2,1)}, f32[16,64,256]{2,1,0:T(8,128)S(1)}, f32[8,32,128]{2,1,0:T(8,128)S(1)}, f32[8,128,128]{2,1,0:T(8,128)}) custom-call(f32[64,32,256]{2,1,0:T(8,128)S(1)} %copy-done, f32[32,256]{1,0:T(8,128)S(1)} %copy-done.2, f32[8,128,128]{2,1,0:T(8,128)S(1)} %copy-done.4, ...), custom_call_target="tpu_custom_call" | custom-call | tf_op jit(solution)/shard_map/forecast_interior/pallas_call | solution.py:393
  28.3 4.0 %forecast_edges.1 = (f32[34,64,256]{2,1,0:T(8,128)}, bf16[8,608,128]{2,1,0:T(8,128)(2,1)}, f32[8,128]{1,0:T(8,128)}) custom-call(f32[328,256]{1,0:T(8,128)S(1)} %collective-permute-done.above_ref, f32[328,256]{1,0:T(8,128)S(1)} %collective-permute-done.1.below_ref, f32[32,256]{1,0:T(8,128)S(1)} %copy-done.2, ...), custom_call_target="tpu_custom_call", output_to_operand_aliasing={{0}: (5, {}), {1}: (6, {})} | custom-call | tf_op jit(solution)/shard_map/forecast_edges/pallas_call | solution.py:415
  32.3 2.7 %collective-permute-done.5.refs_3_ = bf16[2,512,128]{2,1,0:T(8,128)(2,1)S(1)} collective-permute-done((bf16[2,512,128]{2,1,0:T(8,128)(2,1)S(1)}, bf16[2,512,128]{2,1,0:T(8,128)(2,1)S(1)}, u32[]{:S(2)}, u32[]{:S(2)}) %collective-permute-start.5) | collective-permute-done | bytes 262176 | tf_op jit(solution)/shard_map/ppermute | solution.py:280
  35.8 1.2 %join_eight.1 = (bf16[8,512,128]{2,1,0:T(8,128)(2,1)S(1)}, bf16[4,512,128]{2,1,0:T(8,128)(2,1)}, bf16[4,512,128]{2,1,0:T(8,128)(2,1)}) custom-call(bf16[2,512,128]{2,1,0:T(8,128)(2,1)S(1)} %get-tuple-element.36.refs_0_, bf16[2,512,128]{2,1,0:T(8,128)(2,1)S(1)} %collective-permute-done.3.refs_1_, bf16[2,512,128]{2,1,0:T(8,128)(2,1)S(1)} %collective-permute-done.4.refs_2_, ...), custom_call_target="tpu_custom_call" | custom-call | tf_op jit(solution)/shard_map/join_eight/pallas_call | solution.py:307
  36.9 3.3 %collective-permute-start.6 = (bf16[8,512,128]{2,1,0:T(8,128)(2,1)S(1)}, bf16[8,512,128]{2,1,0:T(8,128)(2,1)S(1)}, u32[]{:S(2)}, u32[]{:S(2)}) collective-permute-start(bf16[8,512,128]{2,1,0:T(8,128)(2,1)S(1)} %get-tuple-element.38.rest_0_), channel_id=1, source_target_pairs={{1,0},{2,1},{3,2},{4,3},{5,4},{6,5},{7,6},{0,7},{9,8},{10,9},{11,1... | collective-permute-start | bytes 3145736 | tf_op jit(solution)/shard_map/ppermute | solution.py:280
  40.2 1.6 %collective-permute-start.11 = (bf16[4,512,128]{2,1,0:T(8,128)(2,1)}, bf16[4,512,128]{2,1,0:T(8,128)(2,1)}, u32[]{:S(2)}, u32[]{:S(2)}) collective-permute-start(bf16[4,512,128]{2,1,0:T(8,128)(2,1)} %get-tuple-element.41), channel_id=1, source_target_pairs={{2,0},{3,1},{4,2},{5,3},{6,4},{7,5},{0,6},{1,7},{10,8},{11,9},{12,... | collective-permute-start | bytes 1572872 | tf_op jit(solution)/shard_map/ppermute | solution.py:280
  41.8 1.3 %collective-permute-start.12 = (bf16[4,512,128]{2,1,0:T(8,128)(2,1)}, bf16[4,512,128]{2,1,0:T(8,128)(2,1)}, u32[]{:S(2)}, u32[]{:S(2)}) collective-permute-start(bf16[4,512,128]{2,1,0:T(8,128)(2,1)} %get-tuple-element.42), channel_id=1, source_target_pairs={{6,0},{7,1},{0,2},{1,3},{2,4},{3,5},{4,6},{5,7},{14,8},{15,9},{8,1... | collective-permute-start | bytes 1572872 | tf_op jit(solution)/shard_map/ppermute | solution.py:280
  43.2 6.9 %all-to-all-start = ((bf16[8,608,128]{2,1,0:T(8,128)(2,1)}), bf16[8,608,128]{2,1,0:T(8,128)(2,1)S(1)}, u32[]{:S(2)}, u32[]{:S(2)}) async-start(bf16[8,608,128]{2,1,0:T(8,128)(2,1)} %get-tuple-element.35), calls=%async_computation | async-start | bytes 2490368 | tf_op jit(solution)/shard_map/all_to_all | solution.py:435
  50.1 13.1 %collective-permute-done.6.rest_1_ = bf16[8,512,128]{2,1,0:T(8,128)(2,1)S(1)} collective-permute-done((bf16[8,512,128]{2,1,0:T(8,128)(2,1)S(1)}, bf16[8,512,128]{2,1,0:T(8,128)(2,1)S(1)}, u32[]{:S(2)}, u32[]{:S(2)}) %collective-permute-start.6) | collective-permute-done | bytes 1048608 | tf_op jit(solution)/shard_map/ppermute | solution.py:280
  63.2 3.5 %collective-permute-done.7.rest_2_ = bf16[8,512,128]{2,1,0:T(8,128)(2,1)} collective-permute-done((bf16[8,512,128]{2,1,0:T(8,128)(2,1)S(1)}, bf16[8,512,128]{2,1,0:T(8,128)(2,1)}, u32[]{:S(2)}, u32[]{:S(2)}) %collective-permute-start.7) | collective-permute-done | bytes 1048608 | tf_op jit(solution)/shard_map/ppermute | solution.py:280
  66.9 0.7 fusion.13
  68.6 1.1 %collective-permute-done.10.rest_5_ = bf16[8,512,128]{2,1,0:T(8,128)(2,1)} collective-permute-done((bf16[8,512,128]{2,1,0:T(8,128)(2,1)}, bf16[8,512,128]{2,1,0:T(8,128)(2,1)}, u32[]{:S(2)}, u32[]{:S(2)}) %collective-permute-start.10) | collective-permute-done | bytes 1048608 | tf_op jit(solution)/shard_map/ppermute | solution.py:280
  69.7 3.0 %collect.1 = (bf16[2,24,512,128]{3,2,1,0:T(8,128)(2,1)S(1)}, bf16[9,512,128]{2,1,0:T(8,128)(2,1)S(1)}) custom-call(bf16[8,608,128]{2,1,0:T(8,128)(2,1)S(1)} %all-to-all-done.recv_ref, bf16[8,512,128]{2,1,0:T(8,128)(2,1)S(1)} %get-tuple-element.38.rest_0_, bf16[8,512,128]{2,1,0:T(8,128)(2,1)S(1)} %collective-permute-done.6.rest_1_, ...), custom_call_target="tpu_custom_call" | custom-call | tf_op jit(solution)/shard_map/collect/pallas_call | solution.py:446
  72.8 5.6 %analysis.1 = bf16[8,576,128]{2,1,0:T(8,128)(2,1)S(1)} custom-call(s32[9,4]{1,0:T(8,128)S(1)} %get-tuple-element.44.anom_at_ref, s32[9,4]{1,0:T(8,128)S(1)} %get-tuple-element.43.weight_at_ref, s32[9,4]{1,0:T(8,128)S(1)} %pad_add_fusion.1.tapers_ref, f32[8,128,128]{2,1,0:T(8,128)S(1)} %copy-done.3, bf16[9,512,128]{2,1,0:T(8,128)(2,1)S(1)} %get-tuple-element.39.centred_ref, ...), custom_call_target="tpu_custom_call" | custom-call | tf_op jit(solution)/shard_map/analysis/pallas_call | solution.py:457
  78.4 21.0 %all_to_all.10.inc_ref = bf16[8,576,128]{2,1,0:T(8,128)(2,1)S(1)} all-to-all(bf16[8,576,128]{2,1,0:T(8,128)(2,1)S(1)} %analysis.1), channel_id=1, replica_groups=mesh['mem'=8,'state'=32] {'mem'}, dimensions={0} | all-to-all | bytes 2359296 | tf_op jit(solution)/shard_map/all_to_all | solution.py:466
  99.4 2.9 %final_step.1 = f32[64,32,256]{2,1,0:T(8,128)} custom-call(f32[34,64,256]{2,1,0:T(8,128)S(1)} %copy-done.1, bf16[8,576,128]{2,1,0:T(8,128)(2,1)S(1)} %all_to_all.10.inc_ref, f32[32,256]{1,0:T(8,128)S(1)} %copy-done.2), custom_call_target="tpu_custom_call" | custom-call | tf_op jit(solution)/shard_map/final_step/pallas_call | solution.py:468
  (53 shorter events, 1.9 us)
Async XLA Ops:
  1.7 14.1 %collective-permute-start.2 = (bf16[1,512,128]{2,1,0:T(8,128)(2,1)}, bf16[1,512,128]{2,1,0:T(8,128)(2,1)S(1)}, u32[]{:S(2)}, u32[]{:S(2)}) collective-permute-start(bf16[1,512,128]{2,1,0:T(8,128)(2,1)} %get-tuple-element.27.own_ref), channel_id=1, source_target_pairs={{4,0},{5,1},{6,2},{7,3},{0,4},{1,5},{2,6},{3,7},{12,8},{13,9},{14,... | collective-permute-start | bytes 393224 | tf_op jit(solution)/shard_map/ppermute | solution.py:280
  9.5 6.3 %copy-start.7 = (bf16[1,512,128]{2,1,0:T(8,128)(2,1)S(1)}, bf16[1,512,128]{2,1,0:T(8,128)(2,1)}, u32[]{:S(2)}) copy-start(bf16[1,512,128]{2,1,0:T(8,128)(2,1)} %get-tuple-element.27.own_ref) | copy-start | bytes 393220
  9.5 12.1 %copy-start = (f32[64,32,256]{2,1,0:T(8,128)S(1)}, f32[64,32,256]{2,1,0:T(8,128)}, u32[]{:S(2)}) copy-start(f32[64,32,256]{2,1,0:T(8,128)} %x_ref.1) | copy-start | bytes 6291460
  9.5 12.1 %copy-start.2 = (f32[32,256]{1,0:T(8,128)S(1)}, f32[32,256]{1,0:T(8,128)}, u32[]{:S(2)}) copy-start(f32[32,256]{1,0:T(8,128)} %coef_ref.7) | copy-start | bytes 98308
  9.5 12.1 %copy-start.4 = (f32[8,128,128]{2,1,0:T(8,128)S(1)}, f32[8,128,128]{2,1,0:T(8,128)}, u32[]{:S(2)}) copy-start(f32[8,128,128]{2,1,0:T(8,128)} %taper_ref.1) | copy-start | bytes 1572868
  11.9 16.4 %collective-permute-start = (f32[328,256]{1,0:T(8,128)}, f32[328,256]{1,0:T(8,128)S(1)}, u32[]{:S(2)}, u32[]{:S(2)}) collective-permute-start(f32[328,256]{1,0:T(8,128)} %get-tuple-element.25), channel_id=1, source_target_pairs={{0,1},{1,2},{2,3},{3,4},{4,5},{5,6},{6,7},{7,8},{8,9},{9,10},{10,1... | collective-permute-start | bytes 1007624 | tf_op jit(solution)/shard_map/ppermute | solution.py:389
  14.5 13.7 %collective-permute-start.1 = (f32[328,256]{1,0:T(8,128)}, f32[328,256]{1,0:T(8,128)S(1)}, u32[]{:S(2)}, u32[]{:S(2)}) collective-permute-start(f32[328,256]{1,0:T(8,128)} %get-tuple-element.26), channel_id=1, source_target_pairs={{1,0},{2,1},{3,2},{4,3},{5,4},{6,5},{7,6},{8,7},{9,8},{10,9},{11,1... | collective-permute-start | bytes 1007624 | tf_op jit(solution)/shard_map/ppermute | solution.py:388
  15.9 16.5 %collective-permute-start.3 = (bf16[2,512,128]{2,1,0:T(8,128)(2,1)S(1)}, bf16[2,512,128]{2,1,0:T(8,128)(2,1)S(1)}, u32[]{:S(2)}, u32[]{:S(2)}) collective-permute-start(bf16[2,512,128]{2,1,0:T(8,128)(2,1)S(1)} %get-tuple-element.36.refs_0_), channel_id=1, source_target_pairs={{8,0},{9,1},{10,2},{11,3},{12,4},{13,5},{14,6},{15,7},{16,8},{17,9... | collective-permute-start | bytes 786440 | tf_op jit(solution)/shard_map/ppermute | solution.py:280
  19.5 12.8 %collective-permute-start.4 = (bf16[2,512,128]{2,1,0:T(8,128)(2,1)S(1)}, bf16[2,512,128]{2,1,0:T(8,128)(2,1)S(1)}, u32[]{:S(2)}, u32[]{:S(2)}) collective-permute-start(bf16[2,512,128]{2,1,0:T(8,128)(2,1)S(1)} %get-tuple-element.36.refs_0_), channel_id=1, source_target_pairs={{24,0},{25,1},{26,2},{27,3},{28,4},{29,5},{30,6},{31,7},{0,8},{1,9... | collective-permute-start | bytes 786440 | tf_op jit(solution)/shard_map/ppermute | solution.py:280
  19.5 15.6 %collective-permute-start.5 = (bf16[2,512,128]{2,1,0:T(8,128)(2,1)S(1)}, bf16[2,512,128]{2,1,0:T(8,128)(2,1)S(1)}, u32[]{:S(2)}, u32[]{:S(2)}) collective-permute-start(bf16[2,512,128]{2,1,0:T(8,128)(2,1)S(1)} %get-tuple-element.36.refs_0_), channel_id=1, source_target_pairs={{16,0},{17,1},{18,2},{19,3},{20,4},{21,5},{22,6},{23,7},{24,8},{25... | collective-permute-start | bytes 786440 | tf_op jit(solution)/shard_map/ppermute | solution.py:280
  36.9 26.2 %collective-permute-start.6 = (bf16[8,512,128]{2,1,0:T(8,128)(2,1)S(1)}, bf16[8,512,128]{2,1,0:T(8,128)(2,1)S(1)}, u32[]{:S(2)}, u32[]{:S(2)}) collective-permute-start(bf16[8,512,128]{2,1,0:T(8,128)(2,1)S(1)} %get-tuple-element.38.rest_0_), channel_id=1, source_target_pairs={{1,0},{2,1},{3,2},{4,3},{5,4},{6,5},{7,6},{0,7},{9,8},{10,9},{11,1... | collective-permute-start | bytes 3145736 | tf_op jit(solution)/shard_map/ppermute | solution.py:280
  40.2 26.5 %collective-permute-start.7 = (bf16[8,512,128]{2,1,0:T(8,128)(2,1)S(1)}, bf16[8,512,128]{2,1,0:T(8,128)(2,1)}, u32[]{:S(2)}, u32[]{:S(2)}) collective-permute-start(bf16[8,512,128]{2,1,0:T(8,128)(2,1)S(1)} %get-tuple-element.38.rest_0_), channel_id=1, source_target_pairs={{7,0},{0,1},{1,2},{2,3},{3,4},{4,5},{5,6},{6,7},{15,8},{8,9},{9,10... | collective-permute-start | bytes 3145736 | tf_op jit(solution)/shard_map/ppermute | solution.py:280
  40.2 27.6 %collective-permute-start.11 = (bf16[4,512,128]{2,1,0:T(8,128)(2,1)}, bf16[4,512,128]{2,1,0:T(8,128)(2,1)}, u32[]{:S(2)}, u32[]{:S(2)}) collective-permute-start(bf16[4,512,128]{2,1,0:T(8,128)(2,1)} %get-tuple-element.41), channel_id=1, source_target_pairs={{2,0},{3,1},{4,2},{5,3},{6,4},{7,5},{0,6},{1,7},{10,8},{11,9},{12,... | collective-permute-start | bytes 1572872 | tf_op jit(solution)/shard_map/ppermute | solution.py:280
  41.8 26.5 %collective-permute-start.12 = (bf16[4,512,128]{2,1,0:T(8,128)(2,1)}, bf16[4,512,128]{2,1,0:T(8,128)(2,1)}, u32[]{:S(2)}, u32[]{:S(2)}) collective-permute-start(bf16[4,512,128]{2,1,0:T(8,128)(2,1)} %get-tuple-element.42), channel_id=1, source_target_pairs={{6,0},{7,1},{0,2},{1,3},{2,4},{3,5},{4,6},{5,7},{14,8},{15,9},{8,1... | collective-permute-start | bytes 1572872 | tf_op jit(solution)/shard_map/ppermute | solution.py:280
  43.2 23.5 %copy-start.10 = (s32[64,4]{0,1:T(4,128)S(1)}, s32[64,4]{0,1:T(4,128)}, u32[]{:S(2)}) copy-start(s32[64,4]{0,1:T(4,128)} %param.12) | copy-start | bytes 3076
  43.2 23.5 %copy-start.11 = (s32[64,4]{0,1:T(4,128)S(1)}, s32[64,4]{0,1:T(4,128)}, u32[]{:S(2)}) copy-start(s32[64,4]{0,1:T(4,128)} %param.13) | copy-start | bytes 3076
  43.2 25.4 %all-to-all-start = ((bf16[8,608,128]{2,1,0:T(8,128)(2,1)}), bf16[8,608,128]{2,1,0:T(8,128)(2,1)S(1)}, u32[]{:S(2)}, u32[]{:S(2)}) async-start(bf16[8,608,128]{2,1,0:T(8,128)(2,1)} %get-tuple-element.35), calls=%async_computation | async-start | bytes 2490368 | tf_op jit(solution)/shard_map/all_to_all | solution.py:435
  50.1 18.5 %collective-permute-start.8 = (bf16[8,512,128]{2,1,0:T(8,128)(2,1)S(1)}, bf16[8,512,128]{2,1,0:T(8,128)(2,1)}, u32[]{:S(2)}, u32[]{:S(2)}) collective-permute-start(bf16[8,512,128]{2,1,0:T(8,128)(2,1)S(1)} %get-tuple-element.38.rest_0_), channel_id=1, source_target_pairs={{32,0},{33,1},{34,2},{35,3},{36,4},{37,5},{38,6},{39,7},{40,8},{41... | collective-permute-start | bytes 3145736 | tf_op jit(solution)/shard_map/ppermute | solution.py:280
  63.2 5.4 %collective-permute-start.9 = (bf16[8,512,128]{2,1,0:T(8,128)(2,1)S(1)}, bf16[8,512,128]{2,1,0:T(8,128)(2,1)}, u32[]{:S(2)}, u32[]{:S(2)}) collective-permute-start(bf16[8,512,128]{2,1,0:T(8,128)(2,1)S(1)} %collective-permute-done.6.rest_1_), channel_id=1, source_target_pairs={{32,0},{33,1},{34,2},{35,3},{36,4},{37,5},{38,6},{39,7},{40,8},{41... | collective-permute-start | bytes 3145736 | tf_op jit(solution)/shard_map/ppermute | solution.py:280
  66.7 3.0 %collective-permute-start.10 = (bf16[8,512,128]{2,1,0:T(8,128)(2,1)}, bf16[8,512,128]{2,1,0:T(8,128)(2,1)}, u32[]{:S(2)}, u32[]{:S(2)}) collective-permute-start(bf16[8,512,128]{2,1,0:T(8,128)(2,1)} %collective-permute-done.7.rest_2_), channel_id=1, source_target_pairs={{32,0},{33,1},{34,2},{35,3},{36,4},{37,5},{38,6},{39,7},{40,8},{41... | collective-permute-start | bytes 3145736 | tf_op jit(solution)/shard_map/ppermute | solution.py:280
  67.8 4.9 %collective-permute-start.13 = (bf16[4,512,128]{2,1,0:T(8,128)(2,1)}, bf16[4,512,128]{2,1,0:T(8,128)(2,1)}, u32[]{:S(2)}, u32[]{:S(2)}) collective-permute-start(bf16[4,512,128]{2,1,0:T(8,128)(2,1)} %collective-permute-done.11.rest_0_), channel_id=1, source_target_pairs={{32,0},{33,1},{34,2},{35,3},{36,4},{37,5},{38,6},{39,7},{40,8},{41... | collective-permute-start | bytes 1572872 | tf_op jit(solution)/shard_map/ppermute | solution.py:280
  68.4 4.4 %collective-permute-start.14 = (bf16[4,512,128]{2,1,0:T(8,128)(2,1)}, bf16[4,512,128]{2,1,0:T(8,128)(2,1)}, u32[]{:S(2)}, u32[]{:S(2)}) collective-permute-start(bf16[4,512,128]{2,1,0:T(8,128)(2,1)} %collective-permute-done.12.rest_1_), channel_id=1, source_target_pairs={{32,0},{33,1},{34,2},{35,3},{36,4},{37,5},{38,6},{39,7},{40,8},{41... | collective-permute-start | bytes 1572872 | tf_op jit(solution)/shard_map/ppermute | solution.py:280
  68.6 4.2 %copy-start.3 = (f32[8,128,128]{2,1,0:T(8,128)S(1)}, f32[8,128,128]{2,1,0:T(8,128)}, u32[]{:S(2)}) copy-start(f32[8,128,128]{2,1,0:T(8,128)} %get-tuple-element.34.taper_ref) | copy-start | bytes 1572868
  78.4 21.0 %copy-start.1 = (f32[34,64,256]{2,1,0:T(8,128)S(1)}, f32[34,64,256]{2,1,0:T(8,128)}, u32[]{:S(2)}) copy-start(f32[34,64,256]{2,1,0:T(8,128)} %get-tuple-element.33.prior_ref) | copy-start | bytes 6684676
  (4 other events, 9.5 us)

commit v10 on v9

--- a/solution.py
+++ b/solution.py
@@ -110,13 +110,15 @@
         copy.wait()
 
 
-def edge_kernel(above_ref, below_ref, coef_ref, edge_ref, mean_ref, prior_in, pay_in, prior_ref, out_ref, token_ref, a_ref, b_ref, c_ref, pay_ref, m_ref, last_ref, sems):
+def edge_kernel(above_ref, below_ref, coef_ref, edge_ref, mean_ref, prior_in, pay_in, prior_ref, out_ref, ids_ref, token_ref, a_ref, b_ref, c_ref, pay_ref, m_ref, last_ref, sems):
     rows, columns = coef_ref.shape
     members = last_ref.shape[2]
     group, size, _ = out_ref.shape
     per = rows // group
     tiles = 2 * per + 1
     halos = (above_ref, below_ref)
+    sides = [ref[HALO * members :, 0:TILE].astype(jnp.int32) for ref in halos]
+    ids_ref[...] = jnp.where(lax.axis_index("mem") < 2, sides[0], sides[1])
     for side in range(2):
         for t in range(HALO + FSTEPS):
             if t < HALO:
@@ -207,13 +209,19 @@
         centred_ref[t] = (local + delta[:, None, :]).astype(BF16).reshape(members, TILE)
 
 
-def analysis_kernel(anom_at_ref, weight_at_ref, tapers_ref, taper_ref, centred_ref, early_ref, *rest):
+def analysis_kernel(block_ref, pattern_ref, edge_ref, taper_ref, centred_ref, early_ref, *rest):
     pieces, (ret_ref, late_ref) = rest[:-2], rest[-2:]
     tiles, members, _ = centred_ref.shape
     group = ret_ref.shape[0]
     count = members // group
     early = early_ref.shape[1]
     fill(pieces, late_ref)
+    slab, state = lax.axis_index("mem"), lax.axis_index("state")
+    y, z, half = state // 8, lax.rem(state, 8), lax.rem(slab, 2)
+
+    def number(ref, t, k, first):
+        usual = ref[k, slab * (tiles - 1) + jnp.minimum(t, tiles - 2)]
+        return jnp.where(t < tiles - 1, usual, edge_ref[7, first + half * SLOTS + k])
 
     def block(kind, at):
         near = early_ref[kind, jnp.minimum(at, early - 1)]
@@ -223,12 +231,13 @@
     def one(t, carry):
         anoms, weights = [], []
         for k in range(SLOTS):
-            anom = block(0, anom_at_ref[t, k])
+            anom_at, weight_at = places(number(block_ref, t, k, 0), y, z)
+            anom = block(0, anom_at)
             anoms.append(jnp.concatenate([anom[q * TILE : (q + 1) * TILE] for q in range(members // TILE)], axis=1))
-            weights.append(block(1, weight_at_ref[t, k]))
+            weights.append(block(1, weight_at))
         cov = jnp.dot(jnp.concatenate(anoms, axis=0), centred_ref[t], preferred_element_type=F32) * (1.0 / (members - 1.0))
         tapered = [
-            (taper_ref[tapers_ref[t, k]] * cov[k * TILE : (k + 1) * TILE]).astype(BF16) for k in range(SLOTS)
+            (taper_ref[number(pattern_ref, t, k, 2 * SLOTS)] * cov[k * TILE : (k + 1) * TILE]).astype(BF16) for k in range(SLOTS)
         ]
         total = jnp.dot(jnp.concatenate(weights, axis=1), jnp.concatenate(tapered, axis=0), preferred_element_type=F32)
         here = pl.ds(pl.multiple_of(t * count, count), count)
@@ -288,27 +297,34 @@
     return (x, 1 - c, y, z)
 
 
-TOKEN = pltpu.HBM((8, TILE), F32)
+TOKEN = jax.ShapeDtypeStruct((8, TILE), F32)
 
 
 def join(operands, name, after):
     count = len(operands)
 
     def kernel(*refs):
-        outs = refs[count + len(after) :]
+        outs, sems = refs[count + len(after) : -1], refs[-1]
         core = lax.rem(lax.axis_index("mem"), 2)
+        copies = []
+        for a in range(count):
+            copies.append(pltpu.make_async_copy(refs[a].at[0], outs[1].at[a], sems.at[2 * a]))
+            copies.append(pltpu.make_async_copy(refs[a].at[core], outs[2].at[a], sems.at[2 * a + 1]))
+        for copy in copies:
+            copy.start()
         for a in range(count):
             for i in range(2):
                 outs[0][i * count + a] = refs[a][i]
-            outs[1][a] = refs[a][0]
-            outs[2][a] = refs[a][core]
-
-    shapes = [(n, *operands[0].shape[1:]) for n in (2 * count, count, count)]
+        for copy in copies:
+            copy.wait()
+
+    block = operands[0].shape[1:]
     return pl.pallas_call(
         kernel,
-        out_shape=[jax.ShapeDtypeStruct(shape, BF16) for shape in shapes],
+        out_shape=[jax.ShapeDtypeStruct((2 * count, *block), BF16)] + [pltpu.HBM((count, *block), BF16)] * 2,
         in_specs=[VMEM] * count + [HBM] * len(after),
-        out_specs=[VMEM] * len(shapes),
+        out_specs=[VMEM] + [HBM] * 2,
+        scratch_shapes=[pltpu.SemaphoreType.DMA((2 * count,))],
         compiler_params=pltpu.CompilerParams(vmem_limit_bytes=6 << 20),
         name=name,
     )(*operands, *after)
@@ -345,10 +361,10 @@
 
 
 def places(block, y, z):
-    dy, dz = (block // 8 - y) % 4, (block % 8 - z) % 8
-    low = dz % 4
+    dy, dz = (block // 8 - y) & 3, (block - z) & 7
+    low = dz & 3
     gray_y, gray_z = dy ^ (dy >> 1), low ^ (low >> 1)
-    high = 4 * ((dz // 4) ^ (low == 3).astype(jnp.int32))
+    high = 4 * ((dz >> 2) ^ jnp.where(low == 3, 1, 0))
     return 8 * gray_z + high + gray_y, 8 * gray_y + high + gray_z
 
 
@@ -360,7 +376,6 @@
     tiles = 2 * per + 1
     size = tiles * members + 32
 
-    j, at = lax.axis_index("mem"), lax.axis_index("state")
     chips = (group // 2, states // 8, 8)
     packed, obs_packed = pl.pallas_call(
         pack_obs_kernel,
@@ -412,11 +427,11 @@
         compiler_params=pltpu.CompilerParams(vmem_limit_bytes=14 << 20),
         name="forecast_interior",
     )(ensemble, spreading_coefficient, taper_table, started)
-    prior, payload, forecast_done = pl.pallas_call(
+    prior, payload, edge_ids, forecast_done = pl.pallas_call(
         edge_kernel,
-        out_shape=[pltpu.HBM(prior.shape, F32), pltpu.HBM(payload.shape, BF16), TOKEN],
+        out_shape=[pltpu.HBM(prior.shape, F32), pltpu.HBM(payload.shape, BF16), jax.ShapeDtypeStruct((8, TILE), jnp.int32), TOKEN],
         in_specs=[VMEM] * 5 + [HBM] * 2,
-        out_specs=[HBM] * 3,
+        out_specs=[HBM] * 2 + [VMEM, HBM],
         input_output_aliases={5: 0, 6: 1},
         scratch_shapes=[
             pltpu.VMEM((2, HALO + FSTEPS, *row), F32),
@@ -434,13 +449,6 @@
     own, swapped = gather_rest(held, first, second, chips)
     gathered = lax.all_to_all(payload, "mem", split_axis=0, concat_axis=0, tiled=True)
 
-    edge = jnp.where(j < 2, above[-1, :16], below[-1, :16])
-    edge = jnp.where(j % 2 == 0, edge.reshape(-1, 4)[:3:2], edge.reshape(-1, 4)[1:4:2]).astype(jnp.int32)
-    mine = 2 * per * j
-    blocks = jnp.concatenate([lax.dynamic_slice_in_dim(obs_block, mine, 2 * per, 0), edge[0:1]], axis=0)
-    tapers = jnp.concatenate([lax.dynamic_slice_in_dim(taper_id, mine, 2 * per, 0), edge[1:2]], axis=0)
-
-    anom_at, weight_at = places(blocks, at // 8, at % 8)
     late = 2
     early = own[:-late] + swapped[:-late]
     held_early, centred = pl.pallas_call(
@@ -462,7 +470,7 @@
         scratch_shapes=[pltpu.VMEM((2, sum(v.shape[0] for v in own[-late:]), *packed.shape[1:]), BF16)],
         compiler_params=pltpu.CompilerParams(vmem_limit_bytes=18 << 20),
         name="analysis",
-    )(anom_at, weight_at, tapers, turned, centred, held_early, *own[-late:], *swapped[-late:])
+    )(obs_block.T, taper_id.T, edge_ids, turned, centred, held_early, *own[-late:], *swapped[-late:])
     returned = lax.all_to_all(increments, "mem", split_axis=0, concat_axis=0, tiled=True)
 
     return pl.pallas_call(

time: 103 us -> 110 us (1.068)
  starting transfers between devices: 31.3 us -> 42.5 us
  local copies, waits for them, and re-layouts: 1.78 us -> 0.03 us
    ppermute x13, starting transfers between devices: 20.5 us -> 31.7 us  [fetch(): return lax.ppermute(value, AXES, pairs)]
    unnamed x26 -> x16, local copies, waits for them, and re-layouts: 1.56 us -> 0.03 us
  transfers between devices with their start and end apart: 16 -> 16, of which waited for: 4 -> 4; matrix products, arithmetic and copies ran while one was open for 1% -> 0% of each run, Pallas kernels for 15% -> 14%
where the time goes in v10:
time: 110 us
  starting transfers between devices  42.5 us (39%)
  Pallas kernels  26.6 us (24%)
  blocking collectives  21 us (19%)
  waiting for transfers between devices  19.7 us (18%)
    ppermute x13, starting transfers between devices, fetch(): return lax.ppermute(value, AXES, pairs)  31.7 us
    all_to_all x1, blocking collectives, body(): lax.all_to_all(increments, 'mem', split_axis=0, concat_axis=0, tiled=True)  21 us
    ppermute x13, waiting for transfers between devices, fetch(): return lax.ppermute(value, AXES, pairs)  19.7 us
    all_to_all x1, starting transfers between devices, body(): lax.all_to_all(payload, 'mem', split_axis=0, concat_axis=0, tiled=True)  6.82 us
    pallas_call x1, Pallas kernels, body(): pl.pallas_call(interior_kernel, out_shape=[pltpu.HBM((rows + 2, *row), F3...  5.75 us
    pallas_call x1, Pallas kernels, body(): pl.pallas_call(analysis_kernel, out_shape=jax.ShapeDtypeStruct((group, ti...  5.59 us
    pallas_call x1, Pallas kernels, body(): pl.pallas_call(edge_kernel, out_shape=[pltpu.HBM(prior.shape, F32), pltpu...  4.04 us
    pallas_call x1, Pallas kernels, body(): pl.pallas_call(collect_kernel, out_shape=[jax.ShapeDtypeStruct((2, sum((v...  3.1 us
  transfers between devices with their start and end apart: 16, of which 4 were waited for; matrix products, arithmetic and copies ran while one was open for 0% of the time, Pallas kernels for 14%

profile of v10, /device:TPU:1, one launch (start us, length us, event | category | flops | bytes accessed | tf_op | source)
XLA Modules:
  0.0 110.0 jit_solution(6146541131445022484)
XLA Ops:
  0.0 1.7 %pack_obs.1 = (bf16[1,512,128]{2,1,0:T(8,128)(2,1)}, f32[8,128]{1,0:T(8,128)}) custom-call(bf16[1,128,512]{2,1,0:T(8,128)(2,1)} %anom_ref.1, bf16[1,128,512]{2,1,0:T(8,128)(2,1)} %weight_ref.1), custom_call_target="tpu_custom_call" | custom-call | tf_op jit(solution)/shard_map/pack_obs/pallas_call | solution.py:380
  1.7 7.8 %collective-permute-start.2 = (bf16[1,512,128]{2,1,0:T(8,128)(2,1)}, bf16[1,512,128]{2,1,0:T(8,128)(2,1)S(1)}, u32[]{:S(2)}, u32[]{:S(2)}) collective-permute-start(bf16[1,512,128]{2,1,0:T(8,128)(2,1)} %get-tuple-element.28.own_ref), channel_id=1, source_target_pairs={{4,0},{5,1},{6,2},{7,3},{0,4},{1,5},{2,6},{3,7},{12,8},{13,9},{14,... | collective-permute-start | bytes 393224 | tf_op jit(solution)/shard_map/ppermute | solution.py:289
  9.5 2.3 %pack_halo.1 = (f32[328,256]{1,0:T(8,128)}, f32[328,256]{1,0:T(8,128)}) custom-call(f32[64,32,256]{2,1,0:T(8,128)} %x_ref.1, f32[64,32,256]{2,1,0:T(8,128)} %x_ref.1, f32[32,256]{1,0:T(8,128)} %coef_ref.7, s32[4,64]{1,0:T(4,128)} %bitcast.2, s32[4,64]{1,0:T(4,128)} %bitcast.4, f32[8,128]{1,0:T(8,128)} %get-tuple-element.25.after_ref), custom_call_target="tpu_custom_call" | custom-call | tf_op jit(solution)/shard_map/pack_halo/pallas_call | solution.py:388
  11.8 2.7 %collective-permute-start = (f32[328,256]{1,0:T(8,128)}, f32[328,256]{1,0:T(8,128)S(1)}, u32[]{:S(2)}, u32[]{:S(2)}) collective-permute-start(f32[328,256]{1,0:T(8,128)} %get-tuple-element.26), channel_id=1, source_target_pairs={{0,1},{1,2},{2,3},{3,4},{4,5},{5,6},{6,7},{7,8},{8,9},{9,10},{10,1... | collective-permute-start | bytes 1007624 | tf_op jit(solution)/shard_map/ppermute | solution.py:404
  14.5 1.3 %collective-permute-start.1 = (f32[328,256]{1,0:T(8,128)}, f32[328,256]{1,0:T(8,128)S(1)}, u32[]{:S(2)}, u32[]{:S(2)}) collective-permute-start(f32[328,256]{1,0:T(8,128)} %get-tuple-element.27), channel_id=1, source_target_pairs={{1,0},{2,1},{3,2},{4,3},{5,4},{6,5},{7,6},{8,7},{9,8},{10,9},{11,1... | collective-permute-start | bytes 1007624 | tf_op jit(solution)/shard_map/ppermute | solution.py:403
  15.9 3.6 %collective-permute-start.3 = (bf16[2,512,128]{2,1,0:T(8,128)(2,1)S(1)}, bf16[2,512,128]{2,1,0:T(8,128)(2,1)S(1)}, u32[]{:S(2)}, u32[]{:S(2)}) collective-permute-start(bf16[2,512,128]{2,1,0:T(8,128)(2,1)S(1)} %get-tuple-element.38.refs_0_), channel_id=1, source_target_pairs={{8,0},{9,1},{10,2},{11,3},{12,4},{13,5},{14,6},{15,7},{16,8},{17,9... | collective-permute-start | bytes 786440 | tf_op jit(solution)/shard_map/ppermute | solution.py:289
  19.5 2.1 %collective-permute-start.5 = (bf16[2,512,128]{2,1,0:T(8,128)(2,1)S(1)}, bf16[2,512,128]{2,1,0:T(8,128)(2,1)S(1)}, u32[]{:S(2)}, u32[]{:S(2)}) collective-permute-start(bf16[2,512,128]{2,1,0:T(8,128)(2,1)S(1)} %get-tuple-element.38.refs_0_), channel_id=1, source_target_pairs={{16,0},{17,1},{18,2},{19,3},{20,4},{21,5},{22,6},{23,7},{24,8},{25... | collective-permute-start | bytes 786440 | tf_op jit(solution)/shard_map/ppermute | solution.py:289
  21.6 5.8 %forecast_interior.1 = (f32[34,64,256]{2,1,0:T(8,128)}, bf16[8,608,128]{2,1,0:T(8,128)(2,1)}, f32[16,64,256]{2,1,0:T(8,128)S(1)}, f32[8,32,128]{2,1,0:T(8,128)S(1)}, f32[8,128,128]{2,1,0:T(8,128)}) custom-call(f32[64,32,256]{2,1,0:T(8,128)S(1)} %copy-done, f32[32,256]{1,0:T(8,128)S(1)} %copy-done.2, f32[8,128,128]{2,1,0:T(8,128)S(1)} %copy-done.4, ...), custom_call_target="tpu_custom_call" | custom-call | tf_op jit(solution)/shard_map/forecast_interior/pallas_call | solution.py:408
  27.3 4.0 %forecast_edges.1 = (f32[34,64,256]{2,1,0:T(8,128)}, bf16[8,608,128]{2,1,0:T(8,128)(2,1)}, s32[8,128]{1,0:T(8,128)S(1)}, f32[8,128]{1,0:T(8,128)S(1)}) custom-call(f32[328,256]{1,0:T(8,128)S(1)} %collective-permute-done.above_ref, f32[328,256]{1,0:T(8,128)S(1)} %collective-permute-done.1.below_ref, ...), custom_call_target="tpu_custom_call", output_to_operand_aliasing={{0}: (5, {}), {1}: (6, {})} | custom-call | tf_op jit(solution)/shard_map/forecast_edges/pallas_call | solution.py:430
  31.4 3.7 %collective-permute-done.5.refs_3_ = bf16[2,512,128]{2,1,0:T(8,128)(2,1)S(1)} collective-permute-done((bf16[2,512,128]{2,1,0:T(8,128)(2,1)S(1)}, bf16[2,512,128]{2,1,0:T(8,128)(2,1)S(1)}, u32[]{:S(2)}, u32[]{:S(2)}) %collective-permute-start.5) | collective-permute-done | bytes 262176 | tf_op jit(solution)/shard_map/ppermute | solution.py:289
  35.1 1.1 %join_eight.1 = (bf16[8,512,128]{2,1,0:T(8,128)(2,1)S(1)}, bf16[4,512,128]{2,1,0:T(8,128)(2,1)}, bf16[4,512,128]{2,1,0:T(8,128)(2,1)}) custom-call(bf16[2,512,128]{2,1,0:T(8,128)(2,1)S(1)} %get-tuple-element.38.refs_0_, bf16[2,512,128]{2,1,0:T(8,128)(2,1)S(1)} %collective-permute-done.3.refs_1_, bf16[2,512,128]{2,1,0:T(8,128)(2,1)S(1)} %collective-permute-done.4.refs_2_, ...), custom_call_target="tpu_custom_call" | custom-call | tf_op jit(solution)/shard_map/join_eight/pallas_call | solution.py:322
  36.2 3.3 %collective-permute-start.6 = (bf16[8,512,128]{2,1,0:T(8,128)(2,1)S(1)}, bf16[8,512,128]{2,1,0:T(8,128)(2,1)S(1)}, u32[]{:S(2)}, u32[]{:S(2)}) collective-permute-start(bf16[8,512,128]{2,1,0:T(8,128)(2,1)S(1)} %get-tuple-element.40.rest_0_), channel_id=1, source_target_pairs={{1,0},{2,1},{3,2},{4,3},{5,4},{6,5},{7,6},{0,7},{9,8},{10,9},{11,1... | collective-permute-start | bytes 3145736 | tf_op jit(solution)/shard_map/ppermute | solution.py:289
  39.5 6.8 %all-to-all-start = ((bf16[8,608,128]{2,1,0:T(8,128)(2,1)}), bf16[8,608,128]{2,1,0:T(8,128)(2,1)S(1)}, u32[]{:S(2)}, u32[]{:S(2)}) async-start(bf16[8,608,128]{2,1,0:T(8,128)(2,1)} %get-tuple-element.37), calls=%async_computation | async-start | bytes 2490368 | tf_op jit(solution)/shard_map/all_to_all | solution.py:450
  46.4 2.6 %collective-permute-start.11 = (bf16[4,512,128]{2,1,0:T(8,128)(2,1)}, bf16[4,512,128]{2,1,0:T(8,128)(2,1)}, u32[]{:S(2)}, u32[]{:S(2)}) collective-permute-start(bf16[4,512,128]{2,1,0:T(8,128)(2,1)} %get-tuple-element.43), channel_id=1, source_target_pairs={{2,0},{3,1},{4,2},{5,3},{6,4},{7,5},{0,6},{1,7},{10,8},{11,9},{12,... | collective-permute-start | bytes 1572872 | tf_op jit(solution)/shard_map/ppermute | solution.py:289
  49.0 7.9 %collective-permute-done.6.rest_1_ = bf16[8,512,128]{2,1,0:T(8,128)(2,1)S(1)} collective-permute-done((bf16[8,512,128]{2,1,0:T(8,128)(2,1)S(1)}, bf16[8,512,128]{2,1,0:T(8,128)(2,1)S(1)}, u32[]{:S(2)}, u32[]{:S(2)}) %collective-permute-start.6) | collective-permute-done | bytes 1048608 | tf_op jit(solution)/shard_map/ppermute | solution.py:289
  56.9 3.4 %collective-permute-done.7.rest_2_ = bf16[8,512,128]{2,1,0:T(8,128)(2,1)} collective-permute-done((bf16[8,512,128]{2,1,0:T(8,128)(2,1)S(1)}, bf16[8,512,128]{2,1,0:T(8,128)(2,1)}, u32[]{:S(2)}, u32[]{:S(2)}) %collective-permute-start.7) | collective-permute-done | bytes 1048608 | tf_op jit(solution)/shard_map/ppermute | solution.py:289
  60.3 0.5 collective-permute-start.12
  60.8 4.9 %collective-permute-start.13 = (bf16[4,512,128]{2,1,0:T(8,128)(2,1)}, bf16[4,512,128]{2,1,0:T(8,128)(2,1)}, u32[]{:S(2)}, u32[]{:S(2)}) collective-permute-start(bf16[4,512,128]{2,1,0:T(8,128)(2,1)} %collective-permute-done.11.rest_0_), channel_id=1, source_target_pairs={{32,0},{33,1},{34,2},{35,3},{36,4},{37,5},{38,6},{39,7},{40,8},{41... | collective-permute-start | bytes 1572872 | tf_op jit(solution)/shard_map/ppermute | solution.py:289
  65.7 4.8 %collective-permute-done.12.rest_1_ = bf16[4,512,128]{2,1,0:T(8,128)(2,1)} collective-permute-done((bf16[4,512,128]{2,1,0:T(8,128)(2,1)}, bf16[4,512,128]{2,1,0:T(8,128)(2,1)}, u32[]{:S(2)}, u32[]{:S(2)}) %collective-permute-start.12) | collective-permute-done | bytes 524320 | tf_op jit(solution)/shard_map/ppermute | solution.py:289
  70.5 6.8 %collective-permute-start.14 = (bf16[4,512,128]{2,1,0:T(8,128)(2,1)}, bf16[4,512,128]{2,1,0:T(8,128)(2,1)}, u32[]{:S(2)}, u32[]{:S(2)}) collective-permute-start(bf16[4,512,128]{2,1,0:T(8,128)(2,1)} %collective-permute-done.12.rest_1_), channel_id=1, source_target_pairs={{32,0},{33,1},{34,2},{35,3},{36,4},{37,5},{38,6},{39,7},{40,8},{41... | collective-permute-start | bytes 1572872 | tf_op jit(solution)/shard_map/ppermute | solution.py:289
  77.3 3.1 %collect.1 = (bf16[2,24,512,128]{3,2,1,0:T(8,128)(2,1)S(1)}, bf16[9,512,128]{2,1,0:T(8,128)(2,1)S(1)}) custom-call(bf16[8,608,128]{2,1,0:T(8,128)(2,1)S(1)} %all-to-all-done.recv_ref, bf16[8,512,128]{2,1,0:T(8,128)(2,1)S(1)} %get-tuple-element.40.rest_0_, bf16[8,512,128]{2,1,0:T(8,128)(2,1)S(1)} %collective-permute-done.6.rest_1_, ...), custom_call_target="tpu_custom_call" | custom-call | tf_op jit(solution)/shard_map/collect/pallas_call | solution.py:454
  80.5 5.6 %analysis.1 = bf16[8,576,128]{2,1,0:T(8,128)(2,1)S(1)} custom-call(s32[4,64]{1,0:T(4,128)S(1)} %bitcast.3, s32[4,64]{1,0:T(4,128)S(1)} %bitcast.5, s32[8,128]{1,0:T(8,128)S(1)} %get-tuple-element.35.edge_ref, f32[8,128,128]{2,1,0:T(8,128)S(1)} %copy-done.3, bf16[9,512,128]{2,1,0:T(8,128)(2,1)S(1)} %get-tuple-element.41.centred_ref, ...), custom_call_target="tpu_custom_call" | custom-call | tf_op jit(solution)/shard_map/analysis/pallas_call | solution.py:465
  86.1 21.0 %all_to_all.10.inc_ref = bf16[8,576,128]{2,1,0:T(8,128)(2,1)S(1)} all-to-all(bf16[8,576,128]{2,1,0:T(8,128)(2,1)S(1)} %analysis.1), channel_id=1, replica_groups=mesh['mem'=8,'state'=32] {'mem'}, dimensions={0} | all-to-all | bytes 2359296 | tf_op jit(solution)/shard_map/all_to_all | solution.py:474
  107.0 2.9 %final_step.1 = f32[64,32,256]{2,1,0:T(8,128)} custom-call(f32[34,64,256]{2,1,0:T(8,128)S(1)} %copy-done.1, bf16[8,576,128]{2,1,0:T(8,128)(2,1)S(1)} %all_to_all.10.inc_ref, f32[32,256]{1,0:T(8,128)S(1)} %copy-done.2), custom_call_target="tpu_custom_call" | custom-call | tf_op jit(solution)/shard_map/final_step/pallas_call | solution.py:476
  (34 shorter events, 0.1 us)
Async XLA Ops:
  1.7 14.1 %collective-permute-start.2 = (bf16[1,512,128]{2,1,0:T(8,128)(2,1)}, bf16[1,512,128]{2,1,0:T(8,128)(2,1)S(1)}, u32[]{:S(2)}, u32[]{:S(2)}) collective-permute-start(bf16[1,512,128]{2,1,0:T(8,128)(2,1)} %get-tuple-element.28.own_ref), channel_id=1, source_target_pairs={{4,0},{5,1},{6,2},{7,3},{0,4},{1,5},{2,6},{3,7},{12,8},{13,9},{14,... | collective-permute-start | bytes 393224 | tf_op jit(solution)/shard_map/ppermute | solution.py:289
  9.5 6.3 %copy-start.5 = (bf16[1,512,128]{2,1,0:T(8,128)(2,1)S(1)}, bf16[1,512,128]{2,1,0:T(8,128)(2,1)}, u32[]{:S(2)}) copy-start(bf16[1,512,128]{2,1,0:T(8,128)(2,1)} %get-tuple-element.28.own_ref) | copy-start | bytes 393220
  9.5 12.1 %copy-start = (f32[64,32,256]{2,1,0:T(8,128)S(1)}, f32[64,32,256]{2,1,0:T(8,128)}, u32[]{:S(2)}) copy-start(f32[64,32,256]{2,1,0:T(8,128)} %x_ref.1) | copy-start | bytes 6291460
  9.5 12.1 %copy-start.2 = (f32[32,256]{1,0:T(8,128)S(1)}, f32[32,256]{1,0:T(8,128)}, u32[]{:S(2)}) copy-start(f32[32,256]{1,0:T(8,128)} %coef_ref.7) | copy-start | bytes 98308
  9.5 12.1 %copy-start.4 = (f32[8,128,128]{2,1,0:T(8,128)S(1)}, f32[8,128,128]{2,1,0:T(8,128)}, u32[]{:S(2)}) copy-start(f32[8,128,128]{2,1,0:T(8,128)} %taper_ref.1) | copy-start | bytes 1572868
  11.8 15.5 %collective-permute-start = (f32[328,256]{1,0:T(8,128)}, f32[328,256]{1,0:T(8,128)S(1)}, u32[]{:S(2)}, u32[]{:S(2)}) collective-permute-start(f32[328,256]{1,0:T(8,128)} %get-tuple-element.26), channel_id=1, source_target_pairs={{0,1},{1,2},{2,3},{3,4},{4,5},{5,6},{6,7},{7,8},{8,9},{9,10},{10,1... | collective-permute-start | bytes 1007624 | tf_op jit(solution)/shard_map/ppermute | solution.py:404
  14.5 12.8 %collective-permute-start.1 = (f32[328,256]{1,0:T(8,128)}, f32[328,256]{1,0:T(8,128)S(1)}, u32[]{:S(2)}, u32[]{:S(2)}) collective-permute-start(f32[328,256]{1,0:T(8,128)} %get-tuple-element.27), channel_id=1, source_target_pairs={{1,0},{2,1},{3,2},{4,3},{5,4},{6,5},{7,6},{8,7},{9,8},{10,9},{11,1... | collective-permute-start | bytes 1007624 | tf_op jit(solution)/shard_map/ppermute | solution.py:403
  15.9 15.5 %collective-permute-start.3 = (bf16[2,512,128]{2,1,0:T(8,128)(2,1)S(1)}, bf16[2,512,128]{2,1,0:T(8,128)(2,1)S(1)}, u32[]{:S(2)}, u32[]{:S(2)}) collective-permute-start(bf16[2,512,128]{2,1,0:T(8,128)(2,1)S(1)} %get-tuple-element.38.refs_0_), channel_id=1, source_target_pairs={{8,0},{9,1},{10,2},{11,3},{12,4},{13,5},{14,6},{15,7},{16,8},{17,9... | collective-permute-start | bytes 786440 | tf_op jit(solution)/shard_map/ppermute | solution.py:289
  19.5 11.9 %collective-permute-start.4 = (bf16[2,512,128]{2,1,0:T(8,128)(2,1)S(1)}, bf16[2,512,128]{2,1,0:T(8,128)(2,1)S(1)}, u32[]{:S(2)}, u32[]{:S(2)}) collective-permute-start(bf16[2,512,128]{2,1,0:T(8,128)(2,1)S(1)} %get-tuple-element.38.refs_0_), channel_id=1, source_target_pairs={{24,0},{25,1},{26,2},{27,3},{28,4},{29,5},{30,6},{31,7},{0,8},{1,9... | collective-permute-start | bytes 786440 | tf_op jit(solution)/shard_map/ppermute | solution.py:289
  19.5 15.6 %collective-permute-start.5 = (bf16[2,512,128]{2,1,0:T(8,128)(2,1)S(1)}, bf16[2,512,128]{2,1,0:T(8,128)(2,1)S(1)}, u32[]{:S(2)}, u32[]{:S(2)}) collective-permute-start(bf16[2,512,128]{2,1,0:T(8,128)(2,1)S(1)} %get-tuple-element.38.refs_0_), channel_id=1, source_target_pairs={{16,0},{17,1},{18,2},{19,3},{20,4},{21,5},{22,6},{23,7},{24,8},{25... | collective-permute-start | bytes 786440 | tf_op jit(solution)/shard_map/ppermute | solution.py:289
  36.2 20.7 %collective-permute-start.6 = (bf16[8,512,128]{2,1,0:T(8,128)(2,1)S(1)}, bf16[8,512,128]{2,1,0:T(8,128)(2,1)S(1)}, u32[]{:S(2)}, u32[]{:S(2)}) collective-permute-start(bf16[8,512,128]{2,1,0:T(8,128)(2,1)S(1)} %get-tuple-element.40.rest_0_), channel_id=1, source_target_pairs={{1,0},{2,1},{3,2},{4,3},{5,4},{6,5},{7,6},{0,7},{9,8},{10,9},{11,1... | collective-permute-start | bytes 3145736 | tf_op jit(solution)/shard_map/ppermute | solution.py:289
  39.5 20.7 %collective-permute-start.7 = (bf16[8,512,128]{2,1,0:T(8,128)(2,1)S(1)}, bf16[8,512,128]{2,1,0:T(8,128)(2,1)}, u32[]{:S(2)}, u32[]{:S(2)}) collective-permute-start(bf16[8,512,128]{2,1,0:T(8,128)(2,1)S(1)} %get-tuple-element.40.rest_0_), channel_id=1, source_target_pairs={{7,0},{0,1},{1,2},{2,3},{3,4},{4,5},{5,6},{6,7},{15,8},{8,9},{9,10... | collective-permute-start | bytes 3145736 | tf_op jit(solution)/shard_map/ppermute | solution.py:289
  39.5 37.7 %all-to-all-start = ((bf16[8,608,128]{2,1,0:T(8,128)(2,1)}), bf16[8,608,128]{2,1,0:T(8,128)(2,1)S(1)}, u32[]{:S(2)}, u32[]{:S(2)}) async-start(bf16[8,608,128]{2,1,0:T(8,128)(2,1)} %get-tuple-element.37), calls=%async_computation | async-start | bytes 2490368 | tf_op jit(solution)/shard_map/all_to_all | solution.py:450
  46.4 30.9 %collective-permute-start.8 = (bf16[8,512,128]{2,1,0:T(8,128)(2,1)S(1)}, bf16[8,512,128]{2,1,0:T(8,128)(2,1)}, u32[]{:S(2)}, u32[]{:S(2)}) collective-permute-start(bf16[8,512,128]{2,1,0:T(8,128)(2,1)S(1)} %get-tuple-element.40.rest_0_), channel_id=1, source_target_pairs={{32,0},{33,1},{34,2},{35,3},{36,4},{37,5},{38,6},{39,7},{40,8},{41... | collective-permute-start | bytes 3145736 | tf_op jit(solution)/shard_map/ppermute | solution.py:289
  46.4 14.4 %collective-permute-start.11 = (bf16[4,512,128]{2,1,0:T(8,128)(2,1)}, bf16[4,512,128]{2,1,0:T(8,128)(2,1)}, u32[]{:S(2)}, u32[]{:S(2)}) collective-permute-start(bf16[4,512,128]{2,1,0:T(8,128)(2,1)} %get-tuple-element.43), channel_id=1, source_target_pairs={{2,0},{3,1},{4,2},{5,3},{6,4},{7,5},{0,6},{1,7},{10,8},{11,9},{12,... | collective-permute-start | bytes 1572872 | tf_op jit(solution)/shard_map/ppermute | solution.py:289
  56.9 20.4 %collective-permute-start.9 = (bf16[8,512,128]{2,1,0:T(8,128)(2,1)S(1)}, bf16[8,512,128]{2,1,0:T(8,128)(2,1)}, u32[]{:S(2)}, u32[]{:S(2)}) collective-permute-start(bf16[8,512,128]{2,1,0:T(8,128)(2,1)S(1)} %collective-permute-done.6.rest_1_), channel_id=1, source_target_pairs={{32,0},{33,1},{34,2},{35,3},{36,4},{37,5},{38,6},{39,7},{40,8},{41... | collective-permute-start | bytes 3145736 | tf_op jit(solution)/shard_map/ppermute | solution.py:289
  60.3 17.0 %collective-permute-start.10 = (bf16[8,512,128]{2,1,0:T(8,128)(2,1)}, bf16[8,512,128]{2,1,0:T(8,128)(2,1)}, u32[]{:S(2)}, u32[]{:S(2)}) collective-permute-start(bf16[8,512,128]{2,1,0:T(8,128)(2,1)} %collective-permute-done.7.rest_2_), channel_id=1, source_target_pairs={{32,0},{33,1},{34,2},{35,3},{36,4},{37,5},{38,6},{39,7},{40,8},{41... | collective-permute-start | bytes 3145736 | tf_op jit(solution)/shard_map/ppermute | solution.py:289
  60.3 20.2 %copy-start.6 = (s32[64,4]{0,1:T(4,128)S(1)}, s32[64,4]{0,1:T(4,128)}, u32[]{:S(2)}) copy-start(s32[64,4]{0,1:T(4,128)} %param.12) | copy-start | bytes 3076
  60.3 20.2 %copy-start.7 = (s32[64,4]{0,1:T(4,128)S(1)}, s32[64,4]{0,1:T(4,128)}, u32[]{:S(2)}) copy-start(s32[64,4]{0,1:T(4,128)} %param.13) | copy-start | bytes 3076
  60.3 10.2 %collective-permute-start.12 = (bf16[4,512,128]{2,1,0:T(8,128)(2,1)}, bf16[4,512,128]{2,1,0:T(8,128)(2,1)}, u32[]{:S(2)}, u32[]{:S(2)}) collective-permute-start(bf16[4,512,128]{2,1,0:T(8,128)(2,1)} %get-tuple-element.44), channel_id=1, source_target_pairs={{6,0},{7,1},{0,2},{1,3},{2,4},{3,5},{4,6},{5,7},{14,8},{15,9},{8,1... | collective-permute-start | bytes 1572872 | tf_op jit(solution)/shard_map/ppermute | solution.py:289
  60.8 19.6 %collective-permute-start.13 = (bf16[4,512,128]{2,1,0:T(8,128)(2,1)}, bf16[4,512,128]{2,1,0:T(8,128)(2,1)}, u32[]{:S(2)}, u32[]{:S(2)}) collective-permute-start(bf16[4,512,128]{2,1,0:T(8,128)(2,1)} %collective-permute-done.11.rest_0_), channel_id=1, source_target_pairs={{32,0},{33,1},{34,2},{35,3},{36,4},{37,5},{38,6},{39,7},{40,8},{41... | collective-permute-start | bytes 1572872 | tf_op jit(solution)/shard_map/ppermute | solution.py:289
  70.5 9.9 %collective-permute-start.14 = (bf16[4,512,128]{2,1,0:T(8,128)(2,1)}, bf16[4,512,128]{2,1,0:T(8,128)(2,1)}, u32[]{:S(2)}, u32[]{:S(2)}) collective-permute-start(bf16[4,512,128]{2,1,0:T(8,128)(2,1)} %collective-permute-done.12.rest_1_), channel_id=1, source_target_pairs={{32,0},{33,1},{34,2},{35,3},{36,4},{37,5},{38,6},{39,7},{40,8},{41... | collective-permute-start | bytes 1572872 | tf_op jit(solution)/shard_map/ppermute | solution.py:289
  77.3 3.2 %copy-start.3 = (f32[8,128,128]{2,1,0:T(8,128)S(1)}, f32[8,128,128]{2,1,0:T(8,128)}, u32[]{:S(2)}) copy-start(f32[8,128,128]{2,1,0:T(8,128)} %get-tuple-element.36.taper_ref) | copy-start | bytes 1572868
  86.0 21.0 %copy-start.1 = (f32[34,64,256]{2,1,0:T(8,128)S(1)}, f32[34,64,256]{2,1,0:T(8,128)}, u32[]{:S(2)}) copy-start(f32[34,64,256]{2,1,0:T(8,128)} %get-tuple-element.34.prior_ref) | copy-start | bytes 6684676

commit v11 on v9

--- a/solution.py
+++ b/solution.py
@@ -288,7 +288,7 @@
     return (x, 1 - c, y, z)
 
 
-TOKEN = pltpu.HBM((8, TILE), F32)
+TOKEN = jax.ShapeDtypeStruct((8, TILE), F32)
 
 
 def join(operands, name, after):

time: 103 us -> 102 us (level)
  local copies, waits for them, and re-layouts: 1.78 us -> 0.42 us
    unnamed x26 -> x22, local copies, waits for them, and re-layouts: 1.56 us -> 0.2 us
where the time goes in v11:
time: 102 us
  starting transfers between devices  31.3 us (31%)
  Pallas kernels  26.8 us (26%)
  waiting for transfers between devices  21.1 us (21%)
  blocking collectives  21 us (21%)
    ppermute x13, waiting for transfers between devices, fetch(): return lax.ppermute(value, AXES, pairs)  21.1 us
    all_to_all x1, blocking collectives, body(): lax.all_to_all(increments, 'mem', split_axis=0, concat_axis=0, tiled=True)  21 us
    ppermute x13, starting transfers between devices, fetch(): return lax.ppermute(value, AXES, pairs)  20.4 us
    all_to_all x1, starting transfers between devices, body(): lax.all_to_all(payload, 'mem', split_axis=0, concat_axis=0, tiled=True)  6.92 us
    pallas_call x1, Pallas kernels, body(): pl.pallas_call(interior_kernel, out_shape=[pltpu.HBM((rows + 2, *row), F3...  5.97 us
    pallas_call x1, Pallas kernels, body(): pl.pallas_call(analysis_kernel, out_shape=jax.ShapeDtypeStruct((group, ti...  5.58 us
    pallas_call x1, Pallas kernels, body(): pl.pallas_call(edge_kernel, out_shape=[pltpu.HBM(prior.shape, F32), pltpu...  4.04 us
    pallas_call x1, Pallas kernels, body(): pl.pallas_call(collect_kernel, out_shape=[jax.ShapeDtypeStruct((2, sum((v...  3.04 us
  transfers between devices with their start and end apart: 16, of which 4 were waited for; matrix products, arithmetic and copies ran while one was open for 1% of the time, Pallas kernels for 15%

profile of v11, /device:TPU:1, one launch (start us, length us, event | category | flops | bytes accessed | tf_op | source)
XLA Modules:
  0.0 101.7 jit_solution(17223923691529624692)
XLA Ops:
  0.0 1.7 %pack_obs.1 = (bf16[1,512,128]{2,1,0:T(8,128)(2,1)}, f32[8,128]{1,0:T(8,128)}) custom-call(bf16[1,128,512]{2,1,0:T(8,128)(2,1)} %anom_ref.1, bf16[1,128,512]{2,1,0:T(8,128)(2,1)} %weight_ref.1), custom_call_target="tpu_custom_call" | custom-call | tf_op jit(solution)/shard_map/pack_obs/pallas_call | solution.py:365
  1.7 7.8 %collective-permute-start.2 = (bf16[1,512,128]{2,1,0:T(8,128)(2,1)}, bf16[1,512,128]{2,1,0:T(8,128)(2,1)S(1)}, u32[]{:S(2)}, u32[]{:S(2)}) collective-permute-start(bf16[1,512,128]{2,1,0:T(8,128)(2,1)} %get-tuple-element.27.own_ref), channel_id=1, source_target_pairs={{4,0},{5,1},{6,2},{7,3},{0,4},{1,5},{2,6},{3,7},{12,8},{13,9},{14,... | collective-permute-start | bytes 393224 | tf_op jit(solution)/shard_map/ppermute | solution.py:280
  9.5 2.3 %pack_halo.1 = (f32[328,256]{1,0:T(8,128)}, f32[328,256]{1,0:T(8,128)}) custom-call(f32[64,32,256]{2,1,0:T(8,128)} %x_ref.1, f32[64,32,256]{2,1,0:T(8,128)} %x_ref.1, f32[32,256]{1,0:T(8,128)} %coef_ref.7, s32[4,64]{1,0:T(4,128)} %bitcast.2, s32[4,64]{1,0:T(4,128)} %bitcast.3, f32[8,128]{1,0:T(8,128)} %get-tuple-element.24.after_ref), custom_call_target="tpu_custom_call" | custom-call | tf_op jit(solution)/shard_map/pack_halo/pallas_call | solution.py:373
  11.8 2.7 %collective-permute-start = (f32[328,256]{1,0:T(8,128)}, f32[328,256]{1,0:T(8,128)S(1)}, u32[]{:S(2)}, u32[]{:S(2)}) collective-permute-start(f32[328,256]{1,0:T(8,128)} %get-tuple-element.25), channel_id=1, source_target_pairs={{0,1},{1,2},{2,3},{3,4},{4,5},{5,6},{6,7},{7,8},{8,9},{9,10},{10,1... | collective-permute-start | bytes 1007624 | tf_op jit(solution)/shard_map/ppermute | solution.py:389
  14.5 1.3 %collective-permute-start.1 = (f32[328,256]{1,0:T(8,128)}, f32[328,256]{1,0:T(8,128)S(1)}, u32[]{:S(2)}, u32[]{:S(2)}) collective-permute-start(f32[328,256]{1,0:T(8,128)} %get-tuple-element.26), channel_id=1, source_target_pairs={{1,0},{2,1},{3,2},{4,3},{5,4},{6,5},{7,6},{8,7},{9,8},{10,9},{11,1... | collective-permute-start | bytes 1007624 | tf_op jit(solution)/shard_map/ppermute | solution.py:388
  15.9 3.6 %collective-permute-start.3 = (bf16[2,512,128]{2,1,0:T(8,128)(2,1)S(1)}, bf16[2,512,128]{2,1,0:T(8,128)(2,1)S(1)}, u32[]{:S(2)}, u32[]{:S(2)}) collective-permute-start(bf16[2,512,128]{2,1,0:T(8,128)(2,1)S(1)} %get-tuple-element.36.refs_0_), channel_id=1, source_target_pairs={{8,0},{9,1},{10,2},{11,3},{12,4},{13,5},{14,6},{15,7},{16,8},{17,9... | collective-permute-start | bytes 786440 | tf_op jit(solution)/shard_map/ppermute | solution.py:280
  19.5 2.1 %collective-permute-start.5 = (bf16[2,512,128]{2,1,0:T(8,128)(2,1)S(1)}, bf16[2,512,128]{2,1,0:T(8,128)(2,1)S(1)}, u32[]{:S(2)}, u32[]{:S(2)}) collective-permute-start(bf16[2,512,128]{2,1,0:T(8,128)(2,1)S(1)} %get-tuple-element.36.refs_0_), channel_id=1, source_target_pairs={{16,0},{17,1},{18,2},{19,3},{20,4},{21,5},{22,6},{23,7},{24,8},{25... | collective-permute-start | bytes 786440 | tf_op jit(solution)/shard_map/ppermute | solution.py:280
  21.6 6.0 %forecast_interior.1 = (f32[34,64,256]{2,1,0:T(8,128)}, bf16[8,608,128]{2,1,0:T(8,128)(2,1)}, f32[16,64,256]{2,1,0:T(8,128)S(1)}, f32[8,32,128]{2,1,0:T(8,128)S(1)}, f32[8,128,128]{2,1,0:T(8,128)}) custom-call(f32[64,32,256]{2,1,0:T(8,128)S(1)} %copy-done, f32[32,256]{1,0:T(8,128)S(1)} %copy-done.2, f32[8,128,128]{2,1,0:T(8,128)S(1)} %copy-done.4, ...), custom_call_target="tpu_custom_call" | custom-call | tf_op jit(solution)/shard_map/forecast_interior/pallas_call | solution.py:393
  27.6 4.0 %forecast_edges.1 = (f32[34,64,256]{2,1,0:T(8,128)}, bf16[8,608,128]{2,1,0:T(8,128)(2,1)}, f32[8,128]{1,0:T(8,128)S(1)}) custom-call(f32[328,256]{1,0:T(8,128)S(1)} %collective-permute-done.above_ref, f32[328,256]{1,0:T(8,128)S(1)} %collective-permute-done.1.below_ref, f32[32,256]{1,0:T(8,128)S(1)} %copy-done.2, ...), custom_call_target="tpu_custom_call", output_to_operand_aliasing={{0}: (5, {}), {1}: (6, {})} | custom-call | tf_op jit(solution)/shard_map/forecast_edges/pallas_call | solution.py:415
  31.7 3.4 %collective-permute-done.5.refs_3_ = bf16[2,512,128]{2,1,0:T(8,128)(2,1)S(1)} collective-permute-done((bf16[2,512,128]{2,1,0:T(8,128)(2,1)S(1)}, bf16[2,512,128]{2,1,0:T(8,128)(2,1)S(1)}, u32[]{:S(2)}, u32[]{:S(2)}) %collective-permute-start.5) | collective-permute-done | bytes 262176 | tf_op jit(solution)/shard_map/ppermute | solution.py:280
  35.1 1.2 %join_eight.1 = (bf16[8,512,128]{2,1,0:T(8,128)(2,1)S(1)}, bf16[4,512,128]{2,1,0:T(8,128)(2,1)}, bf16[4,512,128]{2,1,0:T(8,128)(2,1)}) custom-call(bf16[2,512,128]{2,1,0:T(8,128)(2,1)S(1)} %get-tuple-element.36.refs_0_, bf16[2,512,128]{2,1,0:T(8,128)(2,1)S(1)} %collective-permute-done.3.refs_1_, bf16[2,512,128]{2,1,0:T(8,128)(2,1)S(1)} %collective-permute-done.4.refs_2_, ...), custom_call_target="tpu_custom_call" | custom-call | tf_op jit(solution)/shard_map/join_eight/pallas_call | solution.py:307
  36.3 3.3 %collective-permute-start.6 = (bf16[8,512,128]{2,1,0:T(8,128)(2,1)S(1)}, bf16[8,512,128]{2,1,0:T(8,128)(2,1)S(1)}, u32[]{:S(2)}, u32[]{:S(2)}) collective-permute-start(bf16[8,512,128]{2,1,0:T(8,128)(2,1)S(1)} %get-tuple-element.38.rest_0_), channel_id=1, source_target_pairs={{1,0},{2,1},{3,2},{4,3},{5,4},{6,5},{7,6},{0,7},{9,8},{10,9},{11,1... | collective-permute-start | bytes 3145736 | tf_op jit(solution)/shard_map/ppermute | solution.py:280
  39.5 1.6 %collective-permute-start.11 = (bf16[4,512,128]{2,1,0:T(8,128)(2,1)}, bf16[4,512,128]{2,1,0:T(8,128)(2,1)}, u32[]{:S(2)}, u32[]{:S(2)}) collective-permute-start(bf16[4,512,128]{2,1,0:T(8,128)(2,1)} %get-tuple-element.41), channel_id=1, source_target_pairs={{2,0},{3,1},{4,2},{5,3},{6,4},{7,5},{0,6},{1,7},{10,8},{11,9},{12,... | collective-permute-start | bytes 1572872 | tf_op jit(solution)/shard_map/ppermute | solution.py:280
  41.2 1.3 %collective-permute-start.12 = (bf16[4,512,128]{2,1,0:T(8,128)(2,1)}, bf16[4,512,128]{2,1,0:T(8,128)(2,1)}, u32[]{:S(2)}, u32[]{:S(2)}) collective-permute-start(bf16[4,512,128]{2,1,0:T(8,128)(2,1)} %get-tuple-element.42), channel_id=1, source_target_pairs={{6,0},{7,1},{0,2},{1,3},{2,4},{3,5},{4,6},{5,7},{14,8},{15,9},{8,1... | collective-permute-start | bytes 1572872 | tf_op jit(solution)/shard_map/ppermute | solution.py:280
  42.5 6.9 %all-to-all-start = ((bf16[8,608,128]{2,1,0:T(8,128)(2,1)}), bf16[8,608,128]{2,1,0:T(8,128)(2,1)S(1)}, u32[]{:S(2)}, u32[]{:S(2)}) async-start(bf16[8,608,128]{2,1,0:T(8,128)(2,1)} %get-tuple-element.35), calls=%async_computation | async-start | bytes 2490368 | tf_op jit(solution)/shard_map/all_to_all | solution.py:435
  49.4 13.1 %collective-permute-done.6.rest_1_ = bf16[8,512,128]{2,1,0:T(8,128)(2,1)S(1)} collective-permute-done((bf16[8,512,128]{2,1,0:T(8,128)(2,1)S(1)}, bf16[8,512,128]{2,1,0:T(8,128)(2,1)S(1)}, u32[]{:S(2)}, u32[]{:S(2)}) %collective-permute-start.6) | collective-permute-done | bytes 1048608 | tf_op jit(solution)/shard_map/ppermute | solution.py:280
  62.5 3.5 %collective-permute-done.7.rest_2_ = bf16[8,512,128]{2,1,0:T(8,128)(2,1)} collective-permute-done((bf16[8,512,128]{2,1,0:T(8,128)(2,1)S(1)}, bf16[8,512,128]{2,1,0:T(8,128)(2,1)}, u32[]{:S(2)}, u32[]{:S(2)}) %collective-permute-start.7) | collective-permute-done | bytes 1048608 | tf_op jit(solution)/shard_map/ppermute | solution.py:280
  66.3 0.7 fusion.13
  67.1 0.6 collective-permute-start.13
  67.9 1.1 %collective-permute-done.10.rest_5_ = bf16[8,512,128]{2,1,0:T(8,128)(2,1)} collective-permute-done((bf16[8,512,128]{2,1,0:T(8,128)(2,1)}, bf16[8,512,128]{2,1,0:T(8,128)(2,1)}, u32[]{:S(2)}, u32[]{:S(2)}) %collective-permute-start.10) | collective-permute-done | bytes 1048608 | tf_op jit(solution)/shard_map/ppermute | solution.py:280
  69.0 3.0 %collect.1 = (bf16[2,24,512,128]{3,2,1,0:T(8,128)(2,1)S(1)}, bf16[9,512,128]{2,1,0:T(8,128)(2,1)S(1)}) custom-call(bf16[8,608,128]{2,1,0:T(8,128)(2,1)S(1)} %all-to-all-done.recv_ref, bf16[8,512,128]{2,1,0:T(8,128)(2,1)S(1)} %get-tuple-element.38.rest_0_, bf16[8,512,128]{2,1,0:T(8,128)(2,1)S(1)} %collective-permute-done.6.rest_1_, ...), custom_call_target="tpu_custom_call" | custom-call | tf_op jit(solution)/shard_map/collect/pallas_call | solution.py:446
  72.1 5.6 %analysis.1 = bf16[8,576,128]{2,1,0:T(8,128)(2,1)S(1)} custom-call(s32[9,4]{1,0:T(8,128)S(1)} %get-tuple-element.44.anom_at_ref, s32[9,4]{1,0:T(8,128)S(1)} %get-tuple-element.43.weight_at_ref, s32[9,4]{1,0:T(8,128)S(1)} %pad_add_fusion.1.tapers_ref, f32[8,128,128]{2,1,0:T(8,128)S(1)} %copy-done.3, bf16[9,512,128]{2,1,0:T(8,128)(2,1)S(1)} %get-tuple-element.39.centred_ref, ...), custom_call_target="tpu_custom_call" | custom-call | tf_op jit(solution)/shard_map/analysis/pallas_call | solution.py:457
  77.7 21.0 %all_to_all.10.inc_ref = bf16[8,576,128]{2,1,0:T(8,128)(2,1)S(1)} all-to-all(bf16[8,576,128]{2,1,0:T(8,128)(2,1)S(1)} %analysis.1), channel_id=1, replica_groups=mesh['mem'=8,'state'=32] {'mem'}, dimensions={0} | all-to-all | bytes 2359296 | tf_op jit(solution)/shard_map/all_to_all | solution.py:466
  98.7 2.9 %final_step.1 = f32[64,32,256]{2,1,0:T(8,128)} custom-call(f32[34,64,256]{2,1,0:T(8,128)S(1)} %copy-done.1, bf16[8,576,128]{2,1,0:T(8,128)(2,1)S(1)} %all_to_all.10.inc_ref, f32[32,256]{1,0:T(8,128)S(1)} %copy-done.2), custom_call_target="tpu_custom_call" | custom-call | tf_op jit(solution)/shard_map/final_step/pallas_call | solution.py:468
  (49 shorter events, 0.7 us)
Async XLA Ops:
  1.7 14.1 %collective-permute-start.2 = (bf16[1,512,128]{2,1,0:T(8,128)(2,1)}, bf16[1,512,128]{2,1,0:T(8,128)(2,1)S(1)}, u32[]{:S(2)}, u32[]{:S(2)}) collective-permute-start(bf16[1,512,128]{2,1,0:T(8,128)(2,1)} %get-tuple-element.27.own_ref), channel_id=1, source_target_pairs={{4,0},{5,1},{6,2},{7,3},{0,4},{1,5},{2,6},{3,7},{12,8},{13,9},{14,... | collective-permute-start | bytes 393224 | tf_op jit(solution)/shard_map/ppermute | solution.py:280
  9.5 6.3 %copy-start.7 = (bf16[1,512,128]{2,1,0:T(8,128)(2,1)S(1)}, bf16[1,512,128]{2,1,0:T(8,128)(2,1)}, u32[]{:S(2)}) copy-start(bf16[1,512,128]{2,1,0:T(8,128)(2,1)} %get-tuple-element.27.own_ref) | copy-start | bytes 393220
  9.5 12.1 %copy-start = (f32[64,32,256]{2,1,0:T(8,128)S(1)}, f32[64,32,256]{2,1,0:T(8,128)}, u32[]{:S(2)}) copy-start(f32[64,32,256]{2,1,0:T(8,128)} %x_ref.1) | copy-start | bytes 6291460
  9.5 12.1 %copy-start.2 = (f32[32,256]{1,0:T(8,128)S(1)}, f32[32,256]{1,0:T(8,128)}, u32[]{:S(2)}) copy-start(f32[32,256]{1,0:T(8,128)} %coef_ref.7) | copy-start | bytes 98308
  9.5 12.1 %copy-start.4 = (f32[8,128,128]{2,1,0:T(8,128)S(1)}, f32[8,128,128]{2,1,0:T(8,128)}, u32[]{:S(2)}) copy-start(f32[8,128,128]{2,1,0:T(8,128)} %taper_ref.1) | copy-start | bytes 1572868
  11.8 15.7 %collective-permute-start = (f32[328,256]{1,0:T(8,128)}, f32[328,256]{1,0:T(8,128)S(1)}, u32[]{:S(2)}, u32[]{:S(2)}) collective-permute-start(f32[328,256]{1,0:T(8,128)} %get-tuple-element.25), channel_id=1, source_target_pairs={{0,1},{1,2},{2,3},{3,4},{4,5},{5,6},{6,7},{7,8},{8,9},{9,10},{10,1... | collective-permute-start | bytes 1007624 | tf_op jit(solution)/shard_map/ppermute | solution.py:389
  14.5 13.1 %collective-permute-start.1 = (f32[328,256]{1,0:T(8,128)}, f32[328,256]{1,0:T(8,128)S(1)}, u32[]{:S(2)}, u32[]{:S(2)}) collective-permute-start(f32[328,256]{1,0:T(8,128)} %get-tuple-element.26), channel_id=1, source_target_pairs={{1,0},{2,1},{3,2},{4,3},{5,4},{6,5},{7,6},{8,7},{9,8},{10,9},{11,1... | collective-permute-start | bytes 1007624 | tf_op jit(solution)/shard_map/ppermute | solution.py:388
  15.9 15.8 %collective-permute-start.3 = (bf16[2,512,128]{2,1,0:T(8,128)(2,1)S(1)}, bf16[2,512,128]{2,1,0:T(8,128)(2,1)S(1)}, u32[]{:S(2)}, u32[]{:S(2)}) collective-permute-start(bf16[2,512,128]{2,1,0:T(8,128)(2,1)S(1)} %get-tuple-element.36.refs_0_), channel_id=1, source_target_pairs={{8,0},{9,1},{10,2},{11,3},{12,4},{13,5},{14,6},{15,7},{16,8},{17,9... | collective-permute-start | bytes 786440 | tf_op jit(solution)/shard_map/ppermute | solution.py:280
  19.5 12.2 %collective-permute-start.4 = (bf16[2,512,128]{2,1,0:T(8,128)(2,1)S(1)}, bf16[2,512,128]{2,1,0:T(8,128)(2,1)S(1)}, u32[]{:S(2)}, u32[]{:S(2)}) collective-permute-start(bf16[2,512,128]{2,1,0:T(8,128)(2,1)S(1)} %get-tuple-element.36.refs_0_), channel_id=1, source_target_pairs={{24,0},{25,1},{26,2},{27,3},{28,4},{29,5},{30,6},{31,7},{0,8},{1,9... | collective-permute-start | bytes 786440 | tf_op jit(solution)/shard_map/ppermute | solution.py:280
  19.5 15.6 %collective-permute-start.5 = (bf16[2,512,128]{2,1,0:T(8,128)(2,1)S(1)}, bf16[2,512,128]{2,1,0:T(8,128)(2,1)S(1)}, u32[]{:S(2)}, u32[]{:S(2)}) collective-permute-start(bf16[2,512,128]{2,1,0:T(8,128)(2,1)S(1)} %get-tuple-element.36.refs_0_), channel_id=1, source_target_pairs={{16,0},{17,1},{18,2},{19,3},{20,4},{21,5},{22,6},{23,7},{24,8},{25... | collective-permute-start | bytes 786440 | tf_op jit(solution)/shard_map/ppermute | solution.py:280
  36.3 26.2 %collective-permute-start.6 = (bf16[8,512,128]{2,1,0:T(8,128)(2,1)S(1)}, bf16[8,512,128]{2,1,0:T(8,128)(2,1)S(1)}, u32[]{:S(2)}, u32[]{:S(2)}) collective-permute-start(bf16[8,512,128]{2,1,0:T(8,128)(2,1)S(1)} %get-tuple-element.38.rest_0_), channel_id=1, source_target_pairs={{1,0},{2,1},{3,2},{4,3},{5,4},{6,5},{7,6},{0,7},{9,8},{10,9},{11,1... | collective-permute-start | bytes 3145736 | tf_op jit(solution)/shard_map/ppermute | solution.py:280
  39.5 26.5 %collective-permute-start.7 = (bf16[8,512,128]{2,1,0:T(8,128)(2,1)S(1)}, bf16[8,512,128]{2,1,0:T(8,128)(2,1)}, u32[]{:S(2)}, u32[]{:S(2)}) collective-permute-start(bf16[8,512,128]{2,1,0:T(8,128)(2,1)S(1)} %get-tuple-element.38.rest_0_), channel_id=1, source_target_pairs={{7,0},{0,1},{1,2},{2,3},{3,4},{4,5},{5,6},{6,7},{15,8},{8,9},{9,10... | collective-permute-start | bytes 3145736 | tf_op jit(solution)/shard_map/ppermute | solution.py:280
  39.5 27.6 %collective-permute-start.11 = (bf16[4,512,128]{2,1,0:T(8,128)(2,1)}, bf16[4,512,128]{2,1,0:T(8,128)(2,1)}, u32[]{:S(2)}, u32[]{:S(2)}) collective-permute-start(bf16[4,512,128]{2,1,0:T(8,128)(2,1)} %get-tuple-element.41), channel_id=1, source_target_pairs={{2,0},{3,1},{4,2},{5,3},{6,4},{7,5},{0,6},{1,7},{10,8},{11,9},{12,... | collective-permute-start | bytes 1572872 | tf_op jit(solution)/shard_map/ppermute | solution.py:280
  41.2 26.6 %collective-permute-start.12 = (bf16[4,512,128]{2,1,0:T(8,128)(2,1)}, bf16[4,512,128]{2,1,0:T(8,128)(2,1)}, u32[]{:S(2)}, u32[]{:S(2)}) collective-permute-start(bf16[4,512,128]{2,1,0:T(8,128)(2,1)} %get-tuple-element.42), channel_id=1, source_target_pairs={{6,0},{7,1},{0,2},{1,3},{2,4},{3,5},{4,6},{5,7},{14,8},{15,9},{8,1... | collective-permute-start | bytes 1572872 | tf_op jit(solution)/shard_map/ppermute | solution.py:280
  42.5 23.5 %copy-start.8 = (s32[64,4]{0,1:T(4,128)S(1)}, s32[64,4]{0,1:T(4,128)}, u32[]{:S(2)}) copy-start(s32[64,4]{0,1:T(4,128)} %param.12) | copy-start | bytes 3076
  42.5 23.5 %copy-start.9 = (s32[64,4]{0,1:T(4,128)S(1)}, s32[64,4]{0,1:T(4,128)}, u32[]{:S(2)}) copy-start(s32[64,4]{0,1:T(4,128)} %param.13) | copy-start | bytes 3076
  42.5 25.4 %all-to-all-start = ((bf16[8,608,128]{2,1,0:T(8,128)(2,1)}), bf16[8,608,128]{2,1,0:T(8,128)(2,1)S(1)}, u32[]{:S(2)}, u32[]{:S(2)}) async-start(bf16[8,608,128]{2,1,0:T(8,128)(2,1)} %get-tuple-element.35), calls=%async_computation | async-start | bytes 2490368 | tf_op jit(solution)/shard_map/all_to_all | solution.py:435
  49.4 18.5 %collective-permute-start.8 = (bf16[8,512,128]{2,1,0:T(8,128)(2,1)S(1)}, bf16[8,512,128]{2,1,0:T(8,128)(2,1)}, u32[]{:S(2)}, u32[]{:S(2)}) collective-permute-start(bf16[8,512,128]{2,1,0:T(8,128)(2,1)S(1)} %get-tuple-element.38.rest_0_), channel_id=1, source_target_pairs={{32,0},{33,1},{34,2},{35,3},{36,4},{37,5},{38,6},{39,7},{40,8},{41... | collective-permute-start | bytes 3145736 | tf_op jit(solution)/shard_map/ppermute | solution.py:280
  62.5 5.4 %collective-permute-start.9 = (bf16[8,512,128]{2,1,0:T(8,128)(2,1)S(1)}, bf16[8,512,128]{2,1,0:T(8,128)(2,1)}, u32[]{:S(2)}, u32[]{:S(2)}) collective-permute-start(bf16[8,512,128]{2,1,0:T(8,128)(2,1)S(1)} %collective-permute-done.6.rest_1_), channel_id=1, source_target_pairs={{32,0},{33,1},{34,2},{35,3},{36,4},{37,5},{38,6},{39,7},{40,8},{41... | collective-permute-start | bytes 3145736 | tf_op jit(solution)/shard_map/ppermute | solution.py:280
  66.0 3.0 %collective-permute-start.10 = (bf16[8,512,128]{2,1,0:T(8,128)(2,1)}, bf16[8,512,128]{2,1,0:T(8,128)(2,1)}, u32[]{:S(2)}, u32[]{:S(2)}) collective-permute-start(bf16[8,512,128]{2,1,0:T(8,128)(2,1)} %collective-permute-done.7.rest_2_), channel_id=1, source_target_pairs={{32,0},{33,1},{34,2},{35,3},{36,4},{37,5},{38,6},{39,7},{40,8},{41... | collective-permute-start | bytes 3145736 | tf_op jit(solution)/shard_map/ppermute | solution.py:280
  67.1 4.9 %collective-permute-start.13 = (bf16[4,512,128]{2,1,0:T(8,128)(2,1)}, bf16[4,512,128]{2,1,0:T(8,128)(2,1)}, u32[]{:S(2)}, u32[]{:S(2)}) collective-permute-start(bf16[4,512,128]{2,1,0:T(8,128)(2,1)} %collective-permute-done.11.rest_0_), channel_id=1, source_target_pairs={{32,0},{33,1},{34,2},{35,3},{36,4},{37,5},{38,6},{39,7},{40,8},{41... | collective-permute-start | bytes 1572872 | tf_op jit(solution)/shard_map/ppermute | solution.py:280
  67.7 4.3 %collective-permute-start.14 = (bf16[4,512,128]{2,1,0:T(8,128)(2,1)}, bf16[4,512,128]{2,1,0:T(8,128)(2,1)}, u32[]{:S(2)}, u32[]{:S(2)}) collective-permute-start(bf16[4,512,128]{2,1,0:T(8,128)(2,1)} %collective-permute-done.12.rest_1_), channel_id=1, source_target_pairs={{32,0},{33,1},{34,2},{35,3},{36,4},{37,5},{38,6},{39,7},{40,8},{41... | collective-permute-start | bytes 1572872 | tf_op jit(solution)/shard_map/ppermute | solution.py:280
  67.9 4.2 %copy-start.3 = (f32[8,128,128]{2,1,0:T(8,128)S(1)}, f32[8,128,128]{2,1,0:T(8,128)}, u32[]{:S(2)}) copy-start(f32[8,128,128]{2,1,0:T(8,128)} %get-tuple-element.34.taper_ref) | copy-start | bytes 1572868
  77.7 21.0 %copy-start.1 = (f32[34,64,256]{2,1,0:T(8,128)S(1)}, f32[34,64,256]{2,1,0:T(8,128)}, u32[]{:S(2)}) copy-start(f32[34,64,256]{2,1,0:T(8,128)} %get-tuple-element.33.prior_ref) | copy-start | bytes 6684676
  (2 other events, 8.2 us)

commit v12 on v11

--- a/solution.py
+++ b/solution.py
@@ -332,7 +332,8 @@
 
 
 def gather_second(held, mesh, after):
-    p, m, q = (fetch(held, mesh, ring(True, step)) for step in (1, -1, 2))
+    p, m = (fetch(held, mesh, ring(True, step)) for step in (1, -1))
+    q = fetch(held, mesh, lambda x, c, y, z: (x, c, y + 2, z) if c == 0 else (x, c, y, z + 2 - 4 * (z % 2)))
     return join([held, p, m, q], "join_eight", after)
 
 
@@ -348,8 +349,9 @@
     dy, dz = (block // 8 - y) % 4, (block % 8 - z) % 8
     low = dz % 4
     gray_y, gray_z = dy ^ (dy >> 1), low ^ (low >> 1)
-    high = 4 * ((dz // 4) ^ (low == 3).astype(jnp.int32))
-    return 8 * gray_z + high + gray_y, 8 * gray_y + high + gray_z
+    high = (dz // 4) ^ (low == 3).astype(jnp.int32)
+    turned = high ^ jnp.where(low == 2, z % 2, 0)
+    return 8 * gray_z + 4 * high + gray_y, 8 * gray_y + 4 * turned + gray_z
 
 
 def body(ensemble, spreading_coefficient, obs_anom, obs_weight, taper_table, obs_block, taper_id):

time: 102 us -> 99.2 us (0.973)
  waiting for transfers between devices: 21.1 us -> 17.9 us
    ppermute x13, waiting for transfers between devices: 21.1 us -> 17.9 us  [fetch(): return lax.ppermute(value, AXES, pairs)]
  transfers between devices with their start and end apart: 16 -> 16, of which waited for: 4 -> 4; matrix products, arithmetic and copies ran while one was open for 1% -> 1% of each run, Pallas kernels for 15% -> 16%
where the time goes in v12:
time: 99.2 us; the launch traced here: 98.8 us
  starting transfers between devices  31.7 us (32%)
  Pallas kernels  26.8 us (27%)
  blocking collectives  21 us (21%)
  waiting for transfers between devices  17.9 us (18%)
    all_to_all x1, blocking collectives, body(): lax.all_to_all(increments, 'mem', split_axis=0, concat_axis=0, tiled=True)  21 us
    ppermute x13, starting transfers between devices, fetch(): return lax.ppermute(value, AXES, pairs)  20.7 us
    ppermute x13, waiting for transfers between devices, fetch(): return lax.ppermute(value, AXES, pairs)  17.9 us
    all_to_all x1, starting transfers between devices, body(): lax.all_to_all(payload, 'mem', split_axis=0, concat_axis=0, tiled=True)  7.04 us
    pallas_call x1, Pallas kernels, body(): pl.pallas_call(interior_kernel, out_shape=[pltpu.HBM((rows + 2, *row), F3...  5.97 us
    pallas_call x1, Pallas kernels, body(): pl.pallas_call(analysis_kernel, out_shape=jax.ShapeDtypeStruct((group, ti...  5.58 us
    pallas_call x1, Pallas kernels, body(): pl.pallas_call(edge_kernel, out_shape=[pltpu.HBM(prior.shape, F32), pltpu...  4.04 us
    pallas_call x1, Pallas kernels, body(): pl.pallas_call(collect_kernel, out_shape=[jax.ShapeDtypeStruct((2, sum((v...  3.04 us
  transfers between devices with their start and end apart: 16, of which 4 were waited for; matrix products, arithmetic and copies ran while one was open for 1% of the time, Pallas kernels for 16%

profile of v12, /device:TPU:1, one launch (start us, length us, event | category | flops | bytes accessed | tf_op | source)
XLA Modules:
  0.0 98.8 jit_solution(16890669549455225879)
XLA Ops:
  0.0 1.7 %pack_obs.1 = (bf16[1,512,128]{2,1,0:T(8,128)(2,1)}, f32[8,128]{1,0:T(8,128)}) custom-call(bf16[1,128,512]{2,1,0:T(8,128)(2,1)} %anom_ref.1, bf16[1,128,512]{2,1,0:T(8,128)(2,1)} %weight_ref.1), custom_call_target="tpu_custom_call" | custom-call | tf_op jit(solution)/shard_map/pack_obs/pallas_call | solution.py:367
  1.7 7.8 %collective-permute-start.2 = (bf16[1,512,128]{2,1,0:T(8,128)(2,1)}, bf16[1,512,128]{2,1,0:T(8,128)(2,1)S(1)}, u32[]{:S(2)}, u32[]{:S(2)}) collective-permute-start(bf16[1,512,128]{2,1,0:T(8,128)(2,1)} %get-tuple-element.27.own_ref), channel_id=1, source_target_pairs={{4,0},{5,1},{6,2},{7,3},{0,4},{1,5},{2,6},{3,7},{12,8},{13,9},{14,... | collective-permute-start | bytes 393224 | tf_op jit(solution)/shard_map/ppermute | solution.py:280
  9.5 2.3 %pack_halo.1 = (f32[328,256]{1,0:T(8,128)}, f32[328,256]{1,0:T(8,128)}) custom-call(f32[64,32,256]{2,1,0:T(8,128)} %x_ref.1, f32[64,32,256]{2,1,0:T(8,128)} %x_ref.1, f32[32,256]{1,0:T(8,128)} %coef_ref.7, s32[4,64]{1,0:T(4,128)} %bitcast.2, s32[4,64]{1,0:T(4,128)} %bitcast.3, f32[8,128]{1,0:T(8,128)} %get-tuple-element.24.after_ref), custom_call_target="tpu_custom_call" | custom-call | tf_op jit(solution)/shard_map/pack_halo/pallas_call | solution.py:375
  11.8 2.7 %collective-permute-start = (f32[328,256]{1,0:T(8,128)}, f32[328,256]{1,0:T(8,128)S(1)}, u32[]{:S(2)}, u32[]{:S(2)}) collective-permute-start(f32[328,256]{1,0:T(8,128)} %get-tuple-element.25), channel_id=1, source_target_pairs={{0,1},{1,2},{2,3},{3,4},{4,5},{5,6},{6,7},{7,8},{8,9},{9,10},{10,1... | collective-permute-start | bytes 1007624 | tf_op jit(solution)/shard_map/ppermute | solution.py:391
  14.5 1.3 %collective-permute-start.1 = (f32[328,256]{1,0:T(8,128)}, f32[328,256]{1,0:T(8,128)S(1)}, u32[]{:S(2)}, u32[]{:S(2)}) collective-permute-start(f32[328,256]{1,0:T(8,128)} %get-tuple-element.26), channel_id=1, source_target_pairs={{1,0},{2,1},{3,2},{4,3},{5,4},{6,5},{7,6},{8,7},{9,8},{10,9},{11,1... | collective-permute-start | bytes 1007624 | tf_op jit(solution)/shard_map/ppermute | solution.py:390
  15.9 3.6 %collective-permute-start.3 = (bf16[2,512,128]{2,1,0:T(8,128)(2,1)S(1)}, bf16[2,512,128]{2,1,0:T(8,128)(2,1)S(1)}, u32[]{:S(2)}, u32[]{:S(2)}) collective-permute-start(bf16[2,512,128]{2,1,0:T(8,128)(2,1)S(1)} %get-tuple-element.36.refs_0_), channel_id=1, source_target_pairs={{8,0},{9,1},{10,2},{11,3},{12,4},{13,5},{14,6},{15,7},{16,8},{17,9... | collective-permute-start | bytes 786440 | tf_op jit(solution)/shard_map/ppermute | solution.py:280
  19.5 2.1 %collective-permute-start.5 = (bf16[2,512,128]{2,1,0:T(8,128)(2,1)S(1)}, bf16[2,512,128]{2,1,0:T(8,128)(2,1)S(1)}, u32[]{:S(2)}, u32[]{:S(2)}) collective-permute-start(bf16[2,512,128]{2,1,0:T(8,128)(2,1)S(1)} %get-tuple-element.36.refs_0_), channel_id=1, source_target_pairs={{16,0},{17,1},{18,2},{19,3},{20,4},{21,5},{22,6},{23,7},{24,8},{25... | collective-permute-start | bytes 786440 | tf_op jit(solution)/shard_map/ppermute | solution.py:280
  21.6 6.0 %forecast_interior.1 = (f32[34,64,256]{2,1,0:T(8,128)}, bf16[8,608,128]{2,1,0:T(8,128)(2,1)}, f32[16,64,256]{2,1,0:T(8,128)S(1)}, f32[8,32,128]{2,1,0:T(8,128)S(1)}, f32[8,128,128]{2,1,0:T(8,128)}) custom-call(f32[64,32,256]{2,1,0:T(8,128)S(1)} %copy-done, f32[32,256]{1,0:T(8,128)S(1)} %copy-done.2, f32[8,128,128]{2,1,0:T(8,128)S(1)} %copy-done.4, ...), custom_call_target="tpu_custom_call" | custom-call | tf_op jit(solution)/shard_map/forecast_interior/pallas_call | solution.py:395
  27.6 4.0 %forecast_edges.1 = (f32[34,64,256]{2,1,0:T(8,128)}, bf16[8,608,128]{2,1,0:T(8,128)(2,1)}, f32[8,128]{1,0:T(8,128)S(1)}) custom-call(f32[328,256]{1,0:T(8,128)S(1)} %collective-permute-done.above_ref, f32[328,256]{1,0:T(8,128)S(1)} %collective-permute-done.1.below_ref, f32[32,256]{1,0:T(8,128)S(1)} %copy-done.2, ...), custom_call_target="tpu_custom_call", output_to_operand_aliasing={{0}: (5, {}), {1}: (6, {})} | custom-call | tf_op jit(solution)/shard_map/forecast_edges/pallas_call | solution.py:417
  31.7 0.9 collective-permute-done.5.refs_3_
  32.6 1.2 %join_eight.1 = (bf16[8,512,128]{2,1,0:T(8,128)(2,1)S(1)}, bf16[4,512,128]{2,1,0:T(8,128)(2,1)}, bf16[4,512,128]{2,1,0:T(8,128)(2,1)}) custom-call(bf16[2,512,128]{2,1,0:T(8,128)(2,1)S(1)} %get-tuple-element.36.refs_0_, bf16[2,512,128]{2,1,0:T(8,128)(2,1)S(1)} %collective-permute-done.3.refs_1_, bf16[2,512,128]{2,1,0:T(8,128)(2,1)S(1)} %collective-permute-done.4.refs_2_, ...), custom_call_target="tpu_custom_call" | custom-call | tf_op jit(solution)/shard_map/join_eight/pallas_call | solution.py:307
  33.7 3.0 %collective-permute-start.6 = (bf16[8,512,128]{2,1,0:T(8,128)(2,1)S(1)}, bf16[8,512,128]{2,1,0:T(8,128)(2,1)S(1)}, u32[]{:S(2)}, u32[]{:S(2)}) collective-permute-start(bf16[8,512,128]{2,1,0:T(8,128)(2,1)S(1)} %get-tuple-element.38.rest_0_), channel_id=1, source_target_pairs={{1,0},{2,1},{3,2},{4,3},{5,4},{6,5},{7,6},{0,7},{9,8},{10,9},{11,1... | collective-permute-start | bytes 3145736 | tf_op jit(solution)/shard_map/ppermute | solution.py:280
  36.7 1.6 %collective-permute-start.11 = (bf16[4,512,128]{2,1,0:T(8,128)(2,1)}, bf16[4,512,128]{2,1,0:T(8,128)(2,1)}, u32[]{:S(2)}, u32[]{:S(2)}) collective-permute-start(bf16[4,512,128]{2,1,0:T(8,128)(2,1)} %get-tuple-element.41), channel_id=1, source_target_pairs={{2,0},{3,1},{4,2},{5,3},{6,4},{7,5},{0,6},{1,7},{10,8},{11,9},{12,... | collective-permute-start | bytes 1572872 | tf_op jit(solution)/shard_map/ppermute | solution.py:280
  38.4 1.3 %collective-permute-start.12 = (bf16[4,512,128]{2,1,0:T(8,128)(2,1)}, bf16[4,512,128]{2,1,0:T(8,128)(2,1)}, u32[]{:S(2)}, u32[]{:S(2)}) collective-permute-start(bf16[4,512,128]{2,1,0:T(8,128)(2,1)} %get-tuple-element.42), channel_id=1, source_target_pairs={{6,0},{7,1},{0,2},{1,3},{2,4},{3,5},{4,6},{5,7},{14,8},{15,9},{8,1... | collective-permute-start | bytes 1572872 | tf_op jit(solution)/shard_map/ppermute | solution.py:280
  39.7 7.0 %all-to-all-start = ((bf16[8,608,128]{2,1,0:T(8,128)(2,1)}), bf16[8,608,128]{2,1,0:T(8,128)(2,1)S(1)}, u32[]{:S(2)}, u32[]{:S(2)}) async-start(bf16[8,608,128]{2,1,0:T(8,128)(2,1)} %get-tuple-element.35), calls=%async_computation | async-start | bytes 2490368 | tf_op jit(solution)/shard_map/all_to_all | solution.py:437
  46.7 13.0 %collective-permute-done.6.rest_1_ = bf16[8,512,128]{2,1,0:T(8,128)(2,1)S(1)} collective-permute-done((bf16[8,512,128]{2,1,0:T(8,128)(2,1)S(1)}, bf16[8,512,128]{2,1,0:T(8,128)(2,1)S(1)}, u32[]{:S(2)}, u32[]{:S(2)}) %collective-permute-start.6) | collective-permute-done | bytes 1048608 | tf_op jit(solution)/shard_map/ppermute | solution.py:280
  59.7 3.5 %collective-permute-done.7.rest_2_ = bf16[8,512,128]{2,1,0:T(8,128)(2,1)} collective-permute-done((bf16[8,512,128]{2,1,0:T(8,128)(2,1)S(1)}, bf16[8,512,128]{2,1,0:T(8,128)(2,1)}, u32[]{:S(2)}, u32[]{:S(2)}) %collective-permute-start.7) | collective-permute-done | bytes 1048608 | tf_op jit(solution)/shard_map/ppermute | solution.py:280
  63.5 0.7 fusion.12
  64.3 0.6 collective-permute-start.13
  64.9 0.7 collective-permute-start.14
  66.2 3.0 %collect.1 = (bf16[2,24,512,128]{3,2,1,0:T(8,128)(2,1)S(1)}, bf16[9,512,128]{2,1,0:T(8,128)(2,1)S(1)}) custom-call(bf16[8,608,128]{2,1,0:T(8,128)(2,1)S(1)} %all-to-all-done.recv_ref, bf16[8,512,128]{2,1,0:T(8,128)(2,1)S(1)} %get-tuple-element.38.rest_0_, bf16[8,512,128]{2,1,0:T(8,128)(2,1)S(1)} %collective-permute-done.6.rest_1_, ...), custom_call_target="tpu_custom_call" | custom-call | tf_op jit(solution)/shard_map/collect/pallas_call | solution.py:448
  69.3 5.6 %analysis.1 = bf16[8,576,128]{2,1,0:T(8,128)(2,1)S(1)} custom-call(s32[9,4]{1,0:T(8,128)S(1)} %get-tuple-element.44.anom_at_ref, s32[9,4]{1,0:T(8,128)S(1)} %get-tuple-element.43.weight_at_ref, s32[9,4]{1,0:T(8,128)S(1)} %pad_add_fusion.1.tapers_ref, f32[8,128,128]{2,1,0:T(8,128)S(1)} %copy-done.3, bf16[9,512,128]{2,1,0:T(8,128)(2,1)S(1)} %get-tuple-element.39.centred_ref, ...), custom_call_target="tpu_custom_call" | custom-call | tf_op jit(solution)/shard_map/analysis/pallas_call | solution.py:459
  74.9 21.0 %all_to_all.10.inc_ref = bf16[8,576,128]{2,1,0:T(8,128)(2,1)S(1)} all-to-all(bf16[8,576,128]{2,1,0:T(8,128)(2,1)S(1)} %analysis.1), channel_id=1, replica_groups=mesh['mem'=8,'state'=32] {'mem'}, dimensions={0} | all-to-all | bytes 2359296 | tf_op jit(solution)/shard_map/all_to_all | solution.py:468
  95.9 2.9 %final_step.1 = f32[64,32,256]{2,1,0:T(8,128)} custom-call(f32[34,64,256]{2,1,0:T(8,128)S(1)} %copy-done.1, bf16[8,576,128]{2,1,0:T(8,128)(2,1)S(1)} %all_to_all.10.inc_ref, f32[32,256]{1,0:T(8,128)S(1)} %copy-done.2), custom_call_target="tpu_custom_call" | custom-call | tf_op jit(solution)/shard_map/final_step/pallas_call | solution.py:470
  (49 shorter events, 1.0 us)
Async XLA Ops:
  1.7 14.1 %collective-permute-start.2 = (bf16[1,512,128]{2,1,0:T(8,128)(2,1)}, bf16[1,512,128]{2,1,0:T(8,128)(2,1)S(1)}, u32[]{:S(2)}, u32[]{:S(2)}) collective-permute-start(bf16[1,512,128]{2,1,0:T(8,128)(2,1)} %get-tuple-element.27.own_ref), channel_id=1, source_target_pairs={{4,0},{5,1},{6,2},{7,3},{0,4},{1,5},{2,6},{3,7},{12,8},{13,9},{14,... | collective-permute-start | bytes 393224 | tf_op jit(solution)/shard_map/ppermute | solution.py:280
  9.5 6.3 %copy-start.7 = (bf16[1,512,128]{2,1,0:T(8,128)(2,1)S(1)}, bf16[1,512,128]{2,1,0:T(8,128)(2,1)}, u32[]{:S(2)}) copy-start(bf16[1,512,128]{2,1,0:T(8,128)(2,1)} %get-tuple-element.27.own_ref) | copy-start | bytes 393220
  9.5 12.1 %copy-start = (f32[64,32,256]{2,1,0:T(8,128)S(1)}, f32[64,32,256]{2,1,0:T(8,128)}, u32[]{:S(2)}) copy-start(f32[64,32,256]{2,1,0:T(8,128)} %x_ref.1) | copy-start | bytes 6291460
  9.5 12.1 %copy-start.2 = (f32[32,256]{1,0:T(8,128)S(1)}, f32[32,256]{1,0:T(8,128)}, u32[]{:S(2)}) copy-start(f32[32,256]{1,0:T(8,128)} %coef_ref.7) | copy-start | bytes 98308
  9.5 12.1 %copy-start.4 = (f32[8,128,128]{2,1,0:T(8,128)S(1)}, f32[8,128,128]{2,1,0:T(8,128)}, u32[]{:S(2)}) copy-start(f32[8,128,128]{2,1,0:T(8,128)} %taper_ref.1) | copy-start | bytes 1572868
  11.8 15.7 %collective-permute-start = (f32[328,256]{1,0:T(8,128)}, f32[328,256]{1,0:T(8,128)S(1)}, u32[]{:S(2)}, u32[]{:S(2)}) collective-permute-start(f32[328,256]{1,0:T(8,128)} %get-tuple-element.25), channel_id=1, source_target_pairs={{0,1},{1,2},{2,3},{3,4},{4,5},{5,6},{6,7},{7,8},{8,9},{9,10},{10,1... | collective-permute-start | bytes 1007624 | tf_op jit(solution)/shard_map/ppermute | solution.py:391
  14.5 13.1 %collective-permute-start.1 = (f32[328,256]{1,0:T(8,128)}, f32[328,256]{1,0:T(8,128)S(1)}, u32[]{:S(2)}, u32[]{:S(2)}) collective-permute-start(f32[328,256]{1,0:T(8,128)} %get-tuple-element.26), channel_id=1, source_target_pairs={{1,0},{2,1},{3,2},{4,3},{5,4},{6,5},{7,6},{8,7},{9,8},{10,9},{11,1... | collective-permute-start | bytes 1007624 | tf_op jit(solution)/shard_map/ppermute | solution.py:390
  15.9 15.8 %collective-permute-start.3 = (bf16[2,512,128]{2,1,0:T(8,128)(2,1)S(1)}, bf16[2,512,128]{2,1,0:T(8,128)(2,1)S(1)}, u32[]{:S(2)}, u32[]{:S(2)}) collective-permute-start(bf16[2,512,128]{2,1,0:T(8,128)(2,1)S(1)} %get-tuple-element.36.refs_0_), channel_id=1, source_target_pairs={{8,0},{9,1},{10,2},{11,3},{12,4},{13,5},{14,6},{15,7},{16,8},{17,9... | collective-permute-start | bytes 786440 | tf_op jit(solution)/shard_map/ppermute | solution.py:280
  19.5 12.2 %collective-permute-start.4 = (bf16[2,512,128]{2,1,0:T(8,128)(2,1)S(1)}, bf16[2,512,128]{2,1,0:T(8,128)(2,1)S(1)}, u32[]{:S(2)}, u32[]{:S(2)}) collective-permute-start(bf16[2,512,128]{2,1,0:T(8,128)(2,1)S(1)} %get-tuple-element.36.refs_0_), channel_id=1, source_target_pairs={{24,0},{25,1},{26,2},{27,3},{28,4},{29,5},{30,6},{31,7},{0,8},{1,9... | collective-permute-start | bytes 786440 | tf_op jit(solution)/shard_map/ppermute | solution.py:280
  19.5 13.1 %collective-permute-start.5 = (bf16[2,512,128]{2,1,0:T(8,128)(2,1)S(1)}, bf16[2,512,128]{2,1,0:T(8,128)(2,1)S(1)}, u32[]{:S(2)}, u32[]{:S(2)}) collective-permute-start(bf16[2,512,128]{2,1,0:T(8,128)(2,1)S(1)} %get-tuple-element.36.refs_0_), channel_id=1, source_target_pairs={{16,0},{17,1},{18,2},{19,3},{20,4},{21,5},{22,6},{23,7},{24,8},{25... | collective-permute-start | bytes 786440 | tf_op jit(solution)/shard_map/ppermute | solution.py:280
  27.6 4.1 %copy-start.5 = (f32[328,256]{1,0:T(8,128)}, f32[328,256]{1,0:T(8,128)S(1)}, u32[]{:S(2)}) copy-start(f32[328,256]{1,0:T(8,128)S(1)} %collective-permute-done.above_ref) | copy-start | bytes 1007620
  33.7 25.9 %collective-permute-start.6 = (bf16[8,512,128]{2,1,0:T(8,128)(2,1)S(1)}, bf16[8,512,128]{2,1,0:T(8,128)(2,1)S(1)}, u32[]{:S(2)}, u32[]{:S(2)}) collective-permute-start(bf16[8,512,128]{2,1,0:T(8,128)(2,1)S(1)} %get-tuple-element.38.rest_0_), channel_id=1, source_target_pairs={{1,0},{2,1},{3,2},{4,3},{5,4},{6,5},{7,6},{0,7},{9,8},{10,9},{11,1... | collective-permute-start | bytes 3145736 | tf_op jit(solution)/shard_map/ppermute | solution.py:280
  36.7 26.5 %collective-permute-start.7 = (bf16[8,512,128]{2,1,0:T(8,128)(2,1)S(1)}, bf16[8,512,128]{2,1,0:T(8,128)(2,1)}, u32[]{:S(2)}, u32[]{:S(2)}) collective-permute-start(bf16[8,512,128]{2,1,0:T(8,128)(2,1)S(1)} %get-tuple-element.38.rest_0_), channel_id=1, source_target_pairs={{7,0},{0,1},{1,2},{2,3},{3,4},{4,5},{5,6},{6,7},{15,8},{8,9},{9,10... | collective-permute-start | bytes 3145736 | tf_op jit(solution)/shard_map/ppermute | solution.py:280
  36.7 27.6 %collective-permute-start.11 = (bf16[4,512,128]{2,1,0:T(8,128)(2,1)}, bf16[4,512,128]{2,1,0:T(8,128)(2,1)}, u32[]{:S(2)}, u32[]{:S(2)}) collective-permute-start(bf16[4,512,128]{2,1,0:T(8,128)(2,1)} %get-tuple-element.41), channel_id=1, source_target_pairs={{2,0},{3,1},{4,2},{5,3},{6,4},{7,5},{0,6},{1,7},{10,8},{11,9},{12,... | collective-permute-start | bytes 1572872 | tf_op jit(solution)/shard_map/ppermute | solution.py:280
  38.4 26.6 %collective-permute-start.12 = (bf16[4,512,128]{2,1,0:T(8,128)(2,1)}, bf16[4,512,128]{2,1,0:T(8,128)(2,1)}, u32[]{:S(2)}, u32[]{:S(2)}) collective-permute-start(bf16[4,512,128]{2,1,0:T(8,128)(2,1)} %get-tuple-element.42), channel_id=1, source_target_pairs={{6,0},{7,1},{0,2},{1,3},{2,4},{3,5},{4,6},{5,7},{14,8},{15,9},{8,1... | collective-permute-start | bytes 1572872 | tf_op jit(solution)/shard_map/ppermute | solution.py:280
  39.7 23.5 %copy-start.8 = (s32[64,4]{0,1:T(4,128)S(1)}, s32[64,4]{0,1:T(4,128)}, u32[]{:S(2)}) copy-start(s32[64,4]{0,1:T(4,128)} %param.12) | copy-start | bytes 3076
  39.7 23.5 %copy-start.9 = (s32[64,4]{0,1:T(4,128)S(1)}, s32[64,4]{0,1:T(4,128)}, u32[]{:S(2)}) copy-start(s32[64,4]{0,1:T(4,128)} %param.13) | copy-start | bytes 3076
  39.7 26.0 %all-to-all-start = ((bf16[8,608,128]{2,1,0:T(8,128)(2,1)}), bf16[8,608,128]{2,1,0:T(8,128)(2,1)S(1)}, u32[]{:S(2)}, u32[]{:S(2)}) async-start(bf16[8,608,128]{2,1,0:T(8,128)(2,1)} %get-tuple-element.35), calls=%async_computation | async-start | bytes 2490368 | tf_op jit(solution)/shard_map/all_to_all | solution.py:437
  46.7 19.0 %collective-permute-start.8 = (bf16[8,512,128]{2,1,0:T(8,128)(2,1)S(1)}, bf16[8,512,128]{2,1,0:T(8,128)(2,1)}, u32[]{:S(2)}, u32[]{:S(2)}) collective-permute-start(bf16[8,512,128]{2,1,0:T(8,128)(2,1)S(1)} %get-tuple-element.38.rest_0_), channel_id=1, source_target_pairs={{32,0},{33,1},{34,2},{35,3},{36,4},{37,5},{38,6},{39,7},{40,8},{41... | collective-permute-start | bytes 3145736 | tf_op jit(solution)/shard_map/ppermute | solution.py:280
  59.7 6.0 %collective-permute-start.9 = (bf16[8,512,128]{2,1,0:T(8,128)(2,1)S(1)}, bf16[8,512,128]{2,1,0:T(8,128)(2,1)}, u32[]{:S(2)}, u32[]{:S(2)}) collective-permute-start(bf16[8,512,128]{2,1,0:T(8,128)(2,1)S(1)} %collective-permute-done.6.rest_1_), channel_id=1, source_target_pairs={{32,0},{33,1},{34,2},{35,3},{36,4},{37,5},{38,6},{39,7},{40,8},{41... | collective-permute-start | bytes 3145736 | tf_op jit(solution)/shard_map/ppermute | solution.py:280
  63.2 3.0 %collective-permute-start.10 = (bf16[8,512,128]{2,1,0:T(8,128)(2,1)}, bf16[8,512,128]{2,1,0:T(8,128)(2,1)}, u32[]{:S(2)}, u32[]{:S(2)}) collective-permute-start(bf16[8,512,128]{2,1,0:T(8,128)(2,1)} %collective-permute-done.7.rest_2_), channel_id=1, source_target_pairs={{32,0},{33,1},{34,2},{35,3},{36,4},{37,5},{38,6},{39,7},{40,8},{41... | collective-permute-start | bytes 3145736 | tf_op jit(solution)/shard_map/ppermute | solution.py:280
  64.3 4.9 %collective-permute-start.13 = (bf16[4,512,128]{2,1,0:T(8,128)(2,1)}, bf16[4,512,128]{2,1,0:T(8,128)(2,1)}, u32[]{:S(2)}, u32[]{:S(2)}) collective-permute-start(bf16[4,512,128]{2,1,0:T(8,128)(2,1)} %collective-permute-done.11.rest_0_), channel_id=1, source_target_pairs={{32,0},{33,1},{34,2},{35,3},{36,4},{37,5},{38,6},{39,7},{40,8},{41... | collective-permute-start | bytes 1572872 | tf_op jit(solution)/shard_map/ppermute | solution.py:280
  64.9 4.3 %collective-permute-start.14 = (bf16[4,512,128]{2,1,0:T(8,128)(2,1)}, bf16[4,512,128]{2,1,0:T(8,128)(2,1)}, u32[]{:S(2)}, u32[]{:S(2)}) collective-permute-start(bf16[4,512,128]{2,1,0:T(8,128)(2,1)} %collective-permute-done.12.rest_1_), channel_id=1, source_target_pairs={{32,0},{33,1},{34,2},{35,3},{36,4},{37,5},{38,6},{39,7},{40,8},{41... | collective-permute-start | bytes 1572872 | tf_op jit(solution)/shard_map/ppermute | solution.py:280
  74.9 21.0 %copy-start.1 = (f32[34,64,256]{2,1,0:T(8,128)S(1)}, f32[34,64,256]{2,1,0:T(8,128)}, u32[]{:S(2)}) copy-start(f32[34,64,256]{2,1,0:T(8,128)} %get-tuple-element.33.prior_ref) | copy-start | bytes 6684676
  (2 other events, 7.6 us)

commit v13 on v12

--- a/solution.py
+++ b/solution.py
@@ -235,7 +235,7 @@
         ret_ref[:, here, :] = total.astype(BF16).reshape(group, count, TILE)
         return carry
 
-    lax.fori_loop(0, tiles, one, 0, unroll=3)
+    lax.fori_loop(0, tiles, one, 0, unroll=9)
 
 
 def final_kernel(prior_ref, inc_ref, coef_ref, out_ref, v_ref):

time: 99.2 us -> 98.2 us (0.990)
  Pallas kernels: 26.8 us -> 25.8 us
where the time goes in v13:
time: 98.2 us; the launch traced here: 97.9 us
  starting transfers between devices  31.7 us (32%)
  Pallas kernels  25.8 us (26%)
  blocking collectives  21 us (21%)
  waiting for transfers between devices  17.9 us (18%)
    all_to_all x1, blocking collectives, body(): lax.all_to_all(increments, 'mem', split_axis=0, concat_axis=0, tiled=True)  21 us
    ppermute x13, starting transfers between devices, fetch(): return lax.ppermute(value, AXES, pairs)  20.7 us
    ppermute x13, waiting for transfers between devices, fetch(): return lax.ppermute(value, AXES, pairs)  17.9 us
    all_to_all x1, starting transfers between devices, body(): lax.all_to_all(payload, 'mem', split_axis=0, concat_axis=0, tiled=True)  7.04 us
    pallas_call x1, Pallas kernels, body(): pl.pallas_call(interior_kernel, out_shape=[pltpu.HBM((rows + 2, *row), F3...  5.97 us
    pallas_call x1, Pallas kernels, body(): pl.pallas_call(analysis_kernel, out_shape=jax.ShapeDtypeStruct((group, ti...  4.64 us
    pallas_call x1, Pallas kernels, body(): pl.pallas_call(edge_kernel, out_shape=[pltpu.HBM(prior.shape, F32), pltpu...  4.04 us
    pallas_call x1, Pallas kernels, body(): pl.pallas_call(collect_kernel, out_shape=[jax.ShapeDtypeStruct((2, sum((v...  3.04 us
  transfers between devices with their start and end apart: 16, of which 4 were waited for; matrix products, arithmetic and copies ran while one was open for 1% of the time, Pallas kernels for 16%

profile of v13, /device:TPU:1, one launch (start us, length us, event | category | flops | bytes accessed | tf_op | source)
XLA Modules:
  0.0 97.9 jit_solution(7127165410782774763)
XLA Ops:
  0.0 1.7 %pack_obs.1 = (bf16[1,512,128]{2,1,0:T(8,128)(2,1)}, f32[8,128]{1,0:T(8,128)}) custom-call(bf16[1,128,512]{2,1,0:T(8,128)(2,1)} %anom_ref.1, bf16[1,128,512]{2,1,0:T(8,128)(2,1)} %weight_ref.1), custom_call_target="tpu_custom_call" | custom-call | tf_op jit(solution)/shard_map/pack_obs/pallas_call | solution.py:367
  1.7 7.8 %collective-permute-start.2 = (bf16[1,512,128]{2,1,0:T(8,128)(2,1)}, bf16[1,512,128]{2,1,0:T(8,128)(2,1)S(1)}, u32[]{:S(2)}, u32[]{:S(2)}) collective-permute-start(bf16[1,512,128]{2,1,0:T(8,128)(2,1)} %get-tuple-element.27.own_ref), channel_id=1, source_target_pairs={{4,0},{5,1},{6,2},{7,3},{0,4},{1,5},{2,6},{3,7},{12,8},{13,9},{14,... | collective-permute-start | bytes 393224 | tf_op jit(solution)/shard_map/ppermute | solution.py:280
  9.5 2.3 %pack_halo.1 = (f32[328,256]{1,0:T(8,128)}, f32[328,256]{1,0:T(8,128)}) custom-call(f32[64,32,256]{2,1,0:T(8,128)} %x_ref.1, f32[64,32,256]{2,1,0:T(8,128)} %x_ref.1, f32[32,256]{1,0:T(8,128)} %coef_ref.7, s32[4,64]{1,0:T(4,128)} %bitcast.2, s32[4,64]{1,0:T(4,128)} %bitcast.3, f32[8,128]{1,0:T(8,128)} %get-tuple-element.24.after_ref), custom_call_target="tpu_custom_call" | custom-call | tf_op jit(solution)/shard_map/pack_halo/pallas_call | solution.py:375
  11.8 2.7 %collective-permute-start = (f32[328,256]{1,0:T(8,128)}, f32[328,256]{1,0:T(8,128)S(1)}, u32[]{:S(2)}, u32[]{:S(2)}) collective-permute-start(f32[328,256]{1,0:T(8,128)} %get-tuple-element.25), channel_id=1, source_target_pairs={{0,1},{1,2},{2,3},{3,4},{4,5},{5,6},{6,7},{7,8},{8,9},{9,10},{10,1... | collective-permute-start | bytes 1007624 | tf_op jit(solution)/shard_map/ppermute | solution.py:391
  14.5 1.3 %collective-permute-start.1 = (f32[328,256]{1,0:T(8,128)}, f32[328,256]{1,0:T(8,128)S(1)}, u32[]{:S(2)}, u32[]{:S(2)}) collective-permute-start(f32[328,256]{1,0:T(8,128)} %get-tuple-element.26), channel_id=1, source_target_pairs={{1,0},{2,1},{3,2},{4,3},{5,4},{6,5},{7,6},{8,7},{9,8},{10,9},{11,1... | collective-permute-start | bytes 1007624 | tf_op jit(solution)/shard_map/ppermute | solution.py:390
  15.9 3.6 %collective-permute-start.3 = (bf16[2,512,128]{2,1,0:T(8,128)(2,1)S(1)}, bf16[2,512,128]{2,1,0:T(8,128)(2,1)S(1)}, u32[]{:S(2)}, u32[]{:S(2)}) collective-permute-start(bf16[2,512,128]{2,1,0:T(8,128)(2,1)S(1)} %get-tuple-element.36.refs_0_), channel_id=1, source_target_pairs={{8,0},{9,1},{10,2},{11,3},{12,4},{13,5},{14,6},{15,7},{16,8},{17,9... | collective-permute-start | bytes 786440 | tf_op jit(solution)/shard_map/ppermute | solution.py:280
  19.5 2.1 %collective-permute-start.5 = (bf16[2,512,128]{2,1,0:T(8,128)(2,1)S(1)}, bf16[2,512,128]{2,1,0:T(8,128)(2,1)S(1)}, u32[]{:S(2)}, u32[]{:S(2)}) collective-permute-start(bf16[2,512,128]{2,1,0:T(8,128)(2,1)S(1)} %get-tuple-element.36.refs_0_), channel_id=1, source_target_pairs={{16,0},{17,1},{18,2},{19,3},{20,4},{21,5},{22,6},{23,7},{24,8},{25... | collective-permute-start | bytes 786440 | tf_op jit(solution)/shard_map/ppermute | solution.py:280
  21.6 6.0 %forecast_interior.1 = (f32[34,64,256]{2,1,0:T(8,128)}, bf16[8,608,128]{2,1,0:T(8,128)(2,1)}, f32[16,64,256]{2,1,0:T(8,128)S(1)}, f32[8,32,128]{2,1,0:T(8,128)S(1)}, f32[8,128,128]{2,1,0:T(8,128)}) custom-call(f32[64,32,256]{2,1,0:T(8,128)S(1)} %copy-done, f32[32,256]{1,0:T(8,128)S(1)} %copy-done.2, f32[8,128,128]{2,1,0:T(8,128)S(1)} %copy-done.4, ...), custom_call_target="tpu_custom_call" | custom-call | tf_op jit(solution)/shard_map/forecast_interior/pallas_call | solution.py:395
  27.6 4.0 %forecast_edges.1 = (f32[34,64,256]{2,1,0:T(8,128)}, bf16[8,608,128]{2,1,0:T(8,128)(2,1)}, f32[8,128]{1,0:T(8,128)S(1)}) custom-call(f32[328,256]{1,0:T(8,128)S(1)} %collective-permute-done.above_ref, f32[328,256]{1,0:T(8,128)S(1)} %collective-permute-done.1.below_ref, f32[32,256]{1,0:T(8,128)S(1)} %copy-done.2, ...), custom_call_target="tpu_custom_call", output_to_operand_aliasing={{0}: (5, {}), {1}: (6, {})} | custom-call | tf_op jit(solution)/shard_map/forecast_edges/pallas_call | solution.py:417
  31.7 0.9 collective-permute-done.5.refs_3_
  32.6 1.2 %join_eight.1 = (bf16[8,512,128]{2,1,0:T(8,128)(2,1)S(1)}, bf16[4,512,128]{2,1,0:T(8,128)(2,1)}, bf16[4,512,128]{2,1,0:T(8,128)(2,1)}) custom-call(bf16[2,512,128]{2,1,0:T(8,128)(2,1)S(1)} %get-tuple-element.36.refs_0_, bf16[2,512,128]{2,1,0:T(8,128)(2,1)S(1)} %collective-permute-done.3.refs_1_, bf16[2,512,128]{2,1,0:T(8,128)(2,1)S(1)} %collective-permute-done.4.refs_2_, ...), custom_call_target="tpu_custom_call" | custom-call | tf_op jit(solution)/shard_map/join_eight/pallas_call | solution.py:307
  33.7 3.0 %collective-permute-start.6 = (bf16[8,512,128]{2,1,0:T(8,128)(2,1)S(1)}, bf16[8,512,128]{2,1,0:T(8,128)(2,1)S(1)}, u32[]{:S(2)}, u32[]{:S(2)}) collective-permute-start(bf16[8,512,128]{2,1,0:T(8,128)(2,1)S(1)} %get-tuple-element.38.rest_0_), channel_id=1, source_target_pairs={{1,0},{2,1},{3,2},{4,3},{5,4},{6,5},{7,6},{0,7},{9,8},{10,9},{11,1... | collective-permute-start | bytes 3145736 | tf_op jit(solution)/shard_map/ppermute | solution.py:280
  36.7 1.6 %collective-permute-start.11 = (bf16[4,512,128]{2,1,0:T(8,128)(2,1)}, bf16[4,512,128]{2,1,0:T(8,128)(2,1)}, u32[]{:S(2)}, u32[]{:S(2)}) collective-permute-start(bf16[4,512,128]{2,1,0:T(8,128)(2,1)} %get-tuple-element.41), channel_id=1, source_target_pairs={{2,0},{3,1},{4,2},{5,3},{6,4},{7,5},{0,6},{1,7},{10,8},{11,9},{12,... | collective-permute-start | bytes 1572872 | tf_op jit(solution)/shard_map/ppermute | solution.py:280
  38.4 1.3 %collective-permute-start.12 = (bf16[4,512,128]{2,1,0:T(8,128)(2,1)}, bf16[4,512,128]{2,1,0:T(8,128)(2,1)}, u32[]{:S(2)}, u32[]{:S(2)}) collective-permute-start(bf16[4,512,128]{2,1,0:T(8,128)(2,1)} %get-tuple-element.42), channel_id=1, source_target_pairs={{6,0},{7,1},{0,2},{1,3},{2,4},{3,5},{4,6},{5,7},{14,8},{15,9},{8,1... | collective-permute-start | bytes 1572872 | tf_op jit(solution)/shard_map/ppermute | solution.py:280
  39.7 7.0 %all-to-all-start = ((bf16[8,608,128]{2,1,0:T(8,128)(2,1)}), bf16[8,608,128]{2,1,0:T(8,128)(2,1)S(1)}, u32[]{:S(2)}, u32[]{:S(2)}) async-start(bf16[8,608,128]{2,1,0:T(8,128)(2,1)} %get-tuple-element.35), calls=%async_computation | async-start | bytes 2490368 | tf_op jit(solution)/shard_map/all_to_all | solution.py:437
  46.7 13.0 %collective-permute-done.6.rest_1_ = bf16[8,512,128]{2,1,0:T(8,128)(2,1)S(1)} collective-permute-done((bf16[8,512,128]{2,1,0:T(8,128)(2,1)S(1)}, bf16[8,512,128]{2,1,0:T(8,128)(2,1)S(1)}, u32[]{:S(2)}, u32[]{:S(2)}) %collective-permute-start.6) | collective-permute-done | bytes 1048608 | tf_op jit(solution)/shard_map/ppermute | solution.py:280
  59.7 3.5 %collective-permute-done.7.rest_2_ = bf16[8,512,128]{2,1,0:T(8,128)(2,1)} collective-permute-done((bf16[8,512,128]{2,1,0:T(8,128)(2,1)S(1)}, bf16[8,512,128]{2,1,0:T(8,128)(2,1)}, u32[]{:S(2)}, u32[]{:S(2)}) %collective-permute-start.7) | collective-permute-done | bytes 1048608 | tf_op jit(solution)/shard_map/ppermute | solution.py:280
  63.5 0.7 fusion.12
  64.3 0.6 collective-permute-start.13
  64.9 0.7 collective-permute-start.14
  66.2 3.0 %collect.1 = (bf16[2,24,512,128]{3,2,1,0:T(8,128)(2,1)S(1)}, bf16[9,512,128]{2,1,0:T(8,128)(2,1)S(1)}) custom-call(bf16[8,608,128]{2,1,0:T(8,128)(2,1)S(1)} %all-to-all-done.recv_ref, bf16[8,512,128]{2,1,0:T(8,128)(2,1)S(1)} %get-tuple-element.38.rest_0_, bf16[8,512,128]{2,1,0:T(8,128)(2,1)S(1)} %collective-permute-done.6.rest_1_, ...), custom_call_target="tpu_custom_call" | custom-call | tf_op jit(solution)/shard_map/collect/pallas_call | solution.py:448
  69.3 4.6 %analysis.1 = bf16[8,576,128]{2,1,0:T(8,128)(2,1)S(1)} custom-call(s32[9,4]{1,0:T(8,128)S(1)} %get-tuple-element.44.anom_at_ref, s32[9,4]{1,0:T(8,128)S(1)} %get-tuple-element.43.weight_at_ref, s32[9,4]{1,0:T(8,128)S(1)} %pad_add_fusion.1.tapers_ref, f32[8,128,128]{2,1,0:T(8,128)S(1)} %copy-done.3, bf16[9,512,128]{2,1,0:T(8,128)(2,1)S(1)} %get-tuple-element.39.centred_ref, ...), custom_call_target="tpu_custom_call" | custom-call | tf_op jit(solution)/shard_map/analysis/pallas_call | solution.py:459
  73.9 21.0 %all_to_all.10.inc_ref = bf16[8,576,128]{2,1,0:T(8,128)(2,1)S(1)} all-to-all(bf16[8,576,128]{2,1,0:T(8,128)(2,1)S(1)} %analysis.1), channel_id=1, replica_groups=mesh['mem'=8,'state'=32] {'mem'}, dimensions={0} | all-to-all | bytes 2359296 | tf_op jit(solution)/shard_map/all_to_all | solution.py:468
  95.0 2.9 %final_step.1 = f32[64,32,256]{2,1,0:T(8,128)} custom-call(f32[34,64,256]{2,1,0:T(8,128)S(1)} %copy-done.1, bf16[8,576,128]{2,1,0:T(8,128)(2,1)S(1)} %all_to_all.10.inc_ref, f32[32,256]{1,0:T(8,128)S(1)} %copy-done.2), custom_call_target="tpu_custom_call" | custom-call | tf_op jit(solution)/shard_map/final_step/pallas_call | solution.py:470
  (49 shorter events, 1.0 us)
Async XLA Ops:
  1.7 14.1 %collective-permute-start.2 = (bf16[1,512,128]{2,1,0:T(8,128)(2,1)}, bf16[1,512,128]{2,1,0:T(8,128)(2,1)S(1)}, u32[]{:S(2)}, u32[]{:S(2)}) collective-permute-start(bf16[1,512,128]{2,1,0:T(8,128)(2,1)} %get-tuple-element.27.own_ref), channel_id=1, source_target_pairs={{4,0},{5,1},{6,2},{7,3},{0,4},{1,5},{2,6},{3,7},{12,8},{13,9},{14,... | collective-permute-start | bytes 393224 | tf_op jit(solution)/shard_map/ppermute | solution.py:280
  9.5 6.3 %copy-start.7 = (bf16[1,512,128]{2,1,0:T(8,128)(2,1)S(1)}, bf16[1,512,128]{2,1,0:T(8,128)(2,1)}, u32[]{:S(2)}) copy-start(bf16[1,512,128]{2,1,0:T(8,128)(2,1)} %get-tuple-element.27.own_ref) | copy-start | bytes 393220
  9.5 12.1 %copy-start = (f32[64,32,256]{2,1,0:T(8,128)S(1)}, f32[64,32,256]{2,1,0:T(8,128)}, u32[]{:S(2)}) copy-start(f32[64,32,256]{2,1,0:T(8,128)} %x_ref.1) | copy-start | bytes 6291460
  9.5 12.1 %copy-start.2 = (f32[32,256]{1,0:T(8,128)S(1)}, f32[32,256]{1,0:T(8,128)}, u32[]{:S(2)}) copy-start(f32[32,256]{1,0:T(8,128)} %coef_ref.7) | copy-start | bytes 98308
  9.5 12.1 %copy-start.4 = (f32[8,128,128]{2,1,0:T(8,128)S(1)}, f32[8,128,128]{2,1,0:T(8,128)}, u32[]{:S(2)}) copy-start(f32[8,128,128]{2,1,0:T(8,128)} %taper_ref.1) | copy-start | bytes 1572868
  11.8 15.7 %collective-permute-start = (f32[328,256]{1,0:T(8,128)}, f32[328,256]{1,0:T(8,128)S(1)}, u32[]{:S(2)}, u32[]{:S(2)}) collective-permute-start(f32[328,256]{1,0:T(8,128)} %get-tuple-element.25), channel_id=1, source_target_pairs={{0,1},{1,2},{2,3},{3,4},{4,5},{5,6},{6,7},{7,8},{8,9},{9,10},{10,1... | collective-permute-start | bytes 1007624 | tf_op jit(solution)/shard_map/ppermute | solution.py:391
  14.5 13.1 %collective-permute-start.1 = (f32[328,256]{1,0:T(8,128)}, f32[328,256]{1,0:T(8,128)S(1)}, u32[]{:S(2)}, u32[]{:S(2)}) collective-permute-start(f32[328,256]{1,0:T(8,128)} %get-tuple-element.26), channel_id=1, source_target_pairs={{1,0},{2,1},{3,2},{4,3},{5,4},{6,5},{7,6},{8,7},{9,8},{10,9},{11,1... | collective-permute-start | bytes 1007624 | tf_op jit(solution)/shard_map/ppermute | solution.py:390
  15.9 15.8 %collective-permute-start.3 = (bf16[2,512,128]{2,1,0:T(8,128)(2,1)S(1)}, bf16[2,512,128]{2,1,0:T(8,128)(2,1)S(1)}, u32[]{:S(2)}, u32[]{:S(2)}) collective-permute-start(bf16[2,512,128]{2,1,0:T(8,128)(2,1)S(1)} %get-tuple-element.36.refs_0_), channel_id=1, source_target_pairs={{8,0},{9,1},{10,2},{11,3},{12,4},{13,5},{14,6},{15,7},{16,8},{17,9... | collective-permute-start | bytes 786440 | tf_op jit(solution)/shard_map/ppermute | solution.py:280
  19.5 12.2 %collective-permute-start.4 = (bf16[2,512,128]{2,1,0:T(8,128)(2,1)S(1)}, bf16[2,512,128]{2,1,0:T(8,128)(2,1)S(1)}, u32[]{:S(2)}, u32[]{:S(2)}) collective-permute-start(bf16[2,512,128]{2,1,0:T(8,128)(2,1)S(1)} %get-tuple-element.36.refs_0_), channel_id=1, source_target_pairs={{24,0},{25,1},{26,2},{27,3},{28,4},{29,5},{30,6},{31,7},{0,8},{1,9... | collective-permute-start | bytes 786440 | tf_op jit(solution)/shard_map/ppermute | solution.py:280
  19.5 13.1 %collective-permute-start.5 = (bf16[2,512,128]{2,1,0:T(8,128)(2,1)S(1)}, bf16[2,512,128]{2,1,0:T(8,128)(2,1)S(1)}, u32[]{:S(2)}, u32[]{:S(2)}) collective-permute-start(bf16[2,512,128]{2,1,0:T(8,128)(2,1)S(1)} %get-tuple-element.36.refs_0_), channel_id=1, source_target_pairs={{16,0},{17,1},{18,2},{19,3},{20,4},{21,5},{22,6},{23,7},{24,8},{25... | collective-permute-start | bytes 786440 | tf_op jit(solution)/shard_map/ppermute | solution.py:280
  27.6 4.1 %copy-start.5 = (f32[328,256]{1,0:T(8,128)}, f32[328,256]{1,0:T(8,128)S(1)}, u32[]{:S(2)}) copy-start(f32[328,256]{1,0:T(8,128)S(1)} %collective-permute-done.above_ref) | copy-start | bytes 1007620
  33.7 25.9 %collective-permute-start.6 = (bf16[8,512,128]{2,1,0:T(8,128)(2,1)S(1)}, bf16[8,512,128]{2,1,0:T(8,128)(2,1)S(1)}, u32[]{:S(2)}, u32[]{:S(2)}) collective-permute-start(bf16[8,512,128]{2,1,0:T(8,128)(2,1)S(1)} %get-tuple-element.38.rest_0_), channel_id=1, source_target_pairs={{1,0},{2,1},{3,2},{4,3},{5,4},{6,5},{7,6},{0,7},{9,8},{10,9},{11,1... | collective-permute-start | bytes 3145736 | tf_op jit(solution)/shard_map/ppermute | solution.py:280
  36.7 26.5 %collective-permute-start.7 = (bf16[8,512,128]{2,1,0:T(8,128)(2,1)S(1)}, bf16[8,512,128]{2,1,0:T(8,128)(2,1)}, u32[]{:S(2)}, u32[]{:S(2)}) collective-permute-start(bf16[8,512,128]{2,1,0:T(8,128)(2,1)S(1)} %get-tuple-element.38.rest_0_), channel_id=1, source_target_pairs={{7,0},{0,1},{1,2},{2,3},{3,4},{4,5},{5,6},{6,7},{15,8},{8,9},{9,10... | collective-permute-start | bytes 3145736 | tf_op jit(solution)/shard_map/ppermute | solution.py:280
  36.7 27.6 %collective-permute-start.11 = (bf16[4,512,128]{2,1,0:T(8,128)(2,1)}, bf16[4,512,128]{2,1,0:T(8,128)(2,1)}, u32[]{:S(2)}, u32[]{:S(2)}) collective-permute-start(bf16[4,512,128]{2,1,0:T(8,128)(2,1)} %get-tuple-element.41), channel_id=1, source_target_pairs={{2,0},{3,1},{4,2},{5,3},{6,4},{7,5},{0,6},{1,7},{10,8},{11,9},{12,... | collective-permute-start | bytes 1572872 | tf_op jit(solution)/shard_map/ppermute | solution.py:280
  38.4 26.6 %collective-permute-start.12 = (bf16[4,512,128]{2,1,0:T(8,128)(2,1)}, bf16[4,512,128]{2,1,0:T(8,128)(2,1)}, u32[]{:S(2)}, u32[]{:S(2)}) collective-permute-start(bf16[4,512,128]{2,1,0:T(8,128)(2,1)} %get-tuple-element.42), channel_id=1, source_target_pairs={{6,0},{7,1},{0,2},{1,3},{2,4},{3,5},{4,6},{5,7},{14,8},{15,9},{8,1... | collective-permute-start | bytes 1572872 | tf_op jit(solution)/shard_map/ppermute | solution.py:280
  39.7 23.5 %copy-start.8 = (s32[64,4]{0,1:T(4,128)S(1)}, s32[64,4]{0,1:T(4,128)}, u32[]{:S(2)}) copy-start(s32[64,4]{0,1:T(4,128)} %param.12) | copy-start | bytes 3076
  39.7 23.5 %copy-start.9 = (s32[64,4]{0,1:T(4,128)S(1)}, s32[64,4]{0,1:T(4,128)}, u32[]{:S(2)}) copy-start(s32[64,4]{0,1:T(4,128)} %param.13) | copy-start | bytes 3076
  39.7 26.0 %all-to-all-start = ((bf16[8,608,128]{2,1,0:T(8,128)(2,1)}), bf16[8,608,128]{2,1,0:T(8,128)(2,1)S(1)}, u32[]{:S(2)}, u32[]{:S(2)}) async-start(bf16[8,608,128]{2,1,0:T(8,128)(2,1)} %get-tuple-element.35), calls=%async_computation | async-start | bytes 2490368 | tf_op jit(solution)/shard_map/all_to_all | solution.py:437
  46.7 19.0 %collective-permute-start.8 = (bf16[8,512,128]{2,1,0:T(8,128)(2,1)S(1)}, bf16[8,512,128]{2,1,0:T(8,128)(2,1)}, u32[]{:S(2)}, u32[]{:S(2)}) collective-permute-start(bf16[8,512,128]{2,1,0:T(8,128)(2,1)S(1)} %get-tuple-element.38.rest_0_), channel_id=1, source_target_pairs={{32,0},{33,1},{34,2},{35,3},{36,4},{37,5},{38,6},{39,7},{40,8},{41... | collective-permute-start | bytes 3145736 | tf_op jit(solution)/shard_map/ppermute | solution.py:280
  59.7 6.0 %collective-permute-start.9 = (bf16[8,512,128]{2,1,0:T(8,128)(2,1)S(1)}, bf16[8,512,128]{2,1,0:T(8,128)(2,1)}, u32[]{:S(2)}, u32[]{:S(2)}) collective-permute-start(bf16[8,512,128]{2,1,0:T(8,128)(2,1)S(1)} %collective-permute-done.6.rest_1_), channel_id=1, source_target_pairs={{32,0},{33,1},{34,2},{35,3},{36,4},{37,5},{38,6},{39,7},{40,8},{41... | collective-permute-start | bytes 3145736 | tf_op jit(solution)/shard_map/ppermute | solution.py:280
  63.2 3.0 %collective-permute-start.10 = (bf16[8,512,128]{2,1,0:T(8,128)(2,1)}, bf16[8,512,128]{2,1,0:T(8,128)(2,1)}, u32[]{:S(2)}, u32[]{:S(2)}) collective-permute-start(bf16[8,512,128]{2,1,0:T(8,128)(2,1)} %collective-permute-done.7.rest_2_), channel_id=1, source_target_pairs={{32,0},{33,1},{34,2},{35,3},{36,4},{37,5},{38,6},{39,7},{40,8},{41... | collective-permute-start | bytes 3145736 | tf_op jit(solution)/shard_map/ppermute | solution.py:280
  64.3 4.9 %collective-permute-start.13 = (bf16[4,512,128]{2,1,0:T(8,128)(2,1)}, bf16[4,512,128]{2,1,0:T(8,128)(2,1)}, u32[]{:S(2)}, u32[]{:S(2)}) collective-permute-start(bf16[4,512,128]{2,1,0:T(8,128)(2,1)} %collective-permute-done.11.rest_0_), channel_id=1, source_target_pairs={{32,0},{33,1},{34,2},{35,3},{36,4},{37,5},{38,6},{39,7},{40,8},{41... | collective-permute-start | bytes 1572872 | tf_op jit(solution)/shard_map/ppermute | solution.py:280
  64.9 4.3 %collective-permute-start.14 = (bf16[4,512,128]{2,1,0:T(8,128)(2,1)}, bf16[4,512,128]{2,1,0:T(8,128)(2,1)}, u32[]{:S(2)}, u32[]{:S(2)}) collective-permute-start(bf16[4,512,128]{2,1,0:T(8,128)(2,1)} %collective-permute-done.12.rest_1_), channel_id=1, source_target_pairs={{32,0},{33,1},{34,2},{35,3},{36,4},{37,5},{38,6},{39,7},{40,8},{41... | collective-permute-start | bytes 1572872 | tf_op jit(solution)/shard_map/ppermute | solution.py:280
  73.9 21.0 %copy-start.1 = (f32[34,64,256]{2,1,0:T(8,128)S(1)}, f32[34,64,256]{2,1,0:T(8,128)}, u32[]{:S(2)}) copy-start(f32[34,64,256]{2,1,0:T(8,128)} %get-tuple-element.33.prior_ref) | copy-start | bytes 6684676
  (2 other events, 7.6 us)
